TPU v7x, 128 devices: a whole 4x4x4 slice. The times are simulated.
128 devices in a mesh: row: 8 (over y, z_hi), col: 16 (over x, z_lo, core).
Axes of the slice: x: 4, y: 4, z: 4 (z_hi: 2, z_lo: 2; z = z_hi * 2 + z_lo), core: 2. Of those that a mesh axis runs over, the one named last changes fastest.
Arguments:
- parent_front: bfloat16 [28672, 28672], P('row', 'col'), may hold values from -6 to 6
- child_update: bfloat16 [2, 14336, 14336], P(None, 'row', 'col'), may hold values from -6 to 6
- parent_test: bfloat16 [28672, 448], P('col'), may hold values from -0.03125 to 0.03125
- child_test: bfloat16 [2, 14336, 448], P(None, 'col'), may hold values from -0.046875 to 0.046875
- child_map: int32 [2, 112], replicated, may hold values from 0 to 223, as said below
Outputs:
- leaf_basis: bfloat16 [224, 128, 448], P('row', 'col')
- couplings: float32 [32, 448, 448], P('row', 'col')
Inputs may be any that keep to these rules, and one draw needn't show every extreme that they name: `child_map`: for each child the entries rise strictly along its blocks, and entry j is at least j.
All inputs are finite; a program needn't handle non-finite values.
Results may differ from a plain program's by a relative error of at most 0.006.
Values may be sent and summed in bfloat16 or wider, within the bound.
No kernel may reach another device: no remote copies, remote signals or barrier semaphores. Data moves between devices by JAX's collectives and lax.ppermute only.
A program may use at most 192 MiB of HBM per device.

v0:
```python
import math

import jax
import jax.numpy as jnp
from jax import lax
from jax.sharding import Mesh
from jax.sharding import PartitionSpec as P

LEAF = 896
BLOCK = 128
ROW = ("row_0", "row_1")


HIGH = lax.Precision.HIGHEST


def in_blocks(shard, dim, devices):
    dims = shard.shape
    parts = shard.reshape(*dims[:dim], devices, dims[dim] // devices, *dims[dim + 1 :])
    return jnp.moveaxis(parts, dim, 0)


def one_scatter(arrays, axis, dims):
    devices = lax.axis_size(axis)
    parts = [in_blocks(a, dim, devices) for a, dim in zip(arrays, dims)]
    lines = jnp.concatenate([b.reshape(devices, -1) for b in parts], axis=1)
    width = max(16, -(-lines.shape[1] // 1024) * 8)
    lines = jnp.pad(lines, ((0, 0), (0, width * 128 - lines.shape[1]))).reshape(-1, 128)
    ravelled, at, gathered = (lax.psum_scatter(lines, axis, tiled=True).reshape(-1), 0, [])
    for b in parts:
        part = b[0]
        gathered.append(ravelled[at : at + part.size].reshape(part.shape))
        at += part.size
    return tuple(gathered)


def gather_axes(shard, axes, dim):
    for axis in reversed(axes):
        shard = lax.all_gather(shard, axis, axis=dim, tiled=True)
    return shard


def finish(leaves, gram_matrix):
    factor = jnp.linalg.cholesky(gram_matrix)
    solved = lax.linalg.triangular_solve(
        factor, leaves, left_side=False, lower=True, transpose_a=True
    )
    return (solved * math.sqrt(LEAF)).astype(jnp.bfloat16)


def local(parent_front, child_update, parent_test, child_test, child_map):
    row_count = lax.axis_size(ROW)
    col_count = lax.axis_size("col")
    row_index = lax.axis_index(ROW)
    col_index = lax.axis_index("col")
    slab_rows = BLOCK // col_count
    own_blocks = parent_front.shape[0] // BLOCK
    kid_blocks = child_update.shape[1] // BLOCK
    probes = parent_test.shape[1]
    own_probe = jnp.dot(parent_front, parent_test, preferred_element_type=jnp.float32)
    own_probe = own_probe.reshape(own_blocks, BLOCK, probes)
    kid_probe = jnp.stack(
        [
            jnp.dot(child_update[which], child_test[which], preferred_element_type=jnp.float32)
            for which in range(2)
        ]
    )
    kid_probe = kid_probe.reshape(2, kid_blocks, BLOCK, probes)
    own_share, kid_share = one_scatter((own_probe, kid_probe), "col", (1, 2))
    first_block = row_index * own_blocks
    targets = jnp.arange(own_blocks, dtype=jnp.int32)
    mapped = child_map - first_block
    onehot = (mapped[:, None, :] == targets[None, :, None]).astype(jnp.float32)
    sample = own_share + jnp.einsum(
        "cpn,cnsr->psr", onehot, gather_axes(kid_share, ROW, 1), precision=HIGH
    )
    per_leaf = LEAF // BLOCK
    leaf_count = own_blocks // per_leaf
    leaves = sample.reshape(leaf_count, per_leaf * slab_rows, probes)
    whole_sample = lax.all_gather(sample, "col", axis=1, tiled=True)
    whole_leaves = whole_sample.reshape(leaf_count, LEAF, probes)
    gram_matrix = jnp.einsum("lkr,lks->lrs", whole_leaves, whole_leaves, precision=HIGH)
    leaf_basis = finish(leaves, gram_matrix).reshape(own_blocks, slab_rows, probes)
    whole_basis = lax.all_gather(leaf_basis, "col", axis=1, tiled=True)
    bases = whole_basis.reshape(leaf_count, LEAF, probes)
    col_leaves = parent_front.shape[1] // LEAF
    shrink = 1.0 / math.sqrt(LEAF)

    def sibling_product(position):
        leaf_index = col_index * col_leaves + position
        sibling = jnp.bitwise_xor(leaf_index, 1)
        row_start = leaf_index % leaf_count * LEAF
        col_start = (sibling - col_index * col_leaves) * LEAF
        front_tile = lax.dynamic_slice(parent_front, (row_start, col_start), (LEAF, LEAF))
        product = (
            jnp.dot(front_tile, bases[sibling % leaf_count], preferred_element_type=jnp.float32)
            * shrink
        )
        return product.astype(jnp.bfloat16)

    products = lax.map(sibling_product, jnp.arange(col_leaves, dtype=jnp.int32))
    owner_span = col_count // row_count
    own_bases = lax.dynamic_slice_in_dim(bases, col_index * col_leaves % leaf_count, col_leaves, 0)
    cores = (
        jnp.einsum("lkr,lks->lrs", own_bases, products, preferred_element_type=jnp.float32) * shrink
    )
    arrived = lax.all_to_all(
        cores.astype(jnp.bfloat16), "col", split_axis=1, concat_axis=0, tiled=True
    ).astype(cores.dtype)
    couplings = lax.dynamic_slice_in_dim(
        arrived, row_index * owner_span * col_leaves, leaf_count, 0
    )
    return (leaf_basis, couplings)


def solution(mesh):
    split = Mesh(mesh.devices.reshape(4, 2, mesh.shape["col"]), ("row_0", "row_1", "col"))
    placed = (P(ROW, "col"), P(None, ROW, "col"), P("col", None), P(None, "col", None), P())
    return jax.shard_map(
        local,
        mesh=split,
        in_specs=placed,
        out_specs=(P(ROW, "col", None), P(ROW, "col", None)),
        check_vma=False,
    )
```

profile of v0, /device:TPU:1, one launch (start us, length us, event | category | flops | bytes accessed | tf_op | source)
XLA Modules:
  0.0 918.2 jit_solution(13614437378058214146)
XLA Ops:
  7.2 3.5 fusion.63
  10.8 2.1 convolution_bitcast_fusion
  12.9 2.1 convolution_bitcast_fusion.1
  16.4 4.2 copy.125
  20.6 7.3 reshape.116
  27.9 9.5 %fusion.65 = f32[3584,448]{1,0:T(8,128)S(1)} fusion(bf16[3584,1792]{1,0:T(8,128)(2,1)} %param.7, bf16[1792,448]{0,1:T(8,128)(2,1)S(1)} %copy-done), kind=kOutput, calls=%fused_computation.108 | convolution fusion | flops 5754585088 | bytes 20873216 | tf_op jit(solution)/shard_map/dot_general | solution.py:60
  37.4 4.2 copy.124
  41.6 7.2 reshape.113
  48.8 11.0 %pad_maximum_fusion = f32[16,200704]{1,0:T(8,128)} fusion(f32[16,100352]{1,0:T(8,128)} %reshape.116, f32[16,100352]{1,0:T(8,128)} %reshape.113), kind=kLoop, calls=%fused_computation.10 | loop fusion | flops 3211264 | bytes 25690112 | tf_op jit(solution)/shard_map/concatenate | solution.py:26
  59.8 12.8 %reshape.117 = f32[25088,128]{1,0:T(8,128)} reshape(f32[16,200704]{1,0:T(8,128)} %pad_maximum_fusion) | data formatting | bytes 25690112 | tf_op jit(solution)/shard_map/reshape | solution.py:28
  72.7 144.5 %reduce-scatter.2.cloned.1.call-done = f32[1568,128]{1,0:T(8,128)} async-done(((f32[25088,128]{1,0:T(8,128)}), f32[1568,128]{1,0:T(8,128)}) %reduce-scatter.2.cloned.1.call-update) | async-done | bytes 802832 | tf_op jit(solution)/shard_map/reduce_scatter | solution.py:29
  218.6 12.2 %all_gather.12 = f32[2,28,8,448]{3,2,0,1:T(8,128)} all-gather(f32[2,14,8,448]{3,2,0,1:T(8,128)S(1)} %copy.126), channel_id=1, replica_groups=mesh['row_0'=4,'row_1'=2,'col'=16] {'row_1'}, dimensions={1}, use_global_device_ids=true | all-gather | bytes 1204224 | tf_op jit(solution)/shard_map/all_gather | solution.py:39
  231.1 44.0 %all-gather.4.cloned.1.call-done = f32[2,112,8,448]{3,2,0,1:T(8,128)} async-done(((f32[2,28,8,448]{3,2,0,1:T(8,128)}), f32[2,112,8,448]{3,2,0,1:T(8,128)}) %all-gather.4.cloned.1.call-update) | async-done | bytes 3211280 | tf_op jit(solution)/shard_map/all_gather | solution.py:39
  275.1 5.3 fusion.20
  282.2 47.4 %all-gather.6.cloned.1.call-done = f32[28,128,448]{2,1,0:T(8,128)} async-done(((f32[28,8,448]{2,1,0:T(8,128)}), f32[28,128,448]{2,1,0:T(8,128)}) %all-gather.6.cloned.1.call-update) | async-done | bytes 6422544 | tf_op jit(solution)/shard_map/all_gather | solution.py:80
  329.6 18.3 %fusion.66 = f32[4,448,448]{2,1,0:T(8,128)} fusion(f32[4,896,448]{2,1,0:T(8,128)} %bitcast.126), kind=kOutput, calls=%fused_computation.109 | convolution fusion | flops 8631877632 | bytes 9633792 | tf_op jit(solution)/shard_map/lkr,lks->lrs/dot_general | solution.py:82
  347.8 4.9 copy.132
  352.8 4.1 fusion.13
  356.8 1.8 copy-done.3
  358.7 46.9 %custom-call.34 = f32[4,128,128]{2,1,0:T(8,128)S(1)} custom-call(f32[4,128,128]{2,1,0:T(8,128)S(1)} %cholesky.281), custom_call_target="Cholesky" | custom-call | tf_op jit(solution)/shard_map/jit(cholesky)/cholesky | solution.py:44
  405.6 2.3 cholesky.236
  407.9 39.5 %custom-call.35 = f32[4,1,128,128]{2,3,1,0:T(8,128)S(1)} custom-call(f32[4,1,128,128]{3,2,1,0:T(8,128)S(1)} %select_bitcast_fusion.2), custom_call_target="InvertDiagBlocksLowerTriangular" | custom-call | tf_op jit(solution)/shard_map/jit(cholesky)/cholesky | solution.py:44
  447.4 2.7 constant_dynamic-update-slice_fusion.3
  450.1 1.8 convolution_subtract_fusion
  452.0 46.9 %custom-call.36 = f32[4,128,128]{2,1,0:T(8,128)S(1)} custom-call(f32[4,128,128]{2,1,0:T(8,128)S(1)} %cholesky.285), custom_call_target="Cholesky" | custom-call | tf_op jit(solution)/shard_map/jit(cholesky)/cholesky | solution.py:44
  499.7 39.3 %custom-call.37 = f32[4,1,128,128]{2,3,1,0:T(8,128)S(1)} custom-call(f32[4,1,128,128]{3,2,1,0:T(8,128)S(1)} %get-tuple-element.158), custom_call_target="InvertDiagBlocksLowerTriangular" | custom-call | tf_op jit(solution)/shard_map/jit(cholesky)/cholesky | solution.py:44
  540.3 2.4 convolution_subtract_fusion.1
  542.7 47.1 %custom-call.38 = f32[4,128,128]{2,1,0:T(8,128)S(1)} custom-call(f32[4,128,128]{2,1,0:T(8,128)S(1)} %cholesky.290), custom_call_target="Cholesky" | custom-call | tf_op jit(solution)/shard_map/jit(cholesky)/cholesky | solution.py:44
  590.6 39.3 %custom-call.39 = f32[4,1,128,128]{2,3,1,0:T(8,128)S(1)} custom-call(f32[4,1,128,128]{3,2,1,0:T(8,128)S(1)} %get-tuple-element.156), custom_call_target="InvertDiagBlocksLowerTriangular" | custom-call | tf_op jit(solution)/shard_map/jit(cholesky)/cholesky | solution.py:44
  630.9 1.8 convolution_subtract_fusion.2
  632.7 23.5 %custom-call.40 = f32[4,64,64]{2,1,0:T(8,128)S(1)} custom-call(f32[4,64,64]{2,1,0:T(8,128)S(1)} %convolution_subtract_fusion.2), custom_call_target="Cholesky" | custom-call | tf_op jit(solution)/shard_map/jit(cholesky)/cholesky | solution.py:44
  657.3 2.7 select_select_fusion
  660.1 1.7 copy-done.2
  661.8 9.7 %while.14 = (s32[]{:T(128)}, f32[4,448,448]{2,1,0:T(8,128)}, s32[3,2]{0,1:T(2,128)S(1)}, f32[3,4,128,128]{3,2,0,1:T(8,128)S(1)}, s32[]{:T(128)}) while((s32[]{:T(128)}, f32[4,448,448]{2,1,0:T(8,128)}, s32[3,2]{0,1:T(2,128)S(1)}, f32[3,4,128,128]{3,2,0,1:T(8,128)S(1)}, s32[]{:T(128)}) %tuple.74), condition=%wide.while_cond, body=%wide.while_body.sunk | while | flops 2 | bytes 524405 | solution.py:45
  662.5 2.5 bitcast_dynamic-update-slice_fusion.2
  665.7 2.5 bitcast_dynamic-update-slice_fusion.2
  668.9 2.5 bitcast_dynamic-update-slice_fusion.2
  671.7 157.5 %custom-call.41 = f32[4,4,128,128]{2,3,1,0:T(8,128)S(1)} custom-call(f32[4,4,128,128]{3,2,1,0:T(8,128)S(1)} %pad_maximum_fusion.1), custom_call_target="InvertDiagBlocksLowerTriangular" | custom-call | tf_op jit(solution)/shard_map/triangular_solve | solution.py:45
  836.3 37.7 %all-gather.8.cloned.1.call-done = bf16[28,128,448]{2,1,0:T(8,128)(2,1)} async-done(((bf16[28,8,448]{2,1,0:T(8,128)(2,1)}), bf16[28,128,448]{2,1,0:T(8,128)(2,1)}) %all-gather.8.cloned.1.call-update) | async-done | bytes 3211280 | tf_op jit(solution)/shard_map/all_gather | solution.py:84
  873.9 8.0 while.13
  875.1 2.8 fusion.85
  879.1 2.8 fusion.85
  881.9 2.9 multiply_convert_fusion.1
  884.9 1.9 copy.146
  886.7 4.0 all-to-all-start
  890.7 14.2 %all-to-all-done = bf16[2,448,448]{2,0,1:T(2,128)(2,1)S(1)} async-done(((bf16[2,448,448]{2,0,1:T(2,128)(2,1)}), bf16[2,448,448]{2,0,1:T(2,128)(2,1)S(1)}, u32[]{:S(2)}, u32[]{:S(2)}) %all-to-all-start) | async-done | bytes 802848 | tf_op jit(solution)/shard_map/all_to_all | solution.py:107
  906.9 2.6 reshape.144
  909.5 1.7 constant_dynamic-slice_fusion.1
  (73 shorter events, 22.2 us)
Async XLA Ops:
  7.2 20.7 %copy-start = (bf16[1792,448]{0,1:T(8,128)(2,1)S(1)}, bf16[1792,448]{0,1:T(8,128)(2,1)}, u32[]{:S(2)}) copy-start(bf16[1792,448]{0,1:T(8,128)(2,1)} %param.9) | copy-start | bytes 4816900
  7.2 3.6 copy-start.6
  7.2 210.1 %reduce-scatter.2.cloned.1.call-start = ((), (), s32[]{:S(2)}) async-start(), calls=%async_computation.2 | async-start | bytes 13647872 | tf_op jit(solution)/shard_map/reduce_scatter | solution.py:29
  72.7 158.2 %copy-start.5 = (s32[2,112]{1,0:T(2,128)S(1)}, s32[2,112]{1,0:T(2,128)}, u32[]{:S(2)}) copy-start(s32[2,112]{1,0:T(2,128)} %param.11) | copy-start | bytes 2692
  72.7 202.4 %all-gather.4.cloned.1.call-start = ((), (), s32[]{:S(2)}) async-start(), calls=%async_computation.3 | async-start | bytes 4587520 | tf_op jit(solution)/shard_map/all_gather | solution.py:39
  230.8 98.7 %all-gather.6.cloned.1.call-start = ((), (), s32[]{:S(2)}) async-start(), calls=%async_computation.4 | async-start | bytes 7798784 | tf_op jit(solution)/shard_map/all_gather | solution.py:80
  281.5 592.4 %all-gather.8.cloned.1.call-start = ((), (), s32[]{:S(2)}) async-start(), calls=%async_computation.5 | async-start | bytes 3899392 | tf_op jit(solution)/shard_map/all_gather | solution.py:84
  356.8 1.8 copy-start.3
  660.0 1.8 copy-start.2
  660.0 169.2 %copy-start.4 = (f32[28,8,448]{2,1,0:T(8,128)S(1)}, f32[28,8,448]{2,1,0:T(8,128)}, u32[]{:S(2)}) copy-start(f32[28,8,448]{2,1,0:T(8,128)} %copy_add_fusion) | copy-start | bytes 1204228
  886.7 18.2 %all-to-all-start = ((bf16[2,448,448]{2,0,1:T(2,128)(2,1)}), bf16[2,448,448]{2,0,1:T(2,128)(2,1)S(1)}, u32[]{:S(2)}, u32[]{:S(2)}) async-start(bf16[2,448,448]{2,0,1:T(2,128)(2,1)} %copy.146), calls=%async_computation.1 | async-start | bytes 1835008 | tf_op jit(solution)/shard_map/all_to_all | solution.py:107
  904.9 6.3 copy-start.1
Sparse Core Ops, SparseCore 0:
  72.8 144.4 reduce-scatter.1
  230.9 44.1 all-gather.3
  281.6 47.8 all-gather.5
  836.4 37.5 all-gather.7
where the time goes:
time: 924 us; the launch traced here: 918 us
  other arithmetic  465 us (50%)
  waiting for transfers between devices  288 us (31%)
  local copies, waits for them, and re-layouts  69.6 us (8%)
  matrix products  63.1 us (7%)
  between operations  14.7 us (2%)
  blocking collectives  12.2 us (1%)
    another operation x18, other arithmetic, finish(): factor = jnp.linalg.cholesky(gram_matrix)  285 us
    another operation x8, other arithmetic, finish(): lax.linalg.triangular_solve(factor, leaves, left_side=False, lower=True,...  160 us
    reduce_scatter x1, waiting for transfers between devices, one_scatter(): lax.psum_scatter(lines, axis, tiled=True).reshape(-1)  145 us
    all_gather x1, waiting for transfers between devices, local(): whole_sample = lax.all_gather(sample, 'col', axis=1, tiled=True)  47.4 us
    all_gather x1, waiting for transfers between devices, gather_axes(): shard = lax.all_gather(shard, axis, axis=dim, tiled=True)  44 us
    all_gather x1, waiting for transfers between devices, local(): whole_basis = lax.all_gather(leaf_basis, 'col', axis=1, tiled=True)  37.7 us
  transfers between devices with their start and end apart: 5, of which 5 were waited for; matrix products, arithmetic and copies ran while one was open for 0% of the time, Pallas kernels for 0%

commit v1 on v0

v1 whole, which is shorter than its diff:
```python
import functools
import math

import jax
import jax.numpy as jnp
from jax import lax
from jax.experimental import pallas as pl
from jax.experimental.pallas import tpu as pltpu
from jax.sharding import Mesh
from jax.sharding import PartitionSpec as P

LEAF = 896
BLOCK = 128
ROW = ("y", "zh")
CHIP = ("x", "zl")
COL = ("x", "zl", "core")
F32 = jnp.float32
BF = jnp.bfloat16
HIGH = lax.Precision.HIGHEST
VMEM = pl.BlockSpec(memory_space=pltpu.VMEM)
STEP = 64


def params(mib):
    return pltpu.CompilerParams(vmem_limit_bytes=mib << 20)


def cost(flops, nbytes):
    return pl.CostEstimate(flops=int(flops), bytes_accessed=int(nbytes), transcendentals=0)


def send_kernel(a_ref, b_ref, o_ref):
    o_ref[...] = jnp.dot(a_ref[0], b_ref[0], preferred_element_type=F32)[None]


def keep_kernel(a_ref, b_ref, r_ref, o_ref):
    total = jnp.dot(a_ref[0], b_ref[0], preferred_element_type=F32) + r_ref[0]
    chips, blocks, rows, _ = o_ref.shape
    for block in range(blocks):
        for chip in range(chips):
            start = (block * chips + chip) * rows
            o_ref[chip, block] = total[start : start + rows].astype(BF)


def probe_send(a, b):
    count, rows, depth = a.shape
    half = b.shape[2]
    per = rows // LEAF
    return pl.pallas_call(
        send_kernel,
        grid=(count, per),
        out_shape=jax.ShapeDtypeStruct((count, rows, half), F32),
        in_specs=[
            pl.BlockSpec((1, LEAF, depth), lambda k, i: (k, i, 0)),
            pl.BlockSpec((1, depth, half), lambda k, i: (k, 0, 0)),
        ],
        out_specs=pl.BlockSpec((1, LEAF, half), lambda k, i: (k, i, 0)),
        compiler_params=params(40),
        cost_estimate=cost(2 * count * rows * depth * half, 2 * a.size + 4 * count * rows * half),
    )(a, b)


def probe_keep(a, b, received, chips):
    count, rows, depth = a.shape
    half = b.shape[2]
    per = rows // LEAF
    blocks = LEAF // BLOCK
    slab = BLOCK // chips
    return pl.pallas_call(
        keep_kernel,
        grid=(count, per),
        out_shape=jax.ShapeDtypeStruct((chips, count * rows // BLOCK, slab, half), BF),
        in_specs=[
            pl.BlockSpec((1, LEAF, depth), lambda k, i: (k, i, 0)),
            pl.BlockSpec((1, depth, half), lambda k, i: (k, 0, 0)),
            pl.BlockSpec((1, LEAF, half), lambda k, i: (k, i, 0)),
        ],
        out_specs=pl.BlockSpec((chips, blocks, slab, half), lambda k, i: (0, k * per + i, 0, 0)),
        compiler_params=params(40),
        cost_estimate=cost(2 * count * rows * depth * half, 2 * a.size + 6 * count * rows * half),
    )(a, b, received)


def shift(value, axis, by):
    size = lax.axis_size(axis)
    return lax.ppermute(value, axis, [(i, (i + by) % size) for i in range(size)])


def ring_gather(value, axis):
    size = lax.axis_size(axis)
    return jnp.stack([value] + [shift(value, axis, by) for by in range(1, size)])


def two_way_gather(first, second, big, small):
    first_ring = ring_gather(first, big)
    second_pair = ring_gather(second, small)
    return ring_gather(first_ring, small), ring_gather(second_pair, big)


def sum_kernel(k_ref, o_ref):
    total = k_ref[0].astype(F32)
    for chip in range(1, k_ref.shape[0]):
        total += k_ref[chip].astype(F32)
    o_ref[...] = total.astype(o_ref.dtype)


def sum_shares(shares, dtype):
    return pl.pallas_call(
        sum_kernel,
        out_shape=jax.ShapeDtypeStruct(shares.shape[1:], dtype),
        in_specs=[VMEM],
        out_specs=VMEM,
        compiler_params=params(24),
        cost_estimate=cost(shares.size, 2 * shares.size),
    )(shares)


def extend_kernel(at_ref, p_ref, first_ref, second_ref, o_ref):
    for block in range(p_ref.shape[1]):
        total = p_ref[0, block].astype(F32)
        for chip in range(1, p_ref.shape[0]):
            total += p_ref[chip, block].astype(F32)
        for kid, ref in enumerate((first_ref, second_ref)):
            near, far, place = (at_ref[kid, part, block] for part in range(3))
            there = at_ref[kid, 3, block]
            share = ref[near, far, place].astype(F32)
            total += jnp.where(there > 0, share, 0.0)
        o_ref[block] = total.astype(BF)


def extend_add(at, parent, first, second):
    return pl.pallas_call(
        extend_kernel,
        out_shape=jax.ShapeDtypeStruct(parent.shape[1:], BF),
        in_specs=[pl.BlockSpec(memory_space=pltpu.SMEM), VMEM, VMEM, VMEM],
        out_specs=VMEM,
        compiler_params=params(32),
        cost_estimate=cost(parent.size, 6 * parent.size),
    )(at, parent, first, second)


def halves(x):
    hi = x.astype(BF)
    return hi, (x - hi.astype(F32)).astype(BF)


def contract(a, b, left, right):
    return lax.dot_general(a, b, (((left,), (right,)), ((), ())), preferred_element_type=F32)


def gram_kernel(at_ref, f_ref, a0_ref, b0_ref, a1_ref, b1_ref, gram_ref, cross_ref, y_ref):
    x, zl, core, col = (at_ref[i] for i in range(4))
    step = pl.program_id(0)
    half = a0_ref.shape[-1]
    count = a0_ref.shape[2]
    per = LEAF // BLOCK
    leaves, order, _ = gram_ref.shape

    @pl.when(step == 0)
    def _():
        for first_ref, second_ref, owner in ((a0_ref, b0_ref, core), (a1_ref, b1_ref, 1 - core)):
            lanes = pl.ds(pl.multiple_of(owner * half, half), half)
            for i in range(4):
                for j in range(2):
                    chip = lax.rem(x + 4 - i, 4) * 2 + lax.rem(zl + j, 2)
                    rows = pl.ds(pl.multiple_of(chip * 16, 16), 16)
                    y_ref[:count, rows, lanes] = first_ref[j, i]
                    y_ref[count:, rows, lanes] = second_ref[i, j]
        for leaf in range(leaves):
            y = y_ref[leaf * per : (leaf + 1) * per].reshape(LEAF, 2 * half)
            gram_ref[leaf] = contract(y, y, 0, 0)[:order, :order]

    leaf = lax.rem(col, 2) * 2 + step
    sibling = lax.rem(col, 2) * 2 + 1 - step
    there = y_ref[pl.ds(sibling * per, per)].reshape(LEAF, 2 * half)
    here = y_ref[pl.ds(leaf * per, per)].reshape(LEAF, 2 * half)
    hi, lo = halves(jnp.dot(f_ref[...], there, preferred_element_type=F32))
    cross = contract(here, hi, 0, 0) + contract(here, lo, 0, 0)
    cross_ref[:, 0] = cross.reshape(cross_ref.shape[0], cross_ref.shape[2], 2 * half)


def grams(at, front, mine, other, order):
    a0, b0 = mine
    half = a0.shape[-1]
    wide = 2 * half
    leaves = 2 * a0.shape[2] * BLOCK // LEAF
    whole = pl.BlockSpec(memory_space=pltpu.VMEM)
    return pl.pallas_call(
        gram_kernel,
        grid_spec=pltpu.PrefetchScalarGridSpec(
            num_scalar_prefetch=1,
            grid=(2,),
            in_specs=[
                pl.BlockSpec((LEAF, LEAF), lambda i, at: (lax.rem(at[3], 2) * 2 + i, 1 - i)),
                whole,
                whole,
                whole,
                whole,
            ],
            out_specs=[
                pl.BlockSpec((leaves, order, order), lambda i, at: (0, 0, 0)),
                pl.BlockSpec((16, 1, wide // 16, wide), lambda i, at: (0, i, 0, 0)),
            ],
            scratch_shapes=[pltpu.VMEM((leaves * LEAF // BLOCK, BLOCK, wide), BF)],
        ),
        out_shape=[
            jax.ShapeDtypeStruct((leaves, order, order), F32),
            jax.ShapeDtypeStruct((16, 2, wide // 16, wide), F32),
        ],
        compiler_params=params(52),
        cost_estimate=cost(2 * 10 * LEAF * wide * wide, 4 * LEAF * LEAF + 4 * leaves * LEAF * wide),
    )(at, front, a0, b0, *other)


def product3(a, b):
    ah, al = halves(a)
    bh, bl = halves(b)
    return contract(ah, bh, 1, 0) + (contract(ah, bl, 1, 0) + contract(al, bh, 1, 0))


def eliminate(s, size):
    groups = size // 8
    sub = lax.broadcasted_iota(jnp.int32, (8, 1), 0)
    for j in range(size):
        g, r = divmod(j, 8)
        for rows in s:
            row = rows[g][r : r + 1, :]
            scaled = row * (1.0 / row[:, j : j + 1])
            for i in range(g, groups):
                c = rows[i][:, j : j + 1]
                if i == g:
                    if r == 7:
                        continue
                    c = jnp.where(sub > r, c, 0.0)
                rows[i] = rows[i] - c * scaled


def inverse_kernel(a_ref, w_ref):
    leaves, order, wide = w_ref.shape
    w_ref[:, :, order - order % 128 :] = jnp.zeros((leaves, order, wide - order + order % 128), F32)
    w_ref[:, :, :order] = a_ref[...]
    lane = lax.broadcasted_iota(jnp.int32, (STEP, 128), 1)
    sub = lax.broadcasted_iota(jnp.int32, (STEP, 128), 0)
    col = lax.broadcasted_iota(jnp.int32, (STEP, wide), 1)
    row = lax.broadcasted_iota(jnp.int32, (STEP, wide), 0)

    @pl.loop(0, order // STEP)
    def _(k):
        base = pl.multiple_of(k * STEP, STEP)
        tile = pl.multiple_of(lax.div(base, 128) * 128, 128)
        odd = base - tile > 0
        s = []
        for leaf in range(leaves):
            d = w_ref[leaf, pl.ds(base, STEP), pl.ds(tile, 128)]
            d = jnp.where(odd, pltpu.roll(d, 128 - STEP, 1), d)
            d = jnp.where(lane < STEP, d, (lane - STEP == sub).astype(F32))
            s.append([d[8 * i : 8 * i + 8] for i in range(STEP // 8)])
        eliminate(s, STEP)
        inside = (col >= base) & (col < base + STEP)
        unit = (col - base == row).astype(F32)
        later = col >= base + STEP
        for leaf in range(leaves):
            d = jnp.concatenate(s[leaf], axis=0)
            diagonal = jnp.sum(jnp.where(lane == sub, d, 0.0), axis=1, keepdims=True)
            x = (d * lax.rsqrt(diagonal))[:, STEP:]
            solved = product3(x, jnp.where(inside, unit, w_ref[leaf, pl.ds(base, STEP), :]))
            w_ref[leaf, pl.ds(base, STEP), :] = solved
            hi, lo = halves(solved)
            none = jnp.zeros_like(hi)
            left_hi, left_lo = jnp.where(later, hi, none), jnp.where(later, lo, none)
            left = jnp.concatenate([left_hi, left_hi, left_lo], axis=0)
            update = contract(left, jnp.concatenate([hi, lo, hi], axis=0), 0, 0)
            for i in range(order // STEP):
                rows = slice(i * STEP, (i + 1) * STEP)

                @pl.when(i > k)
                def _(rows=rows):
                    w_ref[leaf, rows, :] = jnp.where(inside, 0.0, w_ref[leaf, rows, :]) - update[rows]

    for leaf in range(leaves):
        for i in range(order // STEP):
            rows = slice(i * STEP, (i + 1) * STEP)
            w_ref[leaf, rows, :] = jnp.where(col <= row + i * STEP, w_ref[leaf, rows, :], 0.0)


def factor_inverse(gram):
    leaves, order, _ = gram.shape
    wide = -(-order // 128) * 128
    return pl.pallas_call(
        inverse_kernel,
        out_shape=jax.ShapeDtypeStruct((leaves, order, wide), F32),
        in_specs=[VMEM],
        out_specs=VMEM,
        compiler_params=params(40),
        cost_estimate=cost(40e9, 8 * gram.size),
    )(gram)


def local(parent_front, child_update, parent_test, child_test, child_map):
    y, zh = lax.axis_index("y"), lax.axis_index("zh")
    x, zl, core = lax.axis_index("x"), lax.axis_index("zl"), lax.axis_index("core")
    row_index, col_index = lax.axis_index(ROW), lax.axis_index(COL)
    probes = parent_test.shape[1]
    half = 256
    chips = lax.axis_size(CHIP)
    own_blocks = parent_front.shape[0] // BLOCK
    kid_blocks = child_update.shape[1] // BLOCK
    leaf_count = own_blocks * BLOCK // LEAF
    swap = [(0, 1), (1, 0)]

    def half_of(test, which):
        padded = jnp.pad(test, ((0, 0), (0, 0), (0, 2 * half - probes)))
        return lax.dynamic_slice_in_dim(padded, which * half, half, 2)

    front, whole_test = parent_front[None], parent_test[None]
    kid_sent = lax.ppermute(
        probe_send(child_update, half_of(child_test, 1 - core)), "core", swap
    )
    own_sent = lax.ppermute(probe_send(front, half_of(whole_test, 1 - core)), "core", swap)
    kid_part = probe_keep(child_update, half_of(child_test, core), kid_sent, chips)
    kid_share = lax.all_to_all(kid_part, CHIP, 0, 0, tiled=True)
    own_part = probe_keep(front, half_of(whole_test, core), own_sent, chips)
    own_share = lax.all_to_all(own_part, CHIP, 0, 0, tiled=True)

    kids = sum_shares(kid_share, BF)
    first, second = two_way_gather(kids[:kid_blocks], kids[kid_blocks:], "y", "zh")

    targets = row_index * own_blocks + jnp.arange(own_blocks, dtype=jnp.int32)
    hit = child_map[:, None, :] == targets[None, :, None]
    there = jnp.any(hit, axis=2).astype(jnp.int32)
    source = jnp.sum(jnp.where(hit, jnp.arange(child_map.shape[1], dtype=jnp.int32), 0), axis=2)
    owner, place = source // kid_blocks, source % kid_blocks
    ring = (y - owner // 2) % 4
    pair = (zh - owner % 2) % 2
    at = jnp.stack(
        [
            jnp.stack([pair[0], ring[0], place[0], there[0]]),
            jnp.stack([ring[1], pair[1], place[1], there[1]]),
        ]
    ).astype(jnp.int32)
    share = extend_add(at, own_share, first, second)

    cut = own_blocks // 2
    mine = two_way_gather(share[:cut], share[cut:], "x", "zl")
    other = tuple(lax.ppermute(part, "core", swap) for part in mine)
    place_of = jnp.stack([x, zl, core, col_index]).astype(jnp.int32)
    gram, cross = grams(place_of, parent_front, mine, other, probes)

    cross = lax.all_to_all(cross, COL, 0, 0, tiled=True)
    cross = lax.dynamic_slice_in_dim(cross, 2 * row_index, 2, 0)
    cross = cross.reshape(leaf_count, cross.shape[2], 2 * half)
    cross = lax.all_gather(cross, COL)
    inverse = factor_inverse(gram)[:, :, :probes]

    own_rows = jnp.where(
        core == 0,
        jnp.concatenate([share, jnp.concatenate([other[0][0, 0], other[1][0, 0]], 0)], axis=2),
        jnp.concatenate([jnp.concatenate([other[0][0, 0], other[1][0, 0]], 0), share], axis=2),
    )
    own_rows = lax.dynamic_slice_in_dim(own_rows, core * 8, 8, 1)[:, :, :probes]
    leaves = own_rows.reshape(leaf_count, -1, probes).astype(F32)
    basis = jnp.einsum("lkr,lsr->lks", leaves, inverse, precision=HIGH) * math.sqrt(LEAF)
    leaf_basis = basis.astype(BF).reshape(own_blocks, 8, probes)

    rows = probes // lax.axis_size(COL)
    left = lax.dynamic_slice_in_dim(inverse, col_index * rows, rows, 1)
    cross = jnp.moveaxis(cross, 0, 1).reshape(leaf_count, 2 * half, 2 * half)[:, :probes, :probes]
    siblings = inverse.reshape(-1, 2, probes, probes)[:, ::-1].reshape(inverse.shape)
    couplings = jnp.einsum("lir,lrs->lis", left, cross, precision=HIGH)
    couplings = jnp.einsum("lis,lts->lit", couplings, siblings, precision=HIGH)
    return (leaf_basis, couplings)


def solution(mesh):
    split = Mesh(mesh.devices.reshape(4, 2, 4, 2, 2), ("y", "zh", "x", "zl", "core"))
    placed = (P(ROW, COL), P(None, ROW, COL), P(COL, None), P(None, COL, None), P())
    return jax.shard_map(
        local,
        mesh=split,
        in_specs=placed,
        out_specs=(P(ROW, COL, None), P(ROW, COL, None)),
        check_vma=False,
    )
```

time: 924 us -> 290 us (0.31)
  other arithmetic: 465 us -> 5.82 us
  waiting for transfers between devices: 288 us -> 86.5 us
  Pallas kernels: 0 us -> 100 us
  matrix products: 63.1 us -> 12.4 us
  local copies, waits for them, and re-layouts: 69.6 us -> 27.1 us
  starting transfers between devices: 4.55 us -> 42.4 us
  blocking collectives: 12.2 us -> 0 us
    another operation x26 -> x11, other arithmetic: 446 us -> 5.29 us  [the longest x8 5.19 us: ring_gather(): jnp.stack([value] + [shift(value, axis, by) for by in range(1, size)])]
    reduce_scatter x1 -> x0, waiting for transfers between devices: 145 us -> none  [one_scatter(): lax.psum_scatter(lines, axis, tiled=True).reshape(-1)]
    all_gather x3 -> x1, waiting for transfers between devices: 129 us -> 0.01 us  [local(): cross = lax.all_gather(cross, COL)]
    pallas_call x0 -> x8, Pallas kernels: none -> 100 us  [the longest x1 61 us: factor_inverse(): pl.pallas_call(inverse_kernel, out_shape=jax.ShapeDtypeStruct((leaves, or...]
    ppermute x0 -> x20, waiting for transfers between devices: none -> 42 us  [the longest x16 38.8 us: shift(): lax.ppermute(value, axis, [(i, (i + by) % size) for i in range(size)])]
    dot_general x8 -> x3, matrix products: 45.9 us -> 12.4 us  [the longest x1 4.59 us: local(): jnp.einsum('lkr,lsr->lks', leaves, inverse, precision=HIGH)]
    all_to_all x1 -> x3, waiting for transfers between devices: 14.2 us -> 44.5 us  [the longest x1 27 us: local(): cross = lax.all_to_all(cross, COL, 0, 0, tiled=True)]
    ppermute x0 -> x20, starting transfers between devices: none -> 29.3 us  [the longest x16 27.2 us: shift(): lax.ppermute(value, axis, [(i, (i + by) % size) for i in range(size)])]
  transfers between devices with their start and end apart: 5 -> 24, of which waited for: 5 -> 15; matrix products, arithmetic and copies ran while one was open for 0% -> 7% of each run, Pallas kernels for 0% -> 29%
where the time goes in v1:
time: 290 us; the launch traced here: 289 us
  Pallas kernels  100 us (34%)
  waiting for transfers between devices  86.5 us (30%)
  starting transfers between devices  42.4 us (15%)
  local copies, waits for them, and re-layouts  27.1 us (9%)
  between operations  14.3 us (5%)
  matrix products  12.4 us (4%)
  other arithmetic  5.82 us (2%)
    pallas_call x1, Pallas kernels, factor_inverse(): pl.pallas_call(inverse_kernel, out_shape=jax.ShapeDtypeStruct((leaves, or...  61 us
    ppermute x16, waiting for transfers between devices, shift(): lax.ppermute(value, axis, [(i, (i + by) % size) for i in range(size)])  38.8 us
    ppermute x16, starting transfers between devices, shift(): lax.ppermute(value, axis, [(i, (i + by) % size) for i in range(size)])  27.2 us
    all_to_all x1, waiting for transfers between devices, local(): cross = lax.all_to_all(cross, COL, 0, 0, tiled=True)  27 us
    all_to_all x1, waiting for transfers between devices, local(): kid_share = lax.all_to_all(kid_part, CHIP, 0, 0, tiled=True)  17.5 us
    unnamed x32, local copies, waits for them, and re-layouts  17.3 us
    pallas_call x2, Pallas kernels, probe_keep(): pl.pallas_call(keep_kernel, grid=(count, per), out_shape=jax.ShapeDtypeSt...  14.1 us
    pallas_call x2, Pallas kernels, probe_send(): pl.pallas_call(send_kernel, grid=(count, per), out_shape=jax.ShapeDtypeSt...  13.1 us
  transfers between devices with their start and end apart: 24, of which 15 were waited for; matrix products, arithmetic and copies ran while one was open for 7% of the time, Pallas kernels for 29%

profile of v1, /device:TPU:1, one launch (start us, length us, event | category | flops | bytes accessed | tf_op | source)
XLA Modules:
  0.0 288.6 jit_solution(7678487431332696202)
XLA Ops:
  7.2 2.7 copy.29
  10.3 2.8 copy-done
  13.1 3.9 %shard_map.70 = f32[2,1792,256]{2,1,0:T(8,128)} custom-call(bf16[2,1792,896]{2,1,0:T(8,128)(2,1)S(1)} %copy-done, bf16[2,896,256]{2,1,0:T(8,128)(2,1)S(1)} %get-tuple-element.14.b_ref), custom_call_target="tpu_custom_call" | custom-call | flops 1644167168 | bytes 10092544 | tf_op jit(solution)/shard_map/pallas_call | solution.py:49
  17.0 1.4 collective-permute-start.1
  18.4 2.3 copy.28
  20.7 1.8 pad_dynamic-slice_fusion.2
  22.6 9.3 %shard_map.68 = f32[1,3584,256]{2,1,0:T(8,128)} custom-call(bf16[1,3584,1792]{2,1,0:T(8,128)(2,1)} %bitcast.62, bf16[1,1792,256]{2,1,0:T(8,128)(2,1)S(1)} %get-tuple-element.16.b_ref), custom_call_target="tpu_custom_call" | custom-call | flops 3288334336 | bytes 16515072 | tf_op jit(solution)/shard_map/pallas_call | solution.py:49
  31.9 5.4 %shard_map.71 = bf16[8,28,16,256]{3,2,1,0:T(8,128)(2,1)} custom-call(bf16[2,1792,896]{2,1,0:T(8,128)(2,1)S(1)} %bitcast.59, bf16[2,896,256]{2,1,0:T(8,128)(2,1)S(1)} %get-tuple-element.15.b_ref, f32[2,1792,256]{2,1,0:T(8,128)} %collective-permute-done.1.r_ref), custom_call_target="tpu_custom_call" | custom-call | flops 1644167168 | bytes 11927552 | tf_op jit(solution)/shard_map/pallas_call | solution.py:69
  37.3 5.6 %all-to-all-start.1 = ((bf16[8,28,16,256]{3,2,1,0:T(8,128)(2,1)}), bf16[8,28,16,256]{3,2,1,0:T(8,128)(2,1)S(1)}, u32[]{:S(2)}, u32[]{:S(2)}) async-start(bf16[8,28,16,256]{3,2,1,0:T(8,128)(2,1)} %shard_map.71), calls=%async_computation.1 | async-start | bytes 3670016 | tf_op jit(solution)/shard_map/all_to_all | solution.py:321
  43.5 8.8 %shard_map.69 = bf16[8,28,16,256]{3,2,1,0:T(8,128)(2,1)} custom-call(bf16[1,3584,1792]{2,1,0:T(8,128)(2,1)} %bitcast.63, bf16[1,1792,256]{2,1,0:T(8,128)(2,1)S(1)} %get-tuple-element.17.b_ref, f32[1,3584,256]{2,1,0:T(8,128)} %collective-permute-done.r_ref), custom_call_target="tpu_custom_call" | custom-call | flops 3288334336 | bytes 18350080 | tf_op jit(solution)/shard_map/pallas_call | solution.py:69
  52.2 17.5 %all-to-all-done.1.k_ref = bf16[8,28,16,256]{3,2,1,0:T(8,128)(2,1)S(1)} async-done(((bf16[8,28,16,256]{3,2,1,0:T(8,128)(2,1)}), bf16[8,28,16,256]{3,2,1,0:T(8,128)(2,1)S(1)}, u32[]{:S(2)}, u32[]{:S(2)}) %all-to-all-start.1) | async-done | bytes 1835040 | tf_op jit(solution)/shard_map/all_to_all | solution.py:321
  69.8 1.2 copy-done.2
  71.0 3.6 %all-to-all-start = ((bf16[8,28,16,256]{3,2,1,0:T(8,128)(2,1)}), bf16[8,28,16,256]{3,2,1,0:T(8,128)(2,1)S(1)}, u32[]{:S(2)}, u32[]{:S(2)}) async-start(bf16[8,28,16,256]{3,2,1,0:T(8,128)(2,1)} %shard_map.69), calls=%async_computation | async-start | bytes 3670016 | tf_op jit(solution)/shard_map/all_to_all | solution.py:323
  74.7 1.5 copy-done.3
  76.4 3.4 %collective-permute-start.6 = (bf16[14,16,256]{2,1,0:T(8,128)(2,1)S(1)}, bf16[14,16,256]{2,1,0:T(8,128)(2,1)S(1)}, u32[]{:S(2)}, u32[]{:S(2)}) collective-permute-start(bf16[14,16,256]{2,1,0:T(8,128)(2,1)S(1)} %get-tuple-element.32), channel_id=1, source_target_pairs={{0,16},{16,0},{1,17},{17,1},{2,18},{18,2},{3,19},{19,3},{4,20},{20... | collective-permute-start | bytes 344072 | tf_op jit(solution)/shard_map/ppermute | solution.py:86
  79.9 2.7 collective-permute-start.4
  83.7 12.8 %collective-permute-done.6 = bf16[14,16,256]{2,1,0:T(8,128)(2,1)S(1)} collective-permute-done((bf16[14,16,256]{2,1,0:T(8,128)(2,1)S(1)}, bf16[14,16,256]{2,1,0:T(8,128)(2,1)S(1)}, u32[]{:S(2)}, u32[]{:S(2)}) %collective-permute-start.6) | collective-permute-done | bytes 114720 | tf_op jit(solution)/shard_map/ppermute | solution.py:86
  97.2 2.7 collective-permute-start.9
  100.9 0.9 fusion.22
  102.4 3.3 %collective-permute-done.9 = bf16[2,14,16,256]{3,2,1,0:T(8,128)(2,1)S(1)} collective-permute-done((bf16[2,14,16,256]{3,2,1,0:T(8,128)(2,1)}, bf16[2,14,16,256]{3,2,1,0:T(8,128)(2,1)S(1)}, u32[]{:S(2)}, u32[]{:S(2)}) %collective-permute-start.9) | collective-permute-done | bytes 229408 | tf_op jit(solution)/shard_map/ppermute | solution.py:86
  105.6 0.9 collective-permute-done.8
  106.6 2.4 collective-permute-done.7
  109.6 1.3 pad_maximum_fusion.1.second_ref
  111.1 2.0 pad_maximum_fusion.first_ref
  113.2 1.2 copy-done.4
  114.4 0.9 shard_map.73
  115.3 12.3 %collective-permute-start.12 = (bf16[14,16,256]{2,1,0:T(8,128)(2,1)S(1)}, bf16[14,16,256]{2,1,0:T(8,128)(2,1)S(1)}, u32[]{:S(2)}, u32[]{:S(2)}) collective-permute-start(bf16[14,16,256]{2,1,0:T(8,128)(2,1)S(1)} %get-tuple-element.27), channel_id=1, source_target_pairs={{0,12},{4,0},{8,4},{12,8},{1,13},{5,1},{9,5},{13,9},{2,14},{6,2},{... | collective-permute-start | bytes 344072 | tf_op jit(solution)/shard_map/ppermute | solution.py:86
  129.5 2.6 collective-permute-done.12
  132.1 1.1 collective-permute-done.11
  133.1 3.4 %collective-permute-done.10 = bf16[14,16,256]{2,1,0:T(8,128)(2,1)S(1)} collective-permute-done((bf16[14,16,256]{2,1,0:T(8,128)(2,1)S(1)}, bf16[14,16,256]{2,1,0:T(8,128)(2,1)S(1)}, u32[]{:S(2)}, u32[]{:S(2)}) %collective-permute-start.10) | collective-permute-done | bytes 114720 | tf_op jit(solution)/shard_map/ppermute | solution.py:86
  136.9 1.2 collective-permute-start.17
  138.8 4.5 %collective-permute-done.18 = bf16[2,14,16,256]{3,2,1,0:T(8,128)(2,1)S(1)} collective-permute-done((bf16[2,14,16,256]{3,2,1,0:T(8,128)(2,1)S(1)}, bf16[2,14,16,256]{3,2,1,0:T(8,128)(2,1)S(1)}, u32[]{:S(2)}, u32[]{:S(2)}) %collective-permute-start.18) | collective-permute-done | bytes 229408 | tf_op jit(solution)/shard_map/ppermute | solution.py:86
  143.4 1.1 collective-permute-done.17
  144.5 6.4 %collective-permute-done.16 = bf16[2,14,16,256]{3,2,1,0:T(8,128)(2,1)S(1)} collective-permute-done((bf16[2,14,16,256]{3,2,1,0:T(8,128)(2,1)S(1)}, bf16[2,14,16,256]{3,2,1,0:T(8,128)(2,1)S(1)}, u32[]{:S(2)}, u32[]{:S(2)}) %collective-permute-start.16) | collective-permute-done | bytes 229408 | tf_op jit(solution)/shard_map/ppermute | solution.py:86
  151.8 2.0 collective-permute-done.19.b1_ref
  153.8 1.3 collective-permute-done.14.a1_ref
  155.1 10.7 %shard_map.74 = (f32[4,448,448]{2,1,0:T(8,128)}, f32[16,2,32,512]{3,2,1,0:T(8,128)}) custom-call(s32[4]{0:T(128)S(1)} %pad_add_fusion.1.at_ref, bf16[3584,1792]{1,0:T(8,128)(2,1)} %f_ref.1, bf16[2,4,14,16,256]{4,3,2,1,0:T(8,128)(2,1)S(1)} %pad_maximum_fusion.2.a0_ref, bf16[4,2,14,16,256]{4,3,2,1,0:T(8,128)(2,1)S(1)} %pad_maximum_fusion.3.b0_ref, ...), custom_call_target="tpu_custom_call" | custom-call | flops 4697620480 | bytes 10551296 | tf_op jit(solution)/shard_map/pallas_call | solution.py:188
  165.8 3.9 %all-to-all-start.2 = ((f32[16,2,32,512]{3,2,1,0:T(8,128)}), f32[16,2,32,512]{3,2,1,0:T(8,128)S(1)}, u32[]{:S(2)}, u32[]{:S(2)}) async-start(f32[16,2,32,512]{3,2,1,0:T(8,128)} %get-tuple-element.5), calls=%async_computation.2 | async-start | bytes 4194304 | tf_op jit(solution)/shard_map/all_to_all | solution.py:349
  169.7 27.0 %all-to-all-done.2 = f32[16,2,32,512]{3,2,1,0:T(8,128)S(1)} async-done(((f32[16,2,32,512]{3,2,1,0:T(8,128)}), f32[16,2,32,512]{3,2,1,0:T(8,128)S(1)}, u32[]{:S(2)}, u32[]{:S(2)}) %all-to-all-start.2) | async-done | bytes 2097184 | tf_op jit(solution)/shard_map/all_to_all | solution.py:349
  197.5 0.9 slice_bitcast_fusion
  198.4 2.0 copy-done.5
  200.4 61.0 %shard_map.75 = f32[4,448,512]{2,1,0:T(8,128)S(1)} custom-call(f32[4,448,448]{2,1,0:T(8,128)S(1)} %copy-done.5), custom_call_target="tpu_custom_call" | custom-call | flops 40000000000 | bytes 6422528 | tf_op jit(solution)/shard_map/pallas_call | solution.py:289
  261.5 1.8 copy-done.1
  263.3 4.2 %rev.3 = f32[2,2,448,448]{3,2,1,0:T(8,128)} reverse(f32[2,2,448,448]{3,2,1,0:T(8,128)} %bitcast.60), dimensions={1} | reverse | bytes 6422528 | tf_op jit(solution)/shard_map/rev | solution.py:368
  267.5 0.9 slice_bitcast_fusion.1
  268.5 4.6 %fusion.2 = bf16[4,56,448]{2,1,0:T(8,128)(2,1)} fusion(bf16[4,56,448]{2,1,0:T(8,128)(2,1)S(1)} %bitcast.68, f32[4,448,512]{2,1,0:T(8,128)} %copy-done.1), kind=kOutput, calls=%fused_computation.7 | convolution fusion | flops 539693056 | bytes 4071424 | tf_op jit(solution)/shard_map/lkr,lsr->lks/dot_general | solution.py:362
  273.1 4.5 %fusion = f32[4,28,448]{2,1,0:T(8,128)S(1)} fusion(f32[4,512,512]{2,1,0:T(8,128)} %bitcast.66, f32[4,448,448]{2,1,0:T(8,128)} %bitcast.61, s32[]{:T(128)S(6)} %select_n.68), kind=kOutput, calls=%fused_computation | convolution fusion | flops 269746176 | bytes 4132868 | tf_op jit(solution)/shard_map/lir,lrs->lis/dot_general | solution.py:369
  277.7 3.3 %fusion.27 = f32[4,28,448]{2,1,0:T(8,128)S(1)} fusion(f32[4,28,448]{2,1,0:T(8,128)S(1)} %fusion, f32[4,448,448]{2,1,0:T(8,128)S(1)} %bitcast.64), kind=kOutput, calls=%fused_computation.76 | convolution fusion | flops 269746176 | bytes 3612672 | tf_op jit(solution)/shard_map/lis,lts->lit/dot_general | solution.py:370
  (80 shorter events, 11.3 us)
Async XLA Ops:
  10.3 2.8 copy-start
  13.1 5.3 %copy-start.7 = (bf16[1792,448]{0,1:T(8,128)(2,1)S(1)}, bf16[1792,448]{0,1:T(8,128)(2,1)}, u32[]{:S(2)}) copy-start(bf16[1792,448]{0,1:T(8,128)(2,1)} %param.7) | copy-start | bytes 4816900
  17.0 14.9 %collective-permute-start.1 = (f32[2,1792,256]{2,1,0:T(8,128)}, f32[2,1792,256]{2,1,0:T(8,128)}, u32[]{:S(2)}, u32[]{:S(2)}) collective-permute-start(f32[2,1792,256]{2,1,0:T(8,128)} %shard_map.70), channel_id=1, source_target_pairs={{0,1},{1,0},{2,3},{3,2},{4,5},{5,4},{6,7},{7,6},{8,9},{9,8},{10,11... | collective-permute-start | bytes 11010056 | tf_op jit(solution)/shard_map/ppermute | solution.py:316
  22.5 9.3 %slice-start = ((s8[6422528]{0:T(1024)(128)(4,1)}), s8[4194304]{0:T(1024)(128)(4,1)S(1)}, s32[]{:S(2)}) async-start(s8[6422528]{0:T(1024)(128)(4,1)} %bitcast.58), calls=%async_computation.4 | async-start | bytes 8388608
  22.6 9.3 %slice-start.1 = ((s8[6422528]{0:T(1024)(128)(4,1)}), s8[2228224]{0:T(1024)(128)(4,1)S(1)}, s32[]{:S(2)}) async-start(s8[6422528]{0:T(1024)(128)(4,1)} %bitcast.58), calls=%async_computation.5 | async-start | bytes 4456448
  31.8 11.6 %collective-permute-start = (f32[1,3584,256]{2,1,0:T(8,128)}, f32[1,3584,256]{2,1,0:T(8,128)}, u32[]{:S(2)}, u32[]{:S(2)}) collective-permute-start(f32[1,3584,256]{2,1,0:T(8,128)} %shard_map.68), channel_id=1, source_target_pairs={{0,1},{1,0},{2,3},{3,2},{4,5},{5,4},{6,7},{7,6},{8,9},{9,8},{10,11... | collective-permute-start | bytes 11010056 | tf_op jit(solution)/shard_map/ppermute | solution.py:319
  37.3 5.6 %copy-start.11 = (s32[2,112]{1,0:T(2,128)S(1)}, s32[2,112]{1,0:T(2,128)}, u32[]{:S(2)}) copy-start(s32[2,112]{1,0:T(2,128)} %param.9) | copy-start | bytes 2692
  37.3 32.5 %all-to-all-start.1 = ((bf16[8,28,16,256]{3,2,1,0:T(8,128)(2,1)}), bf16[8,28,16,256]{3,2,1,0:T(8,128)(2,1)S(1)}, u32[]{:S(2)}, u32[]{:S(2)}) async-start(bf16[8,28,16,256]{3,2,1,0:T(8,128)(2,1)} %shard_map.71), calls=%async_computation.1 | async-start | bytes 3670016 | tf_op jit(solution)/shard_map/all_to_all | solution.py:321
  69.8 1.2 copy-start.2
  71.0 42.2 %all-to-all-start = ((bf16[8,28,16,256]{3,2,1,0:T(8,128)(2,1)}), bf16[8,28,16,256]{3,2,1,0:T(8,128)(2,1)S(1)}, u32[]{:S(2)}, u32[]{:S(2)}) async-start(bf16[8,28,16,256]{3,2,1,0:T(8,128)(2,1)} %shard_map.69), calls=%async_computation | async-start | bytes 3670016 | tf_op jit(solution)/shard_map/all_to_all | solution.py:323
  74.7 1.5 copy-start.3
  76.4 20.0 %collective-permute-start.6 = (bf16[14,16,256]{2,1,0:T(8,128)(2,1)S(1)}, bf16[14,16,256]{2,1,0:T(8,128)(2,1)S(1)}, u32[]{:S(2)}, u32[]{:S(2)}) collective-permute-start(bf16[14,16,256]{2,1,0:T(8,128)(2,1)S(1)} %get-tuple-element.32), channel_id=1, source_target_pairs={{0,16},{16,0},{1,17},{17,1},{2,18},{18,2},{3,19},{19,3},{4,20},{20... | collective-permute-start | bytes 344072 | tf_op jit(solution)/shard_map/ppermute | solution.py:86
  79.9 20.4 %collective-permute-start.4 = (bf16[14,16,256]{2,1,0:T(8,128)(2,1)S(1)}, bf16[14,16,256]{2,1,0:T(8,128)(2,1)S(1)}, u32[]{:S(2)}, u32[]{:S(2)}) collective-permute-start(bf16[14,16,256]{2,1,0:T(8,128)(2,1)S(1)} %get-tuple-element.33), channel_id=1, source_target_pairs={{0,96},{32,0},{64,32},{96,64},{1,97},{33,1},{65,33},{97,65},{2,98}... | collective-permute-start | bytes 344072 | tf_op jit(solution)/shard_map/ppermute | solution.py:86
  82.6 18.3 %collective-permute-start.3 = (bf16[14,16,256]{2,1,0:T(8,128)(2,1)S(1)}, bf16[14,16,256]{2,1,0:T(8,128)(2,1)S(1)}, u32[]{:S(2)}, u32[]{:S(2)}) collective-permute-start(bf16[14,16,256]{2,1,0:T(8,128)(2,1)S(1)} %get-tuple-element.33), channel_id=1, source_target_pairs={{0,64},{32,96},{64,0},{96,32},{1,65},{33,97},{65,1},{97,33},{2,66}... | collective-permute-start | bytes 344072 | tf_op jit(solution)/shard_map/ppermute | solution.py:86
  83.0 18.0 %collective-permute-start.2 = (bf16[14,16,256]{2,1,0:T(8,128)(2,1)S(1)}, bf16[14,16,256]{2,1,0:T(8,128)(2,1)S(1)}, u32[]{:S(2)}, u32[]{:S(2)}) collective-permute-start(bf16[14,16,256]{2,1,0:T(8,128)(2,1)S(1)} %get-tuple-element.33), channel_id=1, source_target_pairs={{0,32},{32,64},{64,96},{96,0},{1,33},{33,65},{65,97},{97,1},{2,34}... | collective-permute-start | bytes 344072 | tf_op jit(solution)/shard_map/ppermute | solution.py:86
  97.2 8.5 %collective-permute-start.9 = (bf16[2,14,16,256]{3,2,1,0:T(8,128)(2,1)}, bf16[2,14,16,256]{3,2,1,0:T(8,128)(2,1)S(1)}, u32[]{:S(2)}, u32[]{:S(2)}) collective-permute-start(bf16[2,14,16,256]{3,2,1,0:T(8,128)(2,1)} %get-tuple-element.29), channel_id=1, source_target_pairs={{0,96},{32,0},{64,32},{96,64},{1,97},{33,1},{65,33},{97,65},{2,98}... | collective-permute-start | bytes 688136 | tf_op jit(solution)/shard_map/ppermute | solution.py:86
  99.9 6.7 %collective-permute-start.8 = (bf16[2,14,16,256]{3,2,1,0:T(8,128)(2,1)}, bf16[2,14,16,256]{3,2,1,0:T(8,128)(2,1)S(1)}, u32[]{:S(2)}, u32[]{:S(2)}) collective-permute-start(bf16[2,14,16,256]{3,2,1,0:T(8,128)(2,1)} %get-tuple-element.29), channel_id=1, source_target_pairs={{0,64},{32,96},{64,0},{96,32},{1,65},{33,97},{65,1},{97,33},{2,66}... | collective-permute-start | bytes 688136 | tf_op jit(solution)/shard_map/ppermute | solution.py:86
  100.2 8.7 %collective-permute-start.7 = (bf16[2,14,16,256]{3,2,1,0:T(8,128)(2,1)}, bf16[2,14,16,256]{3,2,1,0:T(8,128)(2,1)S(1)}, u32[]{:S(2)}, u32[]{:S(2)}) collective-permute-start(bf16[2,14,16,256]{3,2,1,0:T(8,128)(2,1)} %get-tuple-element.29), channel_id=1, source_target_pairs={{0,32},{32,64},{64,96},{96,0},{1,33},{33,65},{65,97},{97,1},{2,34}... | collective-permute-start | bytes 688136 | tf_op jit(solution)/shard_map/ppermute | solution.py:86
  101.8 9.3 %collective-permute-start.5 = (bf16[4,14,16,256]{3,2,1,0:T(8,128)(2,1)}, bf16[4,14,16,256]{3,2,1,0:T(8,128)(2,1)}, u32[]{:S(2)}, u32[]{:S(2)}) collective-permute-start(bf16[4,14,16,256]{3,2,1,0:T(8,128)(2,1)} %get-tuple-element.21), channel_id=1, source_target_pairs={{0,16},{16,0},{1,17},{17,1},{2,18},{18,2},{3,19},{19,3},{4,20},{20... | collective-permute-start | bytes 1376264 | tf_op jit(solution)/shard_map/ppermute | solution.py:86
  105.6 3.3 %copy-start.8 = (bf16[2,14,16,256]{3,2,1,0:T(8,128)(2,1)}, bf16[2,14,16,256]{3,2,1,0:T(8,128)(2,1)S(1)}, u32[]{:S(2)}) copy-start(bf16[2,14,16,256]{3,2,1,0:T(8,128)(2,1)S(1)} %collective-permute-done.9) | copy-start | bytes 688132
  106.6 2.4 copy-start.9
  108.9 0.7 copy-start.10
  113.2 1.2 copy-start.4
  115.3 16.7 %collective-permute-start.12 = (bf16[14,16,256]{2,1,0:T(8,128)(2,1)S(1)}, bf16[14,16,256]{2,1,0:T(8,128)(2,1)S(1)}, u32[]{:S(2)}, u32[]{:S(2)}) collective-permute-start(bf16[14,16,256]{2,1,0:T(8,128)(2,1)S(1)} %get-tuple-element.27), channel_id=1, source_target_pairs={{0,12},{4,0},{8,4},{12,8},{1,13},{5,1},{9,5},{13,9},{2,14},{6,2},{... | collective-permute-start | bytes 344072 | tf_op jit(solution)/shard_map/ppermute | solution.py:86
  127.7 5.5 %collective-permute-start.11 = (bf16[14,16,256]{2,1,0:T(8,128)(2,1)S(1)}, bf16[14,16,256]{2,1,0:T(8,128)(2,1)S(1)}, u32[]{:S(2)}, u32[]{:S(2)}) collective-permute-start(bf16[14,16,256]{2,1,0:T(8,128)(2,1)S(1)} %get-tuple-element.27), channel_id=1, source_target_pairs={{0,8},{4,12},{8,0},{12,4},{1,9},{5,13},{9,1},{13,5},{2,10},{6,14},... | collective-permute-start | bytes 344072 | tf_op jit(solution)/shard_map/ppermute | solution.py:86
  128.3 8.3 %collective-permute-start.10 = (bf16[14,16,256]{2,1,0:T(8,128)(2,1)S(1)}, bf16[14,16,256]{2,1,0:T(8,128)(2,1)S(1)}, u32[]{:S(2)}, u32[]{:S(2)}) collective-permute-start(bf16[14,16,256]{2,1,0:T(8,128)(2,1)S(1)} %get-tuple-element.27), channel_id=1, source_target_pairs={{0,4},{4,8},{8,12},{12,0},{1,5},{5,9},{9,13},{13,1},{2,6},{6,10},{... | collective-permute-start | bytes 344072 | tf_op jit(solution)/shard_map/ppermute | solution.py:86
  129.0 7.7 %collective-permute-start.15 = (bf16[14,16,256]{2,1,0:T(8,128)(2,1)S(1)}, bf16[14,16,256]{2,1,0:T(8,128)(2,1)S(1)}, u32[]{:S(2)}, u32[]{:S(2)}) collective-permute-start(bf16[14,16,256]{2,1,0:T(8,128)(2,1)S(1)} %get-tuple-element.26), channel_id=1, source_target_pairs={{0,2},{2,0},{1,3},{3,1},{4,6},{6,4},{5,7},{7,5},{8,10},{10,8},{9,1... | collective-permute-start | bytes 344072 | tf_op jit(solution)/shard_map/ppermute | solution.py:86
  136.6 14.9 %collective-permute-start.13 = (bf16[4,14,16,256]{3,2,1,0:T(8,128)(2,1)S(1)}, bf16[4,14,16,256]{3,2,1,0:T(8,128)(2,1)S(1)}, u32[]{:S(2)}, u32[]{:S(2)}) collective-permute-start(bf16[4,14,16,256]{3,2,1,0:T(8,128)(2,1)S(1)} %get-tuple-element.19), channel_id=1, source_target_pairs={{0,2},{2,0},{1,3},{3,1},{4,6},{6,4},{5,7},{7,5},{8,10},{10,8},{9,1... | collective-permute-start | bytes 1376264 | tf_op jit(solution)/shard_map/ppermute | solution.py:86
  136.8 6.6 %collective-permute-start.18 = (bf16[2,14,16,256]{3,2,1,0:T(8,128)(2,1)S(1)}, bf16[2,14,16,256]{3,2,1,0:T(8,128)(2,1)S(1)}, u32[]{:S(2)}, u32[]{:S(2)}) collective-permute-start(bf16[2,14,16,256]{3,2,1,0:T(8,128)(2,1)S(1)} %get-tuple-element.23), channel_id=1, source_target_pairs={{0,12},{4,0},{8,4},{12,8},{1,13},{5,1},{9,5},{13,9},{2,14},{6,2},{... | collective-permute-start | bytes 688136 | tf_op jit(solution)/shard_map/ppermute | solution.py:86
  136.9 7.6 %collective-permute-start.17 = (bf16[2,14,16,256]{3,2,1,0:T(8,128)(2,1)S(1)}, bf16[2,14,16,256]{3,2,1,0:T(8,128)(2,1)S(1)}, u32[]{:S(2)}, u32[]{:S(2)}) collective-permute-start(bf16[2,14,16,256]{3,2,1,0:T(8,128)(2,1)S(1)} %get-tuple-element.23), channel_id=1, source_target_pairs={{0,8},{4,12},{8,0},{12,4},{1,9},{5,13},{9,1},{13,5},{2,10},{6,14},... | collective-permute-start | bytes 688136 | tf_op jit(solution)/shard_map/ppermute | solution.py:86
  138.0 12.8 %collective-permute-start.16 = (bf16[2,14,16,256]{3,2,1,0:T(8,128)(2,1)S(1)}, bf16[2,14,16,256]{3,2,1,0:T(8,128)(2,1)S(1)}, u32[]{:S(2)}, u32[]{:S(2)}) collective-permute-start(bf16[2,14,16,256]{3,2,1,0:T(8,128)(2,1)S(1)} %get-tuple-element.23), channel_id=1, source_target_pairs={{0,4},{4,8},{8,12},{12,0},{1,5},{5,9},{9,13},{13,1},{2,6},{6,10},{... | collective-permute-start | bytes 688136 | tf_op jit(solution)/shard_map/ppermute | solution.py:86
  151.0 2.8 collective-permute-start.19
  151.7 3.5 %collective-permute-start.14 = (bf16[2,4,14,16,256]{4,3,2,1,0:T(8,128)(2,1)S(1)}, bf16[2,4,14,16,256]{4,3,2,1,0:T(8,128)(2,1)}, u32[]{:S(2)}, u32[]{:S(2)}) collective-permute-start(bf16[2,4,14,16,256]{4,3,2,1,0:T(8,128)(2,1)S(1)} %pad_maximum_fusion.2.a0_ref), channel_id=1, source_target_pairs={{0,1},{1,0},{2,3},{3,2},{4,5},{5,4},{6,7},{7,6},{8,9},{9,8},{10,11... | collective-permute-start | bytes 2752520 | tf_op jit(solution)/shard_map/ppermute | solution.py:345
  165.8 30.9 %all-to-all-start.2 = ((f32[16,2,32,512]{3,2,1,0:T(8,128)}), f32[16,2,32,512]{3,2,1,0:T(8,128)S(1)}, u32[]{:S(2)}, u32[]{:S(2)}) async-start(f32[16,2,32,512]{3,2,1,0:T(8,128)} %get-tuple-element.5), calls=%async_computation.2 | async-start | bytes 4194304 | tf_op jit(solution)/shard_map/all_to_all | solution.py:349
  169.7 103.4 %all-gather.2.cloned.1.call-start = ((), (), s32[]{:S(2)}) async-start(), calls=%async_computation.3 | async-start | bytes 4456448 | tf_op jit(solution)/shard_map/all_gather | solution.py:352
  198.4 2.0 copy-start.5
  261.5 1.8 copy-start.1
  273.1 4.5 %copy-start.6 = (f32[2,2,448,448]{3,2,1,0:T(8,128)S(1)}, f32[2,2,448,448]{3,2,1,0:T(8,128)}, u32[]{:S(2)}) copy-start(f32[2,2,448,448]{3,2,1,0:T(8,128)} %rev.3) | copy-start | bytes 9633796
Sparse Core Ops, SparseCore 0:
  197.6 34.8 all-gather.1

commit v2 on v1

--- a/solution.py
+++ b/solution.py
@@ -16,8 +16,8 @@
 COL = ("x", "zl", "core")
 F32 = jnp.float32
 BF = jnp.bfloat16
-HIGH = lax.Precision.HIGHEST
 VMEM = pl.BlockSpec(memory_space=pltpu.VMEM)
+SMEM = pl.BlockSpec(memory_space=pltpu.SMEM)
 STEP = 64
 
 
@@ -29,56 +29,75 @@
     return pl.CostEstimate(flops=int(flops), bytes_accessed=int(nbytes), transcendentals=0)
 
 
-def send_kernel(a_ref, b_ref, o_ref):
-    o_ref[...] = jnp.dot(a_ref[0], b_ref[0], preferred_element_type=F32)[None]
-
-
-def keep_kernel(a_ref, b_ref, r_ref, o_ref):
-    total = jnp.dot(a_ref[0], b_ref[0], preferred_element_type=F32) + r_ref[0]
+def probe_kernel(at_ref, a_ref, b_ref, sent_ref, kept_ref):
+    total = contract(a_ref[0], b_ref[0], 1, 1)
+    half = sent_ref.shape[2]
+    low = total[:, :half]
+    pad = jnp.zeros((total.shape[0], 2 * half - total.shape[1]), F32)
+    high = jnp.concatenate([total[:, half:], pad], axis=1)
+    first = at_ref[2] == 0
+    kept_ref[0] = jnp.where(first, low, high)
+    sent_ref[0] = jnp.where(first, high, low)
+
+
+def probe(at, a, b, half):
+    count, rows, depth = a.shape
+    probes = b.shape[1]
+    part = jax.ShapeDtypeStruct((count, rows, half), F32)
+    return pl.pallas_call(
+        probe_kernel,
+        grid=(count, rows // LEAF),
+        out_shape=[part, part],
+        in_specs=[
+            SMEM,
+            pl.BlockSpec((1, LEAF, depth), lambda k, i: (k, i, 0)),
+            pl.BlockSpec((1, probes, depth), lambda k, i: (k, 0, 0)),
+        ],
+        out_specs=[pl.BlockSpec((1, LEAF, half), lambda k, i: (k, i, 0))] * 2,
+        compiler_params=params(40),
+        cost_estimate=cost(4 * count * rows * depth * half, 2 * a.size + 8 * count * rows * half),
+    )(at, a, b)
+
+
+def pack_kernel(at_ref, a_ref, b_ref, o_ref, own_ref, sum_ref):
+    total = a_ref[0] + b_ref[0]
+    sum_ref[...] = total
     chips, blocks, rows, _ = o_ref.shape
+    chip_here = at_ref[0] * 2 + at_ref[1]
     for block in range(blocks):
         for chip in range(chips):
             start = (block * chips + chip) * rows
             o_ref[chip, block] = total[start : start + rows].astype(BF)
-
-
-def probe_send(a, b):
-    count, rows, depth = a.shape
-    half = b.shape[2]
-    per = rows // LEAF
-    return pl.pallas_call(
-        send_kernel,
-        grid=(count, per),
-        out_shape=jax.ShapeDtypeStruct((count, rows, half), F32),
-        in_specs=[
-            pl.BlockSpec((1, LEAF, depth), lambda k, i: (k, i, 0)),
-            pl.BlockSpec((1, depth, half), lambda k, i: (k, 0, 0)),
-        ],
-        out_specs=pl.BlockSpec((1, LEAF, half), lambda k, i: (k, i, 0)),
-        compiler_params=params(40),
-        cost_estimate=cost(2 * count * rows * depth * half, 2 * a.size + 4 * count * rows * half),
-    )(a, b)
-
-
-def probe_keep(a, b, received, chips):
-    count, rows, depth = a.shape
-    half = b.shape[2]
+        own = pl.multiple_of((block * chips + chip_here) * rows, rows)
+        own_ref[block] = sum_ref[pl.ds(own, rows), :]
+
+
+def pack(at, kept, received, chips):
+    count, rows, half = kept.shape
     per = rows // LEAF
     blocks = LEAF // BLOCK
     slab = BLOCK // chips
-    return pl.pallas_call(
-        keep_kernel,
+    whole = count * rows // BLOCK
+    return pl.pallas_call(
+        pack_kernel,
         grid=(count, per),
-        out_shape=jax.ShapeDtypeStruct((chips, count * rows // BLOCK, slab, half), BF),
+        out_shape=[
+            jax.ShapeDtypeStruct((chips, whole, slab, half), BF),
+            jax.ShapeDtypeStruct((whole, slab, half), F32),
+        ],
         in_specs=[
-            pl.BlockSpec((1, LEAF, depth), lambda k, i: (k, i, 0)),
-            pl.BlockSpec((1, depth, half), lambda k, i: (k, 0, 0)),
+            SMEM,
             pl.BlockSpec((1, LEAF, half), lambda k, i: (k, i, 0)),
-        ],
-        out_specs=pl.BlockSpec((chips, blocks, slab, half), lambda k, i: (0, k * per + i, 0, 0)),
-        compiler_params=params(40),
-        cost_estimate=cost(2 * count * rows * depth * half, 2 * a.size + 6 * count * rows * half),
-    )(a, b, received)
+            pl.BlockSpec((1, LEAF, half), lambda k, i: (k, i, 0)),
+        ],
+        out_specs=[
+            pl.BlockSpec((chips, blocks, slab, half), lambda k, i: (0, k * per + i, 0, 0)),
+            pl.BlockSpec((blocks, slab, half), lambda k, i: (k * per + i, 0, 0)),
+        ],
+        scratch_shapes=[pltpu.VMEM((LEAF, half), F32)],
+        compiler_params=params(24),
+        cost_estimate=cost(kept.size, 10 * kept.size),
+    )(at, kept, received)
 
 
 def shift(value, axis, by):
@@ -97,46 +116,49 @@
     return ring_gather(first_ring, small), ring_gather(second_pair, big)
 
 
-def sum_kernel(k_ref, o_ref):
-    total = k_ref[0].astype(F32)
-    for chip in range(1, k_ref.shape[0]):
-        total += k_ref[chip].astype(F32)
-    o_ref[...] = total.astype(o_ref.dtype)
-
-
-def sum_shares(shares, dtype):
+def sum_of(shares_ref, own, here, at):
+    for chip in range(shares_ref.shape[0]):
+        own += jnp.where(here != chip, shares_ref[(chip, *at)].astype(F32), 0.0)
+    return own
+
+
+def sum_kernel(at_ref, k_ref, own_ref, o_ref):
+    here = at_ref[0] * 2 + at_ref[1]
+    for block in range(o_ref.shape[0]):
+        o_ref[block] = sum_of(k_ref, own_ref[block], here, (block,)).astype(o_ref.dtype)
+
+
+def sum_shares(at, shares, own, dtype):
     return pl.pallas_call(
         sum_kernel,
         out_shape=jax.ShapeDtypeStruct(shares.shape[1:], dtype),
-        in_specs=[VMEM],
+        in_specs=[SMEM, VMEM, VMEM],
         out_specs=VMEM,
         compiler_params=params(24),
         cost_estimate=cost(shares.size, 2 * shares.size),
-    )(shares)
-
-
-def extend_kernel(at_ref, p_ref, first_ref, second_ref, o_ref):
+    )(at, shares, own)
+
+
+def extend_kernel(at_ref, from_ref, p_ref, own_ref, first_ref, second_ref, o_ref):
+    here = at_ref[0] * 2 + at_ref[1]
     for block in range(p_ref.shape[1]):
-        total = p_ref[0, block].astype(F32)
-        for chip in range(1, p_ref.shape[0]):
-            total += p_ref[chip, block].astype(F32)
+        total = sum_of(p_ref, own_ref[block], here, (block,))
         for kid, ref in enumerate((first_ref, second_ref)):
-            near, far, place = (at_ref[kid, part, block] for part in range(3))
-            there = at_ref[kid, 3, block]
-            share = ref[near, far, place].astype(F32)
-            total += jnp.where(there > 0, share, 0.0)
+            near, far, place = (from_ref[kid, part, block] for part in range(3))
+            there = from_ref[kid, 3, block]
+            total += jnp.where(there > 0, ref[near, far, place].astype(F32), 0.0)
         o_ref[block] = total.astype(BF)
 
 
-def extend_add(at, parent, first, second):
+def extend_add(at, source, parent, own, first, second):
     return pl.pallas_call(
         extend_kernel,
         out_shape=jax.ShapeDtypeStruct(parent.shape[1:], BF),
-        in_specs=[pl.BlockSpec(memory_space=pltpu.SMEM), VMEM, VMEM, VMEM],
+        in_specs=[SMEM, SMEM, VMEM, VMEM, VMEM, VMEM],
         out_specs=VMEM,
         compiler_params=params(32),
         cost_estimate=cost(parent.size, 6 * parent.size),
-    )(at, parent, first, second)
+    )(at, source, parent, own, first, second)
 
 
 def halves(x):
@@ -168,7 +190,7 @@
                     y_ref[count:, rows, lanes] = second_ref[i, j]
         for leaf in range(leaves):
             y = y_ref[leaf * per : (leaf + 1) * per].reshape(LEAF, 2 * half)
-            gram_ref[leaf] = contract(y, y, 0, 0)[:order, :order]
+            gram_ref[leaf] = contract(y, y, 0, 0)[:order]
 
     leaf = lax.rem(col, 2) * 2 + step
     sibling = lax.rem(col, 2) * 2 + 1 - step
@@ -198,13 +220,13 @@
                 whole,
             ],
             out_specs=[
-                pl.BlockSpec((leaves, order, order), lambda i, at: (0, 0, 0)),
+                pl.BlockSpec((leaves, order, wide), lambda i, at: (0, 0, 0)),
                 pl.BlockSpec((16, 1, wide // 16, wide), lambda i, at: (0, i, 0, 0)),
             ],
             scratch_shapes=[pltpu.VMEM((leaves * LEAF // BLOCK, BLOCK, wide), BF)],
         ),
         out_shape=[
-            jax.ShapeDtypeStruct((leaves, order, order), F32),
+            jax.ShapeDtypeStruct((leaves, order, wide), F32),
             jax.ShapeDtypeStruct((16, 2, wide // 16, wide), F32),
         ],
         compiler_params=params(52),
@@ -235,16 +257,15 @@
                 rows[i] = rows[i] - c * scaled
 
 
-def inverse_kernel(a_ref, w_ref):
+def inverse_kernel(a_ref, w_ref, *, first, last):
     leaves, order, wide = w_ref.shape
-    w_ref[:, :, order - order % 128 :] = jnp.zeros((leaves, order, wide - order + order % 128), F32)
-    w_ref[:, :, :order] = a_ref[...]
+    w_ref[...] = a_ref[...]
     lane = lax.broadcasted_iota(jnp.int32, (STEP, 128), 1)
     sub = lax.broadcasted_iota(jnp.int32, (STEP, 128), 0)
     col = lax.broadcasted_iota(jnp.int32, (STEP, wide), 1)
     row = lax.broadcasted_iota(jnp.int32, (STEP, wide), 0)
 
-    @pl.loop(0, order // STEP)
+    @pl.loop(first, last)
     def _(k):
         base = pl.multiple_of(k * STEP, STEP)
         tile = pl.multiple_of(lax.div(base, 128) * 128, 128)
@@ -277,23 +298,58 @@
                 def _(rows=rows):
                     w_ref[leaf, rows, :] = jnp.where(inside, 0.0, w_ref[leaf, rows, :]) - update[rows]
 
+    if last < order // STEP:
+        return
     for leaf in range(leaves):
         for i in range(order // STEP):
             rows = slice(i * STEP, (i + 1) * STEP)
             w_ref[leaf, rows, :] = jnp.where(col <= row + i * STEP, w_ref[leaf, rows, :], 0.0)
 
 
-def factor_inverse(gram):
-    leaves, order, _ = gram.shape
-    wide = -(-order // 128) * 128
-    return pl.pallas_call(
-        inverse_kernel,
-        out_shape=jax.ShapeDtypeStruct((leaves, order, wide), F32),
+def factor_inverse(work, first, last):
+    return pl.pallas_call(
+        functools.partial(inverse_kernel, first=first, last=last),
+        out_shape=jax.ShapeDtypeStruct(work.shape, F32),
         in_specs=[VMEM],
         out_specs=VMEM,
         compiler_params=params(40),
-        cost_estimate=cost(40e9, 8 * gram.size),
-    )(gram)
+        cost_estimate=cost((last - first) * 10e9, 8 * work.size),
+    )(work)
+
+
+def finish_kernel(at_ref, w_ref, own_ref, cross_ref, basis_ref, core_ref):
+    leaves, order, wide = w_ref.shape
+    rows = core_ref.shape[1]
+    base = at_ref[3] * rows
+    odd = lax.rem(base, 8)
+    base = pl.multiple_of(base - odd, 8)
+    tall = rows + 4
+    for leaf in range(leaves):
+        hi, lo = halves(w_ref[leaf])
+        own = own_ref[leaf].astype(BF)
+        basis_ref[leaf] = (contract(own, hi, 1, 1) + contract(own, lo, 1, 1)) * math.sqrt(LEAF)
+        left = w_ref[leaf, pl.ds(base, tall), :]
+        left = jnp.where(odd > 0, jnp.concatenate([left[4:], left[:4]], axis=0), left)
+        cross = cross_ref[:, leaf].reshape(wide, wide)
+        half_way, rest = halves(product3(left, cross))
+        hi, lo = halves(w_ref[leaf ^ 1])
+        core = contract(half_way, hi, 1, 1) + (contract(half_way, lo, 1, 1) + contract(rest, hi, 1, 1))
+        core_ref[leaf] = core[:rows]
+
+
+def finish(at, inverse, own, cross, rows):
+    leaves, order, _ = inverse.shape
+    return pl.pallas_call(
+        finish_kernel,
+        out_shape=[
+            jax.ShapeDtypeStruct((leaves, own.shape[1], order), F32),
+            jax.ShapeDtypeStruct((leaves, rows, order), F32),
+        ],
+        in_specs=[SMEM, VMEM, VMEM, VMEM],
+        out_specs=[VMEM, VMEM],
+        compiler_params=params(40),
+        cost_estimate=cost(4e9, 4 * (inverse.size + cross.size)),
+    )(at, inverse, own, cross)
 
 
 def local(parent_front, child_update, parent_test, child_test, child_map):
@@ -308,21 +364,17 @@
     leaf_count = own_blocks * BLOCK // LEAF
     swap = [(0, 1), (1, 0)]
 
-    def half_of(test, which):
-        padded = jnp.pad(test, ((0, 0), (0, 0), (0, 2 * half - probes)))
-        return lax.dynamic_slice_in_dim(padded, which * half, half, 2)
-
-    front, whole_test = parent_front[None], parent_test[None]
-    kid_sent = lax.ppermute(
-        probe_send(child_update, half_of(child_test, 1 - core)), "core", swap
-    )
-    own_sent = lax.ppermute(probe_send(front, half_of(whole_test, 1 - core)), "core", swap)
-    kid_part = probe_keep(child_update, half_of(child_test, core), kid_sent, chips)
+    at = jnp.stack([x, zl, core, col_index]).astype(jnp.int32)
+    kid_sent, kid_kept = probe(at, child_update, jnp.swapaxes(child_test, 1, 2), half)
+    kid_sent = lax.ppermute(kid_sent, "core", swap)
+    own_sent, own_kept = probe(at, parent_front[None], parent_test.T[None], half)
+    own_sent = lax.ppermute(own_sent, "core", swap)
+    kid_part, kid_rest = pack(at, kid_kept, kid_sent, chips)
     kid_share = lax.all_to_all(kid_part, CHIP, 0, 0, tiled=True)
-    own_part = probe_keep(front, half_of(whole_test, core), own_sent, chips)
+    own_part, own_rest = pack(at, own_kept, own_sent, chips)
     own_share = lax.all_to_all(own_part, CHIP, 0, 0, tiled=True)
 
-    kids = sum_shares(kid_share, BF)
+    kids = sum_shares(at, kid_share, kid_rest, BF)
     first, second = two_way_gather(kids[:kid_blocks], kids[kid_blocks:], "y", "zh")
 
     targets = row_index * own_blocks + jnp.arange(own_blocks, dtype=jnp.int32)
@@ -332,43 +384,36 @@
     owner, place = source // kid_blocks, source % kid_blocks
     ring = (y - owner // 2) % 4
     pair = (zh - owner % 2) % 2
-    at = jnp.stack(
+    origin = jnp.stack(
         [
             jnp.stack([pair[0], ring[0], place[0], there[0]]),
             jnp.stack([ring[1], pair[1], place[1], there[1]]),
         ]
     ).astype(jnp.int32)
-    share = extend_add(at, own_share, first, second)
+    share = extend_add(at, origin, own_share, own_rest, first, second)
 
     cut = own_blocks // 2
     mine = two_way_gather(share[:cut], share[cut:], "x", "zl")
     other = tuple(lax.ppermute(part, "core", swap) for part in mine)
-    place_of = jnp.stack([x, zl, core, col_index]).astype(jnp.int32)
-    gram, cross = grams(place_of, parent_front, mine, other, probes)
-
-    cross = lax.all_to_all(cross, COL, 0, 0, tiled=True)
-    cross = lax.dynamic_slice_in_dim(cross, 2 * row_index, 2, 0)
-    cross = cross.reshape(leaf_count, cross.shape[2], 2 * half)
-    cross = lax.all_gather(cross, COL)
-    inverse = factor_inverse(gram)[:, :, :probes]
+    gram, cross = grams(at, parent_front, mine, other, probes)
 
     own_rows = jnp.where(
         core == 0,
         jnp.concatenate([share, jnp.concatenate([other[0][0, 0], other[1][0, 0]], 0)], axis=2),
         jnp.concatenate([jnp.concatenate([other[0][0, 0], other[1][0, 0]], 0), share], axis=2),
     )
-    own_rows = lax.dynamic_slice_in_dim(own_rows, core * 8, 8, 1)[:, :, :probes]
-    leaves = own_rows.reshape(leaf_count, -1, probes).astype(F32)
-    basis = jnp.einsum("lkr,lsr->lks", leaves, inverse, precision=HIGH) * math.sqrt(LEAF)
-    leaf_basis = basis.astype(BF).reshape(own_blocks, 8, probes)
-
-    rows = probes // lax.axis_size(COL)
-    left = lax.dynamic_slice_in_dim(inverse, col_index * rows, rows, 1)
-    cross = jnp.moveaxis(cross, 0, 1).reshape(leaf_count, 2 * half, 2 * half)[:, :probes, :probes]
-    siblings = inverse.reshape(-1, 2, probes, probes)[:, ::-1].reshape(inverse.shape)
-    couplings = jnp.einsum("lir,lrs->lis", left, cross, precision=HIGH)
-    couplings = jnp.einsum("lis,lts->lit", couplings, siblings, precision=HIGH)
-    return (leaf_basis, couplings)
+    own_rows = lax.dynamic_slice_in_dim(own_rows, core * 8, 8, 1).astype(F32)
+    own_rows = own_rows.reshape(leaf_count, -1, 2 * half)
+
+    cross = lax.all_to_all(cross, COL, 0, 0, tiled=True)
+    cross = lax.dynamic_slice_in_dim(cross, 2 * row_index, 2, 0)
+    cross = cross.reshape(leaf_count, cross.shape[2], 2 * half)
+    work = factor_inverse(gram, 0, 3)
+    work, cross = lax.optimization_barrier((work, cross))
+    cross = lax.all_gather(cross, COL)
+    inverse = factor_inverse(work, 3, probes // STEP)
+    basis, couplings = finish(at, inverse, own_rows, cross, probes // lax.axis_size(COL))
+    return (basis.astype(BF).reshape(own_blocks, 8, probes), couplings)
 
 
 def solution(mesh):

time: 290 us -> 253 us (0.87)
  waiting for transfers between devices: 86.5 us -> 50.7 us
  matrix products: 12.4 us -> 0 us
  starting transfers between devices: 42.4 us -> 52 us
    all_to_all x1, waiting for transfers between devices: 27 us -> 0.01 us  [local(): cross = lax.all_to_all(cross, COL, 0, 0, tiled=True)]
    dot_general x3 -> x0, matrix products: 12.4 us -> none  [the longest x1 4.59 us: local(): jnp.einsum('lkr,lsr->lks', leaves, inverse, precision=HIGH)]
    ppermute x16, waiting for transfers between devices: 38.8 us -> 27.4 us  [shift(): lax.ppermute(value, axis, [(i, (i + by) % size) for i in range(size)])]
    unnamed x32 -> x44, local copies, waits for them, and re-layouts: 17.3 us -> 24.2 us
    ppermute x16, starting transfers between devices: 27.2 us -> 31.8 us  [shift(): lax.ppermute(value, axis, [(i, (i + by) % size) for i in range(size)])]
    ppermute x2, starting transfers between devices: 0.68 us -> 4.99 us  [local(): other = tuple((lax.ppermute(part, 'core', swap) for part in mine))]
    rev x1 -> x0, local copies, waits for them, and re-layouts: 4.22 us -> none  [local(): inverse.reshape(-1, 2, probes, probes)[:, ::-1].reshape(inverse.shape)]
    pallas_call x5 -> x7, Pallas kernels: 88.3 us -> 87.9 us  [the longest x2 61.7 us: factor_inverse(): pl.pallas_call(functools.partial(inverse_kernel, first=first, last=last),...]
  transfers between devices with their start and end apart: 24 -> 24, of which waited for: 15 -> 11; matrix products, arithmetic and copies ran while one was open for 7% -> 3% of each run, Pallas kernels for 29% -> 31%
where the time goes in v2:
time: 253 us; the launch traced here: 252 us
  Pallas kernels  101 us (40%)
  starting transfers between devices  52 us (21%)
  waiting for transfers between devices  50.7 us (20%)
  local copies, waits for them, and re-layouts  27.5 us (11%)
  between operations  14.3 us (6%)
  other arithmetic  6.77 us (3%)
    pallas_call x2, Pallas kernels, factor_inverse(): pl.pallas_call(functools.partial(inverse_kernel, first=first, last=last),...  61.7 us
    ppermute x16, starting transfers between devices, shift(): lax.ppermute(value, axis, [(i, (i + by) % size) for i in range(size)])  31.8 us
    ppermute x16, waiting for transfers between devices, shift(): lax.ppermute(value, axis, [(i, (i + by) % size) for i in range(size)])  27.4 us
    unnamed x44, local copies, waits for them, and re-layouts  24.2 us
    all_to_all x1, waiting for transfers between devices, local(): kid_share = lax.all_to_all(kid_part, CHIP, 0, 0, tiled=True)  20.1 us
    pallas_call x2, Pallas kernels, probe(): pl.pallas_call(probe_kernel, grid=(count, rows // LEAF), out_shape=[part,...  17.3 us
    pallas_call x1, Pallas kernels, grams(): pl.pallas_call(gram_kernel, grid_spec=pltpu.PrefetchScalarGridSpec(num_sc...  10.7 us
    all_to_all x1, starting transfers between devices, local(): kid_share = lax.all_to_all(kid_part, CHIP, 0, 0, tiled=True)  5.59 us
  transfers between devices with their start and end apart: 24, of which 11 were waited for; matrix products, arithmetic and copies ran while one was open for 3% of the time, Pallas kernels for 31%

profile of v2, /device:TPU:1, one launch (start us, length us, event | category | flops | bytes accessed | tf_op | source)
XLA Modules:
  0.0 251.9 jit_solution(3955991371099775215)
XLA Ops:
  7.3 1.4 copy-done.8
  8.7 6.5 %shard_map.70 = (f32[2,1792,256]{2,1,0:T(8,128)S(1)}, f32[2,1792,256]{2,1,0:T(8,128)S(1)}) custom-call(s32[4]{0:T(128)S(1)} %pad_add_fusion.1.at_ref, bf16[2,1792,896]{2,1,0:T(8,128)(2,1)} %a_ref.1, bf16[2,448,896]{2,1,0:T(8,128)(2,1)S(1)} %bitcast.57), custom_call_target="tpu_custom_call" | custom-call | flops 3288334336 | bytes 13762560 | tf_op jit(solution)/shard_map/pallas_call | solution.py:47
  15.2 1.5 collective-permute-start.1
  16.7 10.8 %shard_map.68 = (f32[1,3584,256]{2,1,0:T(8,128)}, f32[1,3584,256]{2,1,0:T(8,128)S(1)}) custom-call(s32[4]{0:T(128)S(1)} %pad_add_fusion.1.at_ref, bf16[1,3584,1792]{2,1,0:T(8,128)(2,1)} %bitcast.77, bf16[1,448,1792]{2,1,0:T(8,128)(2,1)S(1)} %bitcast.58), custom_call_target="tpu_custom_call" | custom-call | flops 6576668672 | bytes 20185088 | tf_op jit(solution)/shard_map/pallas_call | solution.py:47
  27.5 1.3 shard_map.71
  29.3 1.4 copy-done.6
  30.6 5.6 %all-to-all-start.1 = ((bf16[8,28,16,256]{3,2,1,0:T(8,128)(2,1)}), bf16[8,28,16,256]{3,2,1,0:T(8,128)(2,1)S(1)}, u32[]{:S(2)}, u32[]{:S(2)}) async-start(bf16[8,28,16,256]{3,2,1,0:T(8,128)(2,1)} %copy-done.6), calls=%async_computation.1 | async-start | bytes 3670016 | tf_op jit(solution)/shard_map/all_to_all | solution.py:373
  37.4 2.0 copy-done.3
  39.5 3.1 %shard_map.69 = (bf16[8,28,16,256]{3,2,1,0:T(8,128)(2,1)S(1)}, f32[28,16,256]{2,1,0:T(8,128)S(1)}) custom-call(s32[4]{0:T(128)S(1)} %pad_add_fusion.1.at_ref, f32[1,3584,256]{2,1,0:T(8,128)S(1)} %copy-done.3, f32[1,3584,256]{2,1,0:T(8,128)} %collective-permute-done.b_ref), custom_call_target="tpu_custom_call" | custom-call | flops 917504 | bytes 9175040 | tf_op jit(solution)/shard_map/pallas_call | solution.py:81
  42.6 1.2 copy-done.5
  43.8 20.1 %all-to-all-done.1.k_ref = bf16[8,28,16,256]{3,2,1,0:T(8,128)(2,1)S(1)} async-done(((bf16[8,28,16,256]{3,2,1,0:T(8,128)(2,1)}), bf16[8,28,16,256]{3,2,1,0:T(8,128)(2,1)S(1)}, u32[]{:S(2)}, u32[]{:S(2)}) %all-to-all-start.1) | async-done | bytes 1835040 | tf_op jit(solution)/shard_map/all_to_all | solution.py:373
  64.0 1.2 copy-done
  65.2 3.6 %all-to-all-start = ((bf16[8,28,16,256]{3,2,1,0:T(8,128)(2,1)}), bf16[8,28,16,256]{3,2,1,0:T(8,128)(2,1)S(1)}, u32[]{:S(2)}, u32[]{:S(2)}) async-start(bf16[8,28,16,256]{3,2,1,0:T(8,128)(2,1)} %copy-done.5), calls=%async_computation | async-start | bytes 3670016 | tf_op jit(solution)/shard_map/all_to_all | solution.py:375
  68.9 1.5 copy-done.1
  71.3 3.4 %collective-permute-start.6 = (bf16[14,16,256]{2,1,0:T(8,128)(2,1)S(1)}, bf16[14,16,256]{2,1,0:T(8,128)(2,1)S(1)}, u32[]{:S(2)}, u32[]{:S(2)}) collective-permute-start(bf16[14,16,256]{2,1,0:T(8,128)(2,1)S(1)} %get-tuple-element.52), channel_id=1, source_target_pairs={{0,16},{16,0},{1,17},{17,1},{2,18},{18,2},{3,19},{19,3},{4,20},{20... | collective-permute-start | bytes 344072 | tf_op jit(solution)/shard_map/ppermute | solution.py:105
  74.8 1.3 collective-permute-start.2
  76.1 2.6 %collective-permute-start.3 = (bf16[14,16,256]{2,1,0:T(8,128)(2,1)S(1)}, bf16[14,16,256]{2,1,0:T(8,128)(2,1)S(1)}, u32[]{:S(2)}, u32[]{:S(2)}) collective-permute-start(bf16[14,16,256]{2,1,0:T(8,128)(2,1)S(1)} %get-tuple-element.53), channel_id=1, source_target_pairs={{0,64},{32,96},{64,0},{96,32},{1,65},{33,97},{65,1},{97,33},{2,66}... | collective-permute-start | bytes 344072 | tf_op jit(solution)/shard_map/ppermute | solution.py:105
  79.8 10.5 %collective-permute-done.6 = bf16[14,16,256]{2,1,0:T(8,128)(2,1)S(1)} collective-permute-done((bf16[14,16,256]{2,1,0:T(8,128)(2,1)S(1)}, bf16[14,16,256]{2,1,0:T(8,128)(2,1)S(1)}, u32[]{:S(2)}, u32[]{:S(2)}) %collective-permute-start.6) | collective-permute-done | bytes 114720 | tf_op jit(solution)/shard_map/ppermute | solution.py:105
  90.3 1.4 collective-permute-start.7
  91.7 2.6 %collective-permute-start.8 = (bf16[2,14,16,256]{3,2,1,0:T(8,128)(2,1)S(1)}, bf16[2,14,16,256]{3,2,1,0:T(8,128)(2,1)S(1)}, u32[]{:S(2)}, u32[]{:S(2)}) collective-permute-start(bf16[2,14,16,256]{3,2,1,0:T(8,128)(2,1)S(1)} %get-tuple-element.49), channel_id=1, source_target_pairs={{0,64},{32,96},{64,0},{96,32},{1,65},{33,97},{65,1},{97,33},{2,66}... | collective-permute-start | bytes 688136 | tf_op jit(solution)/shard_map/ppermute | solution.py:105
  94.3 1.1 collective-permute-start.9
  97.0 3.2 %collective-permute-done.8 = bf16[2,14,16,256]{3,2,1,0:T(8,128)(2,1)S(1)} collective-permute-done((bf16[2,14,16,256]{3,2,1,0:T(8,128)(2,1)S(1)}, bf16[2,14,16,256]{3,2,1,0:T(8,128)(2,1)S(1)}, u32[]{:S(2)}, u32[]{:S(2)}) %collective-permute-start.8) | collective-permute-done | bytes 229408 | tf_op jit(solution)/shard_map/ppermute | solution.py:105
  101.0 1.3 pad_maximum_fusion.1.second_ref
  102.3 3.5 %collective-permute-done.5 = bf16[4,14,16,256]{3,2,1,0:T(8,128)(2,1)} collective-permute-done((bf16[4,14,16,256]{3,2,1,0:T(8,128)(2,1)}, bf16[4,14,16,256]{3,2,1,0:T(8,128)(2,1)}, u32[]{:S(2)}, u32[]{:S(2)}) %collective-permute-start.5) | collective-permute-done | bytes 458784 | tf_op jit(solution)/shard_map/ppermute | solution.py:105
  105.8 2.2 pad_maximum_fusion.first_ref
  107.9 1.2 copy-done.4
  109.1 1.1 shard_map.73
  110.2 9.6 %collective-permute-start.10 = (bf16[14,16,256]{2,1,0:T(8,128)(2,1)S(1)}, bf16[14,16,256]{2,1,0:T(8,128)(2,1)S(1)}, u32[]{:S(2)}, u32[]{:S(2)}) collective-permute-start(bf16[14,16,256]{2,1,0:T(8,128)(2,1)S(1)} %get-tuple-element.47), channel_id=1, source_target_pairs={{0,4},{4,8},{8,12},{12,0},{1,5},{5,9},{9,13},{13,1},{2,6},{6,10},{... | collective-permute-start | bytes 344072 | tf_op jit(solution)/shard_map/ppermute | solution.py:105
  119.9 2.4 collective-permute-start.11
  122.2 1.4 collective-permute-start.12
  124.1 1.6 collective-permute-done.11
  127.7 3.9 %collective-permute-start.16 = (bf16[2,14,16,256]{3,2,1,0:T(8,128)(2,1)S(1)}, bf16[2,14,16,256]{3,2,1,0:T(8,128)(2,1)S(1)}, u32[]{:S(2)}, u32[]{:S(2)}) collective-permute-start(bf16[2,14,16,256]{3,2,1,0:T(8,128)(2,1)S(1)} %get-tuple-element.43), channel_id=1, source_target_pairs={{0,8},{4,12},{8,0},{12,4},{1,9},{5,13},{9,1},{13,5},{2,10},{6,14},... | collective-permute-start | bytes 688136 | tf_op jit(solution)/shard_map/ppermute | solution.py:105
  131.7 2.2 collective-permute-done.15
  133.9 5.0 %collective-permute-done.16 = bf16[2,14,16,256]{3,2,1,0:T(8,128)(2,1)S(1)} collective-permute-done((bf16[2,14,16,256]{3,2,1,0:T(8,128)(2,1)S(1)}, bf16[2,14,16,256]{3,2,1,0:T(8,128)(2,1)S(1)}, u32[]{:S(2)}, u32[]{:S(2)}) %collective-permute-start.16) | collective-permute-done | bytes 229408 | tf_op jit(solution)/shard_map/ppermute | solution.py:105
  139.0 4.7 %collective-permute-start.19 = (bf16[4,2,14,16,256]{4,3,2,1,0:T(8,128)(2,1)S(1)}, bf16[4,2,14,16,256]{4,3,2,1,0:T(8,128)(2,1)S(1)}, u32[]{:S(2)}, u32[]{:S(2)}) collective-permute-start(bf16[4,2,14,16,256]{4,3,2,1,0:T(8,128)(2,1)S(1)} %pad_maximum_fusion.3.b0_ref), channel_id=1, source_target_pairs={{0,1},{1,0},{2,3},{3,2},{4,5},{5,4},{6,7},{7,6},{8,9},{9,8},{10,11... | collective-permute-start | bytes 2752520 | tf_op jit(solution)/shard_map/ppermute | solution.py:397
  144.0 1.7 collective-permute-done.19.b1_ref
  145.8 1.4 collective-permute-done.18.a1_ref
  147.2 10.7 %shard_map.74 = (f32[4,448,512]{2,1,0:T(8,128)}, f32[16,2,32,512]{3,2,1,0:T(8,128)}) custom-call(s32[4]{0:T(128)S(1)} %pad_add_fusion.1.at_ref, bf16[3584,1792]{1,0:T(8,128)(2,1)} %f_ref.1, bf16[2,4,14,16,256]{4,3,2,1,0:T(8,128)(2,1)S(1)} %pad_maximum_fusion.2.a0_ref, bf16[4,2,14,16,256]{4,3,2,1,0:T(8,128)(2,1)S(1)} %pad_maximum_fusion.3.b0_ref, ...), custom_call_target="tpu_custom_call" | custom-call | flops 4697620480 | bytes 10551296 | tf_op jit(solution)/shard_map/pallas_call | solution.py:210
  157.9 4.4 %all-to-all-start.2 = ((f32[16,2,32,512]{3,2,1,0:T(8,128)}), f32[16,2,32,512]{3,2,1,0:T(8,128)S(1)}, u32[]{:S(2)}, u32[]{:S(2)}) async-start(f32[16,2,32,512]{3,2,1,0:T(8,128)} %get-tuple-element.25), calls=%async_computation.2 | async-start | bytes 4194304 | tf_op jit(solution)/shard_map/all_to_all | solution.py:408
  162.4 2.0 copy-done.10
  164.4 26.7 %shard_map.75.a_ref = f32[4,448,512]{2,1,0:T(8,128)S(1)} custom-call(f32[4,448,512]{2,1,0:T(8,128)S(1)} %copy-done.10), custom_call_target="tpu_custom_call" | custom-call | flops 30000001024 | bytes 7340032 | tf_op jit(solution)/shard_map/pallas_call | solution.py:310
  191.1 1.9 copy-done.13
  195.7 2.0 copy-done.14
  197.7 35.0 %shard_map.76.w_ref = f32[4,448,512]{2,1,0:T(8,128)S(1)} custom-call(f32[4,448,512]{2,1,0:T(8,128)S(1)} %copy-done.14), custom_call_target="tpu_custom_call" | custom-call | flops 40000000000 | bytes 7340032 | tf_op jit(solution)/shard_map/pallas_call | solution.py:310
  232.8 1.9 copy-done.11
  234.6 2.2 copy-done.7
  236.8 2.0 copy-done.12
  238.9 4.6 %shard_map.77 = (f32[4,56,448]{2,1,0:T(8,128)S(1)}, f32[4,28,448]{2,1,0:T(8,128)S(1)}) custom-call(s32[4]{0:T(128)S(1)} %pad_add_fusion.1.at_ref, f32[4,448,512]{2,1,0:T(8,128)S(1)} %copy-done.12, f32[4,56,512]{2,1,0:T(8,128)S(1)} %bitcast_convert_fusion.own_ref, f32[16,4,32,512]{3,2,1,0:T(8,128)S(1)} %bitcast.56), custom_call_target="tpu_custom_call" | custom-call | flops 4000000000 | bytes 7864320 | tf_op jit(solution)/shard_map/pallas_call | solution.py:342
  (89 shorter events, 13.6 us)
Async XLA Ops:
  7.3 1.4 copy-start.8
  8.7 8.0 %copy-start.9 = (bf16[1792,448]{0,1:T(8,128)(2,1)S(1)}, bf16[1792,448]{0,1:T(8,128)(2,1)}, u32[]{:S(2)}) copy-start(bf16[1792,448]{0,1:T(8,128)(2,1)} %param.7) | copy-start | bytes 4816900
  15.2 12.3 %collective-permute-start.1 = (f32[2,1792,256]{2,1,0:T(8,128)S(1)}, f32[2,1792,256]{2,1,0:T(8,128)S(1)}, u32[]{:S(2)}, u32[]{:S(2)}) collective-permute-start(f32[2,1792,256]{2,1,0:T(8,128)S(1)} %get-tuple-element.21), channel_id=1, source_target_pairs={{0,1},{1,0},{2,3},{3,2},{4,5},{5,4},{6,7},{7,6},{8,9},{9,8},{10,11... | collective-permute-start | bytes 11010056 | tf_op jit(solution)/shard_map/ppermute | solution.py:369
  27.5 1.8 copy-start.2
  27.5 10.0 %collective-permute-start = (f32[1,3584,256]{2,1,0:T(8,128)}, f32[1,3584,256]{2,1,0:T(8,128)}, u32[]{:S(2)}, u32[]{:S(2)}) collective-permute-start(f32[1,3584,256]{2,1,0:T(8,128)} %get-tuple-element.17), channel_id=1, source_target_pairs={{0,1},{1,0},{2,3},{3,2},{4,5},{5,4},{6,7},{7,6},{8,9},{9,8},{10,11... | collective-permute-start | bytes 11010056 | tf_op jit(solution)/shard_map/ppermute | solution.py:371
  29.3 1.4 copy-start.6
  30.6 5.6 %copy-start.19 = (s32[2,112]{1,0:T(2,128)S(1)}, s32[2,112]{1,0:T(2,128)}, u32[]{:S(2)}) copy-start(s32[2,112]{1,0:T(2,128)} %param.9) | copy-start | bytes 2692
  30.6 33.3 %all-to-all-start.1 = ((bf16[8,28,16,256]{3,2,1,0:T(8,128)(2,1)}), bf16[8,28,16,256]{3,2,1,0:T(8,128)(2,1)S(1)}, u32[]{:S(2)}, u32[]{:S(2)}) async-start(bf16[8,28,16,256]{3,2,1,0:T(8,128)(2,1)} %copy-done.6), calls=%async_computation.1 | async-start | bytes 3670016 | tf_op jit(solution)/shard_map/all_to_all | solution.py:373
  37.4 2.0 copy-start.3
  42.6 1.3 copy-start.5
  64.0 1.2 copy-start
  65.2 42.7 %all-to-all-start = ((bf16[8,28,16,256]{3,2,1,0:T(8,128)(2,1)}), bf16[8,28,16,256]{3,2,1,0:T(8,128)(2,1)S(1)}, u32[]{:S(2)}, u32[]{:S(2)}) async-start(bf16[8,28,16,256]{3,2,1,0:T(8,128)(2,1)} %copy-done.5), calls=%async_computation | async-start | bytes 3670016 | tf_op jit(solution)/shard_map/all_to_all | solution.py:375
  68.8 27.6 %copy-start.20 = (s32[2,28]{1,0:T(2,128)S(1)}, s32[2,28]{1,0:T(2,128)}, u32[]{:S(2)}) copy-start(s32[2,28]{1,0:T(2,128)} %convert_element_type.7) | copy-start | bytes 676
  68.9 1.5 copy-start.1
  71.3 19.0 %collective-permute-start.6 = (bf16[14,16,256]{2,1,0:T(8,128)(2,1)S(1)}, bf16[14,16,256]{2,1,0:T(8,128)(2,1)S(1)}, u32[]{:S(2)}, u32[]{:S(2)}) collective-permute-start(bf16[14,16,256]{2,1,0:T(8,128)(2,1)S(1)} %get-tuple-element.52), channel_id=1, source_target_pairs={{0,16},{16,0},{1,17},{17,1},{2,18},{18,2},{3,19},{19,3},{4,20},{20... | collective-permute-start | bytes 344072 | tf_op jit(solution)/shard_map/ppermute | solution.py:105
  74.8 19.5 %collective-permute-start.2 = (bf16[14,16,256]{2,1,0:T(8,128)(2,1)S(1)}, bf16[14,16,256]{2,1,0:T(8,128)(2,1)S(1)}, u32[]{:S(2)}, u32[]{:S(2)}) collective-permute-start(bf16[14,16,256]{2,1,0:T(8,128)(2,1)S(1)} %get-tuple-element.53), channel_id=1, source_target_pairs={{0,32},{32,64},{64,96},{96,0},{1,33},{33,65},{65,97},{97,1},{2,34}... | collective-permute-start | bytes 344072 | tf_op jit(solution)/shard_map/ppermute | solution.py:105
  76.1 19.3 %collective-permute-start.3 = (bf16[14,16,256]{2,1,0:T(8,128)(2,1)S(1)}, bf16[14,16,256]{2,1,0:T(8,128)(2,1)S(1)}, u32[]{:S(2)}, u32[]{:S(2)}) collective-permute-start(bf16[14,16,256]{2,1,0:T(8,128)(2,1)S(1)} %get-tuple-element.53), channel_id=1, source_target_pairs={{0,64},{32,96},{64,0},{96,32},{1,65},{33,97},{65,1},{97,33},{2,66}... | collective-permute-start | bytes 344072 | tf_op jit(solution)/shard_map/ppermute | solution.py:105
  78.7 16.7 %collective-permute-start.4 = (bf16[14,16,256]{2,1,0:T(8,128)(2,1)S(1)}, bf16[14,16,256]{2,1,0:T(8,128)(2,1)S(1)}, u32[]{:S(2)}, u32[]{:S(2)}) collective-permute-start(bf16[14,16,256]{2,1,0:T(8,128)(2,1)S(1)} %get-tuple-element.53), channel_id=1, source_target_pairs={{0,96},{32,0},{64,32},{96,64},{1,97},{33,1},{65,33},{97,65},{2,98}... | collective-permute-start | bytes 344072 | tf_op jit(solution)/shard_map/ppermute | solution.py:105
  90.3 6.6 %collective-permute-start.7 = (bf16[2,14,16,256]{3,2,1,0:T(8,128)(2,1)S(1)}, bf16[2,14,16,256]{3,2,1,0:T(8,128)(2,1)S(1)}, u32[]{:S(2)}, u32[]{:S(2)}) collective-permute-start(bf16[2,14,16,256]{3,2,1,0:T(8,128)(2,1)S(1)} %get-tuple-element.49), channel_id=1, source_target_pairs={{0,32},{32,64},{64,96},{96,0},{1,33},{33,65},{65,97},{97,1},{2,34}... | collective-permute-start | bytes 688136 | tf_op jit(solution)/shard_map/ppermute | solution.py:105
  91.7 8.5 %collective-permute-start.8 = (bf16[2,14,16,256]{3,2,1,0:T(8,128)(2,1)S(1)}, bf16[2,14,16,256]{3,2,1,0:T(8,128)(2,1)S(1)}, u32[]{:S(2)}, u32[]{:S(2)}) collective-permute-start(bf16[2,14,16,256]{3,2,1,0:T(8,128)(2,1)S(1)} %get-tuple-element.49), channel_id=1, source_target_pairs={{0,64},{32,96},{64,0},{96,32},{1,65},{33,97},{65,1},{97,33},{2,66}... | collective-permute-start | bytes 688136 | tf_op jit(solution)/shard_map/ppermute | solution.py:105
  94.3 5.9 %collective-permute-start.9 = (bf16[2,14,16,256]{3,2,1,0:T(8,128)(2,1)S(1)}, bf16[2,14,16,256]{3,2,1,0:T(8,128)(2,1)S(1)}, u32[]{:S(2)}, u32[]{:S(2)}) collective-permute-start(bf16[2,14,16,256]{3,2,1,0:T(8,128)(2,1)S(1)} %get-tuple-element.49), channel_id=1, source_target_pairs={{0,96},{32,0},{64,32},{96,64},{1,97},{33,1},{65,33},{97,65},{2,98}... | collective-permute-start | bytes 688136 | tf_op jit(solution)/shard_map/ppermute | solution.py:105
  96.4 9.3 %collective-permute-start.5 = (bf16[4,14,16,256]{3,2,1,0:T(8,128)(2,1)}, bf16[4,14,16,256]{3,2,1,0:T(8,128)(2,1)}, u32[]{:S(2)}, u32[]{:S(2)}) collective-permute-start(bf16[4,14,16,256]{3,2,1,0:T(8,128)(2,1)} %get-tuple-element.41), channel_id=1, source_target_pairs={{0,16},{16,0},{1,17},{17,1},{2,18},{18,2},{3,19},{19,3},{4,20},{20... | collective-permute-start | bytes 1376264 | tf_op jit(solution)/shard_map/ppermute | solution.py:105
  97.0 3.2 %copy-start.15 = (bf16[2,14,16,256]{3,2,1,0:T(8,128)(2,1)}, bf16[2,14,16,256]{3,2,1,0:T(8,128)(2,1)S(1)}, u32[]{:S(2)}) copy-start(bf16[2,14,16,256]{3,2,1,0:T(8,128)(2,1)S(1)} %collective-permute-done.7) | copy-start | bytes 688132
  100.2 0.7 copy-start.16
  100.2 0.8 copy-start.17
  107.9 1.2 copy-start.4
  110.2 13.9 %collective-permute-start.10 = (bf16[14,16,256]{2,1,0:T(8,128)(2,1)S(1)}, bf16[14,16,256]{2,1,0:T(8,128)(2,1)S(1)}, u32[]{:S(2)}, u32[]{:S(2)}) collective-permute-start(bf16[14,16,256]{2,1,0:T(8,128)(2,1)S(1)} %get-tuple-element.47), channel_id=1, source_target_pairs={{0,4},{4,8},{8,12},{12,0},{1,5},{5,9},{9,13},{13,1},{2,6},{6,10},{... | collective-permute-start | bytes 344072 | tf_op jit(solution)/shard_map/ppermute | solution.py:105
  119.9 5.9 %collective-permute-start.11 = (bf16[14,16,256]{2,1,0:T(8,128)(2,1)S(1)}, bf16[14,16,256]{2,1,0:T(8,128)(2,1)S(1)}, u32[]{:S(2)}, u32[]{:S(2)}) collective-permute-start(bf16[14,16,256]{2,1,0:T(8,128)(2,1)S(1)} %get-tuple-element.47), channel_id=1, source_target_pairs={{0,8},{4,12},{8,0},{12,4},{1,9},{5,13},{9,1},{13,5},{2,10},{6,14},... | collective-permute-start | bytes 344072 | tf_op jit(solution)/shard_map/ppermute | solution.py:105
  122.2 4.5 %collective-permute-start.12 = (bf16[14,16,256]{2,1,0:T(8,128)(2,1)S(1)}, bf16[14,16,256]{2,1,0:T(8,128)(2,1)S(1)}, u32[]{:S(2)}, u32[]{:S(2)}) collective-permute-start(bf16[14,16,256]{2,1,0:T(8,128)(2,1)S(1)} %get-tuple-element.47), channel_id=1, source_target_pairs={{0,12},{4,0},{8,4},{12,8},{1,13},{5,1},{9,5},{13,9},{2,14},{6,2},{... | collective-permute-start | bytes 344072 | tf_op jit(solution)/shard_map/ppermute | solution.py:105
  123.7 3.9 %collective-permute-start.14 = (bf16[14,16,256]{2,1,0:T(8,128)(2,1)S(1)}, bf16[14,16,256]{2,1,0:T(8,128)(2,1)S(1)}, u32[]{:S(2)}, u32[]{:S(2)}) collective-permute-start(bf16[14,16,256]{2,1,0:T(8,128)(2,1)S(1)} %get-tuple-element.46), channel_id=1, source_target_pairs={{0,2},{2,0},{1,3},{3,1},{4,6},{6,4},{5,7},{7,5},{8,10},{10,8},{9,1... | collective-permute-start | bytes 344072 | tf_op jit(solution)/shard_map/ppermute | solution.py:105
  126.8 16.9 %collective-permute-start.13 = (bf16[4,14,16,256]{3,2,1,0:T(8,128)(2,1)S(1)}, bf16[4,14,16,256]{3,2,1,0:T(8,128)(2,1)S(1)}, u32[]{:S(2)}, u32[]{:S(2)}) collective-permute-start(bf16[4,14,16,256]{3,2,1,0:T(8,128)(2,1)S(1)} %get-tuple-element.39), channel_id=1, source_target_pairs={{0,2},{2,0},{1,3},{3,1},{4,6},{6,4},{5,7},{7,5},{8,10},{10,8},{9,1... | collective-permute-start | bytes 1376264 | tf_op jit(solution)/shard_map/ppermute | solution.py:105
  127.6 6.2 %collective-permute-start.15 = (bf16[2,14,16,256]{3,2,1,0:T(8,128)(2,1)S(1)}, bf16[2,14,16,256]{3,2,1,0:T(8,128)(2,1)S(1)}, u32[]{:S(2)}, u32[]{:S(2)}) collective-permute-start(bf16[2,14,16,256]{3,2,1,0:T(8,128)(2,1)S(1)} %get-tuple-element.43), channel_id=1, source_target_pairs={{0,4},{4,8},{8,12},{12,0},{1,5},{5,9},{9,13},{13,1},{2,6},{6,10},{... | collective-permute-start | bytes 688136 | tf_op jit(solution)/shard_map/ppermute | solution.py:105
  127.7 11.1 %collective-permute-start.16 = (bf16[2,14,16,256]{3,2,1,0:T(8,128)(2,1)S(1)}, bf16[2,14,16,256]{3,2,1,0:T(8,128)(2,1)S(1)}, u32[]{:S(2)}, u32[]{:S(2)}) collective-permute-start(bf16[2,14,16,256]{3,2,1,0:T(8,128)(2,1)S(1)} %get-tuple-element.43), channel_id=1, source_target_pairs={{0,8},{4,12},{8,0},{12,4},{1,9},{5,13},{9,1},{13,5},{2,10},{6,14},... | collective-permute-start | bytes 688136 | tf_op jit(solution)/shard_map/ppermute | solution.py:105
  131.7 7.2 %collective-permute-start.17 = (bf16[2,14,16,256]{3,2,1,0:T(8,128)(2,1)S(1)}, bf16[2,14,16,256]{3,2,1,0:T(8,128)(2,1)S(1)}, u32[]{:S(2)}, u32[]{:S(2)}) collective-permute-start(bf16[2,14,16,256]{3,2,1,0:T(8,128)(2,1)S(1)} %get-tuple-element.43), channel_id=1, source_target_pairs={{0,12},{4,0},{8,4},{12,8},{1,13},{5,1},{9,5},{13,9},{2,14},{6,2},{... | collective-permute-start | bytes 688136 | tf_op jit(solution)/shard_map/ppermute | solution.py:105
  139.0 6.8 %collective-permute-start.19 = (bf16[4,2,14,16,256]{4,3,2,1,0:T(8,128)(2,1)S(1)}, bf16[4,2,14,16,256]{4,3,2,1,0:T(8,128)(2,1)S(1)}, u32[]{:S(2)}, u32[]{:S(2)}) collective-permute-start(bf16[4,2,14,16,256]{4,3,2,1,0:T(8,128)(2,1)S(1)} %pad_maximum_fusion.3.b0_ref), channel_id=1, source_target_pairs={{0,1},{1,0},{2,3},{3,2},{4,5},{5,4},{6,7},{7,6},{8,9},{9,8},{10,11... | collective-permute-start | bytes 2752520 | tf_op jit(solution)/shard_map/ppermute | solution.py:397
  143.8 3.5 %collective-permute-start.18 = (bf16[2,4,14,16,256]{4,3,2,1,0:T(8,128)(2,1)S(1)}, bf16[2,4,14,16,256]{4,3,2,1,0:T(8,128)(2,1)}, u32[]{:S(2)}, u32[]{:S(2)}) collective-permute-start(bf16[2,4,14,16,256]{4,3,2,1,0:T(8,128)(2,1)S(1)} %pad_maximum_fusion.2.a0_ref), channel_id=1, source_target_pairs={{0,1},{1,0},{2,3},{3,2},{4,5},{5,4},{6,7},{7,6},{8,9},{9,8},{10,11... | collective-permute-start | bytes 2752520 | tf_op jit(solution)/shard_map/ppermute | solution.py:397
  145.8 1.4 copy-start.18
  157.9 35.1 %all-to-all-start.2 = ((f32[16,2,32,512]{3,2,1,0:T(8,128)}), f32[16,2,32,512]{3,2,1,0:T(8,128)S(1)}, u32[]{:S(2)}, u32[]{:S(2)}) async-start(f32[16,2,32,512]{3,2,1,0:T(8,128)} %get-tuple-element.25), calls=%async_computation.2 | async-start | bytes 4194304 | tf_op jit(solution)/shard_map/all_to_all | solution.py:408
  162.3 72.3 %all-gather.3.cloned.1.call-start = ((), (), s32[]{:S(2)}) async-start(), calls=%async_computation.3 | async-start | bytes 4456448 | tf_op jit(solution)/shard_map/all_gather | solution.py:413
  162.4 2.0 copy-start.10
  191.1 1.9 copy-start.13
  195.7 2.0 copy-start.14
  232.8 1.9 copy-start.11
  234.6 2.2 copy-start.7
  236.8 2.0 copy-start.12
Sparse Core Ops, SparseCore 0:
  193.8 35.1 all-gather.2

commit v3 on v2

v3 whole, which is shorter than its diff:
```python
import functools
import math

import jax
import jax.numpy as jnp
from jax import lax
from jax.experimental import pallas as pl
from jax.experimental.pallas import tpu as pltpu
from jax.sharding import Mesh
from jax.sharding import PartitionSpec as P

LEAF = 896
BLOCK = 128
ROW = ("y", "zh")
CHIP = ("x", "zl")
COL = ("x", "zl", "core")
F32 = jnp.float32
BF = jnp.bfloat16
VMEM = pl.BlockSpec(memory_space=pltpu.VMEM)
SMEM = pl.BlockSpec(memory_space=pltpu.SMEM)
STEP = 64


def params(mib):
    return pltpu.CompilerParams(vmem_limit_bytes=mib << 20)


def cost(flops, nbytes):
    return pl.CostEstimate(flops=int(flops), bytes_accessed=int(nbytes), transcendentals=0)


def probe_kernel(at_ref, a_ref, b_ref, sent_ref, kept_ref):
    total = contract(a_ref[0], b_ref[0], 1, 1)
    half = sent_ref.shape[2]
    low = total[:, :half]
    pad = jnp.zeros((total.shape[0], 2 * half - total.shape[1]), F32)
    high = jnp.concatenate([total[:, half:], pad], axis=1)
    first = at_ref[2] == 0
    kept_ref[0] = jnp.where(first, low, high)
    sent_ref[0] = jnp.where(first, high, low)


def probe(at, a, b, half):
    count, rows, depth = a.shape
    probes = b.shape[1]
    part = jax.ShapeDtypeStruct((count, rows, half), F32)
    return pl.pallas_call(
        probe_kernel,
        grid=(count, rows // LEAF),
        out_shape=[part, part],
        in_specs=[
            SMEM,
            pl.BlockSpec((1, LEAF, depth), lambda k, i: (k, i, 0)),
            pl.BlockSpec((1, probes, depth), lambda k, i: (k, 0, 0)),
        ],
        out_specs=[pl.BlockSpec((1, LEAF, half), lambda k, i: (k, i, 0))] * 2,
        compiler_params=params(40),
        cost_estimate=cost(4 * count * rows * depth * half, 2 * a.size + 8 * count * rows * half),
    )(at, a, b)


def pack_kernel(at_ref, a_ref, b_ref, o_ref, own_ref, sum_ref):
    total = a_ref[0] + b_ref[0]
    sum_ref[...] = total
    chips, blocks, rows, _ = o_ref.shape
    chip_here = at_ref[0] * 2 + at_ref[1]
    for block in range(blocks):
        for chip in range(chips):
            start = (block * chips + chip) * rows
            o_ref[chip, block] = total[start : start + rows].astype(BF)
        own = pl.multiple_of((block * chips + chip_here) * rows, rows)
        own_ref[block] = sum_ref[pl.ds(own, rows), :]


def pack(at, kept, received, chips):
    count, rows, half = kept.shape
    per = rows // LEAF
    blocks = LEAF // BLOCK
    slab = BLOCK // chips
    whole = count * rows // BLOCK
    return pl.pallas_call(
        pack_kernel,
        grid=(count, per),
        out_shape=[
            jax.ShapeDtypeStruct((chips, whole, slab, half), BF),
            jax.ShapeDtypeStruct((whole, slab, half), F32),
        ],
        in_specs=[
            SMEM,
            pl.BlockSpec((1, LEAF, half), lambda k, i: (k, i, 0)),
            pl.BlockSpec((1, LEAF, half), lambda k, i: (k, i, 0)),
        ],
        out_specs=[
            pl.BlockSpec((chips, blocks, slab, half), lambda k, i: (0, k * per + i, 0, 0)),
            pl.BlockSpec((blocks, slab, half), lambda k, i: (k * per + i, 0, 0)),
        ],
        scratch_shapes=[pltpu.VMEM((LEAF, half), F32)],
        compiler_params=params(24),
        cost_estimate=cost(kept.size, 10 * kept.size),
    )(at, kept, received)


def shift(value, axis, by):
    size = lax.axis_size(axis)
    return lax.ppermute(value, axis, [(i, (i + by) % size) for i in range(size)])


def ring_gather(value, axis):
    size = lax.axis_size(axis)
    return jnp.stack([value] + [shift(value, axis, by) for by in range(1, size)])


def two_way_gather(first, second, big, small):
    first_ring = ring_gather(first, big)
    second_pair = ring_gather(second, small)
    return ring_gather(first_ring, small), ring_gather(second_pair, big)


def sum_of(shares_ref, own, here, at):
    for chip in range(shares_ref.shape[0]):
        own += jnp.where(here != chip, shares_ref[(chip, *at)].astype(F32), 0.0)
    return own


def sum_kernel(at_ref, k_ref, own_ref, o_ref):
    here = at_ref[0] * 2 + at_ref[1]
    for block in range(o_ref.shape[0]):
        o_ref[block] = sum_of(k_ref, own_ref[block], here, (block,)).astype(o_ref.dtype)


def sum_shares(at, shares, own, dtype):
    return pl.pallas_call(
        sum_kernel,
        out_shape=jax.ShapeDtypeStruct(shares.shape[1:], dtype),
        in_specs=[SMEM, VMEM, VMEM],
        out_specs=VMEM,
        compiler_params=params(24),
        cost_estimate=cost(shares.size, 2 * shares.size),
    )(at, shares, own)


def extend_kernel(at_ref, from_ref, p_ref, own_ref, first_ref, second_ref, keep_ref, send_ref, all_ref):
    here = at_ref[0] * 2 + at_ref[1]
    core = at_ref[2]
    for block in range(p_ref.shape[1]):
        total = sum_of(p_ref, own_ref[block], here, (block,))
        for kid, ref in enumerate((first_ref, second_ref)):
            near, far, place = (from_ref[kid, part, block] for part in range(3))
            there = from_ref[kid, 3, block]
            total += jnp.where(there > 0, ref[near, far, place].astype(F32), 0.0)
        all_ref[block] = total.astype(BF)
    count = keep_ref.shape[0]
    keep_ref[...] = all_ref[pl.ds(core * count, count)]
    send_ref[...] = all_ref[pl.ds((1 - core) * count, count)]


def extend_add(at, source, parent, own, first, second):
    blocks, slab, half = parent.shape[1:]
    pair = jax.ShapeDtypeStruct((blocks // 2, slab, half), BF)
    return pl.pallas_call(
        extend_kernel,
        out_shape=[pair, pair],
        in_specs=[SMEM, SMEM, VMEM, VMEM, VMEM, VMEM],
        out_specs=[VMEM, VMEM],
        scratch_shapes=[pltpu.VMEM(parent.shape[1:], BF)],
        compiler_params=params(16),
        cost_estimate=cost(parent.size, 6 * parent.size),
    )(at, source, parent, own, first, second)


def halves(x):
    hi = x.astype(BF)
    return hi, (x - hi.astype(F32)).astype(BF)


def contract(a, b, left, right):
    return lax.dot_general(a, b, (((left,), (right,)), ((), ())), preferred_element_type=F32)


def product3(a, b):
    ah, al = halves(a)
    bh, bl = halves(b)
    return contract(ah, bh, 1, 0) + (contract(ah, bl, 1, 0) + contract(al, bh, 1, 0))


LEVEL = 8.0


def gram_kernel(at_ref, f_ref, a_ref, b_ref, gram_ref, root_ref, cross_ref, y_ref):
    x, zl, core = (at_ref[i] for i in range(3))
    step = pl.program_id(0)
    half = a_ref.shape[-1]
    per = LEAF // BLOCK
    leaves, order, wide = gram_ref.shape
    row = lax.broadcasted_iota(jnp.int32, (order, wide), 0)
    col = lax.broadcasted_iota(jnp.int32, (order, wide), 1)
    lane = lax.broadcasted_iota(jnp.int32, (1, wide), 1)

    @pl.when(step == 0)
    def _():
        for side, owner in ((0, core), (1, 1 - core)):
            lanes = pl.ds(pl.multiple_of(owner * half, half), half)
            for i in range(4):
                for j in range(2):
                    chip = lax.rem(x + 4 - i, 4) * 2 + lax.rem(zl + j, 2)
                    rows = pl.ds(pl.multiple_of(chip * 16, 16), 16)
                    y_ref[:per, rows, lanes] = a_ref[j, i, side]
                    y_ref[per:, rows, lanes] = b_ref[i, j, side]
        for leaf in range(leaves):
            y = y_ref[leaf * per : (leaf + 1) * per].reshape(LEAF, wide)
            gram = contract(y, y, 0, 0)[:order]
            gram_ref[leaf] = gram
            square = jnp.sum(jnp.where(row == col, gram, 0.0), axis=0, keepdims=True)
            root_ref[leaf] = jnp.sqrt(jnp.where(lane < order, square, 1.0))

    here = y_ref[pl.ds(step * per, per)].reshape(LEAF, wide)
    there = y_ref[pl.ds((1 - step) * per, per)].reshape(LEAF, wide)
    hi, lo = halves(jnp.dot(f_ref[...], there, preferred_element_type=F32) / root_ref[1 - step])
    cross = (contract(here, hi, 0, 0) + contract(here, lo, 0, 0))[:order]
    square = jnp.sum(jnp.where(row == col, gram_ref[step], 0.0), axis=1, keepdims=True)
    cross = cross * lax.rsqrt(square)
    most = jnp.max(jnp.max(jnp.abs(cross), axis=0, keepdims=True), axis=1, keepdims=True)
    power = jnp.ceil(jnp.log2(jnp.maximum(most, 1e-30)))
    cross = jnp.where(col < order, cross * jnp.exp2(LEVEL - power), power)
    cross_ref[:, 0] = cross.reshape(cross_ref.shape[0], cross_ref.shape[2], wide)


def grams(at, front, mine, order, chips):
    half = mine[0].shape[-1]
    wide = 2 * half
    whole = pl.BlockSpec(memory_space=pltpu.VMEM)
    return pl.pallas_call(
        gram_kernel,
        grid_spec=pltpu.PrefetchScalarGridSpec(
            num_scalar_prefetch=1,
            grid=(2,),
            in_specs=[
                pl.BlockSpec((LEAF, LEAF), lambda i, at: (at[2] * 2 + i, 1 - i)),
                whole,
                whole,
            ],
            out_specs=[
                pl.BlockSpec((2, order, wide), lambda i, at: (0, 0, 0)),
                pl.BlockSpec((2, 1, wide), lambda i, at: (0, 0, 0)),
                pl.BlockSpec((chips, 1, order // chips, wide), lambda i, at: (0, i, 0, 0)),
            ],
            scratch_shapes=[pltpu.VMEM((2 * LEAF // BLOCK, BLOCK, wide), BF)],
        ),
        out_shape=[
            jax.ShapeDtypeStruct((2, order, wide), F32),
            jax.ShapeDtypeStruct((2, 1, wide), F32),
            jax.ShapeDtypeStruct((chips, 2, order // chips, wide), F32),
        ],
        compiler_params=params(52),
        cost_estimate=cost(2 * 8 * LEAF * wide * wide, 4 * LEAF * LEAF + 2 * leaves_bytes(wide)),
    )(at, front, *mine)


def leaves_bytes(wide):
    return 2 * LEAF * wide * 2


def eliminate(s, size):
    groups = size // 8
    shape = (8, 128)
    sub = lax.broadcasted_iota(jnp.int32, shape, 0)
    for g in range(groups):
        for rows in s:
            c = {
                (i, k): jnp.broadcast_to(rows[i][:, 8 * g + k : 8 * g + k + 1], shape)
                for i in range(g, groups)
                for k in range(8)
            }
            pivot = [jnp.broadcast_to(rows[g][k : k + 1, :], shape) for k in range(8)]
            d = {
                (i, k): jnp.broadcast_to(c[g, k][i : i + 1, :], shape)
                for i in range(8)
                for k in range(i, 8)
            }
            low = {}
            scaled = []
            for k in range(8):
                inverse = pl.reciprocal(d[k, k], approx=True)
                inverse = inverse * (2.0 - d[k, k] * inverse)
                scaled.append(pivot[k] * inverse)
                for i in range(k + 1, 8):
                    low[i, k] = d[k, i] * inverse
                    pivot[i] = pivot[i] - low[i, k] * pivot[k]
                    for m in range(i, 8):
                        d[i, m] = d[i, m] - low[i, k] * d[k, m]
            for m in reversed(range(8)):
                for k in range(m + 1, 8):
                    scaled[m] = scaled[m] - low[k, m] * scaled[k]
            for i in range(g + 1, groups):
                new = rows[i]
                for k in range(8):
                    new = new - c[i, k] * scaled[k]
                rows[i] = new
            new = pivot[0]
            for k in range(1, 8):
                new = jnp.where(sub == k, pivot[k], new)
            rows[g] = new


def inverse_kernel(a_ref, w_ref, x_ref, d_ref, *, first, last):
    leaves, order, wide = w_ref.shape
    blocks = order // STEP
    w_ref[...] = a_ref[...]
    lane = lax.broadcasted_iota(jnp.int32, (STEP, 128), 1)
    sub = lax.broadcasted_iota(jnp.int32, (STEP, 128), 0)
    col = lax.broadcasted_iota(jnp.int32, (STEP, wide), 1)
    row = lax.broadcasted_iota(jnp.int32, (STEP, wide), 0)
    unit = (lane - STEP == sub).astype(F32)

    def spread(k, live):
        base = pl.multiple_of(k * STEP, STEP)
        inside = (col >= base) & (col < base + STEP)
        own = (col - base == row).astype(F32)
        rest = (col >= base + STEP) & live
        for leaf in range(leaves):
            w = w_ref[leaf, pl.ds(base, STEP), :]
            r = product3(x_ref[leaf], jnp.where(inside, own, w))
            w_ref[leaf, pl.ds(base, STEP), :] = jnp.where(live, r, w)
            hi, lo = halves(r)
            none = jnp.zeros_like(hi)
            left_hi, left_lo = jnp.where(rest, hi, none), jnp.where(rest, lo, none)
            left = jnp.concatenate([left_hi, left_hi, left_lo], axis=0)
            update = contract(left, jnp.concatenate([hi, lo, hi], axis=0), 0, 0)
            for i in range(1, blocks):
                rows = slice(i * STEP, (i + 1) * STEP)
                old = jnp.where(inside & live & (i > k), 0.0, w_ref[leaf, rows, :])
                w_ref[leaf, rows, :] = old - update[rows]

    start, tile = first * STEP, first * STEP // 128 * 128
    for leaf in range(leaves):
        d = w_ref[leaf, start : start + STEP, tile : tile + 128]
        d_ref[leaf] = pltpu.roll(d, 128 - STEP, 1) if start > tile else d
        x_ref[leaf] = jnp.zeros((STEP, STEP), F32)

    @pl.loop(first, last)
    def _(k):
        s = []
        for leaf in range(leaves):
            d = jnp.where(lane < STEP, d_ref[leaf], unit)
            s.append([d[8 * i : 8 * i + 8] for i in range(STEP // 8)])
        spread(jnp.maximum(k - 1, 0), k > first)
        eliminate(s, STEP)
        base = pl.multiple_of(k * STEP, STEP)
        after = pl.multiple_of(jnp.minimum(k + 1, blocks - 1) * STEP, STEP)
        tile = pl.multiple_of(lax.div(after, 128) * 128, 128)
        odd = after - tile > 0
        for leaf in range(leaves):
            d = jnp.concatenate(s[leaf], axis=0)
            diagonal = jnp.sum(jnp.where(lane == sub, d, 0.0), axis=1, keepdims=True)
            x = (d * lax.rsqrt(diagonal))[:, STEP:]
            x_ref[leaf] = x
            hi, lo = halves(product3(x, w_ref[leaf, pl.ds(base, STEP), pl.ds(tile, 128)]))
            left = jnp.concatenate([hi, hi, lo], axis=0)
            update = contract(left, jnp.concatenate([hi, lo, hi], axis=0), 0, 0)
            update = jnp.where(odd, update[STEP:], update[:STEP])
            d = w_ref[leaf, pl.ds(after, STEP), pl.ds(tile, 128)] - update
            d_ref[leaf] = jnp.where(odd, pltpu.roll(d, 128 - STEP, 1), d)

    spread(last - 1, True)
    if last < blocks:
        return
    for leaf in range(leaves):
        for i in range(blocks):
            rows = slice(i * STEP, (i + 1) * STEP)
            w_ref[leaf, rows, :] = jnp.where(col <= row + i * STEP, w_ref[leaf, rows, :], 0.0)


def factor_inverse(work, first, last):
    leaves = work.shape[0]
    return pl.pallas_call(
        functools.partial(inverse_kernel, first=first, last=last),
        out_shape=jax.ShapeDtypeStruct(work.shape, F32),
        in_specs=[VMEM],
        out_specs=VMEM,
        scratch_shapes=[
            pltpu.VMEM((leaves, STEP, STEP), F32),
            pltpu.VMEM((leaves, STEP, 128), F32),
        ],
        compiler_params=params(24),
        cost_estimate=cost((last - first) * 5.5e9, 8 * work.size),
    )(work)


def finish_kernel(at_ref, w_ref, root_ref, own_ref, cross_ref, keep_ref, send_ref):
    leaves, order, wide = w_ref.shape
    slabs = LEAF // BLOCK
    rows = order // cross_ref.shape[0]
    base = pl.multiple_of((at_ref[0] * 2 + at_ref[1]) * rows, 8)
    first = at_ref[2] == 0
    tall = own_ref.shape[1] // 2
    for leaf in range(leaves):
        hi, lo = halves(w_ref[leaf])
        own = own_ref[leaf]
        basis = (contract(own, hi, 1, 1) + contract(own, lo, 1, 1)) * math.sqrt(LEAF)
        parts = basis.reshape(slabs, 2, tall // slabs, order)
        low, high = parts[:, 0].reshape(tall, order), parts[:, 1].reshape(tall, order)
        keep_ref[leaf, :tall] = jnp.where(first, low, high)
        send_ref[leaf, :tall] = jnp.where(first, high, low)
        left = w_ref[leaf, pl.ds(base, rows), :] * root_ref[leaf]
        cross = cross_ref[:, leaf].reshape(order, wide)
        level = jnp.exp2(cross[:1, order : order + 1] - LEVEL)
        half_way, rest = halves(product3(left[:, :order], cross))
        hi, lo = halves(w_ref[1 - leaf] * root_ref[1 - leaf])
        core = contract(half_way, hi, 1, 1) + (contract(half_way, lo, 1, 1) + contract(rest, hi, 1, 1))
        core = core * level
        low, high = core[: rows // 2], core[rows // 2 :]
        keep_ref[leaf, tall:] = jnp.where(first, low, high)
        send_ref[leaf, tall:] = jnp.where(first, high, low)


def finish(at, inverse, root, own, cross):
    leaves, order, _ = inverse.shape
    rows = (own.shape[1] + order // cross.shape[0]) // 2
    part = jax.ShapeDtypeStruct((leaves, rows, order), F32)
    return pl.pallas_call(
        finish_kernel,
        out_shape=[part, part],
        in_specs=[SMEM, VMEM, VMEM, VMEM, VMEM],
        out_specs=[VMEM, VMEM],
        compiler_params=params(24),
        cost_estimate=cost(2e9, 4 * (inverse.size + cross.size)),
    )(at, inverse, root, own, cross)


def local(parent_front, child_update, parent_test, child_test, child_map):
    y, zh = lax.axis_index("y"), lax.axis_index("zh")
    x, zl, core = lax.axis_index("x"), lax.axis_index("zl"), lax.axis_index("core")
    row_index = lax.axis_index(ROW)
    probes = parent_test.shape[1]
    half = 256
    chips = lax.axis_size(CHIP)
    own_blocks = parent_front.shape[0] // BLOCK
    kid_blocks = child_update.shape[1] // BLOCK
    swap = [(0, 1), (1, 0)]

    at = jnp.stack([x, zl, core]).astype(jnp.int32)
    kid_sent, kid_kept = probe(at, child_update, jnp.swapaxes(child_test, 1, 2), half)
    kid_sent = lax.ppermute(kid_sent, "core", swap)
    own_sent, own_kept = probe(at, parent_front[None], parent_test.T[None], half)
    own_sent = lax.ppermute(own_sent, "core", swap)
    kid_part, kid_rest = pack(at, kid_kept, kid_sent, chips)
    kid_share = lax.all_to_all(kid_part, CHIP, 0, 0, tiled=True)
    own_part, own_rest = pack(at, own_kept, own_sent, chips)
    own_share = lax.all_to_all(own_part, CHIP, 0, 0, tiled=True)

    kids = sum_shares(at, kid_share, kid_rest, BF)
    first, second = two_way_gather(kids[:kid_blocks], kids[kid_blocks:], "y", "zh")

    targets = row_index * own_blocks + jnp.arange(own_blocks, dtype=jnp.int32)
    hit = child_map[:, None, :] == targets[None, :, None]
    there = jnp.any(hit, axis=2).astype(jnp.int32)
    source = jnp.sum(jnp.where(hit, jnp.arange(child_map.shape[1], dtype=jnp.int32), 0), axis=2)
    owner, place = source // kid_blocks, source % kid_blocks
    ring = (y - owner // 2) % 4
    pair = (zh - owner % 2) % 2
    origin = jnp.stack(
        [
            jnp.stack([pair[0], ring[0], place[0], there[0]]),
            jnp.stack([ring[1], pair[1], place[1], there[1]]),
        ]
    ).astype(jnp.int32)
    keep, send = extend_add(at, origin, own_share, own_rest, first, second)
    came = lax.ppermute(send, "core", swap)

    per = LEAF // BLOCK
    first = jnp.stack([keep[:per], came[:per]])
    second = jnp.stack([keep[per:], came[per:]])
    mine = two_way_gather(first, second, "x", "zl")
    gram, root, cross = grams(at, parent_front, mine, probes, chips)

    own_rows = jnp.where(
        core == 0,
        jnp.concatenate([keep, came], axis=2),
        jnp.concatenate([came, keep], axis=2),
    ).reshape(2, -1, 2 * half)

    cross = lax.all_to_all(cross.astype(jnp.float16), CHIP, 0, 0, tiled=True)
    cross = lax.dynamic_slice_in_dim(cross, row_index, 1, 0)
    work = factor_inverse(gram, 0, 3)
    work, cross = lax.optimization_barrier((work, cross))
    cross = lax.all_to_all(jnp.broadcast_to(cross, (chips, *cross.shape[1:])), CHIP, 0, 0, tiled=True)
    inverse = factor_inverse(work, 3, probes // STEP)
    inverse, cross = lax.optimization_barrier((inverse, cross))
    keep, send = finish(at, inverse, root, own_rows, cross.astype(F32))
    came = lax.ppermute(send, "core", swap)
    both = jnp.where(core == 0, jnp.concatenate([keep, came]), jnp.concatenate([came, keep]))
    tall = own_rows.shape[1] // 2
    leaf_basis = both[:, :tall].astype(BF).reshape(own_blocks, -1, probes)
    return (leaf_basis, both[:, tall:])


def solution(mesh):
    split = Mesh(mesh.devices.reshape(4, 2, 4, 2, 2), ("y", "zh", "x", "zl", "core"))
    placed = (P(ROW, COL), P(None, ROW, COL), P(COL, None), P(None, COL, None), P())
    return jax.shard_map(
        local,
        mesh=split,
        in_specs=placed,
        out_specs=(P(ROW, COL, None), P(ROW, COL, None)),
        check_vma=False,
    )
```

time: 253 us -> 204 us (0.81)
  Pallas kernels: 101 us -> 66.5 us
  between operations: 14.3 us -> 0.91 us
  local copies, waits for them, and re-layouts: 27.5 us -> 17.4 us
  starting transfers between devices: 52 us -> 57.9 us
    pallas_call x2, Pallas kernels: 61.7 us -> 30.9 us  [factor_inverse(): pl.pallas_call(functools.partial(inverse_kernel, first=first, last=last),...]
    unnamed x44 -> x36, local copies, waits for them, and re-layouts: 24.2 us -> 14.8 us
    ppermute x2, starting transfers between devices: 4.99 us -> 9.54 us  [local(): came = lax.ppermute(send, 'core', swap)]
    all_to_all x1 -> x2, starting transfers between devices: 4.45 us -> 8.94 us  [the longest x1 5.14 us: local(): lax.all_to_all(jnp.broadcast_to(cross, (chips, *cross.shape[1:])), CHIP,...]
    ppermute x16, starting transfers between devices: 31.8 us -> 28.7 us  [shift(): lax.ppermute(value, axis, [(i, (i + by) % size) for i in range(size)])]
    another operation x8 -> x10, other arithmetic: 4.79 us -> 5.51 us  [ring_gather(): jnp.stack([value] + [shift(value, axis, by) for by in range(1, size)])]
  transfers between devices with their start and end apart: 24 -> 24, of which waited for: 11 -> 11; matrix products, arithmetic and copies ran while one was open for 3% -> 3% of each run, Pallas kernels for 31% -> 23%
where the time goes in v3:
time: 204 us
  Pallas kernels  66.5 us (33%)
  starting transfers between devices  57.9 us (28%)
  waiting for transfers between devices  51.6 us (25%)
  local copies, waits for them, and re-layouts  17.4 us (9%)
  other arithmetic  9.22 us (5%)
    pallas_call x2, Pallas kernels, factor_inverse(): pl.pallas_call(functools.partial(inverse_kernel, first=first, last=last),...  30.9 us
    ppermute x16, starting transfers between devices, shift(): lax.ppermute(value, axis, [(i, (i + by) % size) for i in range(size)])  28.7 us
    ppermute x16, waiting for transfers between devices, shift(): lax.ppermute(value, axis, [(i, (i + by) % size) for i in range(size)])  28.7 us
    all_to_all x1, waiting for transfers between devices, local(): kid_share = lax.all_to_all(kid_part, CHIP, 0, 0, tiled=True)  20.7 us
    pallas_call x2, Pallas kernels, probe(): pl.pallas_call(probe_kernel, grid=(count, rows // LEAF), out_shape=[part,...  17.3 us
    unnamed x36, local copies, waits for them, and re-layouts  14.8 us
    ppermute x2, starting transfers between devices, local(): came = lax.ppermute(send, 'core', swap)  9.54 us
    pallas_call x1, Pallas kernels, grams(): pl.pallas_call(gram_kernel, grid_spec=pltpu.PrefetchScalarGridSpec(num_sc...  9.18 us
  transfers between devices with their start and end apart: 24, of which 11 were waited for; matrix products, arithmetic and copies ran while one was open for 3% of the time, Pallas kernels for 23%

profile of v3, /device:TPU:1, one launch (start us, length us, event | category | flops | bytes accessed | tf_op | source)
XLA Modules:
  0.0 203.6 jit_solution(6305217420385854479)
XLA Ops:
  0.7 1.4 copy-done.8
  2.1 6.5 %shard_map.70 = (f32[2,1792,256]{2,1,0:T(8,128)S(1)}, f32[2,1792,256]{2,1,0:T(8,128)S(1)}) custom-call(s32[3]{0:T(128)S(1)} %pad_add_fusion.1.at_ref, bf16[2,1792,896]{2,1,0:T(8,128)(2,1)} %a_ref.1, bf16[2,448,896]{2,1,0:T(8,128)(2,1)S(1)} %bitcast.57), custom_call_target="tpu_custom_call" | custom-call | flops 3288334336 | bytes 13762560 | tf_op jit(solution)/shard_map/pallas_call | solution.py:47
  8.7 1.5 collective-permute-start.1
  10.2 10.7 %shard_map.68 = (f32[1,3584,256]{2,1,0:T(8,128)}, f32[1,3584,256]{2,1,0:T(8,128)S(1)}) custom-call(s32[3]{0:T(128)S(1)} %pad_add_fusion.1.at_ref, bf16[1,3584,1792]{2,1,0:T(8,128)(2,1)} %bitcast.59, bf16[1,448,1792]{2,1,0:T(8,128)(2,1)S(1)} %bitcast.58), custom_call_target="tpu_custom_call" | custom-call | flops 6576668672 | bytes 20185088 | tf_op jit(solution)/shard_map/pallas_call | solution.py:47
  21.0 1.3 shard_map.71
  22.7 1.3 copy-done.6
  24.1 5.6 %all-to-all-start.1 = ((bf16[8,28,16,256]{3,2,1,0:T(8,128)(2,1)}), bf16[8,28,16,256]{3,2,1,0:T(8,128)(2,1)S(1)}, u32[]{:S(2)}, u32[]{:S(2)}) async-start(bf16[8,28,16,256]{3,2,1,0:T(8,128)(2,1)} %copy-done.6), calls=%async_computation.1 | async-start | bytes 3670016 | tf_op jit(solution)/shard_map/all_to_all | solution.py:447
  30.3 2.0 %copy-done.4 = f32[1,3584,256]{2,1,0:T(8,128)S(1)} copy-done((f32[1,3584,256]{2,1,0:T(8,128)S(1)}, f32[1,3584,256]{2,1,0:T(8,128)}, u32[]{:S(2)}) %copy-start.4) | copy-done | bytes 3670040
  32.3 3.1 %shard_map.69 = (bf16[8,28,16,256]{3,2,1,0:T(8,128)(2,1)S(1)}, f32[28,16,256]{2,1,0:T(8,128)S(1)}) custom-call(s32[3]{0:T(128)S(1)} %pad_add_fusion.1.at_ref, f32[1,3584,256]{2,1,0:T(8,128)S(1)} %copy-done.4, f32[1,3584,256]{2,1,0:T(8,128)} %collective-permute-done.b_ref), custom_call_target="tpu_custom_call" | custom-call | flops 917504 | bytes 9175040 | tf_op jit(solution)/shard_map/pallas_call | solution.py:81
  35.4 1.3 copy-done.5
  36.7 20.7 %all-to-all-done.1.k_ref = bf16[8,28,16,256]{3,2,1,0:T(8,128)(2,1)S(1)} async-done(((bf16[8,28,16,256]{3,2,1,0:T(8,128)(2,1)}), bf16[8,28,16,256]{3,2,1,0:T(8,128)(2,1)S(1)}, u32[]{:S(2)}, u32[]{:S(2)}) %all-to-all-start.1) | async-done | bytes 1835040 | tf_op jit(solution)/shard_map/all_to_all | solution.py:447
  57.4 1.2 copy-done
  58.6 3.6 %all-to-all-start = ((bf16[8,28,16,256]{3,2,1,0:T(8,128)(2,1)}), bf16[8,28,16,256]{3,2,1,0:T(8,128)(2,1)S(1)}, u32[]{:S(2)}, u32[]{:S(2)}) async-start(bf16[8,28,16,256]{3,2,1,0:T(8,128)(2,1)} %copy-done.5), calls=%async_computation | async-start | bytes 3670016 | tf_op jit(solution)/shard_map/all_to_all | solution.py:449
  62.3 1.5 copy-done.1
  64.7 3.4 %collective-permute-start.6 = (bf16[14,16,256]{2,1,0:T(8,128)(2,1)S(1)}, bf16[14,16,256]{2,1,0:T(8,128)(2,1)S(1)}, u32[]{:S(2)}, u32[]{:S(2)}) collective-permute-start(bf16[14,16,256]{2,1,0:T(8,128)(2,1)S(1)} %get-tuple-element.56), channel_id=1, source_target_pairs={{0,16},{16,0},{1,17},{17,1},{2,18},{18,2},{3,19},{19,3},{4,20},{20... | collective-permute-start | bytes 344072 | tf_op jit(solution)/shard_map/ppermute | solution.py:105
  68.2 2.9 %collective-permute-start.3 = (bf16[14,16,256]{2,1,0:T(8,128)(2,1)S(1)}, bf16[14,16,256]{2,1,0:T(8,128)(2,1)S(1)}, u32[]{:S(2)}, u32[]{:S(2)}) collective-permute-start(bf16[14,16,256]{2,1,0:T(8,128)(2,1)S(1)} %get-tuple-element.57), channel_id=1, source_target_pairs={{0,64},{32,96},{64,0},{96,32},{1,65},{33,97},{65,1},{97,33},{2,66}... | collective-permute-start | bytes 344072 | tf_op jit(solution)/shard_map/ppermute | solution.py:105
  71.5 2.3 %collective-permute-start.4 = (bf16[14,16,256]{2,1,0:T(8,128)(2,1)S(1)}, bf16[14,16,256]{2,1,0:T(8,128)(2,1)S(1)}, u32[]{:S(2)}, u32[]{:S(2)}) collective-permute-start(bf16[14,16,256]{2,1,0:T(8,128)(2,1)S(1)} %get-tuple-element.57), channel_id=1, source_target_pairs={{0,96},{32,0},{64,32},{96,64},{1,97},{33,1},{65,33},{97,65},{2,98}... | collective-permute-start | bytes 344072 | tf_op jit(solution)/shard_map/ppermute | solution.py:105
  73.8 9.9 %collective-permute-done.6 = bf16[14,16,256]{2,1,0:T(8,128)(2,1)S(1)} collective-permute-done((bf16[14,16,256]{2,1,0:T(8,128)(2,1)S(1)}, bf16[14,16,256]{2,1,0:T(8,128)(2,1)S(1)}, u32[]{:S(2)}, u32[]{:S(2)}) %collective-permute-start.6) | collective-permute-done | bytes 114720 | tf_op jit(solution)/shard_map/ppermute | solution.py:105
  84.4 2.9 %collective-permute-start.8 = (bf16[2,14,16,256]{3,2,1,0:T(8,128)(2,1)S(1)}, bf16[2,14,16,256]{3,2,1,0:T(8,128)(2,1)S(1)}, u32[]{:S(2)}, u32[]{:S(2)}) collective-permute-start(bf16[2,14,16,256]{3,2,1,0:T(8,128)(2,1)S(1)} %get-tuple-element.53), channel_id=1, source_target_pairs={{0,64},{32,96},{64,0},{96,32},{1,65},{33,97},{65,1},{97,33},{2,66}... | collective-permute-start | bytes 688136 | tf_op jit(solution)/shard_map/ppermute | solution.py:105
  87.8 2.3 %collective-permute-start.9 = (bf16[2,14,16,256]{3,2,1,0:T(8,128)(2,1)S(1)}, bf16[2,14,16,256]{3,2,1,0:T(8,128)(2,1)S(1)}, u32[]{:S(2)}, u32[]{:S(2)}) collective-permute-start(bf16[2,14,16,256]{3,2,1,0:T(8,128)(2,1)S(1)} %get-tuple-element.53), channel_id=1, source_target_pairs={{0,96},{32,0},{64,32},{96,64},{1,97},{33,1},{65,33},{97,65},{2,98}... | collective-permute-start | bytes 688136 | tf_op jit(solution)/shard_map/ppermute | solution.py:105
  90.0 1.0 fusion.13
  91.6 1.8 collective-permute-done.7
  94.3 1.4 pad_maximum_fusion.1.second_ref
  95.7 4.5 %collective-permute-done.5 = bf16[4,14,16,256]{3,2,1,0:T(8,128)(2,1)} collective-permute-done((bf16[4,14,16,256]{3,2,1,0:T(8,128)(2,1)}, bf16[4,14,16,256]{3,2,1,0:T(8,128)(2,1)}, u32[]{:S(2)}, u32[]{:S(2)}) %collective-permute-start.5) | collective-permute-done | bytes 458784 | tf_op jit(solution)/shard_map/ppermute | solution.py:105
  100.2 2.0 pad_maximum_fusion.first_ref
  102.3 1.2 copy-done.2
  103.4 1.1 shard_map.73
  104.5 7.5 %collective-permute-start.10 = (bf16[14,16,256]{2,1,0:T(8,128)(2,1)S(1)}, bf16[14,16,256]{2,1,0:T(8,128)(2,1)S(1)}, u32[]{:S(2)}, u32[]{:S(2)}) collective-permute-start(bf16[14,16,256]{2,1,0:T(8,128)(2,1)S(1)} %get-tuple-element.30), channel_id=1, source_target_pairs={{0,1},{1,0},{2,3},{3,2},{4,5},{5,4},{6,7},{7,6},{8,9},{9,8},{10,11... | collective-permute-start | bytes 344072 | tf_op jit(solution)/shard_map/ppermute | solution.py:468
  113.0 6.4 %collective-permute-start.12 = (bf16[2,7,16,256]{3,2,1,0:T(8,128)(2,1)S(1)}, bf16[2,7,16,256]{3,2,1,0:T(8,128)(2,1)S(1)}, u32[]{:S(2)}, u32[]{:S(2)}) collective-permute-start(bf16[2,7,16,256]{3,2,1,0:T(8,128)(2,1)S(1)} %get-tuple-element.65), channel_id=1, source_target_pairs={{0,8},{4,12},{8,0},{12,4},{1,9},{5,13},{9,1},{13,5},{2,10},{6,14},... | collective-permute-start | bytes 344072 | tf_op jit(solution)/shard_map/ppermute | solution.py:105
  119.5 2.6 %collective-permute-start.13 = (bf16[2,7,16,256]{3,2,1,0:T(8,128)(2,1)S(1)}, bf16[2,7,16,256]{3,2,1,0:T(8,128)(2,1)S(1)}, u32[]{:S(2)}, u32[]{:S(2)}) collective-permute-start(bf16[2,7,16,256]{3,2,1,0:T(8,128)(2,1)S(1)} %get-tuple-element.65), channel_id=1, source_target_pairs={{0,12},{4,0},{8,4},{12,8},{1,13},{5,1},{9,5},{13,9},{2,14},{6,2},{... | collective-permute-start | bytes 344072 | tf_op jit(solution)/shard_map/ppermute | solution.py:105
  122.7 2.2 %collective-permute-done.11 = bf16[2,7,16,256]{3,2,1,0:T(8,128)(2,1)S(1)} collective-permute-done((bf16[2,7,16,256]{3,2,1,0:T(8,128)(2,1)S(1)}, bf16[2,7,16,256]{3,2,1,0:T(8,128)(2,1)S(1)}, u32[]{:S(2)}, u32[]{:S(2)}) %collective-permute-start.11) | collective-permute-done | bytes 114720 | tf_op jit(solution)/shard_map/ppermute | solution.py:105
  126.0 1.1 collective-permute-start.17
  127.1 1.2 collective-permute-start.16
  128.3 1.5 collective-permute-start.18
  129.9 2.6 %collective-permute-done.17 = bf16[2,2,7,16,256]{4,3,2,1,0:T(8,128)(2,1)S(1)} collective-permute-done((bf16[2,2,7,16,256]{4,3,2,1,0:T(8,128)(2,1)S(1)}, bf16[2,2,7,16,256]{4,3,2,1,0:T(8,128)(2,1)S(1)}, u32[]{:S(2)}, u32[]{:S(2)}) %collective-permute-start.17) | collective-permute-done | bytes 229408 | tf_op jit(solution)/shard_map/ppermute | solution.py:105
  132.5 7.1 %collective-permute-done.16 = bf16[2,2,7,16,256]{4,3,2,1,0:T(8,128)(2,1)S(1)} collective-permute-done((bf16[2,2,7,16,256]{4,3,2,1,0:T(8,128)(2,1)S(1)}, bf16[2,2,7,16,256]{4,3,2,1,0:T(8,128)(2,1)S(1)}, u32[]{:S(2)}, u32[]{:S(2)}) %collective-permute-start.16) | collective-permute-done | bytes 229408 | tf_op jit(solution)/shard_map/ppermute | solution.py:105
  139.8 9.2 %shard_map.74 = (f32[2,448,512]{2,1,0:T(8,128)}, f32[2,1,512]{2,1,0:T(1,128)S(1)}, f32[8,2,56,512]{3,2,1,0:T(8,128)}) custom-call(s32[3]{0:T(128)S(1)} %pad_add_fusion.1.at_ref, bf16[3584,1792]{1,0:T(8,128)(2,1)} %f_ref.1, bf16[2,4,2,7,16,256]{5,4,3,2,1,0:T(8,128)(2,1)S(1)} %pad_maximum_fusion.2.a_ref, ...), custom_call_target="tpu_custom_call" | custom-call | flops 3758096384 | bytes 6881280 | tf_op jit(solution)/shard_map/pallas_call | solution.py:232
  149.0 2.8 %convert_element_type.11 = f16[8,2,56,512]{3,2,1,0:T(8,128)(2,1)} convert(f32[8,2,56,512]{3,2,1,0:T(8,128)} %get-tuple-element.32) | non-fusion elementwise | flops 458752 | bytes 2752512 | tf_op jit(solution)/shard_map/convert_element_type | solution.py:482
  151.8 3.8 %all-to-all-start.2 = ((f16[8,2,56,512]{3,2,1,0:T(8,128)(2,1)}), f16[8,2,56,512]{3,2,1,0:T(8,128)(2,1)S(1)}, u32[]{:S(2)}, u32[]{:S(2)}) async-start(f16[8,2,56,512]{3,2,1,0:T(8,128)(2,1)} %convert_element_type.11), calls=%async_computation.2 | async-start | bytes 1835008 | tf_op jit(solution)/shard_map/all_to_all | solution.py:482
  155.6 13.4 %shard_map.75.a_ref = f32[2,448,512]{2,1,0:T(8,128)S(1)} custom-call(f32[2,448,512]{2,1,0:T(8,128)S(1)} %copy-done.7), custom_call_target="tpu_custom_call" | custom-call | flops 16499999744 | bytes 3670016 | tf_op jit(solution)/shard_map/pallas_call | solution.py:375
  169.0 1.3 copy-done.10
  170.3 1.0 broadcast_in_dim.28
  171.3 5.1 %all-to-all-start.3 = ((f16[8,2,56,512]{3,2,1,0:T(8,128)(2,1)}), f16[8,2,56,512]{3,2,1,0:T(8,128)(2,1)S(1)}, u32[]{:S(2)}, u32[]{:S(2)}) async-start(f16[8,2,56,512]{3,2,1,0:T(8,128)(2,1)} %broadcast_in_dim.28), calls=%async_computation.3 | async-start | bytes 1835008 | tf_op jit(solution)/shard_map/all_to_all | solution.py:486
  176.5 1.5 copy-done.11
  178.0 17.5 %shard_map.76.w_ref = f32[2,448,512]{2,1,0:T(8,128)S(1)} custom-call(f32[2,448,512]{2,1,0:T(8,128)S(1)} %copy-done.11), custom_call_target="tpu_custom_call" | custom-call | flops 22000001024 | bytes 3670016 | tf_op jit(solution)/shard_map/pallas_call | solution.py:375
  195.7 2.8 %shard_map.77 = (f32[2,84,448]{2,1,0:T(8,128)S(1)}, f32[2,84,448]{2,1,0:T(8,128)S(1)}) custom-call(s32[3]{0:T(128)S(1)} %pad_add_fusion.1.at_ref, f32[2,448,512]{2,1,0:T(8,128)S(1)} %shard_map.76.w_ref, f32[2,1,512]{2,1,0:T(1,128)S(1)} %get-tuple-element.36.root_ref, bf16[2,112,512]{2,1,0:T(8,128)(2,1)S(1)} %maximum_select_fusion.1.own_ref, ...), custom_call_target="tpu_custom_call" | custom-call | flops 2000000000 | bytes 3670016 | tf_op jit(solution)/shard_map/pallas_call | solution.py:420
  198.5 2.1 %collective-permute-start.19 = (f32[2,84,448]{2,1,0:T(8,128)S(1)}, f32[2,84,448]{2,1,0:T(8,128)S(1)}, u32[]{:S(2)}, u32[]{:S(2)}) collective-permute-start(f32[2,84,448]{2,1,0:T(8,128)S(1)} %get-tuple-element.39), channel_id=1, source_target_pairs={{0,1},{1,0},{2,3},{3,2},{4,5},{5,4},{6,7},{7,6},{8,9},{9,8},{10,11... | collective-permute-start | bytes 903176 | tf_op jit(solution)/shard_map/ppermute | solution.py:490
  200.6 1.3 collective-permute-done.19
  (85 shorter events, 10.1 us)
Async XLA Ops:
  0.7 1.4 copy-start.8
  2.1 8.0 %copy-start.9 = (bf16[1792,448]{0,1:T(8,128)(2,1)S(1)}, bf16[1792,448]{0,1:T(8,128)(2,1)}, u32[]{:S(2)}) copy-start(bf16[1792,448]{0,1:T(8,128)(2,1)} %param.7) | copy-start | bytes 4816900
  8.7 12.3 %collective-permute-start.1 = (f32[2,1792,256]{2,1,0:T(8,128)S(1)}, f32[2,1792,256]{2,1,0:T(8,128)S(1)}, u32[]{:S(2)}, u32[]{:S(2)}) collective-permute-start(f32[2,1792,256]{2,1,0:T(8,128)S(1)} %get-tuple-element.26), channel_id=1, source_target_pairs={{0,1},{1,0},{2,3},{3,2},{4,5},{5,4},{6,7},{7,6},{8,9},{9,8},{10,11... | collective-permute-start | bytes 11010056 | tf_op jit(solution)/shard_map/ppermute | solution.py:443
  20.9 1.8 copy-start.3
  20.9 9.4 %collective-permute-start = (f32[1,3584,256]{2,1,0:T(8,128)}, f32[1,3584,256]{2,1,0:T(8,128)}, u32[]{:S(2)}, u32[]{:S(2)}) collective-permute-start(f32[1,3584,256]{2,1,0:T(8,128)} %get-tuple-element.22), channel_id=1, source_target_pairs={{0,1},{1,0},{2,3},{3,2},{4,5},{5,4},{6,7},{7,6},{8,9},{9,8},{10,11... | collective-permute-start | bytes 11010056 | tf_op jit(solution)/shard_map/ppermute | solution.py:445
  22.7 1.3 copy-start.6
  24.1 5.6 %copy-start.16 = (s32[2,112]{1,0:T(2,128)S(1)}, s32[2,112]{1,0:T(2,128)}, u32[]{:S(2)}) copy-start(s32[2,112]{1,0:T(2,128)} %param.9) | copy-start | bytes 2692
  24.1 33.3 %all-to-all-start.1 = ((bf16[8,28,16,256]{3,2,1,0:T(8,128)(2,1)}), bf16[8,28,16,256]{3,2,1,0:T(8,128)(2,1)S(1)}, u32[]{:S(2)}, u32[]{:S(2)}) async-start(bf16[8,28,16,256]{3,2,1,0:T(8,128)(2,1)} %copy-done.6), calls=%async_computation.1 | async-start | bytes 3670016 | tf_op jit(solution)/shard_map/all_to_all | solution.py:447
  30.3 2.0 %copy-start.4 = (f32[1,3584,256]{2,1,0:T(8,128)S(1)}, f32[1,3584,256]{2,1,0:T(8,128)}, u32[]{:S(2)}) copy-start(f32[1,3584,256]{2,1,0:T(8,128)} %copy-done.3) | copy-start | bytes 11010052
  35.4 1.3 copy-start.5
  57.4 1.2 copy-start
  58.6 43.7 %all-to-all-start = ((bf16[8,28,16,256]{3,2,1,0:T(8,128)(2,1)}), bf16[8,28,16,256]{3,2,1,0:T(8,128)(2,1)S(1)}, u32[]{:S(2)}, u32[]{:S(2)}) async-start(bf16[8,28,16,256]{3,2,1,0:T(8,128)(2,1)} %copy-done.5), calls=%async_computation | async-start | bytes 3670016 | tf_op jit(solution)/shard_map/all_to_all | solution.py:449
  62.3 1.5 copy-start.1
  64.7 19.0 %collective-permute-start.6 = (bf16[14,16,256]{2,1,0:T(8,128)(2,1)S(1)}, bf16[14,16,256]{2,1,0:T(8,128)(2,1)S(1)}, u32[]{:S(2)}, u32[]{:S(2)}) collective-permute-start(bf16[14,16,256]{2,1,0:T(8,128)(2,1)S(1)} %get-tuple-element.56), channel_id=1, source_target_pairs={{0,16},{16,0},{1,17},{17,1},{2,18},{18,2},{3,19},{19,3},{4,20},{20... | collective-permute-start | bytes 344072 | tf_op jit(solution)/shard_map/ppermute | solution.py:105
  68.2 19.6 %collective-permute-start.3 = (bf16[14,16,256]{2,1,0:T(8,128)(2,1)S(1)}, bf16[14,16,256]{2,1,0:T(8,128)(2,1)S(1)}, u32[]{:S(2)}, u32[]{:S(2)}) collective-permute-start(bf16[14,16,256]{2,1,0:T(8,128)(2,1)S(1)} %get-tuple-element.57), channel_id=1, source_target_pairs={{0,64},{32,96},{64,0},{96,32},{1,65},{33,97},{65,1},{97,33},{2,66}... | collective-permute-start | bytes 344072 | tf_op jit(solution)/shard_map/ppermute | solution.py:105
  71.1 18.9 %collective-permute-start.2 = (bf16[14,16,256]{2,1,0:T(8,128)(2,1)S(1)}, bf16[14,16,256]{2,1,0:T(8,128)(2,1)S(1)}, u32[]{:S(2)}, u32[]{:S(2)}) collective-permute-start(bf16[14,16,256]{2,1,0:T(8,128)(2,1)S(1)} %get-tuple-element.57), channel_id=1, source_target_pairs={{0,32},{32,64},{64,96},{96,0},{1,33},{33,65},{65,97},{97,1},{2,34}... | collective-permute-start | bytes 344072 | tf_op jit(solution)/shard_map/ppermute | solution.py:105
  71.5 18.5 %collective-permute-start.4 = (bf16[14,16,256]{2,1,0:T(8,128)(2,1)S(1)}, bf16[14,16,256]{2,1,0:T(8,128)(2,1)S(1)}, u32[]{:S(2)}, u32[]{:S(2)}) collective-permute-start(bf16[14,16,256]{2,1,0:T(8,128)(2,1)S(1)} %get-tuple-element.57), channel_id=1, source_target_pairs={{0,96},{32,0},{64,32},{96,64},{1,97},{33,1},{65,33},{97,65},{2,98}... | collective-permute-start | bytes 344072 | tf_op jit(solution)/shard_map/ppermute | solution.py:105
  84.4 7.2 %collective-permute-start.8 = (bf16[2,14,16,256]{3,2,1,0:T(8,128)(2,1)S(1)}, bf16[2,14,16,256]{3,2,1,0:T(8,128)(2,1)S(1)}, u32[]{:S(2)}, u32[]{:S(2)}) collective-permute-start(bf16[2,14,16,256]{3,2,1,0:T(8,128)(2,1)S(1)} %get-tuple-element.53), channel_id=1, source_target_pairs={{0,64},{32,96},{64,0},{96,32},{1,65},{33,97},{65,1},{97,33},{2,66}... | collective-permute-start | bytes 688136 | tf_op jit(solution)/shard_map/ppermute | solution.py:105
  87.4 6.1 %collective-permute-start.7 = (bf16[2,14,16,256]{3,2,1,0:T(8,128)(2,1)S(1)}, bf16[2,14,16,256]{3,2,1,0:T(8,128)(2,1)S(1)}, u32[]{:S(2)}, u32[]{:S(2)}) collective-permute-start(bf16[2,14,16,256]{3,2,1,0:T(8,128)(2,1)S(1)} %get-tuple-element.53), channel_id=1, source_target_pairs={{0,32},{32,64},{64,96},{96,0},{1,33},{33,65},{65,97},{97,1},{2,34}... | collective-permute-start | bytes 688136 | tf_op jit(solution)/shard_map/ppermute | solution.py:105
  87.8 5.9 %collective-permute-start.9 = (bf16[2,14,16,256]{3,2,1,0:T(8,128)(2,1)S(1)}, bf16[2,14,16,256]{3,2,1,0:T(8,128)(2,1)S(1)}, u32[]{:S(2)}, u32[]{:S(2)}) collective-permute-start(bf16[2,14,16,256]{3,2,1,0:T(8,128)(2,1)S(1)} %get-tuple-element.53), channel_id=1, source_target_pairs={{0,96},{32,0},{64,32},{96,64},{1,97},{33,1},{65,33},{97,65},{2,98}... | collective-permute-start | bytes 688136 | tf_op jit(solution)/shard_map/ppermute | solution.py:105
  91.1 9.1 %collective-permute-start.5 = (bf16[4,14,16,256]{3,2,1,0:T(8,128)(2,1)}, bf16[4,14,16,256]{3,2,1,0:T(8,128)(2,1)}, u32[]{:S(2)}, u32[]{:S(2)}) collective-permute-start(bf16[4,14,16,256]{3,2,1,0:T(8,128)(2,1)} %get-tuple-element.49), channel_id=1, source_target_pairs={{0,16},{16,0},{1,17},{17,1},{2,18},{18,2},{3,19},{19,3},{4,20},{20... | collective-permute-start | bytes 1376264 | tf_op jit(solution)/shard_map/ppermute | solution.py:105
  91.6 8.6 %copy-start.12 = (bf16[1,4,14,16,256]{4,3,2,1,0:T(8,128)(2,1)S(1)}, bf16[1,4,14,16,256]{4,3,2,1,0:T(8,128)(2,1)}, u32[]{:S(2)}) copy-start(bf16[1,4,14,16,256]{4,3,2,1,0:T(8,128)(2,1)} %get-tuple-element.48) | copy-start | bytes 1376260
  91.6 2.0 copy-start.13
  93.4 0.7 copy-start.14
  93.6 0.7 copy-start.15
  102.2 1.2 copy-start.2
  104.5 8.4 %collective-permute-start.10 = (bf16[14,16,256]{2,1,0:T(8,128)(2,1)S(1)}, bf16[14,16,256]{2,1,0:T(8,128)(2,1)S(1)}, u32[]{:S(2)}, u32[]{:S(2)}) collective-permute-start(bf16[14,16,256]{2,1,0:T(8,128)(2,1)S(1)} %get-tuple-element.30), channel_id=1, source_target_pairs={{0,1},{1,0},{2,3},{3,2},{4,5},{5,4},{6,7},{7,6},{8,9},{9,8},{10,11... | collective-permute-start | bytes 344072 | tf_op jit(solution)/shard_map/ppermute | solution.py:468
  113.0 9.7 %collective-permute-start.12 = (bf16[2,7,16,256]{3,2,1,0:T(8,128)(2,1)S(1)}, bf16[2,7,16,256]{3,2,1,0:T(8,128)(2,1)S(1)}, u32[]{:S(2)}, u32[]{:S(2)}) collective-permute-start(bf16[2,7,16,256]{3,2,1,0:T(8,128)(2,1)S(1)} %get-tuple-element.65), channel_id=1, source_target_pairs={{0,8},{4,12},{8,0},{12,4},{1,9},{5,13},{9,1},{13,5},{2,10},{6,14},... | collective-permute-start | bytes 344072 | tf_op jit(solution)/shard_map/ppermute | solution.py:105
  119.4 5.5 %collective-permute-start.11 = (bf16[2,7,16,256]{3,2,1,0:T(8,128)(2,1)S(1)}, bf16[2,7,16,256]{3,2,1,0:T(8,128)(2,1)S(1)}, u32[]{:S(2)}, u32[]{:S(2)}) collective-permute-start(bf16[2,7,16,256]{3,2,1,0:T(8,128)(2,1)S(1)} %get-tuple-element.65), channel_id=1, source_target_pairs={{0,4},{4,8},{8,12},{12,0},{1,5},{5,9},{9,13},{13,1},{2,6},{6,10},{... | collective-permute-start | bytes 344072 | tf_op jit(solution)/shard_map/ppermute | solution.py:105
  119.5 5.5 %collective-permute-start.13 = (bf16[2,7,16,256]{3,2,1,0:T(8,128)(2,1)S(1)}, bf16[2,7,16,256]{3,2,1,0:T(8,128)(2,1)S(1)}, u32[]{:S(2)}, u32[]{:S(2)}) collective-permute-start(bf16[2,7,16,256]{3,2,1,0:T(8,128)(2,1)S(1)} %get-tuple-element.65), channel_id=1, source_target_pairs={{0,12},{4,0},{8,4},{12,8},{1,13},{5,1},{9,5},{13,9},{2,14},{6,2},{... | collective-permute-start | bytes 344072 | tf_op jit(solution)/shard_map/ppermute | solution.py:105
  122.1 3.8 %collective-permute-start.15 = (bf16[2,7,16,256]{3,2,1,0:T(8,128)(2,1)S(1)}, bf16[2,7,16,256]{3,2,1,0:T(8,128)(2,1)S(1)}, u32[]{:S(2)}, u32[]{:S(2)}) collective-permute-start(bf16[2,7,16,256]{3,2,1,0:T(8,128)(2,1)S(1)} %get-tuple-element.59), channel_id=1, source_target_pairs={{0,2},{2,0},{1,3},{3,1},{4,6},{6,4},{5,7},{7,5},{8,10},{10,8},{9,1... | collective-permute-start | bytes 344072 | tf_op jit(solution)/shard_map/ppermute | solution.py:105
  125.0 14.7 %collective-permute-start.14 = (bf16[4,2,7,16,256]{4,3,2,1,0:T(8,128)(2,1)S(1)}, bf16[4,2,7,16,256]{4,3,2,1,0:T(8,128)(2,1)S(1)}, u32[]{:S(2)}, u32[]{:S(2)}) collective-permute-start(bf16[4,2,7,16,256]{4,3,2,1,0:T(8,128)(2,1)S(1)} %get-tuple-element.47), channel_id=1, source_target_pairs={{0,2},{2,0},{1,3},{3,1},{4,6},{6,4},{5,7},{7,5},{8,10},{10,8},{9,1... | collective-permute-start | bytes 1376264 | tf_op jit(solution)/shard_map/ppermute | solution.py:105
  126.0 6.6 %collective-permute-start.17 = (bf16[2,2,7,16,256]{4,3,2,1,0:T(8,128)(2,1)S(1)}, bf16[2,2,7,16,256]{4,3,2,1,0:T(8,128)(2,1)S(1)}, u32[]{:S(2)}, u32[]{:S(2)}) collective-permute-start(bf16[2,2,7,16,256]{4,3,2,1,0:T(8,128)(2,1)S(1)} %get-tuple-element.51), channel_id=1, source_target_pairs={{0,8},{4,12},{8,0},{12,4},{1,9},{5,13},{9,1},{13,5},{2,10},{6,14},... | collective-permute-start | bytes 688136 | tf_op jit(solution)/shard_map/ppermute | solution.py:105
  127.1 12.5 %collective-permute-start.16 = (bf16[2,2,7,16,256]{4,3,2,1,0:T(8,128)(2,1)S(1)}, bf16[2,2,7,16,256]{4,3,2,1,0:T(8,128)(2,1)S(1)}, u32[]{:S(2)}, u32[]{:S(2)}) collective-permute-start(bf16[2,2,7,16,256]{4,3,2,1,0:T(8,128)(2,1)S(1)} %get-tuple-element.51), channel_id=1, source_target_pairs={{0,4},{4,8},{8,12},{12,0},{1,5},{5,9},{9,13},{13,1},{2,6},{6,10},{... | collective-permute-start | bytes 688136 | tf_op jit(solution)/shard_map/ppermute | solution.py:105
  128.3 11.3 %collective-permute-start.18 = (bf16[2,2,7,16,256]{4,3,2,1,0:T(8,128)(2,1)S(1)}, bf16[2,2,7,16,256]{4,3,2,1,0:T(8,128)(2,1)S(1)}, u32[]{:S(2)}, u32[]{:S(2)}) collective-permute-start(bf16[2,2,7,16,256]{4,3,2,1,0:T(8,128)(2,1)S(1)} %get-tuple-element.51), channel_id=1, source_target_pairs={{0,12},{4,0},{8,4},{12,8},{1,13},{5,1},{9,5},{13,9},{2,14},{6,2},{... | collective-permute-start | bytes 688136 | tf_op jit(solution)/shard_map/ppermute | solution.py:105
  149.0 6.6 %copy-start.7 = (f32[2,448,512]{2,1,0:T(8,128)S(1)}, f32[2,448,512]{2,1,0:T(8,128)}, u32[]{:S(2)}) copy-start(f32[2,448,512]{2,1,0:T(8,128)} %get-tuple-element.31.a_ref) | copy-start | bytes 5505028
  151.8 18.5 %all-to-all-start.2 = ((f16[8,2,56,512]{3,2,1,0:T(8,128)(2,1)}), f16[8,2,56,512]{3,2,1,0:T(8,128)(2,1)S(1)}, u32[]{:S(2)}, u32[]{:S(2)}) async-start(f16[8,2,56,512]{3,2,1,0:T(8,128)(2,1)} %convert_element_type.11), calls=%async_computation.2 | async-start | bytes 1835008 | tf_op jit(solution)/shard_map/all_to_all | solution.py:482
  169.0 1.3 copy-start.10
  171.3 24.2 %all-to-all-start.3 = ((f16[8,2,56,512]{3,2,1,0:T(8,128)(2,1)}), f16[8,2,56,512]{3,2,1,0:T(8,128)(2,1)S(1)}, u32[]{:S(2)}, u32[]{:S(2)}) async-start(f16[8,2,56,512]{3,2,1,0:T(8,128)(2,1)} %broadcast_in_dim.28), calls=%async_computation.3 | async-start | bytes 1835008 | tf_op jit(solution)/shard_map/all_to_all | solution.py:486
  176.5 1.5 copy-start.11
  198.5 3.4 %collective-permute-start.19 = (f32[2,84,448]{2,1,0:T(8,128)S(1)}, f32[2,84,448]{2,1,0:T(8,128)S(1)}, u32[]{:S(2)}, u32[]{:S(2)}) collective-permute-start(f32[2,84,448]{2,1,0:T(8,128)S(1)} %get-tuple-element.39), channel_id=1, source_target_pairs={{0,1},{1,0},{2,3},{3,2},{4,5},{5,4},{6,7},{7,6},{8,9},{9,8},{10,11... | collective-permute-start | bytes 903176 | tf_op jit(solution)/shard_map/ppermute | solution.py:490

commit v4 on v3

--- a/solution.py
+++ b/solution.py
@@ -16,9 +16,12 @@
 COL = ("x", "zl", "core")
 F32 = jnp.float32
 BF = jnp.bfloat16
-VMEM = pl.BlockSpec(memory_space=pltpu.VMEM)
 SMEM = pl.BlockSpec(memory_space=pltpu.SMEM)
 STEP = 64
+
+
+def whole(array):
+    return pl.BlockSpec(array.shape, lambda *_: (0,) * len(array.shape))
 
 
 def params(mib):
@@ -105,15 +108,14 @@
     return lax.ppermute(value, axis, [(i, (i + by) % size) for i in range(size)])
 
 
-def ring_gather(value, axis):
-    size = lax.axis_size(axis)
-    return jnp.stack([value] + [shift(value, axis, by) for by in range(1, size)])
-
-
-def two_way_gather(first, second, big, small):
-    first_ring = ring_gather(first, big)
-    second_pair = ring_gather(second, small)
-    return ring_gather(first_ring, small), ring_gather(second_pair, big)
+def ring_pieces(value, axis):
+    return [value] + [shift(value, axis, by) for by in range(1, lax.axis_size(axis))]
+
+
+def two_way_pieces(first, second, big, small):
+    first_ring = jnp.stack(ring_pieces(first, big))
+    second_pair = jnp.stack(ring_pieces(second, small))
+    return ring_pieces(first_ring, small), ring_pieces(second_pair, big)
 
 
 def sum_of(shares_ref, own, here, at):
@@ -129,43 +131,66 @@
 
 
 def sum_shares(at, shares, own, dtype):
+    chips, blocks, slab, half = shares.shape
+    step = LEAF // BLOCK
     return pl.pallas_call(
         sum_kernel,
+        grid=(blocks // step,),
         out_shape=jax.ShapeDtypeStruct(shares.shape[1:], dtype),
-        in_specs=[SMEM, VMEM, VMEM],
-        out_specs=VMEM,
-        compiler_params=params(24),
+        in_specs=[
+            SMEM,
+            pl.BlockSpec((chips, step, slab, half), lambda i: (0, i, 0, 0)),
+            pl.BlockSpec((step, slab, half), lambda i: (i, 0, 0)),
+        ],
+        out_specs=pl.BlockSpec((step, slab, half), lambda i: (i, 0, 0)),
+        compiler_params=params(16),
         cost_estimate=cost(shares.size, 2 * shares.size),
     )(at, shares, own)
 
 
-def extend_kernel(at_ref, from_ref, p_ref, own_ref, first_ref, second_ref, keep_ref, send_ref, all_ref):
+def extend_kernel(at_ref, from_ref, p_ref, own_ref, *refs):
+    *kid_refs, keep_ref, send_ref, all_ref = refs
     here = at_ref[0] * 2 + at_ref[1]
     core = at_ref[2]
-    for block in range(p_ref.shape[1]):
+    step = pl.program_id(0)
+    blocks = own_ref.shape[0]
+    for block in range(blocks):
         total = sum_of(p_ref, own_ref[block], here, (block,))
-        for kid, ref in enumerate((first_ref, second_ref)):
-            near, far, place = (from_ref[kid, part, block] for part in range(3))
-            there = from_ref[kid, 3, block]
-            total += jnp.where(there > 0, ref[near, far, place].astype(F32), 0.0)
-        all_ref[block] = total.astype(BF)
-    count = keep_ref.shape[0]
-    keep_ref[...] = all_ref[pl.ds(core * count, count)]
-    send_ref[...] = all_ref[pl.ds((1 - core) * count, count)]
-
-
-def extend_add(at, source, parent, own, first, second):
-    blocks, slab, half = parent.shape[1:]
+        target = step * blocks + block
+        for kid in range(2):
+            ring, pair, place, there = (from_ref[kid, part, target] for part in range(4))
+            for i, ref in enumerate(kid_refs):
+                hit = (there > 0) & (ring == i)
+                total += jnp.where(hit, ref[pair, kid, place].astype(F32), 0.0)
+        all_ref[target] = total.astype(BF)
+
+    @pl.when(step == pl.num_programs(0) - 1)
+    def _():
+        count = keep_ref.shape[0]
+        keep_ref[...] = all_ref[pl.ds(core * count, count)]
+        send_ref[...] = all_ref[pl.ds((1 - core) * count, count)]
+
+
+def extend_add(at, source, parent, own, kids):
+    chips, blocks, slab, half = parent.shape
+    step = LEAF // BLOCK
     pair = jax.ShapeDtypeStruct((blocks // 2, slab, half), BF)
     return pl.pallas_call(
         extend_kernel,
+        grid=(blocks // step,),
         out_shape=[pair, pair],
-        in_specs=[SMEM, SMEM, VMEM, VMEM, VMEM, VMEM],
-        out_specs=[VMEM, VMEM],
+        in_specs=[
+            SMEM,
+            SMEM,
+            pl.BlockSpec((chips, step, slab, half), lambda i: (0, i, 0, 0)),
+            pl.BlockSpec((step, slab, half), lambda i: (i, 0, 0)),
+        ]
+        + [whole(piece) for piece in kids],
+        out_specs=[whole(pair)] * 2,
         scratch_shapes=[pltpu.VMEM(parent.shape[1:], BF)],
-        compiler_params=params(16),
+        compiler_params=params(24),
         cost_estimate=cost(parent.size, 6 * parent.size),
-    )(at, source, parent, own, first, second)
+    )(at, source, parent, own, *kids)
 
 
 def halves(x):
@@ -186,10 +211,12 @@
 LEVEL = 8.0
 
 
-def gram_kernel(at_ref, f_ref, a_ref, b_ref, gram_ref, root_ref, cross_ref, y_ref):
+def gram_kernel(at_ref, f_ref, *refs):
+    a_refs, b_refs = refs[:2], refs[2:6]
+    gram_ref, root_ref, cross_ref, y_ref, t_ref = refs[6:]
     x, zl, core = (at_ref[i] for i in range(3))
     step = pl.program_id(0)
-    half = a_ref.shape[-1]
+    half = y_ref.shape[-1] // 2
     per = LEAF // BLOCK
     leaves, order, wide = gram_ref.shape
     row = lax.broadcasted_iota(jnp.int32, (order, wide), 0)
@@ -204,19 +231,20 @@
                 for j in range(2):
                     chip = lax.rem(x + 4 - i, 4) * 2 + lax.rem(zl + j, 2)
                     rows = pl.ds(pl.multiple_of(chip * 16, 16), 16)
-                    y_ref[:per, rows, lanes] = a_ref[j, i, side]
-                    y_ref[per:, rows, lanes] = b_ref[i, j, side]
+                    y_ref[:per, rows, lanes] = a_refs[j][i, side]
+                    y_ref[per:, rows, lanes] = b_refs[i][j, side]
         for leaf in range(leaves):
             y = y_ref[leaf * per : (leaf + 1) * per].reshape(LEAF, wide)
-            gram = contract(y, y, 0, 0)[:order]
+            t_ref[leaf] = y.T[:order]
+            gram = contract(t_ref[leaf], y, 1, 0)
             gram_ref[leaf] = gram
             square = jnp.sum(jnp.where(row == col, gram, 0.0), axis=0, keepdims=True)
             root_ref[leaf] = jnp.sqrt(jnp.where(lane < order, square, 1.0))
 
-    here = y_ref[pl.ds(step * per, per)].reshape(LEAF, wide)
+    here = t_ref[step]
     there = y_ref[pl.ds((1 - step) * per, per)].reshape(LEAF, wide)
     hi, lo = halves(jnp.dot(f_ref[...], there, preferred_element_type=F32) / root_ref[1 - step])
-    cross = (contract(here, hi, 0, 0) + contract(here, lo, 0, 0))[:order]
+    cross = contract(here, hi, 1, 0) + contract(here, lo, 1, 0)
     square = jnp.sum(jnp.where(row == col, gram_ref[step], 0.0), axis=1, keepdims=True)
     cross = cross * lax.rsqrt(square)
     most = jnp.max(jnp.max(jnp.abs(cross), axis=0, keepdims=True), axis=1, keepdims=True)
@@ -228,7 +256,6 @@
 def grams(at, front, mine, order, chips):
     half = mine[0].shape[-1]
     wide = 2 * half
-    whole = pl.BlockSpec(memory_space=pltpu.VMEM)
     return pl.pallas_call(
         gram_kernel,
         grid_spec=pltpu.PrefetchScalarGridSpec(
@@ -236,15 +263,17 @@
             grid=(2,),
             in_specs=[
                 pl.BlockSpec((LEAF, LEAF), lambda i, at: (at[2] * 2 + i, 1 - i)),
-                whole,
-                whole,
-            ],
+            ]
+            + [whole(piece) for piece in mine],
             out_specs=[
                 pl.BlockSpec((2, order, wide), lambda i, at: (0, 0, 0)),
                 pl.BlockSpec((2, 1, wide), lambda i, at: (0, 0, 0)),
                 pl.BlockSpec((chips, 1, order // chips, wide), lambda i, at: (0, i, 0, 0)),
             ],
-            scratch_shapes=[pltpu.VMEM((2 * LEAF // BLOCK, BLOCK, wide), BF)],
+            scratch_shapes=[
+                pltpu.VMEM((2 * LEAF // BLOCK, BLOCK, wide), BF),
+                pltpu.VMEM((2, order, LEAF), BF),
+            ],
         ),
         out_shape=[
             jax.ShapeDtypeStruct((2, order, wide), F32),
@@ -302,7 +331,8 @@
             rows[g] = new
 
 
-def inverse_kernel(a_ref, w_ref, x_ref, d_ref, *, first, last):
+def inverse_kernel(a_ref, after_ref, w_ref, x_ref, d_ref, *, first, last):
+    del after_ref
     leaves, order, wide = w_ref.shape
     blocks = order // STEP
     w_ref[...] = a_ref[...]
@@ -370,20 +400,21 @@
             w_ref[leaf, rows, :] = jnp.where(col <= row + i * STEP, w_ref[leaf, rows, :], 0.0)
 
 
-def factor_inverse(work, first, last):
+def factor_inverse(work, after, first, last):
     leaves = work.shape[0]
     return pl.pallas_call(
         functools.partial(inverse_kernel, first=first, last=last),
+        grid=(1,),
         out_shape=jax.ShapeDtypeStruct(work.shape, F32),
-        in_specs=[VMEM],
-        out_specs=VMEM,
+        in_specs=[whole(work), pl.BlockSpec(memory_space=pl.ANY)],
+        out_specs=whole(work),
         scratch_shapes=[
             pltpu.VMEM((leaves, STEP, STEP), F32),
             pltpu.VMEM((leaves, STEP, 128), F32),
         ],
         compiler_params=params(24),
         cost_estimate=cost((last - first) * 5.5e9, 8 * work.size),
-    )(work)
+    )(work, after)
 
 
 def finish_kernel(at_ref, w_ref, root_ref, own_ref, cross_ref, keep_ref, send_ref):
@@ -419,9 +450,10 @@
     part = jax.ShapeDtypeStruct((leaves, rows, order), F32)
     return pl.pallas_call(
         finish_kernel,
+        grid=(1,),
         out_shape=[part, part],
-        in_specs=[SMEM, VMEM, VMEM, VMEM, VMEM],
-        out_specs=[VMEM, VMEM],
+        in_specs=[SMEM, whole(inverse), whole(root), whole(own), whole(cross)],
+        out_specs=[whole(part)] * 2,
         compiler_params=params(24),
         cost_estimate=cost(2e9, 4 * (inverse.size + cross.size)),
     )(at, inverse, root, own, cross)
@@ -446,10 +478,17 @@
     kid_part, kid_rest = pack(at, kid_kept, kid_sent, chips)
     kid_share = lax.all_to_all(kid_part, CHIP, 0, 0, tiled=True)
     own_part, own_rest = pack(at, own_kept, own_sent, chips)
+
+    kids = sum_shares(at, kid_share, kid_rest, BF).reshape(2, kid_blocks, -1, half)
+    pair = ring_pieces(kids, "zh")
+    pair[1], own_part = lax.optimization_barrier((pair[1], own_part))
+    pair = jnp.stack(pair)
     own_share = lax.all_to_all(own_part, CHIP, 0, 0, tiled=True)
-
-    kids = sum_shares(at, kid_share, kid_rest, BF)
-    first, second = two_way_gather(kids[:kid_blocks], kids[kid_blocks:], "y", "zh")
+    reach = [(0, 1), (0, 2), (1, 0), (1, 2), (2, 1), (2, 3), (3, 1), (3, 2)]
+    kid_pieces = [pair] + [
+        lax.ppermute(pair, "y", [(i, j) for i, j in reach if (j - i) % 4 == by])
+        for by in range(1, 4)
+    ]
 
     targets = row_index * own_blocks + jnp.arange(own_blocks, dtype=jnp.int32)
     hit = child_map[:, None, :] == targets[None, :, None]
@@ -457,21 +496,16 @@
     source = jnp.sum(jnp.where(hit, jnp.arange(child_map.shape[1], dtype=jnp.int32), 0), axis=2)
     owner, place = source // kid_blocks, source % kid_blocks
     ring = (y - owner // 2) % 4
-    pair = (zh - owner % 2) % 2
-    origin = jnp.stack(
-        [
-            jnp.stack([pair[0], ring[0], place[0], there[0]]),
-            jnp.stack([ring[1], pair[1], place[1], there[1]]),
-        ]
-    ).astype(jnp.int32)
-    keep, send = extend_add(at, origin, own_share, own_rest, first, second)
+    pair_of = (zh - owner % 2) % 2
+    origin = jnp.stack([ring, pair_of, place, there], axis=1).astype(jnp.int32)
+    keep, send = extend_add(at, origin, own_share, own_rest, kid_pieces)
     came = lax.ppermute(send, "core", swap)
 
     per = LEAF // BLOCK
     first = jnp.stack([keep[:per], came[:per]])
     second = jnp.stack([keep[per:], came[per:]])
-    mine = two_way_gather(first, second, "x", "zl")
-    gram, root, cross = grams(at, parent_front, mine, probes, chips)
+    firsts, seconds = two_way_pieces(first, second, "x", "zl")
+    gram, root, cross = grams(at, parent_front, firsts + seconds, probes, chips)
 
     own_rows = jnp.where(
         core == 0,
@@ -480,12 +514,10 @@
     ).reshape(2, -1, 2 * half)
 
     cross = lax.all_to_all(cross.astype(jnp.float16), CHIP, 0, 0, tiled=True)
-    cross = lax.dynamic_slice_in_dim(cross, row_index, 1, 0)
-    work = factor_inverse(gram, 0, 3)
-    work, cross = lax.optimization_barrier((work, cross))
-    cross = lax.all_to_all(jnp.broadcast_to(cross, (chips, *cross.shape[1:])), CHIP, 0, 0, tiled=True)
-    inverse = factor_inverse(work, 3, probes // STEP)
-    inverse, cross = lax.optimization_barrier((inverse, cross))
+    ready = lax.dynamic_slice_in_dim(cross, row_index, 1, 0)
+    work = factor_inverse(gram, own_rows, 0, 3)
+    cross = lax.all_to_all(jnp.broadcast_to(ready, (chips, *ready.shape[1:])), CHIP, 0, 0, tiled=True)
+    inverse = factor_inverse(work, ready[0, 0, :8, :128].astype(F32), 3, probes // STEP)
     keep, send = finish(at, inverse, root, own_rows, cross.astype(F32))
     came = lax.ppermute(send, "core", swap)
     both = jnp.where(core == 0, jnp.concatenate([keep, came]), jnp.concatenate([came, keep]))

time: 204 us -> 186 us (0.912); the launches traced: 204 us -> 182 us
  blocking collectives: 0 us -> 28.4 us
  waiting for transfers between devices: 51.6 us -> 31.1 us
  starting transfers between devices: 57.9 us -> 41.7 us
  local copies, waits for them, and re-layouts: 17.4 us -> 11.8 us
  other arithmetic: 9.22 us -> 4.55 us
  Pallas kernels: 66.5 us -> 63.7 us
    all_to_all x0 -> x1, blocking collectives: none -> 28.4 us  [local(): kid_share = lax.all_to_all(kid_part, CHIP, 0, 0, tiled=True)]
    all_to_all x2 -> x1, waiting for transfers between devices: 20.7 us -> 0.01 us  [local(): lax.all_to_all(jnp.broadcast_to(ready, (chips, *ready.shape[1:])), CHIP,...]
    ppermute x16 -> x9, starting transfers between devices: 28.7 us -> 13 us  [shift(): lax.ppermute(value, axis, [(i, (i + by) % size) for i in range(size)])]
    ppermute x16 -> x9, waiting for transfers between devices: 28.7 us -> 14.9 us  [shift(): lax.ppermute(value, axis, [(i, (i + by) % size) for i in range(size)])]
    ppermute x0 -> x3, waiting for transfers between devices: none -> 11.5 us  [local(): lax.ppermute(pair, 'y', [(i, j) for i, j in reach if (j - i) % 4 == by])]
    ppermute x0 -> x3, starting transfers between devices: none -> 9.05 us  [local(): lax.ppermute(pair, 'y', [(i, j) for i, j in reach if (j - i) % 4 == by])]
    ppermute x2, starting transfers between devices: 9.54 us -> 3.77 us  [local(): came = lax.ppermute(send, 'core', swap)]
    all_to_all x2 -> x1, starting transfers between devices: 10.7 us -> 5.14 us  [local(): lax.all_to_all(jnp.broadcast_to(ready, (chips, *ready.shape[1:])), CHIP,...]
  transfers between devices with their start and end apart: 24 -> 19, of which waited for: 11 -> 11; matrix products, arithmetic and copies ran while one was open for 3% -> 1% of each run, Pallas kernels for 23% -> 24%
where the time goes in v4:
time: 186 us; the launch traced here: 182 us
  Pallas kernels  63.7 us (34%)
  starting transfers between devices  41.7 us (22%)
  waiting for transfers between devices  31.1 us (17%)
  blocking collectives  28.4 us (15%)
  local copies, waits for them, and re-layouts  11.8 us (6%)
  other arithmetic  4.55 us (2%)
    pallas_call x2, Pallas kernels, factor_inverse(): pl.pallas_call(functools.partial(inverse_kernel, first=first, last=last),...  30.8 us
    all_to_all x1, blocking collectives, local(): kid_share = lax.all_to_all(kid_part, CHIP, 0, 0, tiled=True)  28.4 us
    pallas_call x2, Pallas kernels, probe(): pl.pallas_call(probe_kernel, grid=(count, rows // LEAF), out_shape=[part,...  15.9 us
    ppermute x9, waiting for transfers between devices, shift(): lax.ppermute(value, axis, [(i, (i + by) % size) for i in range(size)])  14.9 us
    ppermute x9, starting transfers between devices, shift(): lax.ppermute(value, axis, [(i, (i + by) % size) for i in range(size)])  13 us
    ppermute x3, waiting for transfers between devices, local(): lax.ppermute(pair, 'y', [(i, j) for i, j in reach if (j - i) % 4 == by])  11.5 us
    unnamed x25, local copies, waits for them, and re-layouts  9.95 us
    ppermute x3, starting transfers between devices, local(): lax.ppermute(pair, 'y', [(i, j) for i, j in reach if (j - i) % 4 == by])  9.05 us
  transfers between devices with their start and end apart: 19, of which 11 were waited for; matrix products, arithmetic and copies ran while one was open for 1% of the time, Pallas kernels for 24%

profile of v4, /device:TPU:1, one launch (start us, length us, event | category | flops | bytes accessed | tf_op | source)
XLA Modules:
  0.0 182.1 jit_solution(10470101583840197204)
XLA Ops:
  0.7 1.4 copy-done.6
  2.1 6.5 %shard_map.68 = (f32[2,1792,256]{2,1,0:T(8,128)S(1)}, f32[2,1792,256]{2,1,0:T(8,128)S(1)}) custom-call(s32[3]{0:T(128)S(1)} %pad_add_fusion.1.at_ref, bf16[2,1792,896]{2,1,0:T(8,128)(2,1)} %a_ref.1, bf16[2,448,896]{2,1,0:T(8,128)(2,1)S(1)} %bitcast.51), custom_call_target="tpu_custom_call" | custom-call | flops 3288334336 | bytes 13762560 | tf_op jit(solution)/shard_map/pallas_call | solution.py:50
  8.7 1.5 collective-permute-start
  10.2 9.4 %shard_map.71 = (f32[1,3584,256]{2,1,0:T(8,128)S(1)}, f32[1,3584,256]{2,1,0:T(8,128)S(1)}) custom-call(s32[3]{0:T(128)S(1)} %pad_add_fusion.1.at_ref, bf16[1,3584,1792]{2,1,0:T(8,128)(2,1)} %bitcast.53, bf16[1,448,1792]{2,1,0:T(8,128)(2,1)S(1)} %bitcast.52), custom_call_target="tpu_custom_call" | custom-call | flops 6576668672 | bytes 20185088 | tf_op jit(solution)/shard_map/pallas_call | solution.py:50
  19.7 1.3 shard_map.69
  21.0 28.4 %all_to_all.20.k_ref = bf16[8,28,16,256]{3,2,1,0:T(8,128)(2,1)S(1)} all-to-all(bf16[8,28,16,256]{3,2,1,0:T(8,128)(2,1)S(1)} %get-tuple-element.21), channel_id=1, replica_groups=mesh['y'=4,'zh'=2,'x'=4,'zl'=2,'core'=2] {'x','zl'}, dimensions={0} | all-to-all | bytes 3670016 | tf_op jit(solution)/shard_map/all_to_all | solution.py:479
  49.4 1.1 shard_map.70
  50.5 3.4 %collective-permute-start.1 = (bf16[2,14,16,256]{3,2,1,0:T(8,128)(2,1)S(1)}, bf16[2,14,16,256]{3,2,1,0:T(8,128)(2,1)S(1)}, u32[]{:S(2)}, u32[]{:S(2)}) collective-permute-start(bf16[2,14,16,256]{3,2,1,0:T(8,128)(2,1)S(1)} %bitcast.48), channel_id=1, source_target_pairs={{0,16},{16,0},{1,17},{17,1},{2,18},{18,2},{3,19},{19,3},{4,20},{20... | collective-permute-start | bytes 688136 | tf_op jit(solution)/shard_map/ppermute | solution.py:108
  53.9 1.3 shard_map.72
  55.2 1.2 copy-done
  56.4 1.7 collective-permute-done.1
  58.2 3.7 %all-to-all-start.1 = ((bf16[8,28,16,256]{3,2,1,0:T(8,128)(2,1)}), bf16[8,28,16,256]{3,2,1,0:T(8,128)(2,1)S(1)}, u32[]{:S(2)}, u32[]{:S(2)}) async-start(bf16[8,28,16,256]{3,2,1,0:T(8,128)(2,1)} %copy-done), calls=%async_computation.1 | async-start | bytes 3670016 | tf_op jit(solution)/shard_map/all_to_all | solution.py:486
  62.4 3.2 %collective-permute-start.3 = (bf16[2,2,14,16,256]{4,3,2,1,0:T(8,128)(2,1)S(1)}, bf16[2,2,14,16,256]{4,3,2,1,0:T(8,128)(2,1)S(1)}, u32[]{:S(2)}, u32[]{:S(2)}) collective-permute-start(bf16[2,2,14,16,256]{4,3,2,1,0:T(8,128)(2,1)S(1)} %pad_maximum_fusion.refs_0_), channel_id=1, source_target_pairs={{0,32},{32,64},{64,96},{1,33},{33,65},{65,97},{2,34},{34,66},{66,9... | collective-permute-start | bytes 1376264 | tf_op jit(solution)/shard_map/ppermute | solution.py:489
  65.6 4.5 %collective-permute-start.4 = (bf16[2,2,14,16,256]{4,3,2,1,0:T(8,128)(2,1)S(1)}, bf16[2,2,14,16,256]{4,3,2,1,0:T(8,128)(2,1)S(1)}, u32[]{:S(2)}, u32[]{:S(2)}) collective-permute-start(bf16[2,2,14,16,256]{4,3,2,1,0:T(8,128)(2,1)S(1)} %pad_maximum_fusion.refs_0_), channel_id=1, source_target_pairs={{0,64},{96,32},{1,65},{97,33},{2,66},{98,34},{3,67},{99,35},{4,68}... | collective-permute-start | bytes 1376264 | tf_op jit(solution)/shard_map/ppermute | solution.py:489
  70.2 1.3 collective-permute-start.5
  71.6 1.6 collective-permute-done.3.refs_1_
  73.1 9.9 %collective-permute-done.4.refs_2_ = bf16[2,2,14,16,256]{4,3,2,1,0:T(8,128)(2,1)S(1)} collective-permute-done((bf16[2,2,14,16,256]{4,3,2,1,0:T(8,128)(2,1)S(1)}, bf16[2,2,14,16,256]{4,3,2,1,0:T(8,128)(2,1)S(1)}, u32[]{:S(2)}, u32[]{:S(2)}) %collective-permute-start.4) | collective-permute-done | bytes 458784 | tf_op jit(solution)/shard_map/ppermute | solution.py:489
  83.0 0.8 copy-done.1
  83.8 0.8 copy-done.3
  84.6 2.4 %all-to-all-done.1.p_ref = bf16[8,28,16,256]{3,2,1,0:T(8,128)(2,1)S(1)} async-done(((bf16[8,28,16,256]{3,2,1,0:T(8,128)(2,1)}), bf16[8,28,16,256]{3,2,1,0:T(8,128)(2,1)S(1)}, u32[]{:S(2)}, u32[]{:S(2)}) %all-to-all-start.1) | async-done | bytes 1835040 | tf_op jit(solution)/shard_map/all_to_all | solution.py:486
  87.0 1.0 copy-done.2
  88.0 1.0 copy-done.4
  89.0 1.7 shard_map.73
  90.7 2.4 %collective-permute-start.6 = (bf16[14,16,256]{2,1,0:T(8,128)(2,1)S(1)}, bf16[14,16,256]{2,1,0:T(8,128)(2,1)S(1)}, u32[]{:S(2)}, u32[]{:S(2)}) collective-permute-start(bf16[14,16,256]{2,1,0:T(8,128)(2,1)S(1)} %get-tuple-element.30), channel_id=1, source_target_pairs={{0,1},{1,0},{2,3},{3,2},{4,5},{5,4},{6,7},{7,6},{8,9},{9,8},{10,11... | collective-permute-start | bytes 344072 | tf_op jit(solution)/shard_map/ppermute | solution.py:502
  93.1 1.0 collective-permute-done.6
  94.2 2.2 %collective-permute-start.8 = (bf16[2,7,16,256]{3,2,1,0:T(8,128)(2,1)S(1)}, bf16[2,7,16,256]{3,2,1,0:T(8,128)(2,1)S(1)}, u32[]{:S(2)}, u32[]{:S(2)}) collective-permute-start(bf16[2,7,16,256]{3,2,1,0:T(8,128)(2,1)S(1)} %get-tuple-element.51), channel_id=1, source_target_pairs={{0,8},{4,12},{8,0},{12,4},{1,9},{5,13},{9,1},{13,5},{2,10},{6,14},... | collective-permute-start | bytes 344072 | tf_op jit(solution)/shard_map/ppermute | solution.py:108
  96.4 1.2 collective-permute-start.9
  97.6 1.3 collective-permute-start.11
  98.9 1.3 collective-permute-done.7
  100.2 1.6 collective-permute-done.8
  103.1 1.1 collective-permute-start.12
  104.2 3.0 %collective-permute-start.13 = (bf16[2,2,7,16,256]{4,3,2,1,0:T(8,128)(2,1)S(1)}, bf16[2,2,7,16,256]{4,3,2,1,0:T(8,128)(2,1)S(1)}, u32[]{:S(2)}, u32[]{:S(2)}) collective-permute-start(bf16[2,2,7,16,256]{4,3,2,1,0:T(8,128)(2,1)S(1)} %pad_maximum_fusion.2.refs_2_), channel_id=1, source_target_pairs={{0,8},{4,12},{8,0},{12,4},{1,9},{5,13},{9,1},{13,5},{2,10},{6,14},... | collective-permute-start | bytes 688136 | tf_op jit(solution)/shard_map/ppermute | solution.py:108
  107.5 2.8 %collective-permute-done.12.refs_3_ = bf16[2,2,7,16,256]{4,3,2,1,0:T(8,128)(2,1)S(1)} collective-permute-done((bf16[2,2,7,16,256]{4,3,2,1,0:T(8,128)(2,1)S(1)}, bf16[2,2,7,16,256]{4,3,2,1,0:T(8,128)(2,1)S(1)}, u32[]{:S(2)}, u32[]{:S(2)}) %collective-permute-start.12) | collective-permute-done | bytes 229408 | tf_op jit(solution)/shard_map/ppermute | solution.py:108
  110.3 6.8 %collective-permute-done.13.refs_4_ = bf16[2,2,7,16,256]{4,3,2,1,0:T(8,128)(2,1)S(1)} collective-permute-done((bf16[2,2,7,16,256]{4,3,2,1,0:T(8,128)(2,1)S(1)}, bf16[2,2,7,16,256]{4,3,2,1,0:T(8,128)(2,1)S(1)}, u32[]{:S(2)}, u32[]{:S(2)}) %collective-permute-start.13) | collective-permute-done | bytes 229408 | tf_op jit(solution)/shard_map/ppermute | solution.py:108
  117.1 8.8 %shard_map.74 = (f32[2,448,512]{2,1,0:T(8,128)}, f32[2,1,512]{2,1,0:T(1,128)S(1)}, f32[8,2,56,512]{3,2,1,0:T(8,128)}) custom-call(s32[3]{0:T(128)S(1)} %pad_add_fusion.1.at_ref, bf16[3584,1792]{1,0:T(8,128)(2,1)} %f_ref.1, bf16[4,2,7,16,256]{4,3,2,1,0:T(8,128)(2,1)S(1)} %pad_maximum_fusion.1.refs_0_, ...), custom_call_target="tpu_custom_call" | custom-call | flops 3758096384 | bytes 6881280 | tf_op jit(solution)/shard_map/pallas_call | solution.py:259
  125.9 2.8 %convert_element_type.27 = f16[8,2,56,512]{3,2,1,0:T(8,128)(2,1)} convert(f32[8,2,56,512]{3,2,1,0:T(8,128)} %get-tuple-element.32) | non-fusion elementwise | flops 458752 | bytes 2752512 | tf_op jit(solution)/shard_map/convert_element_type | solution.py:516
  128.7 5.4 %all-to-all-start.2 = ((f16[8,2,56,512]{3,2,1,0:T(8,128)(2,1)}), f16[8,2,56,512]{3,2,1,0:T(8,128)(2,1)S(1)}, u32[]{:S(2)}, u32[]{:S(2)}) async-start(f16[8,2,56,512]{3,2,1,0:T(8,128)(2,1)} %convert_element_type.27), calls=%async_computation.2 | async-start | bytes 1835008 | tf_op jit(solution)/shard_map/all_to_all | solution.py:516
  134.1 13.4 %shard_map.75.a_ref = f32[2,448,512]{2,1,0:T(8,128)S(1)} custom-call(f32[2,448,512]{2,1,0:T(8,128)S(1)} %copy-done.5, bf16[2,112,512]{2,1,0:T(8,128)(2,1)S(1)} %maximum_select_fusion.1.after_ref.own_ref), custom_call_target="tpu_custom_call" | custom-call | flops 16499999744 | bytes 3670016 | tf_op jit(solution)/shard_map/pallas_call | solution.py:405
  147.5 1.2 copy-done.8
  148.7 1.1 broadcast_in_dim.28
  149.9 5.1 %all-to-all-start.3 = ((f16[8,2,56,512]{3,2,1,0:T(8,128)(2,1)}), f16[8,2,56,512]{3,2,1,0:T(8,128)(2,1)S(1)}, u32[]{:S(2)}, u32[]{:S(2)}) async-start(f16[8,2,56,512]{3,2,1,0:T(8,128)(2,1)} %broadcast_in_dim.28), calls=%async_computation.3 | async-start | bytes 1835008 | tf_op jit(solution)/shard_map/all_to_all | solution.py:519
  155.8 1.5 copy-done.9
  157.3 17.5 %shard_map.76.w_ref = f32[2,448,512]{2,1,0:T(8,128)S(1)} custom-call(f32[2,448,512]{2,1,0:T(8,128)S(1)} %copy-done.9, f32[8,128]{1,0:T(8,128)S(1)} %fusion.2.after_ref), custom_call_target="tpu_custom_call" | custom-call | flops 22000001024 | bytes 3670016 | tf_op jit(solution)/shard_map/pallas_call | solution.py:405
  175.0 2.7 %shard_map.77 = (f32[2,84,448]{2,1,0:T(8,128)S(1)}, f32[2,84,448]{2,1,0:T(8,128)S(1)}) custom-call(s32[3]{0:T(128)S(1)} %pad_add_fusion.1.at_ref, f32[2,448,512]{2,1,0:T(8,128)S(1)} %shard_map.76.w_ref, f32[2,1,512]{2,1,0:T(1,128)S(1)} %get-tuple-element.33.root_ref, bf16[2,112,512]{2,1,0:T(8,128)(2,1)S(1)} %maximum_select_fusion.1.after_ref.own_ref, ...), custom_call_target="tpu_custom_call" | custom-call | flops 2000000000 | bytes 3670016 | tf_op jit(solution)/shard_map/pallas_call | solution.py:451
  177.7 1.4 collective-permute-start.15
  179.1 1.3 collective-permute-done.15
  180.6 0.7 slice.38
  181.3 0.8 copy.41
  (52 shorter events, 3.6 us)
Async XLA Ops:
  0.7 1.4 copy-start.6
  2.1 8.0 %copy-start.7 = (bf16[1792,448]{0,1:T(8,128)(2,1)S(1)}, bf16[1792,448]{0,1:T(8,128)(2,1)}, u32[]{:S(2)}) copy-start(bf16[1792,448]{0,1:T(8,128)(2,1)} %param.7) | copy-start | bytes 4816900
  8.7 11.0 %collective-permute-start = (f32[2,1792,256]{2,1,0:T(8,128)S(1)}, f32[2,1792,256]{2,1,0:T(8,128)S(1)}, u32[]{:S(2)}, u32[]{:S(2)}) collective-permute-start(f32[2,1792,256]{2,1,0:T(8,128)S(1)} %get-tuple-element.20), channel_id=1, source_target_pairs={{0,1},{1,0},{2,3},{3,2},{4,5},{5,4},{6,7},{7,6},{8,9},{9,8},{10,11... | collective-permute-start | bytes 11010056 | tf_op jit(solution)/shard_map/ppermute | solution.py:475
  19.6 34.3 %collective-permute-start.2 = (f32[1,3584,256]{2,1,0:T(8,128)S(1)}, f32[1,3584,256]{2,1,0:T(8,128)S(1)}, u32[]{:S(2)}, u32[]{:S(2)}) collective-permute-start(f32[1,3584,256]{2,1,0:T(8,128)S(1)} %get-tuple-element.24), channel_id=1, source_target_pairs={{0,1},{1,0},{2,3},{3,2},{4,5},{5,4},{6,7},{7,6},{8,9},{9,8},{10,11... | collective-permute-start | bytes 11010056 | tf_op jit(solution)/shard_map/ppermute | solution.py:477
  50.5 7.7 %collective-permute-start.1 = (bf16[2,14,16,256]{3,2,1,0:T(8,128)(2,1)S(1)}, bf16[2,14,16,256]{3,2,1,0:T(8,128)(2,1)S(1)}, u32[]{:S(2)}, u32[]{:S(2)}) collective-permute-start(bf16[2,14,16,256]{3,2,1,0:T(8,128)(2,1)S(1)} %bitcast.48), channel_id=1, source_target_pairs={{0,16},{16,0},{1,17},{17,1},{2,18},{18,2},{3,19},{19,3},{4,20},{20... | collective-permute-start | bytes 688136 | tf_op jit(solution)/shard_map/ppermute | solution.py:108
  55.2 1.3 copy-start
  58.2 3.8 %copy-start.11 = (s32[2,112]{1,0:T(2,128)S(1)}, s32[2,112]{1,0:T(2,128)}, u32[]{:S(2)}) copy-start(s32[2,112]{1,0:T(2,128)} %param.9) | copy-start | bytes 2692
  58.2 28.8 %all-to-all-start.1 = ((bf16[8,28,16,256]{3,2,1,0:T(8,128)(2,1)}), bf16[8,28,16,256]{3,2,1,0:T(8,128)(2,1)S(1)}, u32[]{:S(2)}, u32[]{:S(2)}) async-start(bf16[8,28,16,256]{3,2,1,0:T(8,128)(2,1)} %copy-done), calls=%async_computation.1 | async-start | bytes 3670016 | tf_op jit(solution)/shard_map/all_to_all | solution.py:486
  62.4 10.7 %collective-permute-start.3 = (bf16[2,2,14,16,256]{4,3,2,1,0:T(8,128)(2,1)S(1)}, bf16[2,2,14,16,256]{4,3,2,1,0:T(8,128)(2,1)S(1)}, u32[]{:S(2)}, u32[]{:S(2)}) collective-permute-start(bf16[2,2,14,16,256]{4,3,2,1,0:T(8,128)(2,1)S(1)} %pad_maximum_fusion.refs_0_), channel_id=1, source_target_pairs={{0,32},{32,64},{64,96},{1,33},{33,65},{65,97},{2,34},{34,66},{66,9... | collective-permute-start | bytes 1376264 | tf_op jit(solution)/shard_map/ppermute | solution.py:489
  65.6 17.4 %collective-permute-start.4 = (bf16[2,2,14,16,256]{4,3,2,1,0:T(8,128)(2,1)S(1)}, bf16[2,2,14,16,256]{4,3,2,1,0:T(8,128)(2,1)S(1)}, u32[]{:S(2)}, u32[]{:S(2)}) collective-permute-start(bf16[2,2,14,16,256]{4,3,2,1,0:T(8,128)(2,1)S(1)} %pad_maximum_fusion.refs_0_), channel_id=1, source_target_pairs={{0,64},{96,32},{1,65},{97,33},{2,66},{98,34},{3,67},{99,35},{4,68}... | collective-permute-start | bytes 1376264 | tf_op jit(solution)/shard_map/ppermute | solution.py:489
  70.2 13.6 %collective-permute-start.5 = (bf16[2,2,14,16,256]{4,3,2,1,0:T(8,128)(2,1)S(1)}, bf16[2,2,14,16,256]{4,3,2,1,0:T(8,128)(2,1)S(1)}, u32[]{:S(2)}, u32[]{:S(2)}) collective-permute-start(bf16[2,2,14,16,256]{4,3,2,1,0:T(8,128)(2,1)S(1)} %pad_maximum_fusion.refs_0_), channel_id=1, source_target_pairs={{32,0},{64,32},{96,64},{33,1},{65,33},{97,65},{34,2},{66,34},{98,6... | collective-permute-start | bytes 1376264 | tf_op jit(solution)/shard_map/ppermute | solution.py:489
  83.0 0.8 copy-start.1
  83.8 0.8 copy-start.3
  87.0 1.0 copy-start.2
  88.0 1.0 copy-start.4
  90.7 3.3 %collective-permute-start.6 = (bf16[14,16,256]{2,1,0:T(8,128)(2,1)S(1)}, bf16[14,16,256]{2,1,0:T(8,128)(2,1)S(1)}, u32[]{:S(2)}, u32[]{:S(2)}) collective-permute-start(bf16[14,16,256]{2,1,0:T(8,128)(2,1)S(1)} %get-tuple-element.30), channel_id=1, source_target_pairs={{0,1},{1,0},{2,3},{3,2},{4,5},{5,4},{6,7},{7,6},{8,9},{9,8},{10,11... | collective-permute-start | bytes 344072 | tf_op jit(solution)/shard_map/ppermute | solution.py:502
  94.1 6.1 %collective-permute-start.7 = (bf16[2,7,16,256]{3,2,1,0:T(8,128)(2,1)S(1)}, bf16[2,7,16,256]{3,2,1,0:T(8,128)(2,1)S(1)}, u32[]{:S(2)}, u32[]{:S(2)}) collective-permute-start(bf16[2,7,16,256]{3,2,1,0:T(8,128)(2,1)S(1)} %get-tuple-element.51), channel_id=1, source_target_pairs={{0,4},{4,8},{8,12},{12,0},{1,5},{5,9},{9,13},{13,1},{2,6},{6,10},{... | collective-permute-start | bytes 344072 | tf_op jit(solution)/shard_map/ppermute | solution.py:108
  94.2 7.6 %collective-permute-start.8 = (bf16[2,7,16,256]{3,2,1,0:T(8,128)(2,1)S(1)}, bf16[2,7,16,256]{3,2,1,0:T(8,128)(2,1)S(1)}, u32[]{:S(2)}, u32[]{:S(2)}) collective-permute-start(bf16[2,7,16,256]{3,2,1,0:T(8,128)(2,1)S(1)} %get-tuple-element.51), channel_id=1, source_target_pairs={{0,8},{4,12},{8,0},{12,4},{1,9},{5,13},{9,1},{13,5},{2,10},{6,14},... | collective-permute-start | bytes 344072 | tf_op jit(solution)/shard_map/ppermute | solution.py:108
  96.4 6.1 %collective-permute-start.9 = (bf16[2,7,16,256]{3,2,1,0:T(8,128)(2,1)S(1)}, bf16[2,7,16,256]{3,2,1,0:T(8,128)(2,1)S(1)}, u32[]{:S(2)}, u32[]{:S(2)}) collective-permute-start(bf16[2,7,16,256]{3,2,1,0:T(8,128)(2,1)S(1)} %get-tuple-element.51), channel_id=1, source_target_pairs={{0,12},{4,0},{8,4},{12,8},{1,13},{5,1},{9,5},{13,9},{2,14},{6,2},{... | collective-permute-start | bytes 344072 | tf_op jit(solution)/shard_map/ppermute | solution.py:108
  97.6 5.5 %collective-permute-start.11 = (bf16[2,7,16,256]{3,2,1,0:T(8,128)(2,1)S(1)}, bf16[2,7,16,256]{3,2,1,0:T(8,128)(2,1)S(1)}, u32[]{:S(2)}, u32[]{:S(2)}) collective-permute-start(bf16[2,7,16,256]{3,2,1,0:T(8,128)(2,1)S(1)} %get-tuple-element.45), channel_id=1, source_target_pairs={{0,2},{2,0},{1,3},{3,1},{4,6},{6,4},{5,7},{7,5},{8,10},{10,8},{9,1... | collective-permute-start | bytes 344072 | tf_op jit(solution)/shard_map/ppermute | solution.py:108
  102.5 14.5 %collective-permute-start.10 = (bf16[4,2,7,16,256]{4,3,2,1,0:T(8,128)(2,1)S(1)}, bf16[4,2,7,16,256]{4,3,2,1,0:T(8,128)(2,1)S(1)}, u32[]{:S(2)}, u32[]{:S(2)}) collective-permute-start(bf16[4,2,7,16,256]{4,3,2,1,0:T(8,128)(2,1)S(1)} %pad_maximum_fusion.1.refs_0_), channel_id=1, source_target_pairs={{0,2},{2,0},{1,3},{3,1},{4,6},{6,4},{5,7},{7,5},{8,10},{10,8},{9,1... | collective-permute-start | bytes 1376264 | tf_op jit(solution)/shard_map/ppermute | solution.py:108
  103.1 7.1 %collective-permute-start.12 = (bf16[2,2,7,16,256]{4,3,2,1,0:T(8,128)(2,1)S(1)}, bf16[2,2,7,16,256]{4,3,2,1,0:T(8,128)(2,1)S(1)}, u32[]{:S(2)}, u32[]{:S(2)}) collective-permute-start(bf16[2,2,7,16,256]{4,3,2,1,0:T(8,128)(2,1)S(1)} %pad_maximum_fusion.2.refs_2_), channel_id=1, source_target_pairs={{0,4},{4,8},{8,12},{12,0},{1,5},{5,9},{9,13},{13,1},{2,6},{6,10},{... | collective-permute-start | bytes 688136 | tf_op jit(solution)/shard_map/ppermute | solution.py:108
  104.2 12.8 %collective-permute-start.13 = (bf16[2,2,7,16,256]{4,3,2,1,0:T(8,128)(2,1)S(1)}, bf16[2,2,7,16,256]{4,3,2,1,0:T(8,128)(2,1)S(1)}, u32[]{:S(2)}, u32[]{:S(2)}) collective-permute-start(bf16[2,2,7,16,256]{4,3,2,1,0:T(8,128)(2,1)S(1)} %pad_maximum_fusion.2.refs_2_), channel_id=1, source_target_pairs={{0,8},{4,12},{8,0},{12,4},{1,9},{5,13},{9,1},{13,5},{2,10},{6,14},... | collective-permute-start | bytes 688136 | tf_op jit(solution)/shard_map/ppermute | solution.py:108
  107.2 9.9 %collective-permute-start.14 = (bf16[2,2,7,16,256]{4,3,2,1,0:T(8,128)(2,1)S(1)}, bf16[2,2,7,16,256]{4,3,2,1,0:T(8,128)(2,1)S(1)}, u32[]{:S(2)}, u32[]{:S(2)}) collective-permute-start(bf16[2,2,7,16,256]{4,3,2,1,0:T(8,128)(2,1)S(1)} %pad_maximum_fusion.2.refs_2_), channel_id=1, source_target_pairs={{0,12},{4,0},{8,4},{12,8},{1,13},{5,1},{9,5},{13,9},{2,14},{6,2},{... | collective-permute-start | bytes 688136 | tf_op jit(solution)/shard_map/ppermute | solution.py:108
  125.9 8.2 %copy-start.5 = (f32[2,448,512]{2,1,0:T(8,128)S(1)}, f32[2,448,512]{2,1,0:T(8,128)}, u32[]{:S(2)}) copy-start(f32[2,448,512]{2,1,0:T(8,128)} %get-tuple-element.31.a_ref) | copy-start | bytes 5505028
  128.7 20.0 %all-to-all-start.2 = ((f16[8,2,56,512]{3,2,1,0:T(8,128)(2,1)}), f16[8,2,56,512]{3,2,1,0:T(8,128)(2,1)S(1)}, u32[]{:S(2)}, u32[]{:S(2)}) async-start(f16[8,2,56,512]{3,2,1,0:T(8,128)(2,1)} %convert_element_type.27), calls=%async_computation.2 | async-start | bytes 1835008 | tf_op jit(solution)/shard_map/all_to_all | solution.py:516
  147.4 1.3 copy-start.8
  148.7 1.2 copy-start.10
  149.9 24.8 %all-to-all-start.3 = ((f16[8,2,56,512]{3,2,1,0:T(8,128)(2,1)}), f16[8,2,56,512]{3,2,1,0:T(8,128)(2,1)S(1)}, u32[]{:S(2)}, u32[]{:S(2)}) async-start(f16[8,2,56,512]{3,2,1,0:T(8,128)(2,1)} %broadcast_in_dim.28), calls=%async_computation.3 | async-start | bytes 1835008 | tf_op jit(solution)/shard_map/all_to_all | solution.py:519
  155.8 1.5 copy-start.9
  177.7 2.7 %collective-permute-start.15 = (f32[2,84,448]{2,1,0:T(8,128)S(1)}, f32[2,84,448]{2,1,0:T(8,128)S(1)}, u32[]{:S(2)}, u32[]{:S(2)}) collective-permute-start(f32[2,84,448]{2,1,0:T(8,128)S(1)} %get-tuple-element.35), channel_id=1, source_target_pairs={{0,1},{1,0},{2,3},{3,2},{4,5},{5,4},{6,7},{7,6},{8,9},{9,8},{10,11... | collective-permute-start | bytes 903176 | tf_op jit(solution)/shard_map/ppermute | solution.py:522

commit v5 on v4

--- a/solution.py
+++ b/solution.py
@@ -43,21 +43,21 @@
     sent_ref[0] = jnp.where(first, high, low)
 
 
-def probe(at, a, b, half):
+def probe(at, a, b, half, tall):
     count, rows, depth = a.shape
     probes = b.shape[1]
     part = jax.ShapeDtypeStruct((count, rows, half), F32)
     return pl.pallas_call(
         probe_kernel,
-        grid=(count, rows // LEAF),
+        grid=(count, rows // tall),
         out_shape=[part, part],
         in_specs=[
             SMEM,
-            pl.BlockSpec((1, LEAF, depth), lambda k, i: (k, i, 0)),
+            pl.BlockSpec((1, tall, depth), lambda k, i: (k, i, 0)),
             pl.BlockSpec((1, probes, depth), lambda k, i: (k, 0, 0)),
         ],
-        out_specs=[pl.BlockSpec((1, LEAF, half), lambda k, i: (k, i, 0))] * 2,
-        compiler_params=params(40),
+        out_specs=[pl.BlockSpec((1, tall, half), lambda k, i: (k, i, 0))] * 2,
+        compiler_params=params(56),
         cost_estimate=cost(4 * count * rows * depth * half, 2 * a.size + 8 * count * rows * half),
     )(at, a, b)
 
@@ -98,7 +98,7 @@
             pl.BlockSpec((blocks, slab, half), lambda k, i: (k * per + i, 0, 0)),
         ],
         scratch_shapes=[pltpu.VMEM((LEAF, half), F32)],
-        compiler_params=params(24),
+        compiler_params=params(56),
         cost_estimate=cost(kept.size, 10 * kept.size),
     )(at, kept, received)
 
@@ -143,7 +143,7 @@
             pl.BlockSpec((step, slab, half), lambda i: (i, 0, 0)),
         ],
         out_specs=pl.BlockSpec((step, slab, half), lambda i: (i, 0, 0)),
-        compiler_params=params(16),
+        compiler_params=params(56),
         cost_estimate=cost(shares.size, 2 * shares.size),
     )(at, shares, own)
 
@@ -243,7 +243,7 @@
 
     here = t_ref[step]
     there = y_ref[pl.ds((1 - step) * per, per)].reshape(LEAF, wide)
-    hi, lo = halves(jnp.dot(f_ref[...], there, preferred_element_type=F32) / root_ref[1 - step])
+    hi, lo = halves(jnp.dot(f_ref[...], there, preferred_element_type=F32) * (1.0 / root_ref[1 - step]))
     cross = contract(here, hi, 1, 0) + contract(here, lo, 1, 0)
     square = jnp.sum(jnp.where(row == col, gram_ref[step], 0.0), axis=1, keepdims=True)
     cross = cross * lax.rsqrt(square)
@@ -321,10 +321,10 @@
                 for k in range(m + 1, 8):
                     scaled[m] = scaled[m] - low[k, m] * scaled[k]
             for i in range(g + 1, groups):
-                new = rows[i]
-                for k in range(8):
-                    new = new - c[i, k] * scaled[k]
-                rows[i] = new
+                terms = [c[i, k] * scaled[k] for k in range(8)]
+                while len(terms) > 1:
+                    terms = [a + b for a, b in zip(terms[::2], terms[1::2])]
+                rows[i] = rows[i] - terms[0]
             new = pivot[0]
             for k in range(1, 8):
                 new = jnp.where(sub == k, pivot[k], new)
@@ -412,7 +412,7 @@
             pltpu.VMEM((leaves, STEP, STEP), F32),
             pltpu.VMEM((leaves, STEP, 128), F32),
         ],
-        compiler_params=params(24),
+        compiler_params=params(56),
         cost_estimate=cost((last - first) * 5.5e9, 8 * work.size),
     )(work, after)
 
@@ -471,9 +471,9 @@
     swap = [(0, 1), (1, 0)]
 
     at = jnp.stack([x, zl, core]).astype(jnp.int32)
-    kid_sent, kid_kept = probe(at, child_update, jnp.swapaxes(child_test, 1, 2), half)
+    kid_sent, kid_kept = probe(at, child_update, jnp.swapaxes(child_test, 1, 2), half, 2 * LEAF)
     kid_sent = lax.ppermute(kid_sent, "core", swap)
-    own_sent, own_kept = probe(at, parent_front[None], parent_test.T[None], half)
+    own_sent, own_kept = probe(at, parent_front[None], parent_test.T[None], half, LEAF)
     own_sent = lax.ppermute(own_sent, "core", swap)
     kid_part, kid_rest = pack(at, kid_kept, kid_sent, chips)
     kid_share = lax.all_to_all(kid_part, CHIP, 0, 0, tiled=True)
@@ -481,7 +481,6 @@
 
     kids = sum_shares(at, kid_share, kid_rest, BF).reshape(2, kid_blocks, -1, half)
     pair = ring_pieces(kids, "zh")
-    pair[1], own_part = lax.optimization_barrier((pair[1], own_part))
     pair = jnp.stack(pair)
     own_share = lax.all_to_all(own_part, CHIP, 0, 0, tiled=True)
     reach = [(0, 1), (0, 2), (1, 0), (1, 2), (2, 1), (2, 3), (3, 1), (3, 2)]

time: 186 us -> 220 us (1.18)
  waiting for transfers between devices: 31.1 us -> 73.4 us
  blocking collectives: 28.4 us -> 0 us
  Pallas kernels: 63.7 us -> 82.2 us
  starting transfers between devices: 41.7 us -> 48.1 us
  local copies, waits for them, and re-layouts: 11.8 us -> 7.09 us
    all_to_all x1 -> x0, blocking collectives: 28.4 us -> none  [local(): kid_share = lax.all_to_all(kid_part, CHIP, 0, 0, tiled=True)]
    all_to_all x0 -> x1, waiting for transfers between devices: none -> 21.8 us  [local(): kid_share = lax.all_to_all(kid_part, CHIP, 0, 0, tiled=True)]
    ppermute x9, waiting for transfers between devices: 14.9 us -> 34.5 us  [shift(): lax.ppermute(value, axis, [(i, (i + by) % size) for i in range(size)])]
    pallas_call x2, Pallas kernels: 2.58 us -> 10.2 us  [pack(): pl.pallas_call(pack_kernel, grid=(count, per), out_shape=[jax.ShapeDtypeS...]
    all_to_all x0 -> x1, starting transfers between devices: none -> 5.46 us  [local(): kid_share = lax.all_to_all(kid_part, CHIP, 0, 0, tiled=True)]
    unnamed x25 -> x15, local copies, waits for them, and re-layouts: 9.95 us -> 5.29 us
    pallas_call x2, Pallas kernels: 15.9 us -> 20.2 us  [probe(): pl.pallas_call(probe_kernel, grid=(count, rows // tall), out_shape=[part,...]
    pallas_call x2, Pallas kernels: 30.8 us -> 34.5 us  [factor_inverse(): pl.pallas_call(functools.partial(inverse_kernel, first=first, last=last),...]
  transfers between devices with their start and end apart: 19 -> 20, of which waited for: 11 -> 12; matrix products, arithmetic and copies ran while one was open for 1% -> 1% of each run, Pallas kernels for 24% -> 28%
where the time goes in v5:
time: 220 us; the launch traced here: 218 us
  Pallas kernels  82.2 us (37%)
  waiting for transfers between devices  73.4 us (33%)
  starting transfers between devices  48.1 us (22%)
  local copies, waits for them, and re-layouts  7.09 us (3%)
  other arithmetic  6.54 us (3%)
    ppermute x9, waiting for transfers between devices, shift(): lax.ppermute(value, axis, [(i, (i + by) % size) for i in range(size)])  34.5 us
    pallas_call x2, Pallas kernels, factor_inverse(): pl.pallas_call(functools.partial(inverse_kernel, first=first, last=last),...  34.5 us
    all_to_all x1, waiting for transfers between devices, local(): kid_share = lax.all_to_all(kid_part, CHIP, 0, 0, tiled=True)  21.8 us
    pallas_call x2, Pallas kernels, probe(): pl.pallas_call(probe_kernel, grid=(count, rows // tall), out_shape=[part,...  20.2 us
    ppermute x3, waiting for transfers between devices, local(): lax.ppermute(pair, 'y', [(i, j) for i, j in reach if (j - i) % 4 == by])  14.9 us
    ppermute x9, starting transfers between devices, shift(): lax.ppermute(value, axis, [(i, (i + by) % size) for i in range(size)])  14.2 us
    pallas_call x2, Pallas kernels, pack(): pl.pallas_call(pack_kernel, grid=(count, per), out_shape=[jax.ShapeDtypeS...  10.2 us
    ppermute x3, starting transfers between devices, local(): lax.ppermute(pair, 'y', [(i, j) for i, j in reach if (j - i) % 4 == by])  9.72 us
  transfers between devices with their start and end apart: 20, of which 12 were waited for; matrix products, arithmetic and copies ran while one was open for 1% of the time, Pallas kernels for 28%

profile of v5, /device:TPU:1, one launch (start us, length us, event | category | flops | bytes accessed | tf_op | source)
XLA Modules:
  0.0 218.2 jit_solution(6595833761609047665)
XLA Ops:
  0.6 0.6 pad_add_fusion.1.at_ref
  1.3 8.2 %shard_map.70 = (f32[2,1792,256]{2,1,0:T(8,128)}, f32[2,1792,256]{2,1,0:T(8,128)}) custom-call(s32[3]{0:T(128)} %pad_add_fusion.1.at_ref, bf16[2,1792,896]{2,1,0:T(8,128)(2,1)} %a_ref.1, bf16[2,448,896]{2,1,0:T(8,128)(2,1)} %bitcast.62), custom_call_target="tpu_custom_call" | custom-call | flops 3288334336 | bytes 13762560 | tf_op jit(solution)/shard_map/pallas_call | solution.py:50
  9.5 1.4 collective-permute-start.1
  10.9 12.0 %shard_map.68 = (f32[1,3584,256]{2,1,0:T(8,128)}, f32[1,3584,256]{2,1,0:T(8,128)}) custom-call(s32[3]{0:T(128)} %pad_add_fusion.1.at_ref, bf16[1,3584,1792]{2,1,0:T(8,128)(2,1)} %bitcast.49, bf16[1,448,1792]{2,1,0:T(8,128)(2,1)} %bitcast.63), custom_call_target="tpu_custom_call" | custom-call | flops 6576668672 | bytes 20185088 | tf_op jit(solution)/shard_map/pallas_call | solution.py:50
  22.9 1.8 copy-done.5
  24.7 5.1 %shard_map.71 = (bf16[8,28,16,256]{3,2,1,0:T(8,128)(2,1)}, f32[28,16,256]{2,1,0:T(8,128)}) custom-call(s32[3]{0:T(128)} %pad_add_fusion.1.at_ref, f32[2,1792,256]{2,1,0:T(8,128)} %get-tuple-element.21.a_ref, f32[2,1792,256]{2,1,0:T(8,128)} %copy-done.5), custom_call_target="tpu_custom_call" | custom-call | flops 917504 | bytes 9175040 | tf_op jit(solution)/shard_map/pallas_call | solution.py:84
  29.8 5.5 %all-to-all-start.1 = ((bf16[8,28,16,256]{3,2,1,0:T(8,128)(2,1)}), bf16[8,28,16,256]{3,2,1,0:T(8,128)(2,1)S(1)}, u32[]{:S(2)}, u32[]{:S(2)}) async-start(bf16[8,28,16,256]{3,2,1,0:T(8,128)(2,1)} %get-tuple-element.23), calls=%async_computation.1 | async-start | bytes 3670016 | tf_op jit(solution)/shard_map/all_to_all | solution.py:479
  35.3 5.1 %shard_map.69 = (bf16[8,28,16,256]{3,2,1,0:T(8,128)(2,1)}, f32[28,16,256]{2,1,0:T(8,128)}) custom-call(s32[3]{0:T(128)} %pad_add_fusion.1.at_ref, f32[1,3584,256]{2,1,0:T(8,128)} %get-tuple-element.17.a_ref, f32[1,3584,256]{2,1,0:T(8,128)} %collective-permute-done.b_ref), custom_call_target="tpu_custom_call" | custom-call | flops 917504 | bytes 9175040 | tf_op jit(solution)/shard_map/pallas_call | solution.py:84
  40.4 21.8 %all-to-all-done.1.k_ref = bf16[8,28,16,256]{3,2,1,0:T(8,128)(2,1)S(1)} async-done(((bf16[8,28,16,256]{3,2,1,0:T(8,128)(2,1)}), bf16[8,28,16,256]{3,2,1,0:T(8,128)(2,1)S(1)}, u32[]{:S(2)}, u32[]{:S(2)}) %all-to-all-start.1) | async-done | bytes 1835040 | tf_op jit(solution)/shard_map/all_to_all | solution.py:479
  62.2 1.2 copy-done.4
  63.4 3.6 %all-to-all-start = ((bf16[8,28,16,256]{3,2,1,0:T(8,128)(2,1)}), bf16[8,28,16,256]{3,2,1,0:T(8,128)(2,1)S(1)}, u32[]{:S(2)}, u32[]{:S(2)}) async-start(bf16[8,28,16,256]{3,2,1,0:T(8,128)(2,1)} %get-tuple-element.19), calls=%async_computation | async-start | bytes 3670016 | tf_op jit(solution)/shard_map/all_to_all | solution.py:485
  67.3 3.6 %shard_map.72 = bf16[28,16,256]{2,1,0:T(8,128)(2,1)} custom-call(s32[3]{0:T(128)} %pad_add_fusion.1.at_ref, bf16[8,28,16,256]{3,2,1,0:T(8,128)(2,1)} %copy-done.4, f32[28,16,256]{2,1,0:T(8,128)} %get-tuple-element.24.own_ref), custom_call_target="tpu_custom_call" | custom-call | flops 917504 | bytes 1835008 | tf_op jit(solution)/shard_map/pallas_call | solution.py:136
  70.9 3.3 %collective-permute-start.2 = (bf16[2,14,16,256]{3,2,1,0:T(8,128)(2,1)}, bf16[2,14,16,256]{3,2,1,0:T(8,128)(2,1)S(1)}, u32[]{:S(2)}, u32[]{:S(2)}) collective-permute-start(bf16[2,14,16,256]{3,2,1,0:T(8,128)(2,1)} %bitcast.50), channel_id=1, source_target_pairs={{0,16},{16,0},{1,17},{17,1},{2,18},{18,2},{3,19},{19,3},{4,20},{20... | collective-permute-start | bytes 688136 | tf_op jit(solution)/shard_map/ppermute | solution.py:108
  74.4 20.7 %collective-permute-done.2 = bf16[2,14,16,256]{3,2,1,0:T(8,128)(2,1)S(1)} collective-permute-done((bf16[2,14,16,256]{3,2,1,0:T(8,128)(2,1)}, bf16[2,14,16,256]{3,2,1,0:T(8,128)(2,1)S(1)}, u32[]{:S(2)}, u32[]{:S(2)}) %collective-permute-start.2) | collective-permute-done | bytes 229408 | tf_op jit(solution)/shard_map/ppermute | solution.py:108
  95.1 1.0 pad_maximum_fusion.refs_0_
  96.1 1.3 collective-permute-start.5
  97.4 6.4 %collective-permute-start.4 = (bf16[2,2,14,16,256]{4,3,2,1,0:T(8,128)(2,1)S(1)}, bf16[2,2,14,16,256]{4,3,2,1,0:T(8,128)(2,1)}, u32[]{:S(2)}, u32[]{:S(2)}) collective-permute-start(bf16[2,2,14,16,256]{4,3,2,1,0:T(8,128)(2,1)S(1)} %pad_maximum_fusion.refs_0_), channel_id=1, source_target_pairs={{0,64},{96,32},{1,65},{97,33},{2,66},{98,34},{3,67},{99,35},{4,68}... | collective-permute-start | bytes 1376264 | tf_op jit(solution)/shard_map/ppermute | solution.py:488
  103.7 2.1 collective-permute-start.3
  105.9 2.4 %collective-permute-done.5.refs_3_ = bf16[2,2,14,16,256]{4,3,2,1,0:T(8,128)(2,1)S(1)} collective-permute-done((bf16[2,2,14,16,256]{4,3,2,1,0:T(8,128)(2,1)S(1)}, bf16[2,2,14,16,256]{4,3,2,1,0:T(8,128)(2,1)S(1)}, u32[]{:S(2)}, u32[]{:S(2)}) %collective-permute-start.5) | collective-permute-done | bytes 458784 | tf_op jit(solution)/shard_map/ppermute | solution.py:488
  108.3 2.6 %collective-permute-done.4.refs_2_ = bf16[2,2,14,16,256]{4,3,2,1,0:T(8,128)(2,1)} collective-permute-done((bf16[2,2,14,16,256]{4,3,2,1,0:T(8,128)(2,1)S(1)}, bf16[2,2,14,16,256]{4,3,2,1,0:T(8,128)(2,1)}, u32[]{:S(2)}, u32[]{:S(2)}) %collective-permute-start.4) | collective-permute-done | bytes 458784 | tf_op jit(solution)/shard_map/ppermute | solution.py:488
  110.9 9.8 %collective-permute-done.3.refs_1_ = bf16[2,2,14,16,256]{4,3,2,1,0:T(8,128)(2,1)} collective-permute-done((bf16[2,2,14,16,256]{4,3,2,1,0:T(8,128)(2,1)S(1)}, bf16[2,2,14,16,256]{4,3,2,1,0:T(8,128)(2,1)}, u32[]{:S(2)}, u32[]{:S(2)}) %collective-permute-start.3) | collective-permute-done | bytes 458784 | tf_op jit(solution)/shard_map/ppermute | solution.py:488
  120.7 2.2 %shard_map.73 = (bf16[14,16,256]{2,1,0:T(8,128)(2,1)S(1)}, bf16[14,16,256]{2,1,0:T(8,128)(2,1)S(1)}) custom-call(s32[3]{0:T(128)S(1)} %copy-done.2, s32[2,4,28]{2,1,0:T(4,128)S(1)} %pad_add_fusion.from_ref, bf16[8,28,16,256]{3,2,1,0:T(8,128)(2,1)S(1)} %all-to-all-done.p_ref, f32[28,16,256]{2,1,0:T(8,128)S(1)} %copy-done, ...), custom_call_target="tpu_custom_call" | custom-call | flops 917504 | bytes 5505024 | tf_op jit(solution)/shard_map/pallas_call | solution.py:178
  123.0 2.9 %collective-permute-start.6 = (bf16[14,16,256]{2,1,0:T(8,128)(2,1)S(1)}, bf16[14,16,256]{2,1,0:T(8,128)(2,1)S(1)}, u32[]{:S(2)}, u32[]{:S(2)}) collective-permute-start(bf16[14,16,256]{2,1,0:T(8,128)(2,1)S(1)} %get-tuple-element.26), channel_id=1, source_target_pairs={{0,1},{1,0},{2,3},{3,2},{4,5},{5,4},{6,7},{7,6},{8,9},{9,8},{10,11... | collective-permute-start | bytes 344072 | tf_op jit(solution)/shard_map/ppermute | solution.py:501
  125.9 1.0 collective-permute-done.6
  126.9 4.1 %collective-permute-start.8 = (bf16[2,7,16,256]{3,2,1,0:T(8,128)(2,1)S(1)}, bf16[2,7,16,256]{3,2,1,0:T(8,128)(2,1)S(1)}, u32[]{:S(2)}, u32[]{:S(2)}) collective-permute-start(bf16[2,7,16,256]{3,2,1,0:T(8,128)(2,1)S(1)} %get-tuple-element.47), channel_id=1, source_target_pairs={{0,8},{4,12},{8,0},{12,4},{1,9},{5,13},{9,1},{13,5},{2,10},{6,14},... | collective-permute-start | bytes 344072 | tf_op jit(solution)/shard_map/ppermute | solution.py:108
  131.1 2.6 %collective-permute-start.9 = (bf16[2,7,16,256]{3,2,1,0:T(8,128)(2,1)S(1)}, bf16[2,7,16,256]{3,2,1,0:T(8,128)(2,1)S(1)}, u32[]{:S(2)}, u32[]{:S(2)}) collective-permute-start(bf16[2,7,16,256]{3,2,1,0:T(8,128)(2,1)S(1)} %get-tuple-element.47), channel_id=1, source_target_pairs={{0,12},{4,0},{8,4},{12,8},{1,13},{5,1},{9,5},{13,9},{2,14},{6,2},{... | collective-permute-start | bytes 344072 | tf_op jit(solution)/shard_map/ppermute | solution.py:108
  133.7 0.6 collective-permute-start.11
  134.3 2.2 %collective-permute-done.7 = bf16[2,7,16,256]{3,2,1,0:T(8,128)(2,1)S(1)} collective-permute-done((bf16[2,7,16,256]{3,2,1,0:T(8,128)(2,1)S(1)}, bf16[2,7,16,256]{3,2,1,0:T(8,128)(2,1)S(1)}, u32[]{:S(2)}, u32[]{:S(2)}) %collective-permute-start.7) | collective-permute-done | bytes 114720 | tf_op jit(solution)/shard_map/ppermute | solution.py:108
  137.5 1.8 collective-permute-start.14
  139.3 1.1 collective-permute-start.13
  140.4 0.8 maximum_select_fusion.1.after_ref.own_ref
  141.2 1.7 collective-permute-done.14.refs_5_
  142.9 2.8 %collective-permute-done.13.refs_4_ = bf16[2,2,7,16,256]{4,3,2,1,0:T(8,128)(2,1)S(1)} collective-permute-done((bf16[2,2,7,16,256]{4,3,2,1,0:T(8,128)(2,1)S(1)}, bf16[2,2,7,16,256]{4,3,2,1,0:T(8,128)(2,1)S(1)}, u32[]{:S(2)}, u32[]{:S(2)}) %collective-permute-start.13) | collective-permute-done | bytes 229408 | tf_op jit(solution)/shard_map/ppermute | solution.py:108
  145.8 6.7 %collective-permute-done.12.refs_3_ = bf16[2,2,7,16,256]{4,3,2,1,0:T(8,128)(2,1)S(1)} collective-permute-done((bf16[2,2,7,16,256]{4,3,2,1,0:T(8,128)(2,1)S(1)}, bf16[2,2,7,16,256]{4,3,2,1,0:T(8,128)(2,1)S(1)}, u32[]{:S(2)}, u32[]{:S(2)}) %collective-permute-start.12) | collective-permute-done | bytes 229408 | tf_op jit(solution)/shard_map/ppermute | solution.py:108
  152.5 8.8 %shard_map.74 = (f32[2,448,512]{2,1,0:T(8,128)}, f32[2,1,512]{2,1,0:T(1,128)S(1)}, f32[8,2,56,512]{3,2,1,0:T(8,128)}) custom-call(s32[3]{0:T(128)S(1)} %copy-done.2, bf16[3584,1792]{1,0:T(8,128)(2,1)} %f_ref.1, bf16[4,2,7,16,256]{4,3,2,1,0:T(8,128)(2,1)S(1)} %pad_maximum_fusion.1.refs_0_, bf16[4,2,7,16,256]{4,3,2,1,0:T(8,128)(2,1)S(1)} %collective-permute-done.10.refs_1_, ...), custom_call_target="tpu_custom_call" | custom-call | flops 3758096384 | bytes 6881280 | tf_op jit(solution)/shard_map/pallas_call | solution.py:259
  161.3 2.7 %convert_element_type.27 = f16[8,2,56,512]{3,2,1,0:T(8,128)(2,1)} convert(f32[8,2,56,512]{3,2,1,0:T(8,128)} %get-tuple-element.28) | non-fusion elementwise | flops 458752 | bytes 2752512 | tf_op jit(solution)/shard_map/convert_element_type | solution.py:515
  163.9 4.2 %all-to-all-start.2 = ((f16[8,2,56,512]{3,2,1,0:T(8,128)(2,1)}), f16[8,2,56,512]{3,2,1,0:T(8,128)(2,1)S(1)}, u32[]{:S(2)}, u32[]{:S(2)}) async-start(f16[8,2,56,512]{3,2,1,0:T(8,128)(2,1)} %convert_element_type.27), calls=%async_computation.2 | async-start | bytes 1835008 | tf_op jit(solution)/shard_map/all_to_all | solution.py:515
  168.2 15.2 %shard_map.75.a_ref = f32[2,448,512]{2,1,0:T(8,128)} custom-call(f32[2,448,512]{2,1,0:T(8,128)} %get-tuple-element.27.a_ref, bf16[2,112,512]{2,1,0:T(8,128)(2,1)} %maximum_select_fusion.1.after_ref.own_ref), custom_call_target="tpu_custom_call" | custom-call | flops 16499999744 | bytes 3670016 | tf_op jit(solution)/shard_map/pallas_call | solution.py:405
  183.4 1.0 broadcast_in_dim.28
  184.5 5.1 %all-to-all-start.3 = ((f16[8,2,56,512]{3,2,1,0:T(8,128)(2,1)}), f16[8,2,56,512]{3,2,1,0:T(8,128)(2,1)S(1)}, u32[]{:S(2)}, u32[]{:S(2)}) async-start(f16[8,2,56,512]{3,2,1,0:T(8,128)(2,1)} %broadcast_in_dim.28), calls=%async_computation.3 | async-start | bytes 1835008 | tf_op jit(solution)/shard_map/all_to_all | solution.py:518
  190.2 19.3 %shard_map.76.w_ref = f32[2,448,512]{2,1,0:T(8,128)} custom-call(f32[2,448,512]{2,1,0:T(8,128)} %shard_map.75.a_ref, f32[8,128]{1,0:T(8,128)} %fusion.2.after_ref), custom_call_target="tpu_custom_call" | custom-call | flops 22000001024 | bytes 3670016 | tf_op jit(solution)/shard_map/pallas_call | solution.py:405
  209.7 0.7 copy-done.1
  210.4 0.7 copy-done.3
  211.1 2.7 %shard_map.77 = (f32[2,84,448]{2,1,0:T(8,128)S(1)}, f32[2,84,448]{2,1,0:T(8,128)S(1)}) custom-call(s32[3]{0:T(128)S(1)} %copy-done.2, f32[2,448,512]{2,1,0:T(8,128)S(1)} %copy-done.3, f32[2,1,512]{2,1,0:T(1,128)S(1)} %get-tuple-element.29.root_ref, bf16[2,112,512]{2,1,0:T(8,128)(2,1)S(1)} %copy-done.1, f32[8,2,56,512]{3,2,1,0:T(8,128)S(1)} %convert_element_type.30.cross_ref), custom_call_target="tpu_custom_call" | custom-call | flops 2000000000 | bytes 3670016 | tf_op jit(solution)/shard_map/pallas_call | solution.py:451
  213.8 1.4 collective-permute-start.15
  215.3 1.3 collective-permute-done.15
  216.7 0.7 slice.38
  217.4 0.8 copy.41
  (43 shorter events, 2.5 us)
Async XLA Ops:
  9.5 13.4 %collective-permute-start.1 = (f32[2,1792,256]{2,1,0:T(8,128)}, f32[2,1792,256]{2,1,0:T(8,128)S(1)}, u32[]{:S(2)}, u32[]{:S(2)}) collective-permute-start(f32[2,1792,256]{2,1,0:T(8,128)} %get-tuple-element.22), channel_id=1, source_target_pairs={{0,1},{1,0},{2,3},{3,2},{4,5},{5,4},{6,7},{7,6},{8,9},{9,8},{10,11... | collective-permute-start | bytes 11010056 | tf_op jit(solution)/shard_map/ppermute | solution.py:475
  22.9 12.4 %collective-permute-start = (f32[1,3584,256]{2,1,0:T(8,128)}, f32[1,3584,256]{2,1,0:T(8,128)}, u32[]{:S(2)}, u32[]{:S(2)}) collective-permute-start(f32[1,3584,256]{2,1,0:T(8,128)} %get-tuple-element.18), channel_id=1, source_target_pairs={{0,1},{1,0},{2,3},{3,2},{4,5},{5,4},{6,7},{7,6},{8,9},{9,8},{10,11... | collective-permute-start | bytes 11010056 | tf_op jit(solution)/shard_map/ppermute | solution.py:477
  22.9 1.8 copy-start.5
  29.8 32.4 %all-to-all-start.1 = ((bf16[8,28,16,256]{3,2,1,0:T(8,128)(2,1)}), bf16[8,28,16,256]{3,2,1,0:T(8,128)(2,1)S(1)}, u32[]{:S(2)}, u32[]{:S(2)}) async-start(bf16[8,28,16,256]{3,2,1,0:T(8,128)(2,1)} %get-tuple-element.23), calls=%async_computation.1 | async-start | bytes 3670016 | tf_op jit(solution)/shard_map/all_to_all | solution.py:479
  62.2 1.2 copy-start.4
  62.2 4.9 %copy-start.6 = (s32[2,112]{1,0:T(2,128)S(1)}, s32[2,112]{1,0:T(2,128)}, u32[]{:S(2)}) copy-start(s32[2,112]{1,0:T(2,128)} %param.9) | copy-start | bytes 2692
  63.4 42.4 %all-to-all-start = ((bf16[8,28,16,256]{3,2,1,0:T(8,128)(2,1)}), bf16[8,28,16,256]{3,2,1,0:T(8,128)(2,1)S(1)}, u32[]{:S(2)}, u32[]{:S(2)}) async-start(bf16[8,28,16,256]{3,2,1,0:T(8,128)(2,1)} %get-tuple-element.19), calls=%async_computation | async-start | bytes 3670016 | tf_op jit(solution)/shard_map/all_to_all | solution.py:485
  67.0 53.7 %copy-start = (f32[28,16,256]{2,1,0:T(8,128)S(1)}, f32[28,16,256]{2,1,0:T(8,128)}, u32[]{:S(2)}) copy-start(f32[28,16,256]{2,1,0:T(8,128)} %get-tuple-element.20.own_ref) | copy-start | bytes 1376260
  67.0 53.7 %copy-start.2 = (s32[3]{0:T(128)S(1)}, s32[3]{0:T(128)}, u32[]{:S(2)}) copy-start(s32[3]{0:T(128)} %pad_add_fusion.1.at_ref) | copy-start | bytes 40
  70.9 24.2 %collective-permute-start.2 = (bf16[2,14,16,256]{3,2,1,0:T(8,128)(2,1)}, bf16[2,14,16,256]{3,2,1,0:T(8,128)(2,1)S(1)}, u32[]{:S(2)}, u32[]{:S(2)}) collective-permute-start(bf16[2,14,16,256]{3,2,1,0:T(8,128)(2,1)} %bitcast.50), channel_id=1, source_target_pairs={{0,16},{16,0},{1,17},{17,1},{2,18},{18,2},{3,19},{19,3},{4,20},{20... | collective-permute-start | bytes 688136 | tf_op jit(solution)/shard_map/ppermute | solution.py:108
  96.1 12.2 %collective-permute-start.5 = (bf16[2,2,14,16,256]{4,3,2,1,0:T(8,128)(2,1)S(1)}, bf16[2,2,14,16,256]{4,3,2,1,0:T(8,128)(2,1)S(1)}, u32[]{:S(2)}, u32[]{:S(2)}) collective-permute-start(bf16[2,2,14,16,256]{4,3,2,1,0:T(8,128)(2,1)S(1)} %pad_maximum_fusion.refs_0_), channel_id=1, source_target_pairs={{32,0},{64,32},{96,64},{33,1},{65,33},{97,65},{34,2},{66,34},{98,6... | collective-permute-start | bytes 1376264 | tf_op jit(solution)/shard_map/ppermute | solution.py:488
  97.4 13.5 %collective-permute-start.4 = (bf16[2,2,14,16,256]{4,3,2,1,0:T(8,128)(2,1)S(1)}, bf16[2,2,14,16,256]{4,3,2,1,0:T(8,128)(2,1)}, u32[]{:S(2)}, u32[]{:S(2)}) collective-permute-start(bf16[2,2,14,16,256]{4,3,2,1,0:T(8,128)(2,1)S(1)} %pad_maximum_fusion.refs_0_), channel_id=1, source_target_pairs={{0,64},{96,32},{1,65},{97,33},{2,66},{98,34},{3,67},{99,35},{4,68}... | collective-permute-start | bytes 1376264 | tf_op jit(solution)/shard_map/ppermute | solution.py:488
  103.7 17.0 %collective-permute-start.3 = (bf16[2,2,14,16,256]{4,3,2,1,0:T(8,128)(2,1)S(1)}, bf16[2,2,14,16,256]{4,3,2,1,0:T(8,128)(2,1)}, u32[]{:S(2)}, u32[]{:S(2)}) collective-permute-start(bf16[2,2,14,16,256]{4,3,2,1,0:T(8,128)(2,1)S(1)} %pad_maximum_fusion.refs_0_), channel_id=1, source_target_pairs={{0,32},{32,64},{64,96},{1,33},{33,65},{65,97},{2,34},{34,66},{66,9... | collective-permute-start | bytes 1376264 | tf_op jit(solution)/shard_map/ppermute | solution.py:488
  123.0 3.9 %collective-permute-start.6 = (bf16[14,16,256]{2,1,0:T(8,128)(2,1)S(1)}, bf16[14,16,256]{2,1,0:T(8,128)(2,1)S(1)}, u32[]{:S(2)}, u32[]{:S(2)}) collective-permute-start(bf16[14,16,256]{2,1,0:T(8,128)(2,1)S(1)} %get-tuple-element.26), channel_id=1, source_target_pairs={{0,1},{1,0},{2,3},{3,2},{4,5},{5,4},{6,7},{7,6},{8,9},{9,8},{10,11... | collective-permute-start | bytes 344072 | tf_op jit(solution)/shard_map/ppermute | solution.py:501
  126.9 7.4 %collective-permute-start.8 = (bf16[2,7,16,256]{3,2,1,0:T(8,128)(2,1)S(1)}, bf16[2,7,16,256]{3,2,1,0:T(8,128)(2,1)S(1)}, u32[]{:S(2)}, u32[]{:S(2)}) collective-permute-start(bf16[2,7,16,256]{3,2,1,0:T(8,128)(2,1)S(1)} %get-tuple-element.47), channel_id=1, source_target_pairs={{0,8},{4,12},{8,0},{12,4},{1,9},{5,13},{9,1},{13,5},{2,10},{6,14},... | collective-permute-start | bytes 344072 | tf_op jit(solution)/shard_map/ppermute | solution.py:108
  131.0 5.5 %collective-permute-start.7 = (bf16[2,7,16,256]{3,2,1,0:T(8,128)(2,1)S(1)}, bf16[2,7,16,256]{3,2,1,0:T(8,128)(2,1)S(1)}, u32[]{:S(2)}, u32[]{:S(2)}) collective-permute-start(bf16[2,7,16,256]{3,2,1,0:T(8,128)(2,1)S(1)} %get-tuple-element.47), channel_id=1, source_target_pairs={{0,4},{4,8},{8,12},{12,0},{1,5},{5,9},{9,13},{13,1},{2,6},{6,10},{... | collective-permute-start | bytes 344072 | tf_op jit(solution)/shard_map/ppermute | solution.py:108
  131.1 5.5 %collective-permute-start.9 = (bf16[2,7,16,256]{3,2,1,0:T(8,128)(2,1)S(1)}, bf16[2,7,16,256]{3,2,1,0:T(8,128)(2,1)S(1)}, u32[]{:S(2)}, u32[]{:S(2)}) collective-permute-start(bf16[2,7,16,256]{3,2,1,0:T(8,128)(2,1)S(1)} %get-tuple-element.47), channel_id=1, source_target_pairs={{0,12},{4,0},{8,4},{12,8},{1,13},{5,1},{9,5},{13,9},{2,14},{6,2},{... | collective-permute-start | bytes 344072 | tf_op jit(solution)/shard_map/ppermute | solution.py:108
  133.7 3.8 %collective-permute-start.11 = (bf16[2,7,16,256]{3,2,1,0:T(8,128)(2,1)S(1)}, bf16[2,7,16,256]{3,2,1,0:T(8,128)(2,1)S(1)}, u32[]{:S(2)}, u32[]{:S(2)}) collective-permute-start(bf16[2,7,16,256]{3,2,1,0:T(8,128)(2,1)S(1)} %get-tuple-element.41), channel_id=1, source_target_pairs={{0,2},{2,0},{1,3},{3,1},{4,6},{6,4},{5,7},{7,5},{8,10},{10,8},{9,1... | collective-permute-start | bytes 344072 | tf_op jit(solution)/shard_map/ppermute | solution.py:108
  136.6 15.9 %collective-permute-start.10 = (bf16[4,2,7,16,256]{4,3,2,1,0:T(8,128)(2,1)S(1)}, bf16[4,2,7,16,256]{4,3,2,1,0:T(8,128)(2,1)S(1)}, u32[]{:S(2)}, u32[]{:S(2)}) collective-permute-start(bf16[4,2,7,16,256]{4,3,2,1,0:T(8,128)(2,1)S(1)} %pad_maximum_fusion.1.refs_0_), channel_id=1, source_target_pairs={{0,2},{2,0},{1,3},{3,1},{4,6},{6,4},{5,7},{7,5},{8,10},{10,8},{9,1... | collective-permute-start | bytes 1376264 | tf_op jit(solution)/shard_map/ppermute | solution.py:108
  137.5 5.4 %collective-permute-start.14 = (bf16[2,2,7,16,256]{4,3,2,1,0:T(8,128)(2,1)S(1)}, bf16[2,2,7,16,256]{4,3,2,1,0:T(8,128)(2,1)S(1)}, u32[]{:S(2)}, u32[]{:S(2)}) collective-permute-start(bf16[2,2,7,16,256]{4,3,2,1,0:T(8,128)(2,1)S(1)} %pad_maximum_fusion.2.refs_2_), channel_id=1, source_target_pairs={{0,12},{4,0},{8,4},{12,8},{1,13},{5,1},{9,5},{13,9},{2,14},{6,2},{... | collective-permute-start | bytes 688136 | tf_op jit(solution)/shard_map/ppermute | solution.py:108
  139.3 6.5 %collective-permute-start.13 = (bf16[2,2,7,16,256]{4,3,2,1,0:T(8,128)(2,1)S(1)}, bf16[2,2,7,16,256]{4,3,2,1,0:T(8,128)(2,1)S(1)}, u32[]{:S(2)}, u32[]{:S(2)}) collective-permute-start(bf16[2,2,7,16,256]{4,3,2,1,0:T(8,128)(2,1)S(1)} %pad_maximum_fusion.2.refs_2_), channel_id=1, source_target_pairs={{0,8},{4,12},{8,0},{12,4},{1,9},{5,13},{9,1},{13,5},{2,10},{6,14},... | collective-permute-start | bytes 688136 | tf_op jit(solution)/shard_map/ppermute | solution.py:108
  140.4 12.0 %collective-permute-start.12 = (bf16[2,2,7,16,256]{4,3,2,1,0:T(8,128)(2,1)S(1)}, bf16[2,2,7,16,256]{4,3,2,1,0:T(8,128)(2,1)S(1)}, u32[]{:S(2)}, u32[]{:S(2)}) collective-permute-start(bf16[2,2,7,16,256]{4,3,2,1,0:T(8,128)(2,1)S(1)} %pad_maximum_fusion.2.refs_2_), channel_id=1, source_target_pairs={{0,4},{4,8},{8,12},{12,0},{1,5},{5,9},{9,13},{13,1},{2,6},{6,10},{... | collective-permute-start | bytes 688136 | tf_op jit(solution)/shard_map/ppermute | solution.py:108
  163.9 19.5 %all-to-all-start.2 = ((f16[8,2,56,512]{3,2,1,0:T(8,128)(2,1)}), f16[8,2,56,512]{3,2,1,0:T(8,128)(2,1)S(1)}, u32[]{:S(2)}, u32[]{:S(2)}) async-start(f16[8,2,56,512]{3,2,1,0:T(8,128)(2,1)} %convert_element_type.27), calls=%async_computation.2 | async-start | bytes 1835008 | tf_op jit(solution)/shard_map/all_to_all | solution.py:515
  184.5 25.0 %all-to-all-start.3 = ((f16[8,2,56,512]{3,2,1,0:T(8,128)(2,1)}), f16[8,2,56,512]{3,2,1,0:T(8,128)(2,1)S(1)}, u32[]{:S(2)}, u32[]{:S(2)}) async-start(f16[8,2,56,512]{3,2,1,0:T(8,128)(2,1)} %broadcast_in_dim.28), calls=%async_computation.3 | async-start | bytes 1835008 | tf_op jit(solution)/shard_map/all_to_all | solution.py:518
  209.4 0.9 copy-start.1
  209.5 1.6 copy-start.3
  213.8 2.7 %collective-permute-start.15 = (f32[2,84,448]{2,1,0:T(8,128)S(1)}, f32[2,84,448]{2,1,0:T(8,128)S(1)}, u32[]{:S(2)}, u32[]{:S(2)}) collective-permute-start(f32[2,84,448]{2,1,0:T(8,128)S(1)} %get-tuple-element.31), channel_id=1, source_target_pairs={{0,1},{1,0},{2,3},{3,2},{4,5},{5,4},{6,7},{7,6},{8,9},{9,8},{10,11... | collective-permute-start | bytes 903176 | tf_op jit(solution)/shard_map/ppermute | solution.py:521

commit v6 on v4

--- a/solution.py
+++ b/solution.py
@@ -208,7 +208,7 @@
     return contract(ah, bh, 1, 0) + (contract(ah, bl, 1, 0) + contract(al, bh, 1, 0))
 
 
-LEVEL = 8.0
+LEVEL = 14.0
 
 
 def gram_kernel(at_ref, f_ref, *refs):
@@ -243,13 +243,14 @@
 
     here = t_ref[step]
     there = y_ref[pl.ds((1 - step) * per, per)].reshape(LEAF, wide)
-    hi, lo = halves(jnp.dot(f_ref[...], there, preferred_element_type=F32) / root_ref[1 - step])
+    hi, lo = halves(jnp.dot(f_ref[...], there, preferred_element_type=F32) * (1.0 / root_ref[1 - step]))
     cross = contract(here, hi, 1, 0) + contract(here, lo, 1, 0)
     square = jnp.sum(jnp.where(row == col, gram_ref[step], 0.0), axis=1, keepdims=True)
     cross = cross * lax.rsqrt(square)
     most = jnp.max(jnp.max(jnp.abs(cross), axis=0, keepdims=True), axis=1, keepdims=True)
     power = jnp.ceil(jnp.log2(jnp.maximum(most, 1e-30)))
     cross = jnp.where(col < order, cross * jnp.exp2(LEVEL - power), power)
+    cross = jnp.round(cross).astype(jnp.int32).astype(jnp.int16)
     cross_ref[:, 0] = cross.reshape(cross_ref.shape[0], cross_ref.shape[2], wide)
 
 
@@ -278,7 +279,7 @@
         out_shape=[
             jax.ShapeDtypeStruct((2, order, wide), F32),
             jax.ShapeDtypeStruct((2, 1, wide), F32),
-            jax.ShapeDtypeStruct((chips, 2, order // chips, wide), F32),
+            jax.ShapeDtypeStruct((chips, 2, order // chips, wide), jnp.int16),
         ],
         compiler_params=params(52),
         cost_estimate=cost(2 * 8 * LEAF * wide * wide, 4 * LEAF * LEAF + 2 * leaves_bytes(wide)),
@@ -321,10 +322,10 @@
                 for k in range(m + 1, 8):
                     scaled[m] = scaled[m] - low[k, m] * scaled[k]
             for i in range(g + 1, groups):
-                new = rows[i]
-                for k in range(8):
-                    new = new - c[i, k] * scaled[k]
-                rows[i] = new
+                terms = [c[i, k] * scaled[k] for k in range(8)]
+                while len(terms) > 1:
+                    terms = [a + b for a, b in zip(terms[::2], terms[1::2])]
+                rows[i] = rows[i] - terms[0]
             new = pivot[0]
             for k in range(1, 8):
                 new = jnp.where(sub == k, pivot[k], new)
@@ -433,7 +434,7 @@
         keep_ref[leaf, :tall] = jnp.where(first, low, high)
         send_ref[leaf, :tall] = jnp.where(first, high, low)
         left = w_ref[leaf, pl.ds(base, rows), :] * root_ref[leaf]
-        cross = cross_ref[:, leaf].reshape(order, wide)
+        cross = cross_ref[:, leaf].astype(jnp.int32).astype(F32).reshape(order, wide)
         level = jnp.exp2(cross[:1, order : order + 1] - LEVEL)
         half_way, rest = halves(product3(left[:, :order], cross))
         hi, lo = halves(w_ref[1 - leaf] * root_ref[1 - leaf])
@@ -513,12 +514,12 @@
         jnp.concatenate([came, keep], axis=2),
     ).reshape(2, -1, 2 * half)
 
-    cross = lax.all_to_all(cross.astype(jnp.float16), CHIP, 0, 0, tiled=True)
+    cross = lax.all_to_all(cross, CHIP, 0, 0, tiled=True)
     ready = lax.dynamic_slice_in_dim(cross, row_index, 1, 0)
     work = factor_inverse(gram, own_rows, 0, 3)
     cross = lax.all_to_all(jnp.broadcast_to(ready, (chips, *ready.shape[1:])), CHIP, 0, 0, tiled=True)
     inverse = factor_inverse(work, ready[0, 0, :8, :128].astype(F32), 3, probes // STEP)
-    keep, send = finish(at, inverse, root, own_rows, cross.astype(F32))
+    keep, send = finish(at, inverse, root, own_rows, cross)
     came = lax.ppermute(send, "core", swap)
     both = jnp.where(core == 0, jnp.concatenate([keep, came]), jnp.concatenate([came, keep]))
     tall = own_rows.shape[1] // 2

time: 186 us -> 183 us (0.984)
  other arithmetic: 4.55 us -> 0.85 us
  local copies, waits for them, and re-layouts: 11.8 us -> 14.4 us
  Pallas kernels: 63.7 us -> 61.8 us
    convert_element_type x2 -> x0, other arithmetic: 3.02 us -> none  [the longest x1 2.78 us: local(): cross = lax.all_to_all(cross.astype(jnp.float16), CHIP, 0, 0, tiled=True)]
    unnamed x25 -> x27, local copies, waits for them, and re-layouts: 9.95 us -> 12.6 us
  transfers between devices with their start and end apart: 19 -> 19, of which waited for: 11 -> 11; matrix products, arithmetic and copies ran while one was open for 1% -> 0% of each run, Pallas kernels for 24% -> 24%
where the time goes in v6:
time: 183 us; the launch traced here: 179 us
  Pallas kernels  61.8 us (34%)
  starting transfers between devices  41.8 us (23%)
  waiting for transfers between devices  31.1 us (17%)
  blocking collectives  28.4 us (16%)
  local copies, waits for them, and re-layouts  14.4 us (8%)
    pallas_call x2, Pallas kernels, factor_inverse(): pl.pallas_call(functools.partial(inverse_kernel, first=first, last=last),...  29 us
    all_to_all x1, blocking collectives, local(): kid_share = lax.all_to_all(kid_part, CHIP, 0, 0, tiled=True)  28.4 us
    pallas_call x2, Pallas kernels, probe(): pl.pallas_call(probe_kernel, grid=(count, rows // LEAF), out_shape=[part,...  15.9 us
    ppermute x9, waiting for transfers between devices, shift(): lax.ppermute(value, axis, [(i, (i + by) % size) for i in range(size)])  14.9 us
    ppermute x9, starting transfers between devices, shift(): lax.ppermute(value, axis, [(i, (i + by) % size) for i in range(size)])  13 us
    unnamed x27, local copies, waits for them, and re-layouts  12.6 us
    ppermute x3, waiting for transfers between devices, local(): lax.ppermute(pair, 'y', [(i, j) for i, j in reach if (j - i) % 4 == by])  11.5 us
    ppermute x3, starting transfers between devices, local(): lax.ppermute(pair, 'y', [(i, j) for i, j in reach if (j - i) % 4 == by])  9.05 us
  transfers between devices with their start and end apart: 19, of which 11 were waited for; matrix products, arithmetic and copies ran while one was open for 0% of the time, Pallas kernels for 24%

profile of v6, /device:TPU:1, one launch (start us, length us, event | category | flops | bytes accessed | tf_op | source)
XLA Modules:
  0.0 179.2 jit_solution(8741924002438629012)
XLA Ops:
  0.7 1.4 copy-done.6
  2.1 6.5 %shard_map.68 = (f32[2,1792,256]{2,1,0:T(8,128)S(1)}, f32[2,1792,256]{2,1,0:T(8,128)S(1)}) custom-call(s32[3]{0:T(128)S(1)} %pad_add_fusion.1.at_ref, bf16[2,1792,896]{2,1,0:T(8,128)(2,1)} %a_ref.1, bf16[2,448,896]{2,1,0:T(8,128)(2,1)S(1)} %bitcast.51), custom_call_target="tpu_custom_call" | custom-call | flops 3288334336 | bytes 13762560 | tf_op jit(solution)/shard_map/pallas_call | solution.py:50
  8.7 1.5 collective-permute-start
  10.2 9.4 %shard_map.71 = (f32[1,3584,256]{2,1,0:T(8,128)S(1)}, f32[1,3584,256]{2,1,0:T(8,128)S(1)}) custom-call(s32[3]{0:T(128)S(1)} %pad_add_fusion.1.at_ref, bf16[1,3584,1792]{2,1,0:T(8,128)(2,1)} %bitcast.53, bf16[1,448,1792]{2,1,0:T(8,128)(2,1)S(1)} %bitcast.52), custom_call_target="tpu_custom_call" | custom-call | flops 6576668672 | bytes 20185088 | tf_op jit(solution)/shard_map/pallas_call | solution.py:50
  19.7 1.3 shard_map.69
  21.0 28.4 %all_to_all.20.k_ref = bf16[8,28,16,256]{3,2,1,0:T(8,128)(2,1)S(1)} all-to-all(bf16[8,28,16,256]{3,2,1,0:T(8,128)(2,1)S(1)} %get-tuple-element.21), channel_id=1, replica_groups=mesh['y'=4,'zh'=2,'x'=4,'zl'=2,'core'=2] {'x','zl'}, dimensions={0} | all-to-all | bytes 3670016 | tf_op jit(solution)/shard_map/all_to_all | solution.py:480
  49.4 1.1 shard_map.70
  50.5 3.4 %collective-permute-start.1 = (bf16[2,14,16,256]{3,2,1,0:T(8,128)(2,1)S(1)}, bf16[2,14,16,256]{3,2,1,0:T(8,128)(2,1)S(1)}, u32[]{:S(2)}, u32[]{:S(2)}) collective-permute-start(bf16[2,14,16,256]{3,2,1,0:T(8,128)(2,1)S(1)} %bitcast.48), channel_id=1, source_target_pairs={{0,16},{16,0},{1,17},{17,1},{2,18},{18,2},{3,19},{19,3},{4,20},{20... | collective-permute-start | bytes 688136 | tf_op jit(solution)/shard_map/ppermute | solution.py:108
  53.9 1.3 shard_map.72
  55.2 1.2 copy-done
  56.4 1.7 collective-permute-done.1
  58.2 3.7 %all-to-all-start.1 = ((bf16[8,28,16,256]{3,2,1,0:T(8,128)(2,1)}), bf16[8,28,16,256]{3,2,1,0:T(8,128)(2,1)S(1)}, u32[]{:S(2)}, u32[]{:S(2)}) async-start(bf16[8,28,16,256]{3,2,1,0:T(8,128)(2,1)} %copy-done), calls=%async_computation.1 | async-start | bytes 3670016 | tf_op jit(solution)/shard_map/all_to_all | solution.py:487
  62.4 3.2 %collective-permute-start.3 = (bf16[2,2,14,16,256]{4,3,2,1,0:T(8,128)(2,1)S(1)}, bf16[2,2,14,16,256]{4,3,2,1,0:T(8,128)(2,1)S(1)}, u32[]{:S(2)}, u32[]{:S(2)}) collective-permute-start(bf16[2,2,14,16,256]{4,3,2,1,0:T(8,128)(2,1)S(1)} %pad_maximum_fusion.refs_0_), channel_id=1, source_target_pairs={{0,32},{32,64},{64,96},{1,33},{33,65},{65,97},{2,34},{34,66},{66,9... | collective-permute-start | bytes 1376264 | tf_op jit(solution)/shard_map/ppermute | solution.py:490
  65.6 4.5 %collective-permute-start.4 = (bf16[2,2,14,16,256]{4,3,2,1,0:T(8,128)(2,1)S(1)}, bf16[2,2,14,16,256]{4,3,2,1,0:T(8,128)(2,1)S(1)}, u32[]{:S(2)}, u32[]{:S(2)}) collective-permute-start(bf16[2,2,14,16,256]{4,3,2,1,0:T(8,128)(2,1)S(1)} %pad_maximum_fusion.refs_0_), channel_id=1, source_target_pairs={{0,64},{96,32},{1,65},{97,33},{2,66},{98,34},{3,67},{99,35},{4,68}... | collective-permute-start | bytes 1376264 | tf_op jit(solution)/shard_map/ppermute | solution.py:490
  70.2 1.3 collective-permute-start.5
  71.6 1.6 collective-permute-done.3.refs_1_
  73.1 9.9 %collective-permute-done.4.refs_2_ = bf16[2,2,14,16,256]{4,3,2,1,0:T(8,128)(2,1)S(1)} collective-permute-done((bf16[2,2,14,16,256]{4,3,2,1,0:T(8,128)(2,1)S(1)}, bf16[2,2,14,16,256]{4,3,2,1,0:T(8,128)(2,1)S(1)}, u32[]{:S(2)}, u32[]{:S(2)}) %collective-permute-start.4) | collective-permute-done | bytes 458784 | tf_op jit(solution)/shard_map/ppermute | solution.py:490
  83.0 0.8 copy-done.1
  83.8 0.8 copy-done.3
  84.6 2.4 %all-to-all-done.1.p_ref = bf16[8,28,16,256]{3,2,1,0:T(8,128)(2,1)S(1)} async-done(((bf16[8,28,16,256]{3,2,1,0:T(8,128)(2,1)}), bf16[8,28,16,256]{3,2,1,0:T(8,128)(2,1)S(1)}, u32[]{:S(2)}, u32[]{:S(2)}) %all-to-all-start.1) | async-done | bytes 1835040 | tf_op jit(solution)/shard_map/all_to_all | solution.py:487
  87.0 1.0 copy-done.2
  88.0 1.0 copy-done.4
  89.0 1.7 shard_map.73
  90.7 2.4 %collective-permute-start.6 = (bf16[14,16,256]{2,1,0:T(8,128)(2,1)S(1)}, bf16[14,16,256]{2,1,0:T(8,128)(2,1)S(1)}, u32[]{:S(2)}, u32[]{:S(2)}) collective-permute-start(bf16[14,16,256]{2,1,0:T(8,128)(2,1)S(1)} %get-tuple-element.30), channel_id=1, source_target_pairs={{0,1},{1,0},{2,3},{3,2},{4,5},{5,4},{6,7},{7,6},{8,9},{9,8},{10,11... | collective-permute-start | bytes 344072 | tf_op jit(solution)/shard_map/ppermute | solution.py:503
  93.1 1.0 collective-permute-done.6
  94.2 2.2 %collective-permute-start.8 = (bf16[2,7,16,256]{3,2,1,0:T(8,128)(2,1)S(1)}, bf16[2,7,16,256]{3,2,1,0:T(8,128)(2,1)S(1)}, u32[]{:S(2)}, u32[]{:S(2)}) collective-permute-start(bf16[2,7,16,256]{3,2,1,0:T(8,128)(2,1)S(1)} %get-tuple-element.51), channel_id=1, source_target_pairs={{0,8},{4,12},{8,0},{12,4},{1,9},{5,13},{9,1},{13,5},{2,10},{6,14},... | collective-permute-start | bytes 344072 | tf_op jit(solution)/shard_map/ppermute | solution.py:108
  96.4 1.2 collective-permute-start.9
  97.6 1.3 collective-permute-start.11
  98.9 1.3 collective-permute-done.7
  100.2 1.6 collective-permute-done.8
  103.1 1.1 collective-permute-start.12
  104.2 3.0 %collective-permute-start.13 = (bf16[2,2,7,16,256]{4,3,2,1,0:T(8,128)(2,1)S(1)}, bf16[2,2,7,16,256]{4,3,2,1,0:T(8,128)(2,1)S(1)}, u32[]{:S(2)}, u32[]{:S(2)}) collective-permute-start(bf16[2,2,7,16,256]{4,3,2,1,0:T(8,128)(2,1)S(1)} %pad_maximum_fusion.2.refs_2_), channel_id=1, source_target_pairs={{0,8},{4,12},{8,0},{12,4},{1,9},{5,13},{9,1},{13,5},{2,10},{6,14},... | collective-permute-start | bytes 688136 | tf_op jit(solution)/shard_map/ppermute | solution.py:108
  107.5 2.8 %collective-permute-done.12.refs_3_ = bf16[2,2,7,16,256]{4,3,2,1,0:T(8,128)(2,1)S(1)} collective-permute-done((bf16[2,2,7,16,256]{4,3,2,1,0:T(8,128)(2,1)S(1)}, bf16[2,2,7,16,256]{4,3,2,1,0:T(8,128)(2,1)S(1)}, u32[]{:S(2)}, u32[]{:S(2)}) %collective-permute-start.12) | collective-permute-done | bytes 229408 | tf_op jit(solution)/shard_map/ppermute | solution.py:108
  110.3 6.8 %collective-permute-done.13.refs_4_ = bf16[2,2,7,16,256]{4,3,2,1,0:T(8,128)(2,1)S(1)} collective-permute-done((bf16[2,2,7,16,256]{4,3,2,1,0:T(8,128)(2,1)S(1)}, bf16[2,2,7,16,256]{4,3,2,1,0:T(8,128)(2,1)S(1)}, u32[]{:S(2)}, u32[]{:S(2)}) %collective-permute-start.13) | collective-permute-done | bytes 229408 | tf_op jit(solution)/shard_map/ppermute | solution.py:108
  117.1 8.7 %shard_map.74 = (f32[2,448,512]{2,1,0:T(8,128)}, f32[2,1,512]{2,1,0:T(1,128)S(1)}, s16[8,2,56,512]{3,2,1,0:T(8,128)(2,1)}) custom-call(s32[3]{0:T(128)S(1)} %pad_add_fusion.1.at_ref, bf16[3584,1792]{1,0:T(8,128)(2,1)} %f_ref.1, bf16[4,2,7,16,256]{4,3,2,1,0:T(8,128)(2,1)S(1)} %pad_maximum_fusion.1.refs_0_, ...), custom_call_target="tpu_custom_call" | custom-call | flops 3758096384 | bytes 6881280 | tf_op jit(solution)/shard_map/pallas_call | solution.py:260
  125.8 5.5 %all-to-all-start.2 = ((s16[8,2,56,512]{3,2,1,0:T(8,128)(2,1)}), s16[8,2,56,512]{3,2,1,0:T(8,128)(2,1)S(1)}, u32[]{:S(2)}, u32[]{:S(2)}) async-start(s16[8,2,56,512]{3,2,1,0:T(8,128)(2,1)} %get-tuple-element.32), calls=%async_computation.2 | async-start | bytes 1835008 | tf_op jit(solution)/shard_map/all_to_all | solution.py:517
  131.4 12.5 %shard_map.75.a_ref = f32[2,448,512]{2,1,0:T(8,128)S(1)} custom-call(f32[2,448,512]{2,1,0:T(8,128)S(1)} %copy-done.5, bf16[2,112,512]{2,1,0:T(8,128)(2,1)S(1)} %maximum_select_fusion.1.after_ref.own_ref), custom_call_target="tpu_custom_call" | custom-call | flops 16499999744 | bytes 3670016 | tf_op jit(solution)/shard_map/pallas_call | solution.py:406
  143.9 1.2 copy-done.10
  145.1 1.0 broadcast_in_dim.28
  146.2 5.1 %all-to-all-start.3 = ((s16[8,2,56,512]{3,2,1,0:T(8,128)(2,1)}), s16[8,2,56,512]{3,2,1,0:T(8,128)(2,1)S(1)}, u32[]{:S(2)}, u32[]{:S(2)}) async-start(s16[8,2,56,512]{3,2,1,0:T(8,128)(2,1)} %broadcast_in_dim.28), calls=%async_computation.3 | async-start | bytes 1835008 | tf_op jit(solution)/shard_map/all_to_all | solution.py:520
  151.3 1.5 copy-done.11
  152.8 16.5 %shard_map.76.w_ref = f32[2,448,512]{2,1,0:T(8,128)S(1)} custom-call(f32[2,448,512]{2,1,0:T(8,128)S(1)} %copy-done.11, f32[8,128]{1,0:T(8,128)S(1)} %fusion.2.after_ref), custom_call_target="tpu_custom_call" | custom-call | flops 22000001024 | bytes 3670016 | tf_op jit(solution)/shard_map/pallas_call | solution.py:406
  169.4 1.2 copy-done.8
  170.6 1.5 copy-done.9
  172.1 2.7 %shard_map.77 = (f32[2,84,448]{2,1,0:T(8,128)S(1)}, f32[2,84,448]{2,1,0:T(8,128)S(1)}) custom-call(s32[3]{0:T(128)S(1)} %pad_add_fusion.1.at_ref, f32[2,448,512]{2,1,0:T(8,128)S(1)} %copy-done.9, f32[2,1,512]{2,1,0:T(1,128)S(1)} %get-tuple-element.33.root_ref, bf16[2,112,512]{2,1,0:T(8,128)(2,1)S(1)} %maximum_select_fusion.1.after_ref.own_ref, ...), custom_call_target="tpu_custom_call" | custom-call | flops 2000000000 | bytes 3670016 | tf_op jit(solution)/shard_map/pallas_call | solution.py:452
  174.8 1.4 collective-permute-start.15
  176.2 1.3 collective-permute-done.15
  178.4 0.8 copy.41
  (52 shorter events, 3.3 us)
Async XLA Ops:
  0.7 1.4 copy-start.6
  2.1 8.0 %copy-start.7 = (bf16[1792,448]{0,1:T(8,128)(2,1)S(1)}, bf16[1792,448]{0,1:T(8,128)(2,1)}, u32[]{:S(2)}) copy-start(bf16[1792,448]{0,1:T(8,128)(2,1)} %param.7) | copy-start | bytes 4816900
  8.7 11.0 %collective-permute-start = (f32[2,1792,256]{2,1,0:T(8,128)S(1)}, f32[2,1792,256]{2,1,0:T(8,128)S(1)}, u32[]{:S(2)}, u32[]{:S(2)}) collective-permute-start(f32[2,1792,256]{2,1,0:T(8,128)S(1)} %get-tuple-element.20), channel_id=1, source_target_pairs={{0,1},{1,0},{2,3},{3,2},{4,5},{5,4},{6,7},{7,6},{8,9},{9,8},{10,11... | collective-permute-start | bytes 11010056 | tf_op jit(solution)/shard_map/ppermute | solution.py:476
  19.6 34.3 %collective-permute-start.2 = (f32[1,3584,256]{2,1,0:T(8,128)S(1)}, f32[1,3584,256]{2,1,0:T(8,128)S(1)}, u32[]{:S(2)}, u32[]{:S(2)}) collective-permute-start(f32[1,3584,256]{2,1,0:T(8,128)S(1)} %get-tuple-element.24), channel_id=1, source_target_pairs={{0,1},{1,0},{2,3},{3,2},{4,5},{5,4},{6,7},{7,6},{8,9},{9,8},{10,11... | collective-permute-start | bytes 11010056 | tf_op jit(solution)/shard_map/ppermute | solution.py:478
  50.5 7.7 %collective-permute-start.1 = (bf16[2,14,16,256]{3,2,1,0:T(8,128)(2,1)S(1)}, bf16[2,14,16,256]{3,2,1,0:T(8,128)(2,1)S(1)}, u32[]{:S(2)}, u32[]{:S(2)}) collective-permute-start(bf16[2,14,16,256]{3,2,1,0:T(8,128)(2,1)S(1)} %bitcast.48), channel_id=1, source_target_pairs={{0,16},{16,0},{1,17},{17,1},{2,18},{18,2},{3,19},{19,3},{4,20},{20... | collective-permute-start | bytes 688136 | tf_op jit(solution)/shard_map/ppermute | solution.py:108
  55.2 1.3 copy-start
  58.2 3.8 %copy-start.12 = (s32[2,112]{1,0:T(2,128)S(1)}, s32[2,112]{1,0:T(2,128)}, u32[]{:S(2)}) copy-start(s32[2,112]{1,0:T(2,128)} %param.9) | copy-start | bytes 2692
  58.2 28.8 %all-to-all-start.1 = ((bf16[8,28,16,256]{3,2,1,0:T(8,128)(2,1)}), bf16[8,28,16,256]{3,2,1,0:T(8,128)(2,1)S(1)}, u32[]{:S(2)}, u32[]{:S(2)}) async-start(bf16[8,28,16,256]{3,2,1,0:T(8,128)(2,1)} %copy-done), calls=%async_computation.1 | async-start | bytes 3670016 | tf_op jit(solution)/shard_map/all_to_all | solution.py:487
  62.4 10.7 %collective-permute-start.3 = (bf16[2,2,14,16,256]{4,3,2,1,0:T(8,128)(2,1)S(1)}, bf16[2,2,14,16,256]{4,3,2,1,0:T(8,128)(2,1)S(1)}, u32[]{:S(2)}, u32[]{:S(2)}) collective-permute-start(bf16[2,2,14,16,256]{4,3,2,1,0:T(8,128)(2,1)S(1)} %pad_maximum_fusion.refs_0_), channel_id=1, source_target_pairs={{0,32},{32,64},{64,96},{1,33},{33,65},{65,97},{2,34},{34,66},{66,9... | collective-permute-start | bytes 1376264 | tf_op jit(solution)/shard_map/ppermute | solution.py:490
  65.6 17.4 %collective-permute-start.4 = (bf16[2,2,14,16,256]{4,3,2,1,0:T(8,128)(2,1)S(1)}, bf16[2,2,14,16,256]{4,3,2,1,0:T(8,128)(2,1)S(1)}, u32[]{:S(2)}, u32[]{:S(2)}) collective-permute-start(bf16[2,2,14,16,256]{4,3,2,1,0:T(8,128)(2,1)S(1)} %pad_maximum_fusion.refs_0_), channel_id=1, source_target_pairs={{0,64},{96,32},{1,65},{97,33},{2,66},{98,34},{3,67},{99,35},{4,68}... | collective-permute-start | bytes 1376264 | tf_op jit(solution)/shard_map/ppermute | solution.py:490
  70.2 13.6 %collective-permute-start.5 = (bf16[2,2,14,16,256]{4,3,2,1,0:T(8,128)(2,1)S(1)}, bf16[2,2,14,16,256]{4,3,2,1,0:T(8,128)(2,1)S(1)}, u32[]{:S(2)}, u32[]{:S(2)}) collective-permute-start(bf16[2,2,14,16,256]{4,3,2,1,0:T(8,128)(2,1)S(1)} %pad_maximum_fusion.refs_0_), channel_id=1, source_target_pairs={{32,0},{64,32},{96,64},{33,1},{65,33},{97,65},{34,2},{66,34},{98,6... | collective-permute-start | bytes 1376264 | tf_op jit(solution)/shard_map/ppermute | solution.py:490
  83.0 0.8 copy-start.1
  83.8 0.8 copy-start.3
  87.0 1.0 copy-start.2
  88.0 1.0 copy-start.4
  90.7 3.3 %collective-permute-start.6 = (bf16[14,16,256]{2,1,0:T(8,128)(2,1)S(1)}, bf16[14,16,256]{2,1,0:T(8,128)(2,1)S(1)}, u32[]{:S(2)}, u32[]{:S(2)}) collective-permute-start(bf16[14,16,256]{2,1,0:T(8,128)(2,1)S(1)} %get-tuple-element.30), channel_id=1, source_target_pairs={{0,1},{1,0},{2,3},{3,2},{4,5},{5,4},{6,7},{7,6},{8,9},{9,8},{10,11... | collective-permute-start | bytes 344072 | tf_op jit(solution)/shard_map/ppermute | solution.py:503
  94.1 6.1 %collective-permute-start.7 = (bf16[2,7,16,256]{3,2,1,0:T(8,128)(2,1)S(1)}, bf16[2,7,16,256]{3,2,1,0:T(8,128)(2,1)S(1)}, u32[]{:S(2)}, u32[]{:S(2)}) collective-permute-start(bf16[2,7,16,256]{3,2,1,0:T(8,128)(2,1)S(1)} %get-tuple-element.51), channel_id=1, source_target_pairs={{0,4},{4,8},{8,12},{12,0},{1,5},{5,9},{9,13},{13,1},{2,6},{6,10},{... | collective-permute-start | bytes 344072 | tf_op jit(solution)/shard_map/ppermute | solution.py:108
  94.2 7.6 %collective-permute-start.8 = (bf16[2,7,16,256]{3,2,1,0:T(8,128)(2,1)S(1)}, bf16[2,7,16,256]{3,2,1,0:T(8,128)(2,1)S(1)}, u32[]{:S(2)}, u32[]{:S(2)}) collective-permute-start(bf16[2,7,16,256]{3,2,1,0:T(8,128)(2,1)S(1)} %get-tuple-element.51), channel_id=1, source_target_pairs={{0,8},{4,12},{8,0},{12,4},{1,9},{5,13},{9,1},{13,5},{2,10},{6,14},... | collective-permute-start | bytes 344072 | tf_op jit(solution)/shard_map/ppermute | solution.py:108
  96.4 6.1 %collective-permute-start.9 = (bf16[2,7,16,256]{3,2,1,0:T(8,128)(2,1)S(1)}, bf16[2,7,16,256]{3,2,1,0:T(8,128)(2,1)S(1)}, u32[]{:S(2)}, u32[]{:S(2)}) collective-permute-start(bf16[2,7,16,256]{3,2,1,0:T(8,128)(2,1)S(1)} %get-tuple-element.51), channel_id=1, source_target_pairs={{0,12},{4,0},{8,4},{12,8},{1,13},{5,1},{9,5},{13,9},{2,14},{6,2},{... | collective-permute-start | bytes 344072 | tf_op jit(solution)/shard_map/ppermute | solution.py:108
  97.6 5.5 %collective-permute-start.11 = (bf16[2,7,16,256]{3,2,1,0:T(8,128)(2,1)S(1)}, bf16[2,7,16,256]{3,2,1,0:T(8,128)(2,1)S(1)}, u32[]{:S(2)}, u32[]{:S(2)}) collective-permute-start(bf16[2,7,16,256]{3,2,1,0:T(8,128)(2,1)S(1)} %get-tuple-element.45), channel_id=1, source_target_pairs={{0,2},{2,0},{1,3},{3,1},{4,6},{6,4},{5,7},{7,5},{8,10},{10,8},{9,1... | collective-permute-start | bytes 344072 | tf_op jit(solution)/shard_map/ppermute | solution.py:108
  102.5 14.6 %collective-permute-start.10 = (bf16[4,2,7,16,256]{4,3,2,1,0:T(8,128)(2,1)S(1)}, bf16[4,2,7,16,256]{4,3,2,1,0:T(8,128)(2,1)S(1)}, u32[]{:S(2)}, u32[]{:S(2)}) collective-permute-start(bf16[4,2,7,16,256]{4,3,2,1,0:T(8,128)(2,1)S(1)} %pad_maximum_fusion.1.refs_0_), channel_id=1, source_target_pairs={{0,2},{2,0},{1,3},{3,1},{4,6},{6,4},{5,7},{7,5},{8,10},{10,8},{9,1... | collective-permute-start | bytes 1376264 | tf_op jit(solution)/shard_map/ppermute | solution.py:108
  103.1 7.2 %collective-permute-start.12 = (bf16[2,2,7,16,256]{4,3,2,1,0:T(8,128)(2,1)S(1)}, bf16[2,2,7,16,256]{4,3,2,1,0:T(8,128)(2,1)S(1)}, u32[]{:S(2)}, u32[]{:S(2)}) collective-permute-start(bf16[2,2,7,16,256]{4,3,2,1,0:T(8,128)(2,1)S(1)} %pad_maximum_fusion.2.refs_2_), channel_id=1, source_target_pairs={{0,4},{4,8},{8,12},{12,0},{1,5},{5,9},{9,13},{13,1},{2,6},{6,10},{... | collective-permute-start | bytes 688136 | tf_op jit(solution)/shard_map/ppermute | solution.py:108
  104.2 12.9 %collective-permute-start.13 = (bf16[2,2,7,16,256]{4,3,2,1,0:T(8,128)(2,1)S(1)}, bf16[2,2,7,16,256]{4,3,2,1,0:T(8,128)(2,1)S(1)}, u32[]{:S(2)}, u32[]{:S(2)}) collective-permute-start(bf16[2,2,7,16,256]{4,3,2,1,0:T(8,128)(2,1)S(1)} %pad_maximum_fusion.2.refs_2_), channel_id=1, source_target_pairs={{0,8},{4,12},{8,0},{12,4},{1,9},{5,13},{9,1},{13,5},{2,10},{6,14},... | collective-permute-start | bytes 688136 | tf_op jit(solution)/shard_map/ppermute | solution.py:108
  107.2 9.9 %collective-permute-start.14 = (bf16[2,2,7,16,256]{4,3,2,1,0:T(8,128)(2,1)S(1)}, bf16[2,2,7,16,256]{4,3,2,1,0:T(8,128)(2,1)S(1)}, u32[]{:S(2)}, u32[]{:S(2)}) collective-permute-start(bf16[2,2,7,16,256]{4,3,2,1,0:T(8,128)(2,1)S(1)} %pad_maximum_fusion.2.refs_2_), channel_id=1, source_target_pairs={{0,12},{4,0},{8,4},{12,8},{1,13},{5,1},{9,5},{13,9},{2,14},{6,2},{... | collective-permute-start | bytes 688136 | tf_op jit(solution)/shard_map/ppermute | solution.py:108
  125.8 5.5 %copy-start.5 = (f32[2,448,512]{2,1,0:T(8,128)S(1)}, f32[2,448,512]{2,1,0:T(8,128)}, u32[]{:S(2)}) copy-start(f32[2,448,512]{2,1,0:T(8,128)} %get-tuple-element.31.a_ref) | copy-start | bytes 5505028
  125.8 19.3 %all-to-all-start.2 = ((s16[8,2,56,512]{3,2,1,0:T(8,128)(2,1)}), s16[8,2,56,512]{3,2,1,0:T(8,128)(2,1)S(1)}, u32[]{:S(2)}, u32[]{:S(2)}) async-start(s16[8,2,56,512]{3,2,1,0:T(8,128)(2,1)} %get-tuple-element.32), calls=%async_computation.2 | async-start | bytes 1835008 | tf_op jit(solution)/shard_map/all_to_all | solution.py:517
  143.9 1.3 copy-start.10
  146.2 24.4 %all-to-all-start.3 = ((s16[8,2,56,512]{3,2,1,0:T(8,128)(2,1)}), s16[8,2,56,512]{3,2,1,0:T(8,128)(2,1)S(1)}, u32[]{:S(2)}, u32[]{:S(2)}) async-start(s16[8,2,56,512]{3,2,1,0:T(8,128)(2,1)} %broadcast_in_dim.28), calls=%async_computation.3 | async-start | bytes 1835008 | tf_op jit(solution)/shard_map/all_to_all | solution.py:520
  151.3 1.5 copy-start.11
  169.3 1.3 copy-start.8
  170.6 1.5 copy-start.9
  174.8 2.7 %collective-permute-start.15 = (f32[2,84,448]{2,1,0:T(8,128)S(1)}, f32[2,84,448]{2,1,0:T(8,128)S(1)}, u32[]{:S(2)}, u32[]{:S(2)}) collective-permute-start(f32[2,84,448]{2,1,0:T(8,128)S(1)} %get-tuple-element.35), channel_id=1, source_target_pairs={{0,1},{1,0},{2,3},{3,2},{4,5},{5,4},{6,7},{7,6},{8,9},{9,8},{10,11... | collective-permute-start | bytes 903176 | tf_op jit(solution)/shard_map/ppermute | solution.py:523

commit v7 on v6

--- a/solution.py
+++ b/solution.py
@@ -43,20 +43,20 @@
     sent_ref[0] = jnp.where(first, high, low)
 
 
-def probe(at, a, b, half):
+def probe(at, a, b, half, tall):
     count, rows, depth = a.shape
     probes = b.shape[1]
     part = jax.ShapeDtypeStruct((count, rows, half), F32)
     return pl.pallas_call(
         probe_kernel,
-        grid=(count, rows // LEAF),
+        grid=(count, rows // tall),
         out_shape=[part, part],
         in_specs=[
             SMEM,
-            pl.BlockSpec((1, LEAF, depth), lambda k, i: (k, i, 0)),
+            pl.BlockSpec((1, tall, depth), lambda k, i: (k, i, 0)),
             pl.BlockSpec((1, probes, depth), lambda k, i: (k, 0, 0)),
         ],
-        out_specs=[pl.BlockSpec((1, LEAF, half), lambda k, i: (k, i, 0))] * 2,
+        out_specs=[pl.BlockSpec((1, tall, half), lambda k, i: (k, i, 0))] * 2,
         compiler_params=params(40),
         cost_estimate=cost(4 * count * rows * depth * half, 2 * a.size + 8 * count * rows * half),
     )(at, a, b)
@@ -242,9 +242,10 @@
             root_ref[leaf] = jnp.sqrt(jnp.where(lane < order, square, 1.0))
 
     here = t_ref[step]
+    here = jnp.concatenate([here, here], axis=1)
     there = y_ref[pl.ds((1 - step) * per, per)].reshape(LEAF, wide)
     hi, lo = halves(jnp.dot(f_ref[...], there, preferred_element_type=F32) * (1.0 / root_ref[1 - step]))
-    cross = contract(here, hi, 1, 0) + contract(here, lo, 1, 0)
+    cross = contract(here, jnp.concatenate([hi, lo], axis=0), 1, 0)
     square = jnp.sum(jnp.where(row == col, gram_ref[step], 0.0), axis=1, keepdims=True)
     cross = cross * lax.rsqrt(square)
     most = jnp.max(jnp.max(jnp.abs(cross), axis=0, keepdims=True), axis=1, keepdims=True)
@@ -472,9 +473,9 @@
     swap = [(0, 1), (1, 0)]
 
     at = jnp.stack([x, zl, core]).astype(jnp.int32)
-    kid_sent, kid_kept = probe(at, child_update, jnp.swapaxes(child_test, 1, 2), half)
+    kid_sent, kid_kept = probe(at, child_update, jnp.swapaxes(child_test, 1, 2), half, 2 * LEAF)
     kid_sent = lax.ppermute(kid_sent, "core", swap)
-    own_sent, own_kept = probe(at, parent_front[None], parent_test.T[None], half)
+    own_sent, own_kept = probe(at, parent_front[None], parent_test.T[None], half, LEAF)
     own_sent = lax.ppermute(own_sent, "core", swap)
     kid_part, kid_rest = pack(at, kid_kept, kid_sent, chips)
     kid_share = lax.all_to_all(kid_part, CHIP, 0, 0, tiled=True)

time: 183 us -> 182 us (level)
  no operation moved by 1% of the time
where the time goes in v7:
time: 182 us; the launch traced here: 179 us
  Pallas kernels  61.3 us (34%)
  starting transfers between devices  41.7 us (23%)
  waiting for transfers between devices  31.1 us (17%)
  blocking collectives  28.4 us (16%)
  local copies, waits for them, and re-layouts  14.4 us (8%)
    pallas_call x2, Pallas kernels, factor_inverse(): pl.pallas_call(functools.partial(inverse_kernel, first=first, last=last),...  29.1 us
    all_to_all x1, blocking collectives, local(): kid_share = lax.all_to_all(kid_part, CHIP, 0, 0, tiled=True)  28.4 us
    pallas_call x2, Pallas kernels, probe(): pl.pallas_call(probe_kernel, grid=(count, rows // tall), out_shape=[part,...  15.7 us
    ppermute x9, waiting for transfers between devices, shift(): lax.ppermute(value, axis, [(i, (i + by) % size) for i in range(size)])  15 us
    ppermute x9, starting transfers between devices, shift(): lax.ppermute(value, axis, [(i, (i + by) % size) for i in range(size)])  12.9 us
    unnamed x27, local copies, waits for them, and re-layouts  12.6 us
    ppermute x3, waiting for transfers between devices, local(): lax.ppermute(pair, 'y', [(i, j) for i, j in reach if (j - i) % 4 == by])  11.5 us
    ppermute x3, starting transfers between devices, local(): lax.ppermute(pair, 'y', [(i, j) for i, j in reach if (j - i) % 4 == by])  9.05 us
  transfers between devices with their start and end apart: 19, of which 11 were waited for; matrix products, arithmetic and copies ran while one was open for 0% of the time, Pallas kernels for 24%

profile of v7, /device:TPU:1, one launch (start us, length us, event | category | flops | bytes accessed | tf_op | source)
XLA Modules:
  0.0 178.7 jit_solution(6630406388567032094)
XLA Ops:
  0.7 1.4 copy-done.6
  2.1 6.3 %shard_map.68 = (f32[2,1792,256]{2,1,0:T(8,128)S(1)}, f32[2,1792,256]{2,1,0:T(8,128)S(1)}) custom-call(s32[3]{0:T(128)S(1)} %pad_add_fusion.1.at_ref, bf16[2,1792,896]{2,1,0:T(8,128)(2,1)} %a_ref.1, bf16[2,448,896]{2,1,0:T(8,128)(2,1)S(1)} %bitcast.51), custom_call_target="tpu_custom_call" | custom-call | flops 3288334336 | bytes 13762560 | tf_op jit(solution)/shard_map/pallas_call | solution.py:50
  8.4 1.5 collective-permute-start
  9.9 9.4 %shard_map.71 = (f32[1,3584,256]{2,1,0:T(8,128)S(1)}, f32[1,3584,256]{2,1,0:T(8,128)S(1)}) custom-call(s32[3]{0:T(128)S(1)} %pad_add_fusion.1.at_ref, bf16[1,3584,1792]{2,1,0:T(8,128)(2,1)} %bitcast.53, bf16[1,448,1792]{2,1,0:T(8,128)(2,1)S(1)} %bitcast.52), custom_call_target="tpu_custom_call" | custom-call | flops 6576668672 | bytes 20185088 | tf_op jit(solution)/shard_map/pallas_call | solution.py:50
  19.4 1.3 shard_map.69
  20.8 28.4 %all_to_all.20.k_ref = bf16[8,28,16,256]{3,2,1,0:T(8,128)(2,1)S(1)} all-to-all(bf16[8,28,16,256]{3,2,1,0:T(8,128)(2,1)S(1)} %get-tuple-element.21), channel_id=1, replica_groups=mesh['y'=4,'zh'=2,'x'=4,'zl'=2,'core'=2] {'x','zl'}, dimensions={0} | all-to-all | bytes 3670016 | tf_op jit(solution)/shard_map/all_to_all | solution.py:481
  49.1 1.1 shard_map.70
  50.3 3.4 %collective-permute-start.1 = (bf16[2,14,16,256]{3,2,1,0:T(8,128)(2,1)S(1)}, bf16[2,14,16,256]{3,2,1,0:T(8,128)(2,1)S(1)}, u32[]{:S(2)}, u32[]{:S(2)}) collective-permute-start(bf16[2,14,16,256]{3,2,1,0:T(8,128)(2,1)S(1)} %bitcast.48), channel_id=1, source_target_pairs={{0,16},{16,0},{1,17},{17,1},{2,18},{18,2},{3,19},{19,3},{4,20},{20... | collective-permute-start | bytes 688136 | tf_op jit(solution)/shard_map/ppermute | solution.py:108
  53.7 1.3 shard_map.72
  55.0 1.2 copy-done
  56.2 1.7 collective-permute-done.1
  57.9 3.7 %all-to-all-start.1 = ((bf16[8,28,16,256]{3,2,1,0:T(8,128)(2,1)}), bf16[8,28,16,256]{3,2,1,0:T(8,128)(2,1)S(1)}, u32[]{:S(2)}, u32[]{:S(2)}) async-start(bf16[8,28,16,256]{3,2,1,0:T(8,128)(2,1)} %copy-done), calls=%async_computation.1 | async-start | bytes 3670016 | tf_op jit(solution)/shard_map/all_to_all | solution.py:488
  62.2 3.2 %collective-permute-start.3 = (bf16[2,2,14,16,256]{4,3,2,1,0:T(8,128)(2,1)S(1)}, bf16[2,2,14,16,256]{4,3,2,1,0:T(8,128)(2,1)S(1)}, u32[]{:S(2)}, u32[]{:S(2)}) collective-permute-start(bf16[2,2,14,16,256]{4,3,2,1,0:T(8,128)(2,1)S(1)} %pad_maximum_fusion.refs_0_), channel_id=1, source_target_pairs={{0,32},{32,64},{64,96},{1,33},{33,65},{65,97},{2,34},{34,66},{66,9... | collective-permute-start | bytes 1376264 | tf_op jit(solution)/shard_map/ppermute | solution.py:491
  65.4 4.5 %collective-permute-start.4 = (bf16[2,2,14,16,256]{4,3,2,1,0:T(8,128)(2,1)S(1)}, bf16[2,2,14,16,256]{4,3,2,1,0:T(8,128)(2,1)S(1)}, u32[]{:S(2)}, u32[]{:S(2)}) collective-permute-start(bf16[2,2,14,16,256]{4,3,2,1,0:T(8,128)(2,1)S(1)} %pad_maximum_fusion.refs_0_), channel_id=1, source_target_pairs={{0,64},{96,32},{1,65},{97,33},{2,66},{98,34},{3,67},{99,35},{4,68}... | collective-permute-start | bytes 1376264 | tf_op jit(solution)/shard_map/ppermute | solution.py:491
  69.9 1.3 collective-permute-start.5
  71.3 1.6 collective-permute-done.3.refs_1_
  72.9 9.9 %collective-permute-done.4.refs_2_ = bf16[2,2,14,16,256]{4,3,2,1,0:T(8,128)(2,1)S(1)} collective-permute-done((bf16[2,2,14,16,256]{4,3,2,1,0:T(8,128)(2,1)S(1)}, bf16[2,2,14,16,256]{4,3,2,1,0:T(8,128)(2,1)S(1)}, u32[]{:S(2)}, u32[]{:S(2)}) %collective-permute-start.4) | collective-permute-done | bytes 458784 | tf_op jit(solution)/shard_map/ppermute | solution.py:491
  82.8 0.8 copy-done.1
  83.5 0.8 copy-done.3
  84.3 2.4 %all-to-all-done.1.p_ref = bf16[8,28,16,256]{3,2,1,0:T(8,128)(2,1)S(1)} async-done(((bf16[8,28,16,256]{3,2,1,0:T(8,128)(2,1)}), bf16[8,28,16,256]{3,2,1,0:T(8,128)(2,1)S(1)}, u32[]{:S(2)}, u32[]{:S(2)}) %all-to-all-start.1) | async-done | bytes 1835040 | tf_op jit(solution)/shard_map/all_to_all | solution.py:488
  86.8 1.0 copy-done.2
  87.8 1.0 copy-done.4
  88.8 1.7 shard_map.73
  90.5 2.4 %collective-permute-start.6 = (bf16[14,16,256]{2,1,0:T(8,128)(2,1)S(1)}, bf16[14,16,256]{2,1,0:T(8,128)(2,1)S(1)}, u32[]{:S(2)}, u32[]{:S(2)}) collective-permute-start(bf16[14,16,256]{2,1,0:T(8,128)(2,1)S(1)} %get-tuple-element.30), channel_id=1, source_target_pairs={{0,1},{1,0},{2,3},{3,2},{4,5},{5,4},{6,7},{7,6},{8,9},{9,8},{10,11... | collective-permute-start | bytes 344072 | tf_op jit(solution)/shard_map/ppermute | solution.py:504
  92.9 1.0 collective-permute-done.6
  93.9 2.2 %collective-permute-start.8 = (bf16[2,7,16,256]{3,2,1,0:T(8,128)(2,1)S(1)}, bf16[2,7,16,256]{3,2,1,0:T(8,128)(2,1)S(1)}, u32[]{:S(2)}, u32[]{:S(2)}) collective-permute-start(bf16[2,7,16,256]{3,2,1,0:T(8,128)(2,1)S(1)} %get-tuple-element.51), channel_id=1, source_target_pairs={{0,8},{4,12},{8,0},{12,4},{1,9},{5,13},{9,1},{13,5},{2,10},{6,14},... | collective-permute-start | bytes 344072 | tf_op jit(solution)/shard_map/ppermute | solution.py:108
  96.2 1.2 collective-permute-start.9
  97.3 1.3 collective-permute-start.11
  98.6 1.3 collective-permute-done.7
  99.9 1.6 collective-permute-done.8
  102.9 1.1 collective-permute-start.12
  104.0 3.0 %collective-permute-start.13 = (bf16[2,2,7,16,256]{4,3,2,1,0:T(8,128)(2,1)S(1)}, bf16[2,2,7,16,256]{4,3,2,1,0:T(8,128)(2,1)S(1)}, u32[]{:S(2)}, u32[]{:S(2)}) collective-permute-start(bf16[2,2,7,16,256]{4,3,2,1,0:T(8,128)(2,1)S(1)} %pad_maximum_fusion.2.refs_2_), channel_id=1, source_target_pairs={{0,8},{4,12},{8,0},{12,4},{1,9},{5,13},{9,1},{13,5},{2,10},{6,14},... | collective-permute-start | bytes 688136 | tf_op jit(solution)/shard_map/ppermute | solution.py:108
  107.2 2.8 %collective-permute-done.12.refs_3_ = bf16[2,2,7,16,256]{4,3,2,1,0:T(8,128)(2,1)S(1)} collective-permute-done((bf16[2,2,7,16,256]{4,3,2,1,0:T(8,128)(2,1)S(1)}, bf16[2,2,7,16,256]{4,3,2,1,0:T(8,128)(2,1)S(1)}, u32[]{:S(2)}, u32[]{:S(2)}) %collective-permute-start.12) | collective-permute-done | bytes 229408 | tf_op jit(solution)/shard_map/ppermute | solution.py:108
  110.1 6.8 %collective-permute-done.13.refs_4_ = bf16[2,2,7,16,256]{4,3,2,1,0:T(8,128)(2,1)S(1)} collective-permute-done((bf16[2,2,7,16,256]{4,3,2,1,0:T(8,128)(2,1)S(1)}, bf16[2,2,7,16,256]{4,3,2,1,0:T(8,128)(2,1)S(1)}, u32[]{:S(2)}, u32[]{:S(2)}) %collective-permute-start.13) | collective-permute-done | bytes 229408 | tf_op jit(solution)/shard_map/ppermute | solution.py:108
  116.9 8.5 %shard_map.74 = (f32[2,448,512]{2,1,0:T(8,128)}, f32[2,1,512]{2,1,0:T(1,128)S(1)}, s16[8,2,56,512]{3,2,1,0:T(8,128)(2,1)}) custom-call(s32[3]{0:T(128)S(1)} %pad_add_fusion.1.at_ref, bf16[3584,1792]{1,0:T(8,128)(2,1)} %f_ref.1, bf16[4,2,7,16,256]{4,3,2,1,0:T(8,128)(2,1)S(1)} %pad_maximum_fusion.1.refs_0_, ...), custom_call_target="tpu_custom_call" | custom-call | flops 3758096384 | bytes 6881280 | tf_op jit(solution)/shard_map/pallas_call | solution.py:261
  125.3 5.5 %all-to-all-start.2 = ((s16[8,2,56,512]{3,2,1,0:T(8,128)(2,1)}), s16[8,2,56,512]{3,2,1,0:T(8,128)(2,1)S(1)}, u32[]{:S(2)}, u32[]{:S(2)}) async-start(s16[8,2,56,512]{3,2,1,0:T(8,128)(2,1)} %get-tuple-element.32), calls=%async_computation.2 | async-start | bytes 1835008 | tf_op jit(solution)/shard_map/all_to_all | solution.py:518
  130.9 12.5 %shard_map.75.a_ref = f32[2,448,512]{2,1,0:T(8,128)S(1)} custom-call(f32[2,448,512]{2,1,0:T(8,128)S(1)} %copy-done.5, bf16[2,112,512]{2,1,0:T(8,128)(2,1)S(1)} %maximum_select_fusion.1.after_ref.own_ref), custom_call_target="tpu_custom_call" | custom-call | flops 16499999744 | bytes 3670016 | tf_op jit(solution)/shard_map/pallas_call | solution.py:407
  143.4 1.2 copy-done.10
  144.7 1.0 broadcast_in_dim.28
  145.7 5.1 %all-to-all-start.3 = ((s16[8,2,56,512]{3,2,1,0:T(8,128)(2,1)}), s16[8,2,56,512]{3,2,1,0:T(8,128)(2,1)S(1)}, u32[]{:S(2)}, u32[]{:S(2)}) async-start(s16[8,2,56,512]{3,2,1,0:T(8,128)(2,1)} %broadcast_in_dim.28), calls=%async_computation.3 | async-start | bytes 1835008 | tf_op jit(solution)/shard_map/all_to_all | solution.py:521
  150.8 1.5 copy-done.11
  152.3 16.5 %shard_map.76.w_ref = f32[2,448,512]{2,1,0:T(8,128)S(1)} custom-call(f32[2,448,512]{2,1,0:T(8,128)S(1)} %copy-done.11, f32[8,128]{1,0:T(8,128)S(1)} %fusion.2.after_ref), custom_call_target="tpu_custom_call" | custom-call | flops 22000001024 | bytes 3670016 | tf_op jit(solution)/shard_map/pallas_call | solution.py:407
  168.9 1.2 copy-done.8
  170.1 1.5 copy-done.9
  171.6 2.7 %shard_map.77 = (f32[2,84,448]{2,1,0:T(8,128)S(1)}, f32[2,84,448]{2,1,0:T(8,128)S(1)}) custom-call(s32[3]{0:T(128)S(1)} %pad_add_fusion.1.at_ref, f32[2,448,512]{2,1,0:T(8,128)S(1)} %copy-done.9, f32[2,1,512]{2,1,0:T(1,128)S(1)} %get-tuple-element.33.root_ref, bf16[2,112,512]{2,1,0:T(8,128)(2,1)S(1)} %maximum_select_fusion.1.after_ref.own_ref, ...), custom_call_target="tpu_custom_call" | custom-call | flops 2000000000 | bytes 3670016 | tf_op jit(solution)/shard_map/pallas_call | solution.py:453
  174.4 1.4 collective-permute-start.15
  175.7 1.3 collective-permute-done.15
  177.9 0.8 copy.41
  (52 shorter events, 3.3 us)
Async XLA Ops:
  0.7 1.4 copy-start.6
  2.1 7.8 %copy-start.7 = (bf16[1792,448]{0,1:T(8,128)(2,1)S(1)}, bf16[1792,448]{0,1:T(8,128)(2,1)}, u32[]{:S(2)}) copy-start(bf16[1792,448]{0,1:T(8,128)(2,1)} %param.7) | copy-start | bytes 4816900
  8.4 11.0 %collective-permute-start = (f32[2,1792,256]{2,1,0:T(8,128)S(1)}, f32[2,1792,256]{2,1,0:T(8,128)S(1)}, u32[]{:S(2)}, u32[]{:S(2)}) collective-permute-start(f32[2,1792,256]{2,1,0:T(8,128)S(1)} %get-tuple-element.20), channel_id=1, source_target_pairs={{0,1},{1,0},{2,3},{3,2},{4,5},{5,4},{6,7},{7,6},{8,9},{9,8},{10,11... | collective-permute-start | bytes 11010056 | tf_op jit(solution)/shard_map/ppermute | solution.py:477
  19.3 34.3 %collective-permute-start.2 = (f32[1,3584,256]{2,1,0:T(8,128)S(1)}, f32[1,3584,256]{2,1,0:T(8,128)S(1)}, u32[]{:S(2)}, u32[]{:S(2)}) collective-permute-start(f32[1,3584,256]{2,1,0:T(8,128)S(1)} %get-tuple-element.24), channel_id=1, source_target_pairs={{0,1},{1,0},{2,3},{3,2},{4,5},{5,4},{6,7},{7,6},{8,9},{9,8},{10,11... | collective-permute-start | bytes 11010056 | tf_op jit(solution)/shard_map/ppermute | solution.py:479
  50.3 7.7 %collective-permute-start.1 = (bf16[2,14,16,256]{3,2,1,0:T(8,128)(2,1)S(1)}, bf16[2,14,16,256]{3,2,1,0:T(8,128)(2,1)S(1)}, u32[]{:S(2)}, u32[]{:S(2)}) collective-permute-start(bf16[2,14,16,256]{3,2,1,0:T(8,128)(2,1)S(1)} %bitcast.48), channel_id=1, source_target_pairs={{0,16},{16,0},{1,17},{17,1},{2,18},{18,2},{3,19},{19,3},{4,20},{20... | collective-permute-start | bytes 688136 | tf_op jit(solution)/shard_map/ppermute | solution.py:108
  54.9 1.3 copy-start
  57.9 3.8 %copy-start.12 = (s32[2,112]{1,0:T(2,128)S(1)}, s32[2,112]{1,0:T(2,128)}, u32[]{:S(2)}) copy-start(s32[2,112]{1,0:T(2,128)} %param.9) | copy-start | bytes 2692
  57.9 28.8 %all-to-all-start.1 = ((bf16[8,28,16,256]{3,2,1,0:T(8,128)(2,1)}), bf16[8,28,16,256]{3,2,1,0:T(8,128)(2,1)S(1)}, u32[]{:S(2)}, u32[]{:S(2)}) async-start(bf16[8,28,16,256]{3,2,1,0:T(8,128)(2,1)} %copy-done), calls=%async_computation.1 | async-start | bytes 3670016 | tf_op jit(solution)/shard_map/all_to_all | solution.py:488
  62.2 10.7 %collective-permute-start.3 = (bf16[2,2,14,16,256]{4,3,2,1,0:T(8,128)(2,1)S(1)}, bf16[2,2,14,16,256]{4,3,2,1,0:T(8,128)(2,1)S(1)}, u32[]{:S(2)}, u32[]{:S(2)}) collective-permute-start(bf16[2,2,14,16,256]{4,3,2,1,0:T(8,128)(2,1)S(1)} %pad_maximum_fusion.refs_0_), channel_id=1, source_target_pairs={{0,32},{32,64},{64,96},{1,33},{33,65},{65,97},{2,34},{34,66},{66,9... | collective-permute-start | bytes 1376264 | tf_op jit(solution)/shard_map/ppermute | solution.py:491
  65.4 17.4 %collective-permute-start.4 = (bf16[2,2,14,16,256]{4,3,2,1,0:T(8,128)(2,1)S(1)}, bf16[2,2,14,16,256]{4,3,2,1,0:T(8,128)(2,1)S(1)}, u32[]{:S(2)}, u32[]{:S(2)}) collective-permute-start(bf16[2,2,14,16,256]{4,3,2,1,0:T(8,128)(2,1)S(1)} %pad_maximum_fusion.refs_0_), channel_id=1, source_target_pairs={{0,64},{96,32},{1,65},{97,33},{2,66},{98,34},{3,67},{99,35},{4,68}... | collective-permute-start | bytes 1376264 | tf_op jit(solution)/shard_map/ppermute | solution.py:491
  69.9 13.6 %collective-permute-start.5 = (bf16[2,2,14,16,256]{4,3,2,1,0:T(8,128)(2,1)S(1)}, bf16[2,2,14,16,256]{4,3,2,1,0:T(8,128)(2,1)S(1)}, u32[]{:S(2)}, u32[]{:S(2)}) collective-permute-start(bf16[2,2,14,16,256]{4,3,2,1,0:T(8,128)(2,1)S(1)} %pad_maximum_fusion.refs_0_), channel_id=1, source_target_pairs={{32,0},{64,32},{96,64},{33,1},{65,33},{97,65},{34,2},{66,34},{98,6... | collective-permute-start | bytes 1376264 | tf_op jit(solution)/shard_map/ppermute | solution.py:491
  82.8 0.8 copy-start.1
  83.5 0.8 copy-start.3
  86.8 1.0 copy-start.2
  87.8 1.0 copy-start.4
  90.5 3.3 %collective-permute-start.6 = (bf16[14,16,256]{2,1,0:T(8,128)(2,1)S(1)}, bf16[14,16,256]{2,1,0:T(8,128)(2,1)S(1)}, u32[]{:S(2)}, u32[]{:S(2)}) collective-permute-start(bf16[14,16,256]{2,1,0:T(8,128)(2,1)S(1)} %get-tuple-element.30), channel_id=1, source_target_pairs={{0,1},{1,0},{2,3},{3,2},{4,5},{5,4},{6,7},{7,6},{8,9},{9,8},{10,11... | collective-permute-start | bytes 344072 | tf_op jit(solution)/shard_map/ppermute | solution.py:504
  93.9 6.1 %collective-permute-start.7 = (bf16[2,7,16,256]{3,2,1,0:T(8,128)(2,1)S(1)}, bf16[2,7,16,256]{3,2,1,0:T(8,128)(2,1)S(1)}, u32[]{:S(2)}, u32[]{:S(2)}) collective-permute-start(bf16[2,7,16,256]{3,2,1,0:T(8,128)(2,1)S(1)} %get-tuple-element.51), channel_id=1, source_target_pairs={{0,4},{4,8},{8,12},{12,0},{1,5},{5,9},{9,13},{13,1},{2,6},{6,10},{... | collective-permute-start | bytes 344072 | tf_op jit(solution)/shard_map/ppermute | solution.py:108
  93.9 7.6 %collective-permute-start.8 = (bf16[2,7,16,256]{3,2,1,0:T(8,128)(2,1)S(1)}, bf16[2,7,16,256]{3,2,1,0:T(8,128)(2,1)S(1)}, u32[]{:S(2)}, u32[]{:S(2)}) collective-permute-start(bf16[2,7,16,256]{3,2,1,0:T(8,128)(2,1)S(1)} %get-tuple-element.51), channel_id=1, source_target_pairs={{0,8},{4,12},{8,0},{12,4},{1,9},{5,13},{9,1},{13,5},{2,10},{6,14},... | collective-permute-start | bytes 344072 | tf_op jit(solution)/shard_map/ppermute | solution.py:108
  96.2 6.1 %collective-permute-start.9 = (bf16[2,7,16,256]{3,2,1,0:T(8,128)(2,1)S(1)}, bf16[2,7,16,256]{3,2,1,0:T(8,128)(2,1)S(1)}, u32[]{:S(2)}, u32[]{:S(2)}) collective-permute-start(bf16[2,7,16,256]{3,2,1,0:T(8,128)(2,1)S(1)} %get-tuple-element.51), channel_id=1, source_target_pairs={{0,12},{4,0},{8,4},{12,8},{1,13},{5,1},{9,5},{13,9},{2,14},{6,2},{... | collective-permute-start | bytes 344072 | tf_op jit(solution)/shard_map/ppermute | solution.py:108
  97.3 5.5 %collective-permute-start.11 = (bf16[2,7,16,256]{3,2,1,0:T(8,128)(2,1)S(1)}, bf16[2,7,16,256]{3,2,1,0:T(8,128)(2,1)S(1)}, u32[]{:S(2)}, u32[]{:S(2)}) collective-permute-start(bf16[2,7,16,256]{3,2,1,0:T(8,128)(2,1)S(1)} %get-tuple-element.45), channel_id=1, source_target_pairs={{0,2},{2,0},{1,3},{3,1},{4,6},{6,4},{5,7},{7,5},{8,10},{10,8},{9,1... | collective-permute-start | bytes 344072 | tf_op jit(solution)/shard_map/ppermute | solution.py:108
  102.3 14.6 %collective-permute-start.10 = (bf16[4,2,7,16,256]{4,3,2,1,0:T(8,128)(2,1)S(1)}, bf16[4,2,7,16,256]{4,3,2,1,0:T(8,128)(2,1)S(1)}, u32[]{:S(2)}, u32[]{:S(2)}) collective-permute-start(bf16[4,2,7,16,256]{4,3,2,1,0:T(8,128)(2,1)S(1)} %pad_maximum_fusion.1.refs_0_), channel_id=1, source_target_pairs={{0,2},{2,0},{1,3},{3,1},{4,6},{6,4},{5,7},{7,5},{8,10},{10,8},{9,1... | collective-permute-start | bytes 1376264 | tf_op jit(solution)/shard_map/ppermute | solution.py:108
  102.9 7.2 %collective-permute-start.12 = (bf16[2,2,7,16,256]{4,3,2,1,0:T(8,128)(2,1)S(1)}, bf16[2,2,7,16,256]{4,3,2,1,0:T(8,128)(2,1)S(1)}, u32[]{:S(2)}, u32[]{:S(2)}) collective-permute-start(bf16[2,2,7,16,256]{4,3,2,1,0:T(8,128)(2,1)S(1)} %pad_maximum_fusion.2.refs_2_), channel_id=1, source_target_pairs={{0,4},{4,8},{8,12},{12,0},{1,5},{5,9},{9,13},{13,1},{2,6},{6,10},{... | collective-permute-start | bytes 688136 | tf_op jit(solution)/shard_map/ppermute | solution.py:108
  104.0 12.9 %collective-permute-start.13 = (bf16[2,2,7,16,256]{4,3,2,1,0:T(8,128)(2,1)S(1)}, bf16[2,2,7,16,256]{4,3,2,1,0:T(8,128)(2,1)S(1)}, u32[]{:S(2)}, u32[]{:S(2)}) collective-permute-start(bf16[2,2,7,16,256]{4,3,2,1,0:T(8,128)(2,1)S(1)} %pad_maximum_fusion.2.refs_2_), channel_id=1, source_target_pairs={{0,8},{4,12},{8,0},{12,4},{1,9},{5,13},{9,1},{13,5},{2,10},{6,14},... | collective-permute-start | bytes 688136 | tf_op jit(solution)/shard_map/ppermute | solution.py:108
  106.9 9.9 %collective-permute-start.14 = (bf16[2,2,7,16,256]{4,3,2,1,0:T(8,128)(2,1)S(1)}, bf16[2,2,7,16,256]{4,3,2,1,0:T(8,128)(2,1)S(1)}, u32[]{:S(2)}, u32[]{:S(2)}) collective-permute-start(bf16[2,2,7,16,256]{4,3,2,1,0:T(8,128)(2,1)S(1)} %pad_maximum_fusion.2.refs_2_), channel_id=1, source_target_pairs={{0,12},{4,0},{8,4},{12,8},{1,13},{5,1},{9,5},{13,9},{2,14},{6,2},{... | collective-permute-start | bytes 688136 | tf_op jit(solution)/shard_map/ppermute | solution.py:108
  125.3 5.5 %copy-start.5 = (f32[2,448,512]{2,1,0:T(8,128)S(1)}, f32[2,448,512]{2,1,0:T(8,128)}, u32[]{:S(2)}) copy-start(f32[2,448,512]{2,1,0:T(8,128)} %get-tuple-element.31.a_ref) | copy-start | bytes 5505028
  125.3 19.3 %all-to-all-start.2 = ((s16[8,2,56,512]{3,2,1,0:T(8,128)(2,1)}), s16[8,2,56,512]{3,2,1,0:T(8,128)(2,1)S(1)}, u32[]{:S(2)}, u32[]{:S(2)}) async-start(s16[8,2,56,512]{3,2,1,0:T(8,128)(2,1)} %get-tuple-element.32), calls=%async_computation.2 | async-start | bytes 1835008 | tf_op jit(solution)/shard_map/all_to_all | solution.py:518
  143.4 1.3 copy-start.10
  145.7 24.4 %all-to-all-start.3 = ((s16[8,2,56,512]{3,2,1,0:T(8,128)(2,1)}), s16[8,2,56,512]{3,2,1,0:T(8,128)(2,1)S(1)}, u32[]{:S(2)}, u32[]{:S(2)}) async-start(s16[8,2,56,512]{3,2,1,0:T(8,128)(2,1)} %broadcast_in_dim.28), calls=%async_computation.3 | async-start | bytes 1835008 | tf_op jit(solution)/shard_map/all_to_all | solution.py:521
  150.8 1.5 copy-start.11
  168.9 1.3 copy-start.8
  170.1 1.5 copy-start.9
  174.4 2.7 %collective-permute-start.15 = (f32[2,84,448]{2,1,0:T(8,128)S(1)}, f32[2,84,448]{2,1,0:T(8,128)S(1)}, u32[]{:S(2)}, u32[]{:S(2)}) collective-permute-start(f32[2,84,448]{2,1,0:T(8,128)S(1)} %get-tuple-element.35), channel_id=1, source_target_pairs={{0,1},{1,0},{2,3},{3,2},{4,5},{5,4},{6,7},{7,6},{8,9},{9,8},{10,11... | collective-permute-start | bytes 903176 | tf_op jit(solution)/shard_map/ppermute | solution.py:524

commit v8 on v6

--- a/solution.py
+++ b/solution.py
@@ -480,6 +480,7 @@
     kid_share = lax.all_to_all(kid_part, CHIP, 0, 0, tiled=True)
     own_part, own_rest = pack(at, own_kept, own_sent, chips)
 
+    kid_share, own_part = lax.optimization_barrier((kid_share, own_part))
     kids = sum_shares(at, kid_share, kid_rest, BF).reshape(2, kid_blocks, -1, half)
     pair = ring_pieces(kids, "zh")
     pair[1], own_part = lax.optimization_barrier((pair[1], own_part))

time: 183 us -> 191 us (1.044)
  blocking collectives: 28.4 us -> 0 us
  waiting for transfers between devices: 31.1 us -> 57.1 us
  starting transfers between devices: 41.8 us -> 46.1 us
  local copies, waits for them, and re-layouts: 14.4 us -> 18.2 us
  Pallas kernels: 61.8 us -> 64.9 us
    all_to_all x1 -> x0, blocking collectives: 28.4 us -> none  [local(): kid_share = lax.all_to_all(kid_part, CHIP, 0, 0, tiled=True)]
    all_to_all x0 -> x1, waiting for transfers between devices: none -> 21.3 us  [local(): kid_share = lax.all_to_all(kid_part, CHIP, 0, 0, tiled=True)]
    all_to_all x0 -> x1, starting transfers between devices: none -> 5.46 us  [local(): kid_share = lax.all_to_all(kid_part, CHIP, 0, 0, tiled=True)]
    ppermute x9, waiting for transfers between devices: 14.9 us -> 18.9 us  [shift(): lax.ppermute(value, axis, [(i, (i + by) % size) for i in range(size)])]
    unnamed x27 -> x33, local copies, waits for them, and re-layouts: 12.6 us -> 16.5 us
  transfers between devices with their start and end apart: 19 -> 20, of which waited for: 11 -> 12; matrix products, arithmetic and copies ran while one was open for 0% -> 0% of each run, Pallas kernels for 24% -> 23%
where the time goes in v8:
time: 191 us; the launch traced here: 188 us
  Pallas kernels  64.9 us (34%)
  waiting for transfers between devices  57.1 us (30%)
  starting transfers between devices  46.1 us (24%)
  local copies, waits for them, and re-layouts  18.2 us (10%)
    pallas_call x2, Pallas kernels, factor_inverse(): pl.pallas_call(functools.partial(inverse_kernel, first=first, last=last),...  29 us
    all_to_all x1, waiting for transfers between devices, local(): kid_share = lax.all_to_all(kid_part, CHIP, 0, 0, tiled=True)  21.3 us
    ppermute x9, waiting for transfers between devices, shift(): lax.ppermute(value, axis, [(i, (i + by) % size) for i in range(size)])  18.9 us
    pallas_call x2, Pallas kernels, probe(): pl.pallas_call(probe_kernel, grid=(count, rows // LEAF), out_shape=[part,...  17.3 us
    unnamed x33, local copies, waits for them, and re-layouts  16.5 us
    ppermute x9, starting transfers between devices, shift(): lax.ppermute(value, axis, [(i, (i + by) % size) for i in range(size)])  12.5 us
    ppermute x3, waiting for transfers between devices, local(): lax.ppermute(pair, 'y', [(i, j) for i, j in reach if (j - i) % 4 == by])  12 us
    ppermute x3, starting transfers between devices, local(): lax.ppermute(pair, 'y', [(i, j) for i, j in reach if (j - i) % 4 == by])  9.05 us
  transfers between devices with their start and end apart: 20, of which 12 were waited for; matrix products, arithmetic and copies ran while one was open for 0% of the time, Pallas kernels for 23%

profile of v8, /device:TPU:1, one launch (start us, length us, event | category | flops | bytes accessed | tf_op | source)
XLA Modules:
  0.0 188.1 jit_solution(14823127463308899905)
XLA Ops:
  0.7 1.4 copy-done.9
  2.1 6.5 %shard_map.68 = (f32[2,1792,256]{2,1,0:T(8,128)S(1)}, f32[2,1792,256]{2,1,0:T(8,128)S(1)}) custom-call(s32[3]{0:T(128)S(1)} %pad_add_fusion.1.at_ref, bf16[2,1792,896]{2,1,0:T(8,128)(2,1)} %a_ref.1, bf16[2,448,896]{2,1,0:T(8,128)(2,1)S(1)} %bitcast.51), custom_call_target="tpu_custom_call" | custom-call | flops 3288334336 | bytes 13762560 | tf_op jit(solution)/shard_map/pallas_call | solution.py:50
  8.7 1.5 collective-permute-start
  10.2 10.8 %shard_map.70 = (f32[1,3584,256]{2,1,0:T(8,128)}, f32[1,3584,256]{2,1,0:T(8,128)S(1)}) custom-call(s32[3]{0:T(128)S(1)} %pad_add_fusion.1.at_ref, bf16[1,3584,1792]{2,1,0:T(8,128)(2,1)} %bitcast.53, bf16[1,448,1792]{2,1,0:T(8,128)(2,1)S(1)} %bitcast.52), custom_call_target="tpu_custom_call" | custom-call | flops 6576668672 | bytes 20185088 | tf_op jit(solution)/shard_map/pallas_call | solution.py:50
  21.0 1.3 shard_map.69
  22.7 1.3 copy-done.3
  24.1 5.5 %all-to-all-start = ((bf16[8,28,16,256]{3,2,1,0:T(8,128)(2,1)}), bf16[8,28,16,256]{3,2,1,0:T(8,128)(2,1)S(1)}, u32[]{:S(2)}, u32[]{:S(2)}) async-start(bf16[8,28,16,256]{3,2,1,0:T(8,128)(2,1)} %copy-done.3), calls=%async_computation | async-start | bytes 3670016 | tf_op jit(solution)/shard_map/all_to_all | solution.py:480
  29.5 2.0 %copy-done.1 = f32[1,3584,256]{2,1,0:T(8,128)S(1)} copy-done((f32[1,3584,256]{2,1,0:T(8,128)S(1)}, f32[1,3584,256]{2,1,0:T(8,128)}, u32[]{:S(2)}) %copy-start.1) | copy-done | bytes 3670040
  31.6 3.1 %shard_map.71 = (bf16[8,28,16,256]{3,2,1,0:T(8,128)(2,1)S(1)}, f32[28,16,256]{2,1,0:T(8,128)S(1)}) custom-call(s32[3]{0:T(128)S(1)} %pad_add_fusion.1.at_ref, f32[1,3584,256]{2,1,0:T(8,128)S(1)} %copy-done.1, f32[1,3584,256]{2,1,0:T(8,128)} %collective-permute-done.1.b_ref), custom_call_target="tpu_custom_call" | custom-call | flops 917504 | bytes 9175040 | tf_op jit(solution)/shard_map/pallas_call | solution.py:84
  34.6 1.3 copy-done.2
  35.9 21.3 %all-to-all-done.k_ref = bf16[8,28,16,256]{3,2,1,0:T(8,128)(2,1)S(1)} async-done(((bf16[8,28,16,256]{3,2,1,0:T(8,128)(2,1)}), bf16[8,28,16,256]{3,2,1,0:T(8,128)(2,1)S(1)}, u32[]{:S(2)}, u32[]{:S(2)}) %all-to-all-start) | async-done | bytes 1835040 | tf_op jit(solution)/shard_map/all_to_all | solution.py:480
  57.2 1.1 shard_map.72
  58.4 3.4 %collective-permute-start.2 = (bf16[2,14,16,256]{3,2,1,0:T(8,128)(2,1)S(1)}, bf16[2,14,16,256]{3,2,1,0:T(8,128)(2,1)S(1)}, u32[]{:S(2)}, u32[]{:S(2)}) collective-permute-start(bf16[2,14,16,256]{3,2,1,0:T(8,128)(2,1)S(1)} %bitcast.48), channel_id=1, source_target_pairs={{0,16},{16,0},{1,17},{17,1},{2,18},{18,2},{3,19},{19,3},{4,20},{20... | collective-permute-start | bytes 688136 | tf_op jit(solution)/shard_map/ppermute | solution.py:108
  61.8 4.8 %collective-permute-done.2 = bf16[2,14,16,256]{3,2,1,0:T(8,128)(2,1)S(1)} collective-permute-done((bf16[2,14,16,256]{3,2,1,0:T(8,128)(2,1)S(1)}, bf16[2,14,16,256]{3,2,1,0:T(8,128)(2,1)S(1)}, u32[]{:S(2)}, u32[]{:S(2)}) %collective-permute-start.2) | collective-permute-done | bytes 229408 | tf_op jit(solution)/shard_map/ppermute | solution.py:108
  66.6 3.6 %all-to-all-start.1 = ((bf16[8,28,16,256]{3,2,1,0:T(8,128)(2,1)}), bf16[8,28,16,256]{3,2,1,0:T(8,128)(2,1)S(1)}, u32[]{:S(2)}, u32[]{:S(2)}) async-start(bf16[8,28,16,256]{3,2,1,0:T(8,128)(2,1)} %copy-done.2), calls=%async_computation.1 | async-start | bytes 3670016 | tf_op jit(solution)/shard_map/all_to_all | solution.py:488
  70.7 3.2 %collective-permute-start.3 = (bf16[2,2,14,16,256]{4,3,2,1,0:T(8,128)(2,1)S(1)}, bf16[2,2,14,16,256]{4,3,2,1,0:T(8,128)(2,1)S(1)}, u32[]{:S(2)}, u32[]{:S(2)}) collective-permute-start(bf16[2,2,14,16,256]{4,3,2,1,0:T(8,128)(2,1)S(1)} %pad_maximum_fusion.refs_0_), channel_id=1, source_target_pairs={{0,32},{32,64},{64,96},{1,33},{33,65},{65,97},{2,34},{34,66},{66,9... | collective-permute-start | bytes 1376264 | tf_op jit(solution)/shard_map/ppermute | solution.py:491
  73.9 4.5 %collective-permute-start.4 = (bf16[2,2,14,16,256]{4,3,2,1,0:T(8,128)(2,1)S(1)}, bf16[2,2,14,16,256]{4,3,2,1,0:T(8,128)(2,1)S(1)}, u32[]{:S(2)}, u32[]{:S(2)}) collective-permute-start(bf16[2,2,14,16,256]{4,3,2,1,0:T(8,128)(2,1)S(1)} %pad_maximum_fusion.refs_0_), channel_id=1, source_target_pairs={{0,64},{96,32},{1,65},{97,33},{2,66},{98,34},{3,67},{99,35},{4,68}... | collective-permute-start | bytes 1376264 | tf_op jit(solution)/shard_map/ppermute | solution.py:491
  78.4 1.3 collective-permute-start.5
  79.8 2.1 %collective-permute-done.3.refs_1_ = bf16[2,2,14,16,256]{4,3,2,1,0:T(8,128)(2,1)S(1)} collective-permute-done((bf16[2,2,14,16,256]{4,3,2,1,0:T(8,128)(2,1)S(1)}, bf16[2,2,14,16,256]{4,3,2,1,0:T(8,128)(2,1)S(1)}, u32[]{:S(2)}, u32[]{:S(2)}) %collective-permute-start.3) | collective-permute-done | bytes 458784 | tf_op jit(solution)/shard_map/ppermute | solution.py:491
  81.9 9.9 %collective-permute-done.4.refs_2_ = bf16[2,2,14,16,256]{4,3,2,1,0:T(8,128)(2,1)S(1)} collective-permute-done((bf16[2,2,14,16,256]{4,3,2,1,0:T(8,128)(2,1)S(1)}, bf16[2,2,14,16,256]{4,3,2,1,0:T(8,128)(2,1)S(1)}, u32[]{:S(2)}, u32[]{:S(2)}) %collective-permute-start.4) | collective-permute-done | bytes 458784 | tf_op jit(solution)/shard_map/ppermute | solution.py:491
  93.3 2.6 %all-to-all-done.1.p_ref = bf16[8,28,16,256]{3,2,1,0:T(8,128)(2,1)S(1)} async-done(((bf16[8,28,16,256]{3,2,1,0:T(8,128)(2,1)}), bf16[8,28,16,256]{3,2,1,0:T(8,128)(2,1)S(1)}, u32[]{:S(2)}, u32[]{:S(2)}) %all-to-all-start.1) | async-done | bytes 1835040 | tf_op jit(solution)/shard_map/all_to_all | solution.py:488
  95.9 1.0 copy-done.5
  97.0 1.0 copy-done.7
  98.0 1.7 shard_map.73
  99.7 2.1 %collective-permute-start.6 = (bf16[14,16,256]{2,1,0:T(8,128)(2,1)S(1)}, bf16[14,16,256]{2,1,0:T(8,128)(2,1)S(1)}, u32[]{:S(2)}, u32[]{:S(2)}) collective-permute-start(bf16[14,16,256]{2,1,0:T(8,128)(2,1)S(1)} %get-tuple-element.34), channel_id=1, source_target_pairs={{0,1},{1,0},{2,3},{3,2},{4,5},{5,4},{6,7},{7,6},{8,9},{9,8},{10,11... | collective-permute-start | bytes 344072 | tf_op jit(solution)/shard_map/ppermute | solution.py:504
  101.8 1.0 collective-permute-done.6
  102.9 1.8 collective-permute-start.8
  104.6 1.2 collective-permute-start.9
  105.8 1.3 collective-permute-start.11
  107.1 2.1 %collective-permute-done.7 = bf16[2,7,16,256]{3,2,1,0:T(8,128)(2,1)S(1)} collective-permute-done((bf16[2,7,16,256]{3,2,1,0:T(8,128)(2,1)S(1)}, bf16[2,7,16,256]{3,2,1,0:T(8,128)(2,1)S(1)}, u32[]{:S(2)}, u32[]{:S(2)}) %collective-permute-start.7) | collective-permute-done | bytes 114720 | tf_op jit(solution)/shard_map/ppermute | solution.py:108
  110.0 1.1 collective-permute-done.9
  111.4 1.1 collective-permute-start.12
  112.5 3.6 %collective-permute-start.13 = (bf16[2,2,7,16,256]{4,3,2,1,0:T(8,128)(2,1)S(1)}, bf16[2,2,7,16,256]{4,3,2,1,0:T(8,128)(2,1)S(1)}, u32[]{:S(2)}, u32[]{:S(2)}) collective-permute-start(bf16[2,2,7,16,256]{4,3,2,1,0:T(8,128)(2,1)S(1)} %pad_maximum_fusion.2.refs_2_), channel_id=1, source_target_pairs={{0,8},{4,12},{8,0},{12,4},{1,9},{5,13},{9,1},{13,5},{2,10},{6,14},... | collective-permute-start | bytes 688136 | tf_op jit(solution)/shard_map/ppermute | solution.py:108
  116.1 3.6 %collective-permute-done.12.refs_3_ = bf16[2,2,7,16,256]{4,3,2,1,0:T(8,128)(2,1)S(1)} collective-permute-done((bf16[2,2,7,16,256]{4,3,2,1,0:T(8,128)(2,1)S(1)}, bf16[2,2,7,16,256]{4,3,2,1,0:T(8,128)(2,1)S(1)}, u32[]{:S(2)}, u32[]{:S(2)}) %collective-permute-start.12) | collective-permute-done | bytes 229408 | tf_op jit(solution)/shard_map/ppermute | solution.py:108
  119.7 6.4 %collective-permute-done.13.refs_4_ = bf16[2,2,7,16,256]{4,3,2,1,0:T(8,128)(2,1)S(1)} collective-permute-done((bf16[2,2,7,16,256]{4,3,2,1,0:T(8,128)(2,1)S(1)}, bf16[2,2,7,16,256]{4,3,2,1,0:T(8,128)(2,1)S(1)}, u32[]{:S(2)}, u32[]{:S(2)}) %collective-permute-start.13) | collective-permute-done | bytes 229408 | tf_op jit(solution)/shard_map/ppermute | solution.py:108
  126.1 8.7 %shard_map.74 = (f32[2,448,512]{2,1,0:T(8,128)}, f32[2,1,512]{2,1,0:T(1,128)S(1)}, s16[8,2,56,512]{3,2,1,0:T(8,128)(2,1)}) custom-call(s32[3]{0:T(128)S(1)} %pad_add_fusion.1.at_ref, bf16[3584,1792]{1,0:T(8,128)(2,1)} %f_ref.1, bf16[4,2,7,16,256]{4,3,2,1,0:T(8,128)(2,1)S(1)} %pad_maximum_fusion.1.refs_0_, ...), custom_call_target="tpu_custom_call" | custom-call | flops 3758096384 | bytes 6881280 | tf_op jit(solution)/shard_map/pallas_call | solution.py:260
  134.9 5.3 %all-to-all-start.2 = ((s16[8,2,56,512]{3,2,1,0:T(8,128)(2,1)}), s16[8,2,56,512]{3,2,1,0:T(8,128)(2,1)S(1)}, u32[]{:S(2)}, u32[]{:S(2)}) async-start(s16[8,2,56,512]{3,2,1,0:T(8,128)(2,1)} %get-tuple-element.36), calls=%async_computation.2 | async-start | bytes 1835008 | tf_op jit(solution)/shard_map/all_to_all | solution.py:518
  140.1 12.5 %shard_map.75.a_ref = f32[2,448,512]{2,1,0:T(8,128)S(1)} custom-call(f32[2,448,512]{2,1,0:T(8,128)S(1)} %copy-done.8, bf16[2,112,512]{2,1,0:T(8,128)(2,1)S(1)} %maximum_select_fusion.1.after_ref.own_ref), custom_call_target="tpu_custom_call" | custom-call | flops 16499999744 | bytes 3670016 | tf_op jit(solution)/shard_map/pallas_call | solution.py:406
  152.7 1.3 copy-done.13
  154.0 1.0 broadcast_in_dim.28
  155.0 5.1 %all-to-all-start.3 = ((s16[8,2,56,512]{3,2,1,0:T(8,128)(2,1)}), s16[8,2,56,512]{3,2,1,0:T(8,128)(2,1)S(1)}, u32[]{:S(2)}, u32[]{:S(2)}) async-start(s16[8,2,56,512]{3,2,1,0:T(8,128)(2,1)} %broadcast_in_dim.28), calls=%async_computation.3 | async-start | bytes 1835008 | tf_op jit(solution)/shard_map/all_to_all | solution.py:521
  160.1 1.5 copy-done.14
  161.6 16.5 %shard_map.76.w_ref = f32[2,448,512]{2,1,0:T(8,128)S(1)} custom-call(f32[2,448,512]{2,1,0:T(8,128)S(1)} %copy-done.14, f32[8,128]{1,0:T(8,128)S(1)} %fusion.2.after_ref), custom_call_target="tpu_custom_call" | custom-call | flops 22000001024 | bytes 3670016 | tf_op jit(solution)/shard_map/pallas_call | solution.py:406
  178.2 1.3 copy-done.11
  179.4 1.5 copy-done.12
  180.9 2.7 %shard_map.77 = (f32[2,84,448]{2,1,0:T(8,128)S(1)}, f32[2,84,448]{2,1,0:T(8,128)S(1)}) custom-call(s32[3]{0:T(128)S(1)} %pad_add_fusion.1.at_ref, f32[2,448,512]{2,1,0:T(8,128)S(1)} %copy-done.12, f32[2,1,512]{2,1,0:T(1,128)S(1)} %get-tuple-element.37.root_ref, bf16[2,112,512]{2,1,0:T(8,128)(2,1)S(1)} %maximum_select_fusion.1.after_ref.own_ref, ...), custom_call_target="tpu_custom_call" | custom-call | flops 2000000000 | bytes 3670016 | tf_op jit(solution)/shard_map/pallas_call | solution.py:452
  183.7 1.4 collective-permute-start.15
  185.1 1.3 collective-permute-done.15
  (59 shorter events, 5.5 us)
Async XLA Ops:
  0.7 1.4 copy-start.9
  2.1 8.0 %copy-start.10 = (bf16[1792,448]{0,1:T(8,128)(2,1)S(1)}, bf16[1792,448]{0,1:T(8,128)(2,1)}, u32[]{:S(2)}) copy-start(bf16[1792,448]{0,1:T(8,128)(2,1)} %param.7) | copy-start | bytes 4816900
  8.7 12.3 %collective-permute-start = (f32[2,1792,256]{2,1,0:T(8,128)S(1)}, f32[2,1792,256]{2,1,0:T(8,128)S(1)}, u32[]{:S(2)}, u32[]{:S(2)}) collective-permute-start(f32[2,1792,256]{2,1,0:T(8,128)S(1)} %get-tuple-element.22), channel_id=1, source_target_pairs={{0,1},{1,0},{2,3},{3,2},{4,5},{5,4},{6,7},{7,6},{8,9},{9,8},{10,11... | collective-permute-start | bytes 11010056 | tf_op jit(solution)/shard_map/ppermute | solution.py:476
  20.9 1.8 copy-start
  20.9 8.6 %collective-permute-start.1 = (f32[1,3584,256]{2,1,0:T(8,128)}, f32[1,3584,256]{2,1,0:T(8,128)}, u32[]{:S(2)}, u32[]{:S(2)}) collective-permute-start(f32[1,3584,256]{2,1,0:T(8,128)} %get-tuple-element.25), channel_id=1, source_target_pairs={{0,1},{1,0},{2,3},{3,2},{4,5},{5,4},{6,7},{7,6},{8,9},{9,8},{10,11... | collective-permute-start | bytes 11010056 | tf_op jit(solution)/shard_map/ppermute | solution.py:478
  22.7 1.3 copy-start.3
  24.1 33.2 %all-to-all-start = ((bf16[8,28,16,256]{3,2,1,0:T(8,128)(2,1)}), bf16[8,28,16,256]{3,2,1,0:T(8,128)(2,1)S(1)}, u32[]{:S(2)}, u32[]{:S(2)}) async-start(bf16[8,28,16,256]{3,2,1,0:T(8,128)(2,1)} %copy-done.3), calls=%async_computation | async-start | bytes 3670016 | tf_op jit(solution)/shard_map/all_to_all | solution.py:480
  29.5 2.0 %copy-start.1 = (f32[1,3584,256]{2,1,0:T(8,128)S(1)}, f32[1,3584,256]{2,1,0:T(8,128)}, u32[]{:S(2)}) copy-start(f32[1,3584,256]{2,1,0:T(8,128)} %copy-done) | copy-start | bytes 11010052
  34.6 1.3 copy-start.2
  58.4 11.8 %copy-start.15 = (s32[2,112]{1,0:T(2,128)S(1)}, s32[2,112]{1,0:T(2,128)}, u32[]{:S(2)}) copy-start(s32[2,112]{1,0:T(2,128)} %param.9) | copy-start | bytes 2692
  58.4 8.2 %collective-permute-start.2 = (bf16[2,14,16,256]{3,2,1,0:T(8,128)(2,1)S(1)}, bf16[2,14,16,256]{3,2,1,0:T(8,128)(2,1)S(1)}, u32[]{:S(2)}, u32[]{:S(2)}) collective-permute-start(bf16[2,14,16,256]{3,2,1,0:T(8,128)(2,1)S(1)} %bitcast.48), channel_id=1, source_target_pairs={{0,16},{16,0},{1,17},{17,1},{2,18},{18,2},{3,19},{19,3},{4,20},{20... | collective-permute-start | bytes 688136 | tf_op jit(solution)/shard_map/ppermute | solution.py:108
  66.6 29.4 %all-to-all-start.1 = ((bf16[8,28,16,256]{3,2,1,0:T(8,128)(2,1)}), bf16[8,28,16,256]{3,2,1,0:T(8,128)(2,1)S(1)}, u32[]{:S(2)}, u32[]{:S(2)}) async-start(bf16[8,28,16,256]{3,2,1,0:T(8,128)(2,1)} %copy-done.2), calls=%async_computation.1 | async-start | bytes 3670016 | tf_op jit(solution)/shard_map/all_to_all | solution.py:488
  70.7 11.2 %collective-permute-start.3 = (bf16[2,2,14,16,256]{4,3,2,1,0:T(8,128)(2,1)S(1)}, bf16[2,2,14,16,256]{4,3,2,1,0:T(8,128)(2,1)S(1)}, u32[]{:S(2)}, u32[]{:S(2)}) collective-permute-start(bf16[2,2,14,16,256]{4,3,2,1,0:T(8,128)(2,1)S(1)} %pad_maximum_fusion.refs_0_), channel_id=1, source_target_pairs={{0,32},{32,64},{64,96},{1,33},{33,65},{65,97},{2,34},{34,66},{66,9... | collective-permute-start | bytes 1376264 | tf_op jit(solution)/shard_map/ppermute | solution.py:491
  73.9 17.9 %collective-permute-start.4 = (bf16[2,2,14,16,256]{4,3,2,1,0:T(8,128)(2,1)S(1)}, bf16[2,2,14,16,256]{4,3,2,1,0:T(8,128)(2,1)S(1)}, u32[]{:S(2)}, u32[]{:S(2)}) collective-permute-start(bf16[2,2,14,16,256]{4,3,2,1,0:T(8,128)(2,1)S(1)} %pad_maximum_fusion.refs_0_), channel_id=1, source_target_pairs={{0,64},{96,32},{1,65},{97,33},{2,66},{98,34},{3,67},{99,35},{4,68}... | collective-permute-start | bytes 1376264 | tf_op jit(solution)/shard_map/ppermute | solution.py:491
  78.4 14.1 %collective-permute-start.5 = (bf16[2,2,14,16,256]{4,3,2,1,0:T(8,128)(2,1)S(1)}, bf16[2,2,14,16,256]{4,3,2,1,0:T(8,128)(2,1)S(1)}, u32[]{:S(2)}, u32[]{:S(2)}) collective-permute-start(bf16[2,2,14,16,256]{4,3,2,1,0:T(8,128)(2,1)S(1)} %pad_maximum_fusion.refs_0_), channel_id=1, source_target_pairs={{32,0},{64,32},{96,64},{33,1},{65,33},{97,65},{34,2},{66,34},{98,6... | collective-permute-start | bytes 1376264 | tf_op jit(solution)/shard_map/ppermute | solution.py:491
  91.8 0.8 copy-start.4
  92.6 0.8 copy-start.6
  95.9 1.0 copy-start.5
  97.0 1.0 copy-start.7
  99.7 3.1 %collective-permute-start.6 = (bf16[14,16,256]{2,1,0:T(8,128)(2,1)S(1)}, bf16[14,16,256]{2,1,0:T(8,128)(2,1)S(1)}, u32[]{:S(2)}, u32[]{:S(2)}) collective-permute-start(bf16[14,16,256]{2,1,0:T(8,128)(2,1)S(1)} %get-tuple-element.34), channel_id=1, source_target_pairs={{0,1},{1,0},{2,3},{3,2},{4,5},{5,4},{6,7},{7,6},{8,9},{9,8},{10,11... | collective-permute-start | bytes 344072 | tf_op jit(solution)/shard_map/ppermute | solution.py:504
  102.8 6.5 %collective-permute-start.7 = (bf16[2,7,16,256]{3,2,1,0:T(8,128)(2,1)S(1)}, bf16[2,7,16,256]{3,2,1,0:T(8,128)(2,1)S(1)}, u32[]{:S(2)}, u32[]{:S(2)}) collective-permute-start(bf16[2,7,16,256]{3,2,1,0:T(8,128)(2,1)S(1)} %get-tuple-element.55), channel_id=1, source_target_pairs={{0,4},{4,8},{8,12},{12,0},{1,5},{5,9},{9,13},{13,1},{2,6},{6,10},{... | collective-permute-start | bytes 344072 | tf_op jit(solution)/shard_map/ppermute | solution.py:108
  102.9 7.2 %collective-permute-start.8 = (bf16[2,7,16,256]{3,2,1,0:T(8,128)(2,1)S(1)}, bf16[2,7,16,256]{3,2,1,0:T(8,128)(2,1)S(1)}, u32[]{:S(2)}, u32[]{:S(2)}) collective-permute-start(bf16[2,7,16,256]{3,2,1,0:T(8,128)(2,1)S(1)} %get-tuple-element.55), channel_id=1, source_target_pairs={{0,8},{4,12},{8,0},{12,4},{1,9},{5,13},{9,1},{13,5},{2,10},{6,14},... | collective-permute-start | bytes 344072 | tf_op jit(solution)/shard_map/ppermute | solution.py:108
  104.6 6.5 %collective-permute-start.9 = (bf16[2,7,16,256]{3,2,1,0:T(8,128)(2,1)S(1)}, bf16[2,7,16,256]{3,2,1,0:T(8,128)(2,1)S(1)}, u32[]{:S(2)}, u32[]{:S(2)}) collective-permute-start(bf16[2,7,16,256]{3,2,1,0:T(8,128)(2,1)S(1)} %get-tuple-element.55), channel_id=1, source_target_pairs={{0,12},{4,0},{8,4},{12,8},{1,13},{5,1},{9,5},{13,9},{2,14},{6,2},{... | collective-permute-start | bytes 344072 | tf_op jit(solution)/shard_map/ppermute | solution.py:108
  105.8 5.5 %collective-permute-start.11 = (bf16[2,7,16,256]{3,2,1,0:T(8,128)(2,1)S(1)}, bf16[2,7,16,256]{3,2,1,0:T(8,128)(2,1)S(1)}, u32[]{:S(2)}, u32[]{:S(2)}) collective-permute-start(bf16[2,7,16,256]{3,2,1,0:T(8,128)(2,1)S(1)} %get-tuple-element.49), channel_id=1, source_target_pairs={{0,2},{2,0},{1,3},{3,1},{4,6},{6,4},{5,7},{7,5},{8,10},{10,8},{9,1... | collective-permute-start | bytes 344072 | tf_op jit(solution)/shard_map/ppermute | solution.py:108
  111.2 14.9 %collective-permute-start.10 = (bf16[4,2,7,16,256]{4,3,2,1,0:T(8,128)(2,1)S(1)}, bf16[4,2,7,16,256]{4,3,2,1,0:T(8,128)(2,1)S(1)}, u32[]{:S(2)}, u32[]{:S(2)}) collective-permute-start(bf16[4,2,7,16,256]{4,3,2,1,0:T(8,128)(2,1)S(1)} %pad_maximum_fusion.1.refs_0_), channel_id=1, source_target_pairs={{0,2},{2,0},{1,3},{3,1},{4,6},{6,4},{5,7},{7,5},{8,10},{10,8},{9,1... | collective-permute-start | bytes 1376264 | tf_op jit(solution)/shard_map/ppermute | solution.py:108
  111.4 8.3 %collective-permute-start.12 = (bf16[2,2,7,16,256]{4,3,2,1,0:T(8,128)(2,1)S(1)}, bf16[2,2,7,16,256]{4,3,2,1,0:T(8,128)(2,1)S(1)}, u32[]{:S(2)}, u32[]{:S(2)}) collective-permute-start(bf16[2,2,7,16,256]{4,3,2,1,0:T(8,128)(2,1)S(1)} %pad_maximum_fusion.2.refs_2_), channel_id=1, source_target_pairs={{0,4},{4,8},{8,12},{12,0},{1,5},{5,9},{9,13},{13,1},{2,6},{6,10},{... | collective-permute-start | bytes 688136 | tf_op jit(solution)/shard_map/ppermute | solution.py:108
  112.5 13.7 %collective-permute-start.13 = (bf16[2,2,7,16,256]{4,3,2,1,0:T(8,128)(2,1)S(1)}, bf16[2,2,7,16,256]{4,3,2,1,0:T(8,128)(2,1)S(1)}, u32[]{:S(2)}, u32[]{:S(2)}) collective-permute-start(bf16[2,2,7,16,256]{4,3,2,1,0:T(8,128)(2,1)S(1)} %pad_maximum_fusion.2.refs_2_), channel_id=1, source_target_pairs={{0,8},{4,12},{8,0},{12,4},{1,9},{5,13},{9,1},{13,5},{2,10},{6,14},... | collective-permute-start | bytes 688136 | tf_op jit(solution)/shard_map/ppermute | solution.py:108
  116.0 10.1 %collective-permute-start.14 = (bf16[2,2,7,16,256]{4,3,2,1,0:T(8,128)(2,1)S(1)}, bf16[2,2,7,16,256]{4,3,2,1,0:T(8,128)(2,1)S(1)}, u32[]{:S(2)}, u32[]{:S(2)}) collective-permute-start(bf16[2,2,7,16,256]{4,3,2,1,0:T(8,128)(2,1)S(1)} %pad_maximum_fusion.2.refs_2_), channel_id=1, source_target_pairs={{0,12},{4,0},{8,4},{12,8},{1,13},{5,1},{9,5},{13,9},{2,14},{6,2},{... | collective-permute-start | bytes 688136 | tf_op jit(solution)/shard_map/ppermute | solution.py:108
  134.9 5.3 %copy-start.8 = (f32[2,448,512]{2,1,0:T(8,128)S(1)}, f32[2,448,512]{2,1,0:T(8,128)}, u32[]{:S(2)}) copy-start(f32[2,448,512]{2,1,0:T(8,128)} %get-tuple-element.35.a_ref) | copy-start | bytes 5505028
  134.9 19.1 %all-to-all-start.2 = ((s16[8,2,56,512]{3,2,1,0:T(8,128)(2,1)}), s16[8,2,56,512]{3,2,1,0:T(8,128)(2,1)S(1)}, u32[]{:S(2)}, u32[]{:S(2)}) async-start(s16[8,2,56,512]{3,2,1,0:T(8,128)(2,1)} %get-tuple-element.36), calls=%async_computation.2 | async-start | bytes 1835008 | tf_op jit(solution)/shard_map/all_to_all | solution.py:518
  152.7 1.3 copy-start.13
  155.0 24.5 %all-to-all-start.3 = ((s16[8,2,56,512]{3,2,1,0:T(8,128)(2,1)}), s16[8,2,56,512]{3,2,1,0:T(8,128)(2,1)S(1)}, u32[]{:S(2)}, u32[]{:S(2)}) async-start(s16[8,2,56,512]{3,2,1,0:T(8,128)(2,1)} %broadcast_in_dim.28), calls=%async_computation.3 | async-start | bytes 1835008 | tf_op jit(solution)/shard_map/all_to_all | solution.py:521
  160.1 1.5 copy-start.14
  178.2 1.3 copy-start.11
  179.4 1.5 copy-start.12
  183.7 2.7 %collective-permute-start.15 = (f32[2,84,448]{2,1,0:T(8,128)S(1)}, f32[2,84,448]{2,1,0:T(8,128)S(1)}, u32[]{:S(2)}, u32[]{:S(2)}) collective-permute-start(f32[2,84,448]{2,1,0:T(8,128)S(1)} %get-tuple-element.39), channel_id=1, source_target_pairs={{0,1},{1,0},{2,3},{3,2},{4,5},{5,4},{6,7},{7,6},{8,9},{9,8},{10,11... | collective-permute-start | bytes 903176 | tf_op jit(solution)/shard_map/ppermute | solution.py:524

commit v9 on v6

--- a/solution.py
+++ b/solution.py
@@ -455,7 +455,7 @@
         out_shape=[part, part],
         in_specs=[SMEM, whole(inverse), whole(root), whole(own), whole(cross)],
         out_specs=[whole(part)] * 2,
-        compiler_params=params(24),
+        compiler_params=params(56),
         cost_estimate=cost(2e9, 4 * (inverse.size + cross.size)),
     )(at, inverse, root, own, cross)
 

time: 183 us -> 183 us (level)
  local copies, waits for them, and re-layouts: 14.4 us -> 11.5 us
  Pallas kernels: 61.8 us -> 64 us
    unnamed x27 -> x31, local copies, waits for them, and re-layouts: 12.6 us -> 9.65 us
    pallas_call x1, Pallas kernels: 2.72 us -> 4.9 us  [finish(): pl.pallas_call(finish_kernel, grid=(1,), out_shape=[part, part], in_specs...]
  transfers between devices with their start and end apart: 19 -> 19, of which waited for: 11 -> 11; matrix products, arithmetic and copies ran while one was open for 0% -> 0% of each run, Pallas kernels for 24% -> 23%
where the time goes in v9:
time: 183 us; the launch traced here: 180 us
  Pallas kernels  64 us (35%)
  starting transfers between devices  41.7 us (23%)
  waiting for transfers between devices  31.3 us (17%)
  blocking collectives  28.4 us (16%)
  local copies, waits for them, and re-layouts  11.5 us (6%)
  other arithmetic  1.97 us (1%)
    pallas_call x2, Pallas kernels, factor_inverse(): pl.pallas_call(functools.partial(inverse_kernel, first=first, last=last),...  29 us
    all_to_all x1, blocking collectives, local(): kid_share = lax.all_to_all(kid_part, CHIP, 0, 0, tiled=True)  28.4 us
    pallas_call x2, Pallas kernels, probe(): pl.pallas_call(probe_kernel, grid=(count, rows // LEAF), out_shape=[part,...  15.9 us
    ppermute x9, waiting for transfers between devices, shift(): lax.ppermute(value, axis, [(i, (i + by) % size) for i in range(size)])  14.9 us
    ppermute x9, starting transfers between devices, shift(): lax.ppermute(value, axis, [(i, (i + by) % size) for i in range(size)])  13 us
    ppermute x3, waiting for transfers between devices, local(): lax.ppermute(pair, 'y', [(i, j) for i, j in reach if (j - i) % 4 == by])  11.5 us
    unnamed x31, local copies, waits for them, and re-layouts  9.65 us
    ppermute x3, starting transfers between devices, local(): lax.ppermute(pair, 'y', [(i, j) for i, j in reach if (j - i) % 4 == by])  9.05 us
  transfers between devices with their start and end apart: 19, of which 11 were waited for; matrix products, arithmetic and copies ran while one was open for 0% of the time, Pallas kernels for 23%

profile of v9, /device:TPU:1, one launch (start us, length us, event | category | flops | bytes accessed | tf_op | source)
XLA Modules:
  0.0 179.7 jit_solution(7946114308106838282)
XLA Ops:
  0.7 1.4 copy-done.8
  2.1 6.5 %shard_map.68 = (f32[2,1792,256]{2,1,0:T(8,128)S(1)}, f32[2,1792,256]{2,1,0:T(8,128)S(1)}) custom-call(s32[3]{0:T(128)S(1)} %pad_add_fusion.1.at_ref, bf16[2,1792,896]{2,1,0:T(8,128)(2,1)} %a_ref.1, bf16[2,448,896]{2,1,0:T(8,128)(2,1)S(1)} %bitcast.51), custom_call_target="tpu_custom_call" | custom-call | flops 3288334336 | bytes 13762560 | tf_op jit(solution)/shard_map/pallas_call | solution.py:50
  8.7 1.5 collective-permute-start
  10.2 9.4 %shard_map.71 = (f32[1,3584,256]{2,1,0:T(8,128)S(1)}, f32[1,3584,256]{2,1,0:T(8,128)S(1)}) custom-call(s32[3]{0:T(128)S(1)} %pad_add_fusion.1.at_ref, bf16[1,3584,1792]{2,1,0:T(8,128)(2,1)} %bitcast.53, bf16[1,448,1792]{2,1,0:T(8,128)(2,1)S(1)} %bitcast.52), custom_call_target="tpu_custom_call" | custom-call | flops 6576668672 | bytes 20185088 | tf_op jit(solution)/shard_map/pallas_call | solution.py:50
  19.7 1.3 shard_map.69
  21.0 28.4 %all_to_all.20.k_ref = bf16[8,28,16,256]{3,2,1,0:T(8,128)(2,1)S(1)} all-to-all(bf16[8,28,16,256]{3,2,1,0:T(8,128)(2,1)S(1)} %get-tuple-element.21), channel_id=1, replica_groups=mesh['y'=4,'zh'=2,'x'=4,'zl'=2,'core'=2] {'x','zl'}, dimensions={0} | all-to-all | bytes 3670016 | tf_op jit(solution)/shard_map/all_to_all | solution.py:480
  49.4 1.1 shard_map.70
  50.5 3.4 %collective-permute-start.1 = (bf16[2,14,16,256]{3,2,1,0:T(8,128)(2,1)S(1)}, bf16[2,14,16,256]{3,2,1,0:T(8,128)(2,1)S(1)}, u32[]{:S(2)}, u32[]{:S(2)}) collective-permute-start(bf16[2,14,16,256]{3,2,1,0:T(8,128)(2,1)S(1)} %bitcast.48), channel_id=1, source_target_pairs={{0,16},{16,0},{1,17},{17,1},{2,18},{18,2},{3,19},{19,3},{4,20},{20... | collective-permute-start | bytes 688136 | tf_op jit(solution)/shard_map/ppermute | solution.py:108
  53.9 1.3 shard_map.72
  55.2 1.3 copy-done
  56.5 1.7 collective-permute-done.1
  58.2 3.7 %all-to-all-start.1 = ((bf16[8,28,16,256]{3,2,1,0:T(8,128)(2,1)}), bf16[8,28,16,256]{3,2,1,0:T(8,128)(2,1)S(1)}, u32[]{:S(2)}, u32[]{:S(2)}) async-start(bf16[8,28,16,256]{3,2,1,0:T(8,128)(2,1)} %copy-done), calls=%async_computation.1 | async-start | bytes 3670016 | tf_op jit(solution)/shard_map/all_to_all | solution.py:487
  62.4 3.2 %collective-permute-start.3 = (bf16[2,2,14,16,256]{4,3,2,1,0:T(8,128)(2,1)S(1)}, bf16[2,2,14,16,256]{4,3,2,1,0:T(8,128)(2,1)S(1)}, u32[]{:S(2)}, u32[]{:S(2)}) collective-permute-start(bf16[2,2,14,16,256]{4,3,2,1,0:T(8,128)(2,1)S(1)} %pad_maximum_fusion.refs_0_), channel_id=1, source_target_pairs={{0,32},{32,64},{64,96},{1,33},{33,65},{65,97},{2,34},{34,66},{66,9... | collective-permute-start | bytes 1376264 | tf_op jit(solution)/shard_map/ppermute | solution.py:490
  65.6 4.5 %collective-permute-start.4 = (bf16[2,2,14,16,256]{4,3,2,1,0:T(8,128)(2,1)S(1)}, bf16[2,2,14,16,256]{4,3,2,1,0:T(8,128)(2,1)S(1)}, u32[]{:S(2)}, u32[]{:S(2)}) collective-permute-start(bf16[2,2,14,16,256]{4,3,2,1,0:T(8,128)(2,1)S(1)} %pad_maximum_fusion.refs_0_), channel_id=1, source_target_pairs={{0,64},{96,32},{1,65},{97,33},{2,66},{98,34},{3,67},{99,35},{4,68}... | collective-permute-start | bytes 1376264 | tf_op jit(solution)/shard_map/ppermute | solution.py:490
  70.2 1.3 collective-permute-start.5
  71.6 1.6 collective-permute-done.3.refs_1_
  73.1 9.9 %collective-permute-done.4.refs_2_ = bf16[2,2,14,16,256]{4,3,2,1,0:T(8,128)(2,1)S(1)} collective-permute-done((bf16[2,2,14,16,256]{4,3,2,1,0:T(8,128)(2,1)S(1)}, bf16[2,2,14,16,256]{4,3,2,1,0:T(8,128)(2,1)S(1)}, u32[]{:S(2)}, u32[]{:S(2)}) %collective-permute-start.4) | collective-permute-done | bytes 458784 | tf_op jit(solution)/shard_map/ppermute | solution.py:490
  83.0 0.8 copy-done.1
  83.8 0.8 copy-done.3
  84.6 2.4 %all-to-all-done.1.p_ref = bf16[8,28,16,256]{3,2,1,0:T(8,128)(2,1)S(1)} async-done(((bf16[8,28,16,256]{3,2,1,0:T(8,128)(2,1)}), bf16[8,28,16,256]{3,2,1,0:T(8,128)(2,1)S(1)}, u32[]{:S(2)}, u32[]{:S(2)}) %all-to-all-start.1) | async-done | bytes 1835040 | tf_op jit(solution)/shard_map/all_to_all | solution.py:487
  87.0 1.0 copy-done.2
  88.0 1.0 copy-done.4
  89.1 1.7 shard_map.73
  90.7 2.4 %collective-permute-start.6 = (bf16[14,16,256]{2,1,0:T(8,128)(2,1)S(1)}, bf16[14,16,256]{2,1,0:T(8,128)(2,1)S(1)}, u32[]{:S(2)}, u32[]{:S(2)}) collective-permute-start(bf16[14,16,256]{2,1,0:T(8,128)(2,1)S(1)} %get-tuple-element.30), channel_id=1, source_target_pairs={{0,1},{1,0},{2,3},{3,2},{4,5},{5,4},{6,7},{7,6},{8,9},{9,8},{10,11... | collective-permute-start | bytes 344072 | tf_op jit(solution)/shard_map/ppermute | solution.py:503
  93.1 1.0 collective-permute-done.6
  94.2 2.2 %collective-permute-start.8 = (bf16[2,7,16,256]{3,2,1,0:T(8,128)(2,1)S(1)}, bf16[2,7,16,256]{3,2,1,0:T(8,128)(2,1)S(1)}, u32[]{:S(2)}, u32[]{:S(2)}) collective-permute-start(bf16[2,7,16,256]{3,2,1,0:T(8,128)(2,1)S(1)} %get-tuple-element.51), channel_id=1, source_target_pairs={{0,8},{4,12},{8,0},{12,4},{1,9},{5,13},{9,1},{13,5},{2,10},{6,14},... | collective-permute-start | bytes 344072 | tf_op jit(solution)/shard_map/ppermute | solution.py:108
  96.4 1.2 collective-permute-start.9
  97.6 1.3 collective-permute-start.11
  98.9 1.3 collective-permute-done.7
  100.2 1.6 collective-permute-done.8
  103.1 1.1 collective-permute-start.12
  104.2 3.0 %collective-permute-start.13 = (bf16[2,2,7,16,256]{4,3,2,1,0:T(8,128)(2,1)S(1)}, bf16[2,2,7,16,256]{4,3,2,1,0:T(8,128)(2,1)S(1)}, u32[]{:S(2)}, u32[]{:S(2)}) collective-permute-start(bf16[2,2,7,16,256]{4,3,2,1,0:T(8,128)(2,1)S(1)} %pad_maximum_fusion.2.refs_2_), channel_id=1, source_target_pairs={{0,8},{4,12},{8,0},{12,4},{1,9},{5,13},{9,1},{13,5},{2,10},{6,14},... | collective-permute-start | bytes 688136 | tf_op jit(solution)/shard_map/ppermute | solution.py:108
  107.5 2.8 %collective-permute-done.12.refs_3_ = bf16[2,2,7,16,256]{4,3,2,1,0:T(8,128)(2,1)S(1)} collective-permute-done((bf16[2,2,7,16,256]{4,3,2,1,0:T(8,128)(2,1)S(1)}, bf16[2,2,7,16,256]{4,3,2,1,0:T(8,128)(2,1)S(1)}, u32[]{:S(2)}, u32[]{:S(2)}) %collective-permute-start.12) | collective-permute-done | bytes 229408 | tf_op jit(solution)/shard_map/ppermute | solution.py:108
  110.3 6.8 %collective-permute-done.13.refs_4_ = bf16[2,2,7,16,256]{4,3,2,1,0:T(8,128)(2,1)S(1)} collective-permute-done((bf16[2,2,7,16,256]{4,3,2,1,0:T(8,128)(2,1)S(1)}, bf16[2,2,7,16,256]{4,3,2,1,0:T(8,128)(2,1)S(1)}, u32[]{:S(2)}, u32[]{:S(2)}) %collective-permute-start.13) | collective-permute-done | bytes 229408 | tf_op jit(solution)/shard_map/ppermute | solution.py:108
  117.1 8.7 %shard_map.74 = (f32[2,448,512]{2,1,0:T(8,128)}, f32[2,1,512]{2,1,0:T(1,128)S(1)}, s16[8,2,56,512]{3,2,1,0:T(8,128)(2,1)}) custom-call(s32[3]{0:T(128)S(1)} %pad_add_fusion.1.at_ref, bf16[3584,1792]{1,0:T(8,128)(2,1)} %f_ref.1, bf16[4,2,7,16,256]{4,3,2,1,0:T(8,128)(2,1)S(1)} %pad_maximum_fusion.1.refs_0_, ...), custom_call_target="tpu_custom_call" | custom-call | flops 3758096384 | bytes 6881280 | tf_op jit(solution)/shard_map/pallas_call | solution.py:260
  125.8 5.5 %all-to-all-start.2 = ((s16[8,2,56,512]{3,2,1,0:T(8,128)(2,1)}), s16[8,2,56,512]{3,2,1,0:T(8,128)(2,1)S(1)}, u32[]{:S(2)}, u32[]{:S(2)}) async-start(s16[8,2,56,512]{3,2,1,0:T(8,128)(2,1)} %get-tuple-element.32), calls=%async_computation.2 | async-start | bytes 1835008 | tf_op jit(solution)/shard_map/all_to_all | solution.py:517
  131.3 12.5 %shard_map.75.a_ref = f32[2,448,512]{2,1,0:T(8,128)S(1)} custom-call(f32[2,448,512]{2,1,0:T(8,128)S(1)} %copy-done.7, bf16[2,112,512]{2,1,0:T(8,128)(2,1)S(1)} %maximum_select_fusion.1.after_ref.own_ref), custom_call_target="tpu_custom_call" | custom-call | flops 16499999744 | bytes 3670016 | tf_op jit(solution)/shard_map/pallas_call | solution.py:406
  143.9 1.3 copy-done.12
  145.1 1.0 broadcast_in_dim.28
  146.2 5.1 %all-to-all-start.3 = ((s16[8,2,56,512]{3,2,1,0:T(8,128)(2,1)}), s16[8,2,56,512]{3,2,1,0:T(8,128)(2,1)}, u32[]{:S(2)}, u32[]{:S(2)}) async-start(s16[8,2,56,512]{3,2,1,0:T(8,128)(2,1)} %broadcast_in_dim.28), calls=%async_computation.3 | async-start | bytes 1835008 | tf_op jit(solution)/shard_map/all_to_all | solution.py:520
  151.3 16.5 %shard_map.76.w_ref = f32[2,448,512]{2,1,0:T(8,128)S(1)} custom-call(f32[2,448,512]{2,1,0:T(8,128)S(1)} %copy-done.13, f32[8,128]{1,0:T(8,128)S(1)} %fusion.2.after_ref), custom_call_target="tpu_custom_call" | custom-call | flops 22000001024 | bytes 3670016 | tf_op jit(solution)/shard_map/pallas_call | solution.py:406
  167.9 1.3 copy-done.11
  169.1 4.9 %shard_map.77 = (f32[2,84,448]{2,1,0:T(8,128)}, f32[2,84,448]{2,1,0:T(8,128)}) custom-call(s32[3]{0:T(128)} %copy-done.6, f32[2,448,512]{2,1,0:T(8,128)} %copy-done.11, f32[2,1,512]{2,1,0:T(1,128)} %copy-done.10, bf16[2,112,512]{2,1,0:T(8,128)(2,1)} %copy-done.5, s16[8,2,56,512]{3,2,1,0:T(8,128)(2,1)} %all-to-all-done.3.cross_ref), custom_call_target="tpu_custom_call" | custom-call | flops 2000000000 | bytes 3670016 | tf_op jit(solution)/shard_map/pallas_call | solution.py:452
  174.1 1.3 collective-permute-start.15
  175.4 1.5 collective-permute-done.15
  176.9 1.2 maximum_select_fusion
  178.1 0.7 slice.38
  178.8 0.8 copy.41
  (56 shorter events, 2.6 us)
Async XLA Ops:
  0.7 116.4 %copy-start.6 = (s32[3]{0:T(128)}, s32[3]{0:T(128)S(1)}, u32[]{:S(2)}) copy-start(s32[3]{0:T(128)S(1)} %pad_add_fusion.1.at_ref) | copy-start | bytes 40
  0.7 1.4 copy-start.8
  2.1 8.0 %copy-start.9 = (bf16[1792,448]{0,1:T(8,128)(2,1)S(1)}, bf16[1792,448]{0,1:T(8,128)(2,1)}, u32[]{:S(2)}) copy-start(bf16[1792,448]{0,1:T(8,128)(2,1)} %param.7) | copy-start | bytes 4816900
  8.7 11.0 %collective-permute-start = (f32[2,1792,256]{2,1,0:T(8,128)S(1)}, f32[2,1792,256]{2,1,0:T(8,128)S(1)}, u32[]{:S(2)}, u32[]{:S(2)}) collective-permute-start(f32[2,1792,256]{2,1,0:T(8,128)S(1)} %get-tuple-element.20), channel_id=1, source_target_pairs={{0,1},{1,0},{2,3},{3,2},{4,5},{5,4},{6,7},{7,6},{8,9},{9,8},{10,11... | collective-permute-start | bytes 11010056 | tf_op jit(solution)/shard_map/ppermute | solution.py:476
  19.6 34.3 %collective-permute-start.2 = (f32[1,3584,256]{2,1,0:T(8,128)S(1)}, f32[1,3584,256]{2,1,0:T(8,128)S(1)}, u32[]{:S(2)}, u32[]{:S(2)}) collective-permute-start(f32[1,3584,256]{2,1,0:T(8,128)S(1)} %get-tuple-element.24), channel_id=1, source_target_pairs={{0,1},{1,0},{2,3},{3,2},{4,5},{5,4},{6,7},{7,6},{8,9},{9,8},{10,11... | collective-permute-start | bytes 11010056 | tf_op jit(solution)/shard_map/ppermute | solution.py:478
  50.5 7.7 %collective-permute-start.1 = (bf16[2,14,16,256]{3,2,1,0:T(8,128)(2,1)S(1)}, bf16[2,14,16,256]{3,2,1,0:T(8,128)(2,1)S(1)}, u32[]{:S(2)}, u32[]{:S(2)}) collective-permute-start(bf16[2,14,16,256]{3,2,1,0:T(8,128)(2,1)S(1)} %bitcast.48), channel_id=1, source_target_pairs={{0,16},{16,0},{1,17},{17,1},{2,18},{18,2},{3,19},{19,3},{4,20},{20... | collective-permute-start | bytes 688136 | tf_op jit(solution)/shard_map/ppermute | solution.py:108
  55.2 1.3 copy-start
  58.2 3.8 %copy-start.14 = (s32[2,112]{1,0:T(2,128)S(1)}, s32[2,112]{1,0:T(2,128)}, u32[]{:S(2)}) copy-start(s32[2,112]{1,0:T(2,128)} %param.9) | copy-start | bytes 2692
  58.2 28.8 %all-to-all-start.1 = ((bf16[8,28,16,256]{3,2,1,0:T(8,128)(2,1)}), bf16[8,28,16,256]{3,2,1,0:T(8,128)(2,1)S(1)}, u32[]{:S(2)}, u32[]{:S(2)}) async-start(bf16[8,28,16,256]{3,2,1,0:T(8,128)(2,1)} %copy-done), calls=%async_computation.1 | async-start | bytes 3670016 | tf_op jit(solution)/shard_map/all_to_all | solution.py:487
  62.4 10.7 %collective-permute-start.3 = (bf16[2,2,14,16,256]{4,3,2,1,0:T(8,128)(2,1)S(1)}, bf16[2,2,14,16,256]{4,3,2,1,0:T(8,128)(2,1)S(1)}, u32[]{:S(2)}, u32[]{:S(2)}) collective-permute-start(bf16[2,2,14,16,256]{4,3,2,1,0:T(8,128)(2,1)S(1)} %pad_maximum_fusion.refs_0_), channel_id=1, source_target_pairs={{0,32},{32,64},{64,96},{1,33},{33,65},{65,97},{2,34},{34,66},{66,9... | collective-permute-start | bytes 1376264 | tf_op jit(solution)/shard_map/ppermute | solution.py:490
  65.6 17.4 %collective-permute-start.4 = (bf16[2,2,14,16,256]{4,3,2,1,0:T(8,128)(2,1)S(1)}, bf16[2,2,14,16,256]{4,3,2,1,0:T(8,128)(2,1)S(1)}, u32[]{:S(2)}, u32[]{:S(2)}) collective-permute-start(bf16[2,2,14,16,256]{4,3,2,1,0:T(8,128)(2,1)S(1)} %pad_maximum_fusion.refs_0_), channel_id=1, source_target_pairs={{0,64},{96,32},{1,65},{97,33},{2,66},{98,34},{3,67},{99,35},{4,68}... | collective-permute-start | bytes 1376264 | tf_op jit(solution)/shard_map/ppermute | solution.py:490
  70.2 13.6 %collective-permute-start.5 = (bf16[2,2,14,16,256]{4,3,2,1,0:T(8,128)(2,1)S(1)}, bf16[2,2,14,16,256]{4,3,2,1,0:T(8,128)(2,1)S(1)}, u32[]{:S(2)}, u32[]{:S(2)}) collective-permute-start(bf16[2,2,14,16,256]{4,3,2,1,0:T(8,128)(2,1)S(1)} %pad_maximum_fusion.refs_0_), channel_id=1, source_target_pairs={{32,0},{64,32},{96,64},{33,1},{65,33},{97,65},{34,2},{66,34},{98,6... | collective-permute-start | bytes 1376264 | tf_op jit(solution)/shard_map/ppermute | solution.py:490
  83.0 0.8 copy-start.1
  83.8 0.8 copy-start.3
  87.0 1.0 copy-start.2
  88.0 1.0 copy-start.4
  90.7 3.3 %collective-permute-start.6 = (bf16[14,16,256]{2,1,0:T(8,128)(2,1)S(1)}, bf16[14,16,256]{2,1,0:T(8,128)(2,1)S(1)}, u32[]{:S(2)}, u32[]{:S(2)}) collective-permute-start(bf16[14,16,256]{2,1,0:T(8,128)(2,1)S(1)} %get-tuple-element.30), channel_id=1, source_target_pairs={{0,1},{1,0},{2,3},{3,2},{4,5},{5,4},{6,7},{7,6},{8,9},{9,8},{10,11... | collective-permute-start | bytes 344072 | tf_op jit(solution)/shard_map/ppermute | solution.py:503
  94.1 6.1 %collective-permute-start.7 = (bf16[2,7,16,256]{3,2,1,0:T(8,128)(2,1)S(1)}, bf16[2,7,16,256]{3,2,1,0:T(8,128)(2,1)S(1)}, u32[]{:S(2)}, u32[]{:S(2)}) collective-permute-start(bf16[2,7,16,256]{3,2,1,0:T(8,128)(2,1)S(1)} %get-tuple-element.51), channel_id=1, source_target_pairs={{0,4},{4,8},{8,12},{12,0},{1,5},{5,9},{9,13},{13,1},{2,6},{6,10},{... | collective-permute-start | bytes 344072 | tf_op jit(solution)/shard_map/ppermute | solution.py:108
  94.2 7.6 %collective-permute-start.8 = (bf16[2,7,16,256]{3,2,1,0:T(8,128)(2,1)S(1)}, bf16[2,7,16,256]{3,2,1,0:T(8,128)(2,1)S(1)}, u32[]{:S(2)}, u32[]{:S(2)}) collective-permute-start(bf16[2,7,16,256]{3,2,1,0:T(8,128)(2,1)S(1)} %get-tuple-element.51), channel_id=1, source_target_pairs={{0,8},{4,12},{8,0},{12,4},{1,9},{5,13},{9,1},{13,5},{2,10},{6,14},... | collective-permute-start | bytes 344072 | tf_op jit(solution)/shard_map/ppermute | solution.py:108
  96.4 6.1 %collective-permute-start.9 = (bf16[2,7,16,256]{3,2,1,0:T(8,128)(2,1)S(1)}, bf16[2,7,16,256]{3,2,1,0:T(8,128)(2,1)S(1)}, u32[]{:S(2)}, u32[]{:S(2)}) collective-permute-start(bf16[2,7,16,256]{3,2,1,0:T(8,128)(2,1)S(1)} %get-tuple-element.51), channel_id=1, source_target_pairs={{0,12},{4,0},{8,4},{12,8},{1,13},{5,1},{9,5},{13,9},{2,14},{6,2},{... | collective-permute-start | bytes 344072 | tf_op jit(solution)/shard_map/ppermute | solution.py:108
  97.6 5.5 %collective-permute-start.11 = (bf16[2,7,16,256]{3,2,1,0:T(8,128)(2,1)S(1)}, bf16[2,7,16,256]{3,2,1,0:T(8,128)(2,1)S(1)}, u32[]{:S(2)}, u32[]{:S(2)}) collective-permute-start(bf16[2,7,16,256]{3,2,1,0:T(8,128)(2,1)S(1)} %get-tuple-element.45), channel_id=1, source_target_pairs={{0,2},{2,0},{1,3},{3,1},{4,6},{6,4},{5,7},{7,5},{8,10},{10,8},{9,1... | collective-permute-start | bytes 344072 | tf_op jit(solution)/shard_map/ppermute | solution.py:108
  102.5 14.6 %collective-permute-start.10 = (bf16[4,2,7,16,256]{4,3,2,1,0:T(8,128)(2,1)S(1)}, bf16[4,2,7,16,256]{4,3,2,1,0:T(8,128)(2,1)S(1)}, u32[]{:S(2)}, u32[]{:S(2)}) collective-permute-start(bf16[4,2,7,16,256]{4,3,2,1,0:T(8,128)(2,1)S(1)} %pad_maximum_fusion.1.refs_0_), channel_id=1, source_target_pairs={{0,2},{2,0},{1,3},{3,1},{4,6},{6,4},{5,7},{7,5},{8,10},{10,8},{9,1... | collective-permute-start | bytes 1376264 | tf_op jit(solution)/shard_map/ppermute | solution.py:108
  103.1 7.2 %collective-permute-start.12 = (bf16[2,2,7,16,256]{4,3,2,1,0:T(8,128)(2,1)S(1)}, bf16[2,2,7,16,256]{4,3,2,1,0:T(8,128)(2,1)S(1)}, u32[]{:S(2)}, u32[]{:S(2)}) collective-permute-start(bf16[2,2,7,16,256]{4,3,2,1,0:T(8,128)(2,1)S(1)} %pad_maximum_fusion.2.refs_2_), channel_id=1, source_target_pairs={{0,4},{4,8},{8,12},{12,0},{1,5},{5,9},{9,13},{13,1},{2,6},{6,10},{... | collective-permute-start | bytes 688136 | tf_op jit(solution)/shard_map/ppermute | solution.py:108
  104.2 12.9 %collective-permute-start.13 = (bf16[2,2,7,16,256]{4,3,2,1,0:T(8,128)(2,1)S(1)}, bf16[2,2,7,16,256]{4,3,2,1,0:T(8,128)(2,1)S(1)}, u32[]{:S(2)}, u32[]{:S(2)}) collective-permute-start(bf16[2,2,7,16,256]{4,3,2,1,0:T(8,128)(2,1)S(1)} %pad_maximum_fusion.2.refs_2_), channel_id=1, source_target_pairs={{0,8},{4,12},{8,0},{12,4},{1,9},{5,13},{9,1},{13,5},{2,10},{6,14},... | collective-permute-start | bytes 688136 | tf_op jit(solution)/shard_map/ppermute | solution.py:108
  107.2 9.9 %collective-permute-start.14 = (bf16[2,2,7,16,256]{4,3,2,1,0:T(8,128)(2,1)S(1)}, bf16[2,2,7,16,256]{4,3,2,1,0:T(8,128)(2,1)S(1)}, u32[]{:S(2)}, u32[]{:S(2)}) collective-permute-start(bf16[2,2,7,16,256]{4,3,2,1,0:T(8,128)(2,1)S(1)} %pad_maximum_fusion.2.refs_2_), channel_id=1, source_target_pairs={{0,12},{4,0},{8,4},{12,8},{1,13},{5,1},{9,5},{13,9},{2,14},{6,2},{... | collective-permute-start | bytes 688136 | tf_op jit(solution)/shard_map/ppermute | solution.py:108
  107.5 23.8 %copy-start.5 = (bf16[2,112,512]{2,1,0:T(8,128)(2,1)}, bf16[2,112,512]{2,1,0:T(8,128)(2,1)S(1)}, u32[]{:S(2)}) copy-start(bf16[2,112,512]{2,1,0:T(8,128)(2,1)S(1)} %maximum_select_fusion.1.after_ref.own_ref) | copy-start | bytes 688132
  125.8 18.0 %copy-start.10 = (f32[2,1,512]{2,1,0:T(1,128)}, f32[2,1,512]{2,1,0:T(1,128)S(1)}, u32[]{:S(2)}) copy-start(f32[2,1,512]{2,1,0:T(1,128)S(1)} %get-tuple-element.33.root_ref) | copy-start | bytes 12292
  125.8 5.5 %copy-start.7 = (f32[2,448,512]{2,1,0:T(8,128)S(1)}, f32[2,448,512]{2,1,0:T(8,128)}, u32[]{:S(2)}) copy-start(f32[2,448,512]{2,1,0:T(8,128)} %get-tuple-element.31.a_ref) | copy-start | bytes 5505028
  125.8 19.3 %all-to-all-start.2 = ((s16[8,2,56,512]{3,2,1,0:T(8,128)(2,1)}), s16[8,2,56,512]{3,2,1,0:T(8,128)(2,1)S(1)}, u32[]{:S(2)}, u32[]{:S(2)}) async-start(s16[8,2,56,512]{3,2,1,0:T(8,128)(2,1)} %get-tuple-element.32), calls=%async_computation.2 | async-start | bytes 1835008 | tf_op jit(solution)/shard_map/all_to_all | solution.py:517
  143.9 1.3 copy-start.12
  145.1 6.2 %copy-start.13 = (f32[2,448,512]{2,1,0:T(8,128)S(1)}, f32[2,448,512]{2,1,0:T(8,128)}, u32[]{:S(2)}) copy-start(f32[2,448,512]{2,1,0:T(8,128)} %copy-done.12) | copy-start | bytes 5505028
  146.2 23.0 %all-to-all-start.3 = ((s16[8,2,56,512]{3,2,1,0:T(8,128)(2,1)}), s16[8,2,56,512]{3,2,1,0:T(8,128)(2,1)}, u32[]{:S(2)}, u32[]{:S(2)}) async-start(s16[8,2,56,512]{3,2,1,0:T(8,128)(2,1)} %broadcast_in_dim.28), calls=%async_computation.3 | async-start | bytes 1835008 | tf_op jit(solution)/shard_map/all_to_all | solution.py:520
  167.9 1.3 copy-start.11
  174.1 2.9 %collective-permute-start.15 = (f32[2,84,448]{2,1,0:T(8,128)}, f32[2,84,448]{2,1,0:T(8,128)S(1)}, u32[]{:S(2)}, u32[]{:S(2)}) collective-permute-start(f32[2,84,448]{2,1,0:T(8,128)} %get-tuple-element.35), channel_id=1, source_target_pairs={{0,1},{1,0},{2,3},{3,2},{4,5},{5,4},{6,7},{7,6},{8,9},{9,8},{10,11... | collective-permute-start | bytes 903176 | tf_op jit(solution)/shard_map/ppermute | solution.py:523
